TPU v7x, 32 devices: a whole 2x2x4 slice. The times are simulated.
32 devices in a mesh: row: 4 (over z), col: 8 (over y, x, core).
Axes of the slice: x: 2, y: 2, z: 4, core: 2. Of those that a mesh axis runs over, the one named last changes fastest.
Arguments:
- features: bfloat16 [4096, 128], P(('row', 'col')), may hold values from -6 to 6
- deg_scale: bfloat16 [4096], P(('row', 'col')), may hold values from 0.049804688 to 0.5
- weight: bfloat16 [128, 256], replicated, may hold values from -0.5 to 0.5
- cotangent: bfloat16 [4096, 256], P(('row', 'col')), may hold values from -6 to 6
- tile_rows: int32 [4, 8, 8], P('row', 'col'), may hold values from 0 to 3, as said below
- tile_cols: int32 [4, 8, 8], P('row', 'col'), may hold values from 0 to 1, as said below
- tile_count: int32 [4, 8], P('row', 'col'), may hold values from 1 to 8, as said below
- tile_bits: int32 [4, 8, 8, 32, 256], P('row', 'col'), may hold values from 0 to 255, as said below
Outputs:
- activations: bfloat16 [4096, 256], P(('row', 'col'))
- input_grad: bfloat16 [4096, 128], P(('row', 'col'))
- weight_grad: float32 [128, 256], replicated
Inputs may be any that keep to these rules, and one draw needn't show every extreme that they name: The 8 slots of one block name distinct pairs (tile_rows, tile_cols). `tile_cols`: paired with tile_rows slot by slot. `tile_count`: some block fills all 8 slots. `tile_bits`: bit k of word [a, b] of a slot is the tile's entry in row 8 a + k and column b.
All inputs are finite; a program needn't handle non-finite values.
Results may differ from a plain program's by a relative error of at most 0.0065.
Values may be sent and summed in bfloat16 or wider, within the bound.
No kernel may reach another device: no remote copies, remote signals or barrier semaphores. Data moves between devices by JAX's collectives and lax.ppermute only.
A program may use at most 64 MiB of HBM per device.

v0:
```python
import math

import jax
import jax.numpy as jnp
from jax import lax
from jax.sharding import PartitionSpec as P


def unpack_tiles(packed):
    shifts = jnp.arange(8, dtype=jnp.int32)
    bit_values = jnp.bitwise_and(
        jnp.right_shift(packed[:, :, None, :], shifts[None, None, :, None]), 1
    )
    return bit_values.reshape(packed.shape[0], packed.shape[1] * 8, packed.shape[2]).astype(
        jnp.bfloat16
    )


def silu_slope(pre_act):
    sigmoid_value = jax.nn.sigmoid(pre_act)
    return sigmoid_value * (1.0 + pre_act * (1.0 - sigmoid_value))


def accumulate(source, packed, pick_ids, place_ids, live_count, places, forward, turn_count):
    per_block = 8
    feature_width = source.shape[-1]
    tile_size = packed.shape[-1]
    slot_ids = jnp.arange(per_block, dtype=jnp.int32)
    targets = jnp.arange(places, dtype=jnp.int32)

    def block_step(step_index, running):
        first_slot = step_index * per_block
        mask_tiles = unpack_tiles(lax.dynamic_slice_in_dim(packed, first_slot, per_block, 0))
        picked = jnp.take(
            source, lax.dynamic_slice_in_dim(pick_ids, first_slot, per_block, 0), axis=0
        )
        if forward:
            products = jnp.einsum(
                "sab,sbf->saf", mask_tiles, picked, preferred_element_type=jnp.float32
            )
        else:
            products = jnp.einsum(
                "sab,saf->sbf", mask_tiles, picked, preferred_element_type=jnp.float32
            )
        live_slots = (first_slot + slot_ids < live_count).astype(jnp.float32)
        chosen = lax.dynamic_slice_in_dim(place_ids, first_slot, per_block, 0)
        onehot = (chosen[None, :] == targets[:, None]).astype(jnp.float32) * live_slots[None, :]
        flat_products = products.reshape(per_block, tile_size * feature_width)
        return running + jnp.dot(
            onehot,
            flat_products,
            precision=lax.Precision.HIGHEST,
            preferred_element_type=jnp.float32,
        )

    initial = jnp.zeros((places, tile_size * feature_width), jnp.float32)
    running = lax.fori_loop(0, turn_count, block_step, initial)
    return running.reshape(places * tile_size, feature_width)


def on_device(features, deg_scale, weight, cotangent, tile_rows, tile_cols, tile_count, tile_bits):
    row_index = tile_rows[0, 0]
    col_index = tile_cols[0, 0]
    live_count = tile_count[0, 0]
    packed = tile_bits[0, 0]
    tile_size = packed.shape[-1]
    feature_width = features.shape[1]
    vertices = features.shape[0]
    row_shards = lax.axis_size("row")
    col_shards = lax.axis_size("col")
    row_tiles = col_shards * vertices // tile_size
    col_tiles = row_shards * vertices // tile_size
    total_verts = vertices * row_shards * col_shards
    turn_count = packed.shape[0] // 8
    scale = deg_scale.astype(jnp.float32)
    scaled = (features.astype(jnp.float32) * scale[:, None]).astype(jnp.bfloat16)
    column_block = lax.all_gather(scaled, "row", axis=0, tiled=True).reshape(
        col_tiles, tile_size, feature_width
    )
    partial_value = accumulate(
        column_block, packed, col_index, row_index, live_count, row_tiles, True, turn_count
    )
    summed = lax.psum_scatter(partial_value, "col", scatter_dimension=0, tiled=True)
    hidden = (summed * scale[:, None]).astype(jnp.bfloat16)
    pre_act = jnp.dot(hidden, weight, preferred_element_type=jnp.float32)
    activations = jax.nn.silu(pre_act).astype(jnp.bfloat16)
    slope_term = (cotangent.astype(jnp.float32) * silu_slope(pre_act)).astype(jnp.bfloat16)
    local_grad = lax.dot_general(
        hidden, slope_term, (((0,), (0,)), ((), ())), preferred_element_type=jnp.float32
    )
    weight_grad = lax.psum(local_grad, ("row", "col")) / math.sqrt(total_verts)
    spread = lax.dot_general(
        slope_term, weight, (((1,), (1,)), ((), ())), preferred_element_type=jnp.float32
    )
    back = (spread * scale[:, None]).astype(jnp.bfloat16)
    row_block = lax.all_gather(back, "col", axis=0, tiled=True)
    sources = row_block.reshape(row_tiles, tile_size, feature_width)
    partial_back = accumulate(
        sources, packed, row_index, col_index, live_count, col_tiles, False, turn_count
    )
    gathered_back = lax.psum_scatter(partial_back, "row", scatter_dimension=0, tiled=True)
    input_grad = (gathered_back * scale[:, None]).astype(jnp.bfloat16)
    return (activations, input_grad, weight_grad)


def solution(mesh):
    in_specs = (
        P(("row", "col"), None),
        P(("row", "col")),
        P(),
        P(("row", "col"), None),
        P("row", "col", None),
        P("row", "col", None),
        P("row", "col"),
        P("row", "col", None, None, None),
    )
    out_specs = (P(("row", "col"), None), P(("row", "col"), None), P())
    return jax.shard_map(
        on_device, mesh=mesh, in_specs=in_specs, out_specs=out_specs, check_vma=False
    )
```

profile of v0, /device:TPU:0, one launch (start us, length us, event | category | flops | bytes accessed | tf_op | source)
XLA Modules:
  0.0 224.1 jit_solution(11111529258616664839)
XLA Ops:
  7.2 0.0 copy-start
  7.2 0.0 copy-start.4
  7.2 0.0 reduce-scatter.3.cloned.1.call-start
  7.2 0.7 compare_and_fusion.1
  8.0 0.7 fusion.28
  9.3 0.7 convert_element_type.50
  9.9 0.1 shift_right_arithmetic.47
  10.0 0.8 multiply_convert_fusion.4
  10.9 15.1 %all_gather.6 = bf16[512,128]{1,0:T(8,128)(2,1)S(1)} all-gather(bf16[128,128]{1,0:T(8,128)(2,1)S(1)} %multiply_convert_fusion.4), channel_id=1, replica_groups=mesh['row'=4,'col'=8] {'row'}, dimensions={0}, use_global_device_ids=true | all-gather | bytes 163840 | tf_op jit(solution)/shard_map/all_gather | solution.py:77
  25.9 0.6 gather_fusion
  26.6 0.0 copy-done.4
  26.6 0.0 copy-start.2
  26.6 0.5 convolution_bitcast_fusion.1
  27.1 0.1 copy-done.2
  27.3 1.5 fusion.8
  28.7 0.0 copy-start.5
  28.8 1.2 reshape.114
  29.9 0.0 reduce-scatter.3.cloned.1.call-update
  29.9 0.0 all-reduce.2.cloned.1.call-start
  30.0 35.5 %reduce-scatter.3.cloned.1.call-done = f32[128,128]{1,0:T(8,128)} async-done(((f32[1024,128]{1,0:T(8,128)}), f32[128,128]{1,0:T(8,128)}) %reduce-scatter.3.cloned.1.call-update) | async-done | bytes 65552 | tf_op jit(solution)/shard_map/reduce_scatter | solution.py:83
  65.5 0.0 copy-done
  65.5 0.0 copy-done.5
  65.5 0.0 copy-start.1
  65.5 1.8 multiply_convert_fusion
  67.3 0.2 fusion.4
  67.5 0.0 copy-done.1
  67.5 0.9 fusion.39
  68.4 0.0 all-reduce.2.cloned.1.call-update
  68.5 0.0 reduce-scatter.5.cloned.1.call-start
  68.5 9.2 %all_gather.7 = bf16[1024,128]{1,0:T(8,128)(2,1)S(1)} all-gather(bf16[128,128]{1,0:T(8,128)(2,1)S(1)} %fusion.4), channel_id=1, replica_groups=mesh['row'=4,'col'=8] {'col'}, dimensions={0}, use_global_device_ids=true | all-gather | bytes 294912 | tf_op jit(solution)/shard_map/all_gather | solution.py:96
  77.7 0.6 gather_fusion.1
  78.4 0.0 copy-start.3
  78.4 0.6 convolution_bitcast_fusion
  79.1 0.0 copy-done.3
  79.1 1.5 fusion.5
  80.5 0.9 reshape.117
  81.5 0.0 reduce-scatter.5.cloned.1.call-update
  81.5 113.5 %all-reduce.2.cloned.1.call-done = f32[128,256]{1,0:T(8,128)} async-done(((f32[128,256]{1,0:T(8,128)}), f32[128,256]{1,0:T(8,128)}) %all-reduce.2.cloned.1.call-update) | async-done | bytes 131088 | tf_op jit(solution)/shard_map/psum | solution.py:91
  195.0 1.6 broadcast_multiply_fusion
  196.6 19.5 %reduce-scatter.5.cloned.1.call-done = f32[128,128]{1,0:T(8,128)} async-done(((f32[512,128]{1,0:T(8,128)}), f32[128,128]{1,0:T(8,128)}) %reduce-scatter.5.cloned.1.call-update) | async-done | bytes 65552 | tf_op jit(solution)/shard_map/reduce_scatter | solution.py:101
  216.1 1.5 multiply_convert_fusion.2
  (6 shorter events, 0.0 us)
Async XLA Ops:
  7.2 58.4 %copy-start = (bf16[128,256]{1,0:T(8,128)(2,1)S(1)}, bf16[128,256]{1,0:T(8,128)(2,1)}, u32[]{:S(2)}) copy-start(bf16[128,256]{1,0:T(8,128)(2,1)} %param.10) | copy-start | bytes 196612
  7.2 19.4 %copy-start.4 = (s32[1,1,8,32,256]{4,3,2,1,0:T(8,128)S(1)}, s32[1,1,8,32,256]{4,3,2,1,0:T(8,128)}, u32[]{:S(2)}) copy-start(s32[1,1,8,32,256]{4,3,2,1,0:T(8,128)} %param.15) | copy-start | bytes 786436
  7.2 58.3 %reduce-scatter.3.cloned.1.call-start = ((), (), s32[]{:S(2)}) async-start(), calls=%async_computation.2 | async-start | bytes 589824 | tf_op jit(solution)/shard_map/reduce_scatter | solution.py:83
  26.6 0.7 copy-start.2
  28.7 36.8 %copy-start.5 = (bf16[128,256]{1,0:T(8,128)(2,1)S(1)}, bf16[128,256]{1,0:T(8,128)(2,1)}, u32[]{:S(2)}) copy-start(bf16[128,256]{1,0:T(8,128)(2,1)} %param.11) | copy-start | bytes 196612
  29.9 165.0 %all-reduce.2.cloned.1.call-start = ((), (), s32[]{:S(2)}) async-start(), calls=%async_computation.4 | async-start | bytes 262144 | tf_op jit(solution)/shard_map/psum | solution.py:91
  65.5 2.0 copy-start.1
  68.5 147.6 %reduce-scatter.5.cloned.1.call-start = ((), (), s32[]{:S(2)}) async-start(), calls=%async_computation.3 | async-start | bytes 327680 | tf_op jit(solution)/shard_map/reduce_scatter | solution.py:101
  78.4 0.7 copy-start.3
Sparse Core Ops, SparseCore 0:
  30.1 35.4 reduce-scatter.2
  72.5 122.3 all-reduce.1
  197.3 18.6 reduce-scatter.4
where the time goes:
time: 225 us; the launch traced here: 224 us
  waiting for transfers between devices  169 us (75%)
  blocking collectives  24.3 us (11%)
  between operations  14.5 us (6%)
  matrix products  6.99 us (3%)
  other arithmetic  6 us (3%)
  local copies, waits for them, and re-layouts  3.63 us (2%)
    psum x1, waiting for transfers between devices, on_device(): weight_grad = lax.psum(local_grad, ('row', 'col')) / math.sqrt(total_verts)  113 us
    reduce_scatter x1, waiting for transfers between devices, on_device(): lax.psum_scatter(partial_value, 'col', scatter_dimension=0, tiled=True)  35.5 us
    reduce_scatter x1, waiting for transfers between devices, on_device(): lax.psum_scatter(partial_back, 'row', scatter_dimension=0, tiled=True)  19.5 us
    all_gather x1, blocking collectives, on_device(): lax.all_gather(scaled, 'row', axis=0, tiled=True)  15.1 us
    all_gather x1, blocking collectives, on_device(): row_block = lax.all_gather(back, 'col', axis=0, tiled=True)  9.23 us
  transfers between devices with their start and end apart: 3, of which 3 were waited for; matrix products, arithmetic and copies ran while one was open for 2% of the time, Pallas kernels for 0%

commit v1 on v0

v1 whole, which is shorter than its diff:
```python
import functools
import math

import jax
import jax.numpy as jnp
from jax import lax
from jax.experimental import pallas as pl
from jax.experimental.pallas import tpu as pltpu
from jax.sharding import PartitionSpec as P

VMEM = pl.BlockSpec(memory_space=pltpu.VMEM)
SMEM = pl.BlockSpec(memory_space=pltpu.SMEM)
LIMIT = pltpu.CompilerParams(vmem_limit_bytes=40 * 1024 * 1024)
DIRECT = 4
AXES = ("row", "col")


def struct(shape, dtype):
    return jax.ShapeDtypeStruct(shape, dtype)


def call(body, out_shape, operands, specs=None, scratch=(), flops=1 << 20, moved=1 << 20):
    single = not isinstance(out_shape, (tuple, list))
    return pl.pallas_call(
        body,
        out_shape=out_shape,
        in_specs=specs or [VMEM] * len(operands),
        out_specs=VMEM if single else [VMEM] * len(out_shape),
        scratch_shapes=list(scratch),
        compiler_params=LIMIT,
        cost_estimate=pl.CostEstimate(flops=flops, bytes_accessed=moved, transcendentals=0),
    )(*operands)


def scale_features(deg_ref, features_ref, scaled_ref, column_ref):
    size = features_ref.shape[0]
    scale_row = deg_ref[...].astype(jnp.float32)
    rows = lax.broadcasted_iota(jnp.int32, (size, size), 0)
    columns = lax.broadcasted_iota(jnp.int32, (size, size), 1)
    diagonal = jnp.where(rows == columns, scale_row, 0.0).astype(jnp.bfloat16)
    spread = jnp.dot(
        diagonal, jnp.ones((size, size), jnp.bfloat16), preferred_element_type=jnp.float32
    )
    column_ref[...] = spread
    scaled_ref[...] = (features_ref[...].astype(jnp.float32) * spread).astype(jnp.bfloat16)


def unpack_tiles(count_ref, bits_ref, after_ref, masks_ref):
    slots, words, tile_size = bits_ref.shape[2:]
    live_count = count_ref[0, 0]

    def one(slot):
        packed = jnp.where(slot < live_count, bits_ref[0, 0, slot], 0)
        repeated = jnp.broadcast_to(packed[:, None, :], (words, 8, tile_size))
        shifts = lax.broadcasted_iota(jnp.int32, (words, 8, tile_size), 1)
        bit_values = jnp.bitwise_and(jnp.right_shift(repeated, shifts), 1)
        masks_ref[slot] = (
            bit_values.reshape(words * 8, tile_size).astype(jnp.float32).astype(jnp.bfloat16)
        )

    each_slot(slots, one)


def each_slot(slots, one):
    if slots <= 8:
        for slot in range(slots):
            one(slot)
    else:
        pl.loop(0, slots)(one)


def forward_partial(me_ref, rows_ref, cols_ref, masks_ref, *refs):
    *blocks, partial_ref, source, total = refs
    slots, tile_size = masks_ref.shape[:2]
    place_blocks(me_ref, blocks, source)
    total[...] = jnp.zeros_like(total)

    def one(slot):
        place = pl.ds(pl.multiple_of(rows_ref[0, 0, slot] * tile_size, tile_size), tile_size)
        pick = pl.ds(pl.multiple_of(cols_ref[0, 0, slot] * tile_size, tile_size), tile_size)
        total[place, :] += jnp.dot(
            masks_ref[slot], source[pick, :], preferred_element_type=jnp.float32
        )

    each_slot(slots, one)
    partial_ref[...] = total[...].astype(jnp.bfloat16).reshape(partial_ref.shape)


def place_blocks(me_ref, blocks, source):
    if len(blocks) == 1:
        source[...] = blocks[0][...].reshape(source.shape)
        return
    shards, size = len(blocks), blocks[0].shape[0]
    for step, block in enumerate(blocks):
        owner = lax.rem(me_ref[0] + shards - step, shards)
        source[pl.ds(pl.multiple_of(owner * size, size), size), :] = block[...]


def vertex_part(received_ref, column_ref, deg_ref, weight_ref, cotangent_ref, act_ref, back_ref, grad_ref):
    summed = jnp.sum(received_ref[...].astype(jnp.float32), axis=0)
    hidden = (summed * column_ref[...]).astype(jnp.bfloat16)
    weight = weight_ref[...]
    pre_act = jnp.dot(hidden, weight, preferred_element_type=jnp.float32)
    sigmoid_value = 1.0 / (1.0 + jnp.exp(-pre_act))
    act_ref[...] = (pre_act * sigmoid_value).astype(jnp.bfloat16)
    slope = sigmoid_value * (1.0 + pre_act * (1.0 - sigmoid_value))
    slope_term = (cotangent_ref[...].astype(jnp.float32) * slope).astype(jnp.bfloat16)
    spread = lax.dot_general(
        weight, slope_term, (((1,), (1,)), ((), ())), preferred_element_type=jnp.float32
    )
    back = (spread * deg_ref[...].astype(jnp.float32)).astype(jnp.bfloat16)
    back_ref[...] = jnp.broadcast_to(back[None], back_ref.shape)
    local_grad = lax.dot_general(
        hidden, slope_term, (((0,), (0,)), ((), ())), preferred_element_type=jnp.float32
    )
    for half in range(grad_ref.shape[0]):
        grad_ref[half] = local_grad[:, half * 128 : (half + 1) * 128]


def backward_partial(me_ref, rows_ref, cols_ref, masks_ref, gathered_ref, *refs):
    *pieces, source, total = refs
    slots, tile_size = masks_ref.shape[:2]
    shards, _, size = gathered_ref.shape
    for shard in range(shards):
        source[:, shard * size : (shard + 1) * size] = gathered_ref[shard]
    total[...] = jnp.zeros_like(total)

    def one(slot):
        pick = pl.ds(pl.multiple_of(rows_ref[0, 0, slot] * tile_size, tile_size), tile_size)
        place = pl.ds(pl.multiple_of(cols_ref[0, 0, slot] * tile_size, tile_size), tile_size)
        total[:, place] += jnp.dot(
            source[:, pick], masks_ref[slot], preferred_element_type=jnp.float32
        )

    each_slot(slots, one)
    if len(pieces) == 1:
        for shard in range(pieces[0].shape[0]):
            pieces[0][shard] = total[:, shard * size : (shard + 1) * size].astype(jnp.bfloat16)
        return
    for step, piece in enumerate(pieces):
        owner = lax.rem(me_ref[0] + step, len(pieces))
        place = pl.ds(pl.multiple_of(owner * size, size), size)
        piece[...] = total[:, place].astype(jnp.bfloat16)


def input_part(deg_ref, *refs):
    *pieces, out_ref = refs
    if len(pieces) == 1:
        total = jnp.sum(pieces[0][...].astype(jnp.float32), axis=0)
    else:
        total = sum(piece[...].astype(jnp.float32) for piece in pieces)
    out_ref[...] = (total * deg_ref[...].astype(jnp.float32)).T.astype(jnp.bfloat16)


def sum_pieces(factor, received_ref, out_ref):
    total = jnp.sum(received_ref[...], axis=0) * factor
    out_ref[...] = jnp.broadcast_to(total[None], out_ref.shape)


def join_halves(whole_ref, out_ref):
    for half in range(whole_ref.shape[0]):
        out_ref[:, half * 128 : (half + 1) * 128] = whole_ref[half]


def shifted(block, axis, shards, step):
    return lax.ppermute(block, axis, [(source, (source + step) % shards) for source in range(shards)])


def on_device(features, deg_scale, weight, cotangent, tile_rows, tile_cols, tile_count, tile_bits):
    size, width = features.shape
    height, out_width = weight.shape
    row_shards = lax.axis_size("row")
    col_shards = lax.axis_size("col")
    devices = row_shards * col_shards
    total_verts = devices * size
    slots, words, tile_size = tile_bits.shape[2:]
    direct = row_shards <= DIRECT
    bf16, f32 = jnp.bfloat16, jnp.float32
    me = lax.axis_index("row").astype(jnp.int32).reshape(1)
    deg_row = deg_scale.reshape(1, size)
    factor = 1.0 / math.sqrt(total_verts)

    scaled, column = call(
        scale_features,
        (struct((size, width), bf16), struct((size, width), f32)),
        (deg_row, features),
    )
    if direct:
        blocks = [scaled] + [shifted(scaled, "row", row_shards, step) for step in range(1, row_shards)]
    else:
        blocks = [lax.all_gather(scaled, "row", axis=0, tiled=True)]
    masks = call(
        unpack_tiles,
        struct((slots, tile_size, tile_size), bf16),
        (tile_count, tile_bits, column),
        [SMEM, VMEM, pl.BlockSpec(memory_space=pl.ANY)],
        flops=1 << 28,
        moved=1 << 21,
    )
    indices = (me, tile_rows, tile_cols, masks)
    partial_value = call(
        forward_partial,
        struct((col_shards, size, width), bf16),
        indices + tuple(blocks),
        [SMEM] * 3 + [VMEM] * (1 + len(blocks)),
        [
            pltpu.VMEM((row_shards * size, width), bf16),
            pltpu.VMEM((col_shards * size, width), f32),
        ],
    )
    received = lax.all_to_all(partial_value, "col", 0, 0)
    halves = out_width // 128
    activations, back, local_grad = call(
        vertex_part,
        (
            struct((size, out_width), bf16),
            struct((col_shards, width, size), bf16),
            struct((halves, height, 128), f32),
        ),
        (received, column, deg_row, weight, cotangent),
    )
    gathered = lax.all_to_all(back, "col", 0, 0)
    scratch = [
        pltpu.VMEM((width, col_shards * size), bf16),
        pltpu.VMEM((width, row_shards * size), f32),
    ]
    if direct:
        piece_shapes = (struct((width, size), bf16),) * row_shards
    else:
        piece_shapes = (struct((row_shards, width, size), bf16),)
    pieces = call(
        backward_partial,
        piece_shapes,
        indices + (gathered,),
        [SMEM] * 3 + [VMEM] * 2,
        scratch,
    )
    if direct:
        arrived = [pieces[0]] + [
            shifted(pieces[step], "row", row_shards, step) for step in range(1, row_shards)
        ]
    else:
        arrived = [lax.all_to_all(pieces[0], "row", 0, 0)]
    input_grad = call(input_part, struct((size, width), bf16), (deg_row, *arrived))

    if height * out_width % (devices * 1024):
        whole = lax.psum(local_grad, AXES) * factor
    else:
        sent = lax.all_to_all(local_grad.reshape(devices, -1, 128), AXES, 0, 0)
        own = call(functools.partial(sum_pieces, factor), struct(sent.shape, f32), (sent,))
        whole = lax.all_to_all(own, AXES, 0, 0).reshape(halves, height, 128)
    weight_grad = call(join_halves, struct((height, out_width), f32), (whole,))
    return (activations, input_grad, weight_grad)


def solution(mesh):
    in_specs = (
        P(("row", "col"), None),
        P(("row", "col")),
        P(),
        P(("row", "col"), None),
        P("row", "col", None),
        P("row", "col", None),
        P("row", "col"),
        P("row", "col", None, None, None),
    )
    out_specs = (P(("row", "col"), None), P(("row", "col"), None), P())
    return jax.shard_map(
        on_device, mesh=mesh, in_specs=in_specs, out_specs=out_specs, check_vma=False
    )
```

time: 225 us -> 59.5 us (0.26)
  waiting for transfers between devices: 169 us -> 11.5 us
  starting transfers between devices: 0.12 us -> 17.7 us
  between operations: 14.5 us -> 1.38 us
  matrix products: 6.99 us -> 0 us
  other arithmetic: 6 us -> 0 us
  Pallas kernels: 0 us -> 5.62 us
  blocking collectives: 24.3 us -> 20.5 us
    psum x1 -> x0, waiting for transfers between devices: 113 us -> none  [on_device(): weight_grad = lax.psum(local_grad, ('row', 'col')) / math.sqrt(total_verts)]
    reduce_scatter x2 -> x0, waiting for transfers between devices: 55 us -> none  [the longest x1 35.5 us: on_device(): lax.psum_scatter(partial_value, 'col', scatter_dimension=0, tiled=True)]
    all_gather x2 -> x0, blocking collectives: 24.3 us -> none  [the longest x1 15.1 us: on_device(): lax.all_gather(scaled, 'row', axis=0, tiled=True)]
    all_to_all x0 -> x2, blocking collectives: none -> 20.5 us  [the longest x1 10.6 us: on_device(): received = lax.all_to_all(partial_value, 'col', 0, 0)]
    ppermute x0 -> x6, starting transfers between devices: none -> 11.7 us  [shifted(): lax.ppermute(block, axis, [(source, (source + step) % shards) for source...]
    dot_general x7 -> x0, matrix products: 6.99 us -> none  [the longest x2 2.96 us: block_step(): jnp.dot(onehot, flat_products, precision=lax.Precision.HIGHEST, preferred...]
    all_to_all x0 -> x2, waiting for transfers between devices: none -> 6.17 us  [the longest x1 6.17 us: on_device(): gathered = lax.all_to_all(back, 'col', 0, 0)]
    all_to_all x0 -> x2, starting transfers between devices: none -> 5.99 us  [the longest x1 3.41 us: on_device(): gathered = lax.all_to_all(back, 'col', 0, 0)]
  transfers between devices with their start and end apart: 3 -> 8, of which waited for: 3 -> 6; matrix products, arithmetic and copies ran while one was open for 2% -> 0% of each run, Pallas kernels for 0% -> 5%
where the time goes in v1:
time: 59.5 us; the launch traced here: 59.1 us
  blocking collectives  20.5 us (34%)
  starting transfers between devices  17.7 us (30%)
  waiting for transfers between devices  11.5 us (19%)
  Pallas kernels  5.62 us (9%)
  local copies, waits for them, and re-layouts  2.38 us (4%)
  between operations  1.38 us (2%)
    ppermute x6, starting transfers between devices, shifted(): lax.ppermute(block, axis, [(source, (source + step) % shards) for source...  11.7 us
    all_to_all x1, blocking collectives, on_device(): received = lax.all_to_all(partial_value, 'col', 0, 0)  10.6 us
    all_to_all x1, blocking collectives, on_device(): sent = lax.all_to_all(local_grad.reshape(devices, -1, 128), AXES, 0, 0)  9.92 us
    all_to_all x1, waiting for transfers between devices, on_device(): gathered = lax.all_to_all(back, 'col', 0, 0)  6.17 us
    pallas_call x8, Pallas kernels, call(): pl.pallas_call(body, out_shape=out_shape, in_specs=specs or [VMEM] * len(...  5.62 us
    ppermute x6, waiting for transfers between devices, shifted(): lax.ppermute(block, axis, [(source, (source + step) % shards) for source...  5.3 us
    all_to_all x1, starting transfers between devices, on_device(): gathered = lax.all_to_all(back, 'col', 0, 0)  3.41 us
    all_to_all x1, starting transfers between devices, on_device(): whole = lax.all_to_all(own, AXES, 0, 0).reshape(halves, height, 128)  2.58 us
  transfers between devices with their start and end apart: 8, of which 6 were waited for; matrix products, arithmetic and copies ran while one was open for 0% of the time, Pallas kernels for 5%

profile of v1, /device:TPU:0, one launch (start us, length us, event | category | flops | bytes accessed | tf_op | source)
XLA Modules:
  0.0 59.1 jit_solution(14084550491325241894)
XLA Ops:
  0.6 0.0 copy-start.4
  0.6 0.6 %copy-done.4 = bf16[128]{0:T(256)(128)(2,1)S(1)} copy-done((bf16[128]{0:T(256)(128)(2,1)S(1)}, bf16[128]{0:T(256)(128)(2,1)}, u32[]{:S(2)}) %copy-start.4) | copy-done | bytes 280
  1.3 0.0 copy-start.3
  1.3 0.8 %copy-done.3 = bf16[128,128]{1,0:T(8,128)(2,1)S(1)} copy-done((bf16[128,128]{1,0:T(8,128)(2,1)S(1)}, bf16[128,128]{1,0:T(8,128)(2,1)}, u32[]{:S(2)}) %copy-start.3) | copy-done | bytes 32792
  2.0 0.1 shard_map.103
  2.2 5.1 %collective-permute-start.2 = (bf16[128,128]{1,0:T(8,128)(2,1)S(1)}, bf16[128,128]{1,0:T(8,128)(2,1)S(1)}, u32[]{:S(2)}, u32[]{:S(2)}) collective-permute-start(bf16[128,128]{1,0:T(8,128)(2,1)S(1)} %get-tuple-element.13.refs_0_), channel_id=1, source_target_pairs={{0,24},{8,0},{16,8},{24,16},{1,25},{9,1},{17,9},{25,17},{2,26},{10... | collective-permute-start | bytes 98312 | tf_op jit(solution)/shard_map/ppermute | solution.py:166
  7.3 0.0 collective-permute-start.1
  7.3 1.0 %collective-permute-start = (bf16[128,128]{1,0:T(8,128)(2,1)S(1)}, bf16[128,128]{1,0:T(8,128)(2,1)S(1)}, u32[]{:S(2)}, u32[]{:S(2)}) collective-permute-start(bf16[128,128]{1,0:T(8,128)(2,1)S(1)} %get-tuple-element.13.refs_0_), channel_id=1, source_target_pairs={{0,8},{8,16},{16,24},{24,0},{1,9},{9,17},{17,25},{25,1},{2,10},{10... | collective-permute-start | bytes 98312 | tf_op jit(solution)/shard_map/ppermute | solution.py:166
  8.9 0.0 copy-start
  8.9 0.9 %copy-done = s32[1,1,8,32,256]{4,3,2,1,0:T(8,128)S(1)} copy-done((s32[1,1,8,32,256]{4,3,2,1,0:T(8,128)S(1)}, s32[1,1,8,32,256]{4,3,2,1,0:T(8,128)}, u32[]{:S(2)}) %copy-start) | copy-done | bytes 262168
  9.9 0.4 shard_map.104.masks_ref
  10.2 0.0 copy-start.5
  10.2 0.0 copy-start.6
  10.3 0.0 collective-permute-done.2.refs_3_
  10.3 1.8 %collective-permute-done.1.refs_2_ = bf16[128,128]{1,0:T(8,128)(2,1)S(1)} collective-permute-done((bf16[128,128]{1,0:T(8,128)(2,1)S(1)}, bf16[128,128]{1,0:T(8,128)(2,1)S(1)}, u32[]{:S(2)}, u32[]{:S(2)}) %collective-permute-start.1) | collective-permute-done | bytes 32800 | tf_op jit(solution)/shard_map/ppermute | solution.py:166
  12.1 0.9 %collective-permute-done.refs_1_ = bf16[128,128]{1,0:T(8,128)(2,1)S(1)} collective-permute-done((bf16[128,128]{1,0:T(8,128)(2,1)S(1)}, bf16[128,128]{1,0:T(8,128)(2,1)S(1)}, u32[]{:S(2)}, u32[]{:S(2)}) %collective-permute-start) | collective-permute-done | bytes 32800 | tf_op jit(solution)/shard_map/ppermute | solution.py:166
  13.0 0.0 copy-done.5
  13.0 0.0 copy-done.6
  13.0 1.0 %shard_map.105 = bf16[8,128,128]{2,1,0:T(8,128)(2,1)S(1)} custom-call(s32[1]{0:T(128)} %bitcast.me_ref, s32[1,1,8]{2,1,0:T(1,128)S(1)} %copy-done.5, s32[1,1,8]{2,1,0:T(1,128)S(1)} %copy-done.6, bf16[8,256,256]{2,1,0:T(8,128)(2,1)S(1)} %shard_map.104.masks_ref, bf16[128,128]{1,0:T(8,128)(2,1)S(1)} %get-tuple-element.13.refs_0_, ...), custom_call_target="tpu_custom_call" | custom-call | flops 1048576 | bytes 1048576 | tf_op jit(solution)/shard_map/pallas_call | solution.py:24
  14.0 0.0 copy-start.1
  14.0 0.0 copy-start.2
  14.0 10.6 %all_to_all.20.received_ref = bf16[8,128,128]{2,1,0:T(8,128)(2,1)S(1)} all-to-all(bf16[8,128,128]{2,1,0:T(8,128)(2,1)S(1)} %shard_map.105), channel_id=1, replica_groups=mesh['row'=4,'col'=8] {'col'}, dimensions={0} | all-to-all | bytes 524288 | tf_op jit(solution)/shard_map/all_to_all | solution.py:211
  24.6 0.0 copy-done.1
  24.6 0.0 copy-done.2
  24.6 1.1 %shard_map.106 = (bf16[128,256]{1,0:T(8,128)(2,1)}, bf16[8,128,128]{2,1,0:T(8,128)(2,1)}, f32[2,128,128]{2,1,0:T(8,128)S(1)}) custom-call(bf16[8,128,128]{2,1,0:T(8,128)(2,1)S(1)} %all_to_all.20.received_ref, f32[128,128]{1,0:T(8,128)S(1)} %get-tuple-element.12.after_ref.column_ref, bf16[1,128]{1,0:T(2,128)(2,1)S(1)} %bitcast.7, ...), custom_call_target="tpu_custom_call" | custom-call | flops 1048576 | bytes 1048576 | tf_op jit(solution)/shard_map/pallas_call | solution.py:24
  25.7 9.9 %all_to_all.21.received_ref = f32[32,8,128]{2,1,0:T(8,128)S(1)} all-to-all(f32[32,8,128]{2,1,0:T(8,128)S(1)} %bitcast.5), channel_id=1, replica_groups=mesh['row'=4,'col'=8] {'row','col'}, dimensions={0} | all-to-all | bytes 262144 | tf_op jit(solution)/shard_map/all_to_all | solution.py:249
  35.6 3.4 %all-to-all-start.1 = ((bf16[8,128,128]{2,1,0:T(8,128)(2,1)}), bf16[8,128,128]{2,1,0:T(8,128)(2,1)S(1)}, u32[]{:S(2)}, u32[]{:S(2)}) async-start(bf16[8,128,128]{2,1,0:T(8,128)(2,1)} %get-tuple-element.15), calls=%async_computation.1 | async-start | bytes 524288 | tf_op jit(solution)/shard_map/all_to_all | solution.py:222
  39.0 0.7 %shard_map.109 = f32[32,8,128]{2,1,0:T(8,128)} custom-call(f32[32,8,128]{2,1,0:T(8,128)S(1)} %all_to_all.21.received_ref), custom_call_target="tpu_custom_call" | custom-call | flops 1048576 | bytes 1048576 | tf_op jit(solution)/shard_map/pallas_call | solution.py:24
  39.7 6.2 %all-to-all-done.1.gathered_ref = bf16[8,128,128]{2,1,0:T(8,128)(2,1)S(1)} async-done(((bf16[8,128,128]{2,1,0:T(8,128)(2,1)}), bf16[8,128,128]{2,1,0:T(8,128)(2,1)S(1)}, u32[]{:S(2)}, u32[]{:S(2)}) %all-to-all-start.1) | async-done | bytes 262176 | tf_op jit(solution)/shard_map/all_to_all | solution.py:222
  45.9 2.6 %all-to-all-start.3 = ((f32[32,8,128]{2,1,0:T(8,128)}), f32[32,8,128]{2,1,0:T(8,128)S(1)}, u32[]{:S(2)}, u32[]{:S(2)}) async-start(f32[32,8,128]{2,1,0:T(8,128)} %shard_map.109), calls=%async_computation.3 | async-start | bytes 262144 | tf_op jit(solution)/shard_map/all_to_all | solution.py:251
  48.5 1.0 %shard_map.107 = (bf16[128,128]{1,0:T(8,128)(2,1)S(1)}, bf16[128,128]{1,0:T(8,128)(2,1)S(1)}, bf16[128,128]{1,0:T(8,128)(2,1)S(1)}, bf16[128,128]{1,0:T(8,128)(2,1)S(1)}) custom-call(s32[1]{0:T(128)} %bitcast.me_ref, s32[1,1,8]{2,1,0:T(1,128)S(1)} %copy-done.5, s32[1,1,8]{2,1,0:T(1,128)S(1)} %copy-done.6, bf16[8,256,256]{2,1,0:T(8,128)(2,1)S(1)} %shard_map.104.masks_ref, ...), custom_call_target="tpu_custom_call" | custom-call | flops 1048576 | bytes 1048576 | tf_op jit(solution)/shard_map/pallas_call | solution.py:24
  49.4 1.7 %collective-permute-start.3 = (bf16[128,128]{1,0:T(8,128)(2,1)S(1)}, bf16[128,128]{1,0:T(8,128)(2,1)S(1)}, u32[]{:S(2)}, u32[]{:S(2)}) collective-permute-start(bf16[128,128]{1,0:T(8,128)(2,1)S(1)} %get-tuple-element.17), channel_id=1, source_target_pairs={{0,8},{8,16},{16,24},{24,0},{1,9},{9,17},{17,25},{25,1},{2,10},{10... | collective-permute-start | bytes 98312 | tf_op jit(solution)/shard_map/ppermute | solution.py:166
  51.2 2.5 %collective-permute-start.4 = (bf16[128,128]{1,0:T(8,128)(2,1)S(1)}, bf16[128,128]{1,0:T(8,128)(2,1)S(1)}, u32[]{:S(2)}, u32[]{:S(2)}) collective-permute-start(bf16[128,128]{1,0:T(8,128)(2,1)S(1)} %get-tuple-element.18), channel_id=1, source_target_pairs={{0,16},{8,24},{16,0},{24,8},{1,17},{9,25},{17,1},{25,9},{2,18},{10... | collective-permute-start | bytes 98312 | tf_op jit(solution)/shard_map/ppermute | solution.py:166
  53.7 1.4 %collective-permute-start.5 = (bf16[128,128]{1,0:T(8,128)(2,1)S(1)}, bf16[128,128]{1,0:T(8,128)(2,1)S(1)}, u32[]{:S(2)}, u32[]{:S(2)}) collective-permute-start(bf16[128,128]{1,0:T(8,128)(2,1)S(1)} %get-tuple-element.19), channel_id=1, source_target_pairs={{0,24},{8,0},{16,8},{24,16},{1,25},{9,1},{17,9},{25,17},{2,26},{10... | collective-permute-start | bytes 98312 | tf_op jit(solution)/shard_map/ppermute | solution.py:166
  55.1 1.5 %collective-permute-done.3.refs_1_ = bf16[128,128]{1,0:T(8,128)(2,1)S(1)} collective-permute-done((bf16[128,128]{1,0:T(8,128)(2,1)S(1)}, bf16[128,128]{1,0:T(8,128)(2,1)S(1)}, u32[]{:S(2)}, u32[]{:S(2)}) %collective-permute-start.3) | collective-permute-done | bytes 32800 | tf_op jit(solution)/shard_map/ppermute | solution.py:166
  56.6 0.8 %collective-permute-done.4.refs_2_ = bf16[128,128]{1,0:T(8,128)(2,1)S(1)} collective-permute-done((bf16[128,128]{1,0:T(8,128)(2,1)S(1)}, bf16[128,128]{1,0:T(8,128)(2,1)S(1)}, u32[]{:S(2)}, u32[]{:S(2)}) %collective-permute-start.4) | collective-permute-done | bytes 32800 | tf_op jit(solution)/shard_map/ppermute | solution.py:166
  57.4 0.3 collective-permute-done.5.refs_3_
  57.7 0.7 %shard_map.108 = bf16[128,128]{1,0:T(8,128)(2,1)} custom-call(bf16[1,128]{1,0:T(2,128)(2,1)S(1)} %bitcast.8, bf16[128,128]{1,0:T(8,128)(2,1)S(1)} %get-tuple-element.16.refs_0_, bf16[128,128]{1,0:T(8,128)(2,1)S(1)} %collective-permute-done.3.refs_1_, bf16[128,128]{1,0:T(8,128)(2,1)S(1)} %collective-permute-done.4.refs_2_, ...), custom_call_target="tpu_custom_call" | custom-call | flops 1048576 | bytes 1048576 | tf_op jit(solution)/shard_map/pallas_call | solution.py:24
  58.4 0.0 all-to-all-done.3
  58.4 0.7 %shard_map.110 = f32[128,256]{1,0:T(8,128)} custom-call(f32[2,128,128]{2,1,0:T(8,128)S(1)} %bitcast.4), custom_call_target="tpu_custom_call" | custom-call | flops 1048576 | bytes 1048576 | tf_op jit(solution)/shard_map/pallas_call | solution.py:24
Async XLA Ops:
  0.6 0.7 %copy-start.4 = (bf16[128]{0:T(256)(128)(2,1)S(1)}, bf16[128]{0:T(256)(128)(2,1)}, u32[]{:S(2)}) copy-start(bf16[128]{0:T(256)(128)(2,1)} %param.9) | copy-start | bytes 772
  1.3 0.8 %copy-start.3 = (bf16[128,128]{1,0:T(8,128)(2,1)S(1)}, bf16[128,128]{1,0:T(8,128)(2,1)}, u32[]{:S(2)}) copy-start(bf16[128,128]{1,0:T(8,128)(2,1)} %features_ref.1) | copy-start | bytes 98308
  2.2 8.1 %collective-permute-start.2 = (bf16[128,128]{1,0:T(8,128)(2,1)S(1)}, bf16[128,128]{1,0:T(8,128)(2,1)S(1)}, u32[]{:S(2)}, u32[]{:S(2)}) collective-permute-start(bf16[128,128]{1,0:T(8,128)(2,1)S(1)} %get-tuple-element.13.refs_0_), channel_id=1, source_target_pairs={{0,24},{8,0},{16,8},{24,16},{1,25},{9,1},{17,9},{25,17},{2,26},{10... | collective-permute-start | bytes 98312 | tf_op jit(solution)/shard_map/ppermute | solution.py:166
  7.3 4.8 %collective-permute-start.1 = (bf16[128,128]{1,0:T(8,128)(2,1)S(1)}, bf16[128,128]{1,0:T(8,128)(2,1)S(1)}, u32[]{:S(2)}, u32[]{:S(2)}) collective-permute-start(bf16[128,128]{1,0:T(8,128)(2,1)S(1)} %get-tuple-element.13.refs_0_), channel_id=1, source_target_pairs={{0,16},{8,24},{16,0},{24,8},{1,17},{9,25},{17,1},{25,9},{2,18},{10... | collective-permute-start | bytes 98312 | tf_op jit(solution)/shard_map/ppermute | solution.py:166
  7.3 5.7 %collective-permute-start = (bf16[128,128]{1,0:T(8,128)(2,1)S(1)}, bf16[128,128]{1,0:T(8,128)(2,1)S(1)}, u32[]{:S(2)}, u32[]{:S(2)}) collective-permute-start(bf16[128,128]{1,0:T(8,128)(2,1)S(1)} %get-tuple-element.13.refs_0_), channel_id=1, source_target_pairs={{0,8},{8,16},{16,24},{24,0},{1,9},{9,17},{17,25},{25,1},{2,10},{10... | collective-permute-start | bytes 98312 | tf_op jit(solution)/shard_map/ppermute | solution.py:166
  8.9 1.0 %copy-start = (s32[1,1,8,32,256]{4,3,2,1,0:T(8,128)S(1)}, s32[1,1,8,32,256]{4,3,2,1,0:T(8,128)}, u32[]{:S(2)}) copy-start(s32[1,1,8,32,256]{4,3,2,1,0:T(8,128)} %bits_ref.1) | copy-start | bytes 786436
  10.2 2.7 %copy-start.5 = (s32[1,1,8]{2,1,0:T(1,128)S(1)}, s32[1,1,8]{2,1,0:T(1,128)}, u32[]{:S(2)}) copy-start(s32[1,1,8]{2,1,0:T(1,128)} %rows_ref.3) | copy-start | bytes 100
  10.2 2.7 %copy-start.6 = (s32[1,1,8]{2,1,0:T(1,128)S(1)}, s32[1,1,8]{2,1,0:T(1,128)}, u32[]{:S(2)}) copy-start(s32[1,1,8]{2,1,0:T(1,128)} %cols_ref.3) | copy-start | bytes 100
  14.0 10.6 %copy-start.1 = (bf16[128,256]{1,0:T(8,128)(2,1)S(1)}, bf16[128,256]{1,0:T(8,128)(2,1)}, u32[]{:S(2)}) copy-start(bf16[128,256]{1,0:T(8,128)(2,1)} %weight_ref.1) | copy-start | bytes 196612
  14.0 10.6 %copy-start.2 = (bf16[128,256]{1,0:T(8,128)(2,1)S(1)}, bf16[128,256]{1,0:T(8,128)(2,1)}, u32[]{:S(2)}) copy-start(bf16[128,256]{1,0:T(8,128)(2,1)} %cotangent_ref.1) | copy-start | bytes 196612
  35.6 10.3 %all-to-all-start.1 = ((bf16[8,128,128]{2,1,0:T(8,128)(2,1)}), bf16[8,128,128]{2,1,0:T(8,128)(2,1)S(1)}, u32[]{:S(2)}, u32[]{:S(2)}) async-start(bf16[8,128,128]{2,1,0:T(8,128)(2,1)} %get-tuple-element.15), calls=%async_computation.1 | async-start | bytes 524288 | tf_op jit(solution)/shard_map/all_to_all | solution.py:222
  45.9 12.5 %all-to-all-start.3 = ((f32[32,8,128]{2,1,0:T(8,128)}), f32[32,8,128]{2,1,0:T(8,128)S(1)}, u32[]{:S(2)}, u32[]{:S(2)}) async-start(f32[32,8,128]{2,1,0:T(8,128)} %shard_map.109), calls=%async_computation.3 | async-start | bytes 262144 | tf_op jit(solution)/shard_map/all_to_all | solution.py:251
  49.4 7.1 %collective-permute-start.3 = (bf16[128,128]{1,0:T(8,128)(2,1)S(1)}, bf16[128,128]{1,0:T(8,128)(2,1)S(1)}, u32[]{:S(2)}, u32[]{:S(2)}) collective-permute-start(bf16[128,128]{1,0:T(8,128)(2,1)S(1)} %get-tuple-element.17), channel_id=1, source_target_pairs={{0,8},{8,16},{16,24},{24,0},{1,9},{9,17},{17,25},{25,1},{2,10},{10... | collective-permute-start | bytes 98312 | tf_op jit(solution)/shard_map/ppermute | solution.py:166
  51.2 6.2 %collective-permute-start.4 = (bf16[128,128]{1,0:T(8,128)(2,1)S(1)}, bf16[128,128]{1,0:T(8,128)(2,1)S(1)}, u32[]{:S(2)}, u32[]{:S(2)}) collective-permute-start(bf16[128,128]{1,0:T(8,128)(2,1)S(1)} %get-tuple-element.18), channel_id=1, source_target_pairs={{0,16},{8,24},{16,0},{24,8},{1,17},{9,25},{17,1},{25,9},{2,18},{10... | collective-permute-start | bytes 98312 | tf_op jit(solution)/shard_map/ppermute | solution.py:166
  53.7 4.0 %collective-permute-start.5 = (bf16[128,128]{1,0:T(8,128)(2,1)S(1)}, bf16[128,128]{1,0:T(8,128)(2,1)S(1)}, u32[]{:S(2)}, u32[]{:S(2)}) collective-permute-start(bf16[128,128]{1,0:T(8,128)(2,1)S(1)} %get-tuple-element.19), channel_id=1, source_target_pairs={{0,24},{8,0},{16,8},{24,16},{1,25},{9,1},{17,9},{25,17},{2,26},{10... | collective-permute-start | bytes 98312 | tf_op jit(solution)/shard_map/ppermute | solution.py:166

commit v2 on v1

--- a/solution.py
+++ b/solution.py
@@ -9,10 +9,11 @@
 from jax.sharding import PartitionSpec as P
 
 VMEM = pl.BlockSpec(memory_space=pltpu.VMEM)
+ANY = pl.BlockSpec(memory_space=pl.ANY)
+HBM = pl.BlockSpec(memory_space=pltpu.HBM)
 SMEM = pl.BlockSpec(memory_space=pltpu.SMEM)
 LIMIT = pltpu.CompilerParams(vmem_limit_bytes=40 * 1024 * 1024)
 DIRECT = 4
-AXES = ("row", "col")
 
 
 def struct(shape, dtype):
@@ -32,7 +33,15 @@
     )(*operands)
 
 
-def scale_features(deg_ref, features_ref, scaled_ref, column_ref):
+def scale_features(deg_hbm, features_hbm, scaled_ref, column_ref, deg_ref, features_ref, sems):
+    copies = [
+        pltpu.make_async_copy(deg_hbm, deg_ref, sems.at[0]),
+        pltpu.make_async_copy(features_hbm, features_ref, sems.at[1]),
+    ]
+    for copy in copies:
+        copy.start()
+    for copy in copies:
+        copy.wait()
     size = features_ref.shape[0]
     scale_row = deg_ref[...].astype(jnp.float32)
     rows = lax.broadcasted_iota(jnp.int32, (size, size), 0)
@@ -96,7 +105,7 @@
         source[pl.ds(pl.multiple_of(owner * size, size), size), :] = block[...]
 
 
-def vertex_part(received_ref, column_ref, deg_ref, weight_ref, cotangent_ref, act_ref, back_ref, grad_ref):
+def vertex_part(received_ref, column_ref, deg_ref, weight_ref, cotangent_ref, act_ref, sent_ref):
     summed = jnp.sum(received_ref[...].astype(jnp.float32), axis=0)
     hidden = (summed * column_ref[...]).astype(jnp.bfloat16)
     weight = weight_ref[...]
@@ -109,20 +118,23 @@
         weight, slope_term, (((1,), (1,)), ((), ())), preferred_element_type=jnp.float32
     )
     back = (spread * deg_ref[...].astype(jnp.float32)).astype(jnp.bfloat16)
-    back_ref[...] = jnp.broadcast_to(back[None], back_ref.shape)
     local_grad = lax.dot_general(
         hidden, slope_term, (((0,), (0,)), ((), ())), preferred_element_type=jnp.float32
-    )
-    for half in range(grad_ref.shape[0]):
-        grad_ref[half] = local_grad[:, half * 128 : (half + 1) * 128]
+    ).astype(jnp.bfloat16)
+    size = back.shape[1]
+    halves = local_grad.shape[1] // size
+    for peer in range(sent_ref.shape[0]):
+        half = peer % halves
+        sent_ref[peer, 0] = back
+        sent_ref[peer, 1] = local_grad[:, half * size : (half + 1) * size]
 
 
 def backward_partial(me_ref, rows_ref, cols_ref, masks_ref, gathered_ref, *refs):
     *pieces, source, total = refs
     slots, tile_size = masks_ref.shape[:2]
-    shards, _, size = gathered_ref.shape
+    shards, _, _, size = gathered_ref.shape
     for shard in range(shards):
-        source[:, shard * size : (shard + 1) * size] = gathered_ref[shard]
+        source[:, shard * size : (shard + 1) * size] = gathered_ref[shard, 0]
     total[...] = jnp.zeros_like(total)
 
     def one(slot):
@@ -133,33 +145,44 @@
         )
 
     each_slot(slots, one)
+    grad = jnp.sum(gathered_ref[:, 1].astype(jnp.float32), axis=0).astype(jnp.bfloat16)
     if len(pieces) == 1:
         for shard in range(pieces[0].shape[0]):
-            pieces[0][shard] = total[:, shard * size : (shard + 1) * size].astype(jnp.bfloat16)
+            pieces[0][shard, 0] = total[:, shard * size : (shard + 1) * size].astype(jnp.bfloat16)
+            pieces[0][shard, 1] = grad
         return
     for step, piece in enumerate(pieces):
         owner = lax.rem(me_ref[0] + step, len(pieces))
         place = pl.ds(pl.multiple_of(owner * size, size), size)
-        piece[...] = total[:, place].astype(jnp.bfloat16)
+        piece[0] = total[:, place].astype(jnp.bfloat16)
+        piece[1] = grad
+
+
+def sum_grad(factor, me_ref, *refs):
+    *pieces, out_ref, ordered = refs
+    if len(pieces) == 1:
+        out_ref[...] = jnp.sum(pieces[0][:, 1].astype(jnp.float32), axis=0) * factor
+        return
+    shards = len(pieces)
+    for step, piece in enumerate(pieces):
+        ordered[lax.rem(me_ref[0] + shards - step, shards)] = piece[1]
+    out_ref[...] = jnp.sum(ordered[...].astype(jnp.float32), axis=0) * factor
 
 
 def input_part(deg_ref, *refs):
     *pieces, out_ref = refs
     if len(pieces) == 1:
-        total = jnp.sum(pieces[0][...].astype(jnp.float32), axis=0)
-    else:
-        total = sum(piece[...].astype(jnp.float32) for piece in pieces)
+        total = jnp.sum(pieces[0][:, 0].astype(jnp.float32), axis=0)
+    else:
+        total = sum(piece[0].astype(jnp.float32) for piece in pieces)
     out_ref[...] = (total * deg_ref[...].astype(jnp.float32)).T.astype(jnp.bfloat16)
 
 
-def sum_pieces(factor, received_ref, out_ref):
-    total = jnp.sum(received_ref[...], axis=0) * factor
-    out_ref[...] = jnp.broadcast_to(total[None], out_ref.shape)
-
-
-def join_halves(whole_ref, out_ref):
-    for half in range(whole_ref.shape[0]):
-        out_ref[:, half * 128 : (half + 1) * 128] = whole_ref[half]
+def join_halves(half_ref, own_ref, other_ref, out_ref):
+    size = own_ref.shape[1]
+    half = half_ref[0]
+    out_ref[:, pl.ds(pl.multiple_of(half * size, size), size)] = own_ref[...]
+    out_ref[:, pl.ds(pl.multiple_of((1 - half) * size, size), size)] = other_ref[...]
 
 
 def shifted(block, axis, shards, step):
@@ -184,6 +207,12 @@
         scale_features,
         (struct((size, width), bf16), struct((size, width), f32)),
         (deg_row, features),
+        [HBM] * 2,
+        [
+            pltpu.VMEM((1, size), bf16),
+            pltpu.VMEM((size, width), bf16),
+            pltpu.SemaphoreType.DMA((2,)),
+        ],
     )
     if direct:
         blocks = [scaled] + [shifted(scaled, "row", row_shards, step) for step in range(1, row_shards)]
@@ -193,7 +222,7 @@
         unpack_tiles,
         struct((slots, tile_size, tile_size), bf16),
         (tile_count, tile_bits, column),
-        [SMEM, VMEM, pl.BlockSpec(memory_space=pl.ANY)],
+        [SMEM, VMEM, ANY],
         flops=1 << 28,
         moved=1 << 21,
     )
@@ -209,25 +238,23 @@
         ],
     )
     received = lax.all_to_all(partial_value, "col", 0, 0)
-    halves = out_width // 128
-    activations, back, local_grad = call(
+    activations, sent = call(
         vertex_part,
         (
             struct((size, out_width), bf16),
-            struct((col_shards, width, size), bf16),
-            struct((halves, height, 128), f32),
+            struct((col_shards, 2, width, size), bf16),
         ),
         (received, column, deg_row, weight, cotangent),
     )
-    gathered = lax.all_to_all(back, "col", 0, 0)
+    gathered = lax.all_to_all(sent, "col", 0, 0)
     scratch = [
         pltpu.VMEM((width, col_shards * size), bf16),
         pltpu.VMEM((width, row_shards * size), f32),
     ]
     if direct:
-        piece_shapes = (struct((width, size), bf16),) * row_shards
-    else:
-        piece_shapes = (struct((row_shards, width, size), bf16),)
+        piece_shapes = (struct((2, width, size), bf16),) * row_shards
+    else:
+        piece_shapes = (struct((row_shards, 2, width, size), bf16),)
     pieces = call(
         backward_partial,
         piece_shapes,
@@ -241,15 +268,23 @@
         ]
     else:
         arrived = [lax.all_to_all(pieces[0], "row", 0, 0)]
+    half_grad = call(
+        functools.partial(sum_grad, factor),
+        struct((height, size), f32),
+        (me, *arrived),
+        [SMEM] + [VMEM] * len(arrived),
+        [pltpu.VMEM((row_shards, height, size), bf16)],
+    )
+    pairs = [(shard, shard + 1 - 2 * (shard % 2)) for shard in range(col_shards)]
+    other_grad = lax.ppermute(half_grad, "col", pairs)
     input_grad = call(input_part, struct((size, width), bf16), (deg_row, *arrived))
-
-    if height * out_width % (devices * 1024):
-        whole = lax.psum(local_grad, AXES) * factor
-    else:
-        sent = lax.all_to_all(local_grad.reshape(devices, -1, 128), AXES, 0, 0)
-        own = call(functools.partial(sum_pieces, factor), struct(sent.shape, f32), (sent,))
-        whole = lax.all_to_all(own, AXES, 0, 0).reshape(halves, height, 128)
-    weight_grad = call(join_halves, struct((height, out_width), f32), (whole,))
+    core = jnp.mod(lax.axis_index("col"), 2).astype(jnp.int32).reshape(1)
+    weight_grad = call(
+        join_halves,
+        struct((height, out_width), f32),
+        (core, half_grad, other_grad),
+        [SMEM] + [VMEM] * 2,
+    )
     return (activations, input_grad, weight_grad)
 
 

time: 59.5 us -> 48.8 us (0.82)
  starting transfers between devices: 17.7 us -> 10.3 us
  waiting for transfers between devices: 11.5 us -> 6.88 us
  blocking collectives: 20.5 us -> 22.7 us
  Pallas kernels: 5.62 us -> 4.8 us
    all_to_all x2 -> x0, waiting for transfers between devices: 6.17 us -> none  [the longest x1 6.17 us: on_device(): gathered = lax.all_to_all(back, 'col', 0, 0)]
    all_to_all x2 -> x0, starting transfers between devices: 5.99 us -> none  [the longest x1 3.41 us: on_device(): gathered = lax.all_to_all(back, 'col', 0, 0)]
    all_to_all x1, blocking collectives: 9.92 us -> 12.1 us  [on_device(): gathered = lax.all_to_all(sent, 'col', 0, 0)]
    ppermute x6, starting transfers between devices: 11.7 us -> 10.2 us  [shifted(): lax.ppermute(block, axis, [(source, (source + step) % shards) for source...]
    ppermute x6, waiting for transfers between devices: 5.3 us -> 6.37 us  [shifted(): lax.ppermute(block, axis, [(source, (source + step) % shards) for source...]
    pallas_call x8, Pallas kernels: 5.62 us -> 4.8 us  [call(): pl.pallas_call(body, out_shape=out_shape, in_specs=specs or [VMEM] * len(...]
  transfers between devices with their start and end apart: 8 -> 7, of which waited for: 6 -> 5; matrix products, arithmetic and copies ran while one was open for 0% -> 0% of each run, Pallas kernels for 5% -> 2%
where the time goes in v2:
time: 48.8 us; the launch traced here: 48.5 us
  blocking collectives  22.7 us (47%)
  starting transfers between devices  10.3 us (21%)
  waiting for transfers between devices  6.88 us (14%)
  Pallas kernels  4.8 us (10%)
  local copies, waits for them, and re-layouts  2.38 us (5%)
  between operations  1.4 us (3%)
    all_to_all x1, blocking collectives, on_device(): gathered = lax.all_to_all(sent, 'col', 0, 0)  12.1 us
    all_to_all x1, blocking collectives, on_device(): received = lax.all_to_all(partial_value, 'col', 0, 0)  10.6 us
    ppermute x6, starting transfers between devices, shifted(): lax.ppermute(block, axis, [(source, (source + step) % shards) for source...  10.2 us
    ppermute x6, waiting for transfers between devices, shifted(): lax.ppermute(block, axis, [(source, (source + step) % shards) for source...  6.37 us
    pallas_call x8, Pallas kernels, call(): pl.pallas_call(body, out_shape=out_shape, in_specs=specs or [VMEM] * len(...  4.8 us
    unnamed x14, local copies, waits for them, and re-layouts  2.38 us
  transfers between devices with their start and end apart: 7, of which 5 were waited for; matrix products, arithmetic and copies ran while one was open for 0% of the time, Pallas kernels for 2%

profile of v2, /device:TPU:0, one launch (start us, length us, event | category | flops | bytes accessed | tf_op | source)
XLA Modules:
  0.0 48.5 jit_solution(5988574618751279626)
XLA Ops:
  0.6 0.0 copy-start.4
  0.6 0.6 %copy-done.4 = bf16[128]{0:T(256)(128)(2,1)S(1)} copy-done((bf16[128]{0:T(256)(128)(2,1)S(1)}, bf16[128]{0:T(256)(128)(2,1)}, u32[]{:S(2)}) %copy-start.4) | copy-done | bytes 280
  1.3 0.0 copy-start.3
  1.3 0.8 %copy-done.3 = bf16[128,128]{1,0:T(8,128)(2,1)S(1)} copy-done((bf16[128,128]{1,0:T(8,128)(2,1)S(1)}, bf16[128,128]{1,0:T(8,128)(2,1)}, u32[]{:S(2)}) %copy-start.3) | copy-done | bytes 32792
  2.0 0.2 shard_map.103
  2.2 5.1 %collective-permute-start.2 = (bf16[128,128]{1,0:T(8,128)(2,1)S(1)}, bf16[128,128]{1,0:T(8,128)(2,1)S(1)}, u32[]{:S(2)}, u32[]{:S(2)}) collective-permute-start(bf16[128,128]{1,0:T(8,128)(2,1)S(1)} %get-tuple-element.12.refs_0_), channel_id=1, source_target_pairs={{0,24},{8,0},{16,8},{24,16},{1,25},{9,1},{17,9},{25,17},{2,26},{10... | collective-permute-start | bytes 98312 | tf_op jit(solution)/shard_map/ppermute | solution.py:189
  7.3 0.0 collective-permute-start.1
  7.3 1.0 %collective-permute-start = (bf16[128,128]{1,0:T(8,128)(2,1)S(1)}, bf16[128,128]{1,0:T(8,128)(2,1)S(1)}, u32[]{:S(2)}, u32[]{:S(2)}) collective-permute-start(bf16[128,128]{1,0:T(8,128)(2,1)S(1)} %get-tuple-element.12.refs_0_), channel_id=1, source_target_pairs={{0,8},{8,16},{16,24},{24,0},{1,9},{9,17},{17,25},{25,1},{2,10},{10... | collective-permute-start | bytes 98312 | tf_op jit(solution)/shard_map/ppermute | solution.py:189
  9.0 0.0 copy-start
  9.0 0.9 %copy-done = s32[1,1,8,32,256]{4,3,2,1,0:T(8,128)S(1)} copy-done((s32[1,1,8,32,256]{4,3,2,1,0:T(8,128)S(1)}, s32[1,1,8,32,256]{4,3,2,1,0:T(8,128)}, u32[]{:S(2)}) %copy-start) | copy-done | bytes 262168
  10.0 0.4 shard_map.104.masks_ref
  10.3 0.0 copy-start.5
  10.3 0.0 copy-start.6
  10.3 0.0 collective-permute-done.2.refs_3_
  10.3 1.8 %collective-permute-done.1.refs_2_ = bf16[128,128]{1,0:T(8,128)(2,1)S(1)} collective-permute-done((bf16[128,128]{1,0:T(8,128)(2,1)S(1)}, bf16[128,128]{1,0:T(8,128)(2,1)S(1)}, u32[]{:S(2)}, u32[]{:S(2)}) %collective-permute-start.1) | collective-permute-done | bytes 32800 | tf_op jit(solution)/shard_map/ppermute | solution.py:189
  12.1 0.9 %collective-permute-done.refs_1_ = bf16[128,128]{1,0:T(8,128)(2,1)S(1)} collective-permute-done((bf16[128,128]{1,0:T(8,128)(2,1)S(1)}, bf16[128,128]{1,0:T(8,128)(2,1)S(1)}, u32[]{:S(2)}, u32[]{:S(2)}) %collective-permute-start) | collective-permute-done | bytes 32800 | tf_op jit(solution)/shard_map/ppermute | solution.py:189
  13.0 0.0 copy-done.5
  13.1 0.0 copy-done.6
  13.1 1.0 %shard_map.105 = bf16[8,128,128]{2,1,0:T(8,128)(2,1)S(1)} custom-call(s32[1]{0:T(128)} %bitcast.me_ref, s32[1,1,8]{2,1,0:T(1,128)S(1)} %copy-done.5, s32[1,1,8]{2,1,0:T(1,128)S(1)} %copy-done.6, bf16[8,256,256]{2,1,0:T(8,128)(2,1)S(1)} %shard_map.104.masks_ref, bf16[128,128]{1,0:T(8,128)(2,1)S(1)} %get-tuple-element.12.refs_0_, ...), custom_call_target="tpu_custom_call" | custom-call | flops 1048576 | bytes 1048576 | tf_op jit(solution)/shard_map/pallas_call | solution.py:25
  14.1 0.0 copy-start.1
  14.1 0.0 copy-start.2
  14.1 10.6 %all_to_all.10.received_ref = bf16[8,128,128]{2,1,0:T(8,128)(2,1)S(1)} all-to-all(bf16[8,128,128]{2,1,0:T(8,128)(2,1)S(1)} %shard_map.105), channel_id=1, replica_groups=mesh['row'=4,'col'=8] {'col'}, dimensions={0} | all-to-all | bytes 524288 | tf_op jit(solution)/shard_map/all_to_all | solution.py:240
  24.7 0.0 copy-done.1
  24.7 0.0 copy-done.2
  24.7 0.8 %shard_map.106 = (bf16[128,256]{1,0:T(8,128)(2,1)}, bf16[8,2,128,128]{3,2,1,0:T(8,128)(2,1)S(1)}) custom-call(bf16[8,128,128]{2,1,0:T(8,128)(2,1)S(1)} %all_to_all.10.received_ref, f32[128,128]{1,0:T(8,128)S(1)} %get-tuple-element.11.after_ref.column_ref, bf16[1,128]{1,0:T(2,128)(2,1)S(1)} %bitcast.4, bf16[128,256]{1,0:T(8,128)(2,1)S(1)} %copy-done.1, ...), custom_call_target="tpu_custom_call" | custom-call | flops 1048576 | bytes 1048576 | tf_op jit(solution)/shard_map/pallas_call | solution.py:25
  25.5 12.1 %all_to_all.11.gathered_ref = bf16[8,2,128,128]{3,2,1,0:T(8,128)(2,1)S(1)} all-to-all(bf16[8,2,128,128]{3,2,1,0:T(8,128)(2,1)S(1)} %get-tuple-element.14), channel_id=1, replica_groups=mesh['row'=4,'col'=8] {'col'}, dimensions={0} | all-to-all | bytes 1048576 | tf_op jit(solution)/shard_map/all_to_all | solution.py:249
  37.7 1.0 %shard_map.107 = (bf16[2,128,128]{2,1,0:T(8,128)(2,1)S(1)}, bf16[2,128,128]{2,1,0:T(8,128)(2,1)S(1)}, bf16[2,128,128]{2,1,0:T(8,128)(2,1)S(1)}, bf16[2,128,128]{2,1,0:T(8,128)(2,1)S(1)}) custom-call(s32[1]{0:T(128)} %bitcast.me_ref, s32[1,1,8]{2,1,0:T(1,128)S(1)} %copy-done.5, s32[1,1,8]{2,1,0:T(1,128)S(1)} %copy-done.6, ...), custom_call_target="tpu_custom_call" | custom-call | flops 1048576 | bytes 1048576 | tf_op jit(solution)/shard_map/pallas_call | solution.py:25
  38.7 0.5 collective-permute-start.3
  39.1 0.9 %collective-permute-start.4 = (bf16[2,128,128]{2,1,0:T(8,128)(2,1)S(1)}, bf16[2,128,128]{2,1,0:T(8,128)(2,1)S(1)}, u32[]{:S(2)}, u32[]{:S(2)}) collective-permute-start(bf16[2,128,128]{2,1,0:T(8,128)(2,1)S(1)} %get-tuple-element.17), channel_id=1, source_target_pairs={{0,16},{8,24},{16,0},{24,8},{1,17},{9,25},{17,1},{25,9},{2,18},{10... | collective-permute-start | bytes 196616 | tf_op jit(solution)/shard_map/ppermute | solution.py:189
  40.0 2.7 %collective-permute-start.5 = (bf16[2,128,128]{2,1,0:T(8,128)(2,1)S(1)}, bf16[2,128,128]{2,1,0:T(8,128)(2,1)S(1)}, u32[]{:S(2)}, u32[]{:S(2)}) collective-permute-start(bf16[2,128,128]{2,1,0:T(8,128)(2,1)S(1)} %get-tuple-element.18), channel_id=1, source_target_pairs={{0,24},{8,0},{16,8},{24,16},{1,25},{9,1},{17,9},{25,17},{2,26},{10... | collective-permute-start | bytes 196616 | tf_op jit(solution)/shard_map/ppermute | solution.py:189
  42.8 2.5 %collective-permute-done.3.refs_1_ = bf16[2,128,128]{2,1,0:T(8,128)(2,1)S(1)} collective-permute-done((bf16[2,128,128]{2,1,0:T(8,128)(2,1)S(1)}, bf16[2,128,128]{2,1,0:T(8,128)(2,1)S(1)}, u32[]{:S(2)}, u32[]{:S(2)}) %collective-permute-start.3) | collective-permute-done | bytes 65568 | tf_op jit(solution)/shard_map/ppermute | solution.py:189
  45.3 1.1 %collective-permute-done.4.refs_2_ = bf16[2,128,128]{2,1,0:T(8,128)(2,1)S(1)} collective-permute-done((bf16[2,128,128]{2,1,0:T(8,128)(2,1)S(1)}, bf16[2,128,128]{2,1,0:T(8,128)(2,1)S(1)}, u32[]{:S(2)}, u32[]{:S(2)}) %collective-permute-start.4) | collective-permute-done | bytes 65568 | tf_op jit(solution)/shard_map/ppermute | solution.py:189
  46.4 0.0 collective-permute-done.5.refs_3_
  46.5 0.1 collective-permute-start.6
  46.6 0.7 %shard_map.108 = bf16[128,128]{1,0:T(8,128)(2,1)} custom-call(bf16[1,128]{1,0:T(2,128)(2,1)S(1)} %bitcast.5, bf16[2,128,128]{2,1,0:T(8,128)(2,1)S(1)} %get-tuple-element.15.refs_0_, bf16[2,128,128]{2,1,0:T(8,128)(2,1)S(1)} %collective-permute-done.3.refs_1_, bf16[2,128,128]{2,1,0:T(8,128)(2,1)S(1)} %collective-permute-done.4.refs_2_, ...), custom_call_target="tpu_custom_call" | custom-call | flops 1048576 | bytes 1048576 | tf_op jit(solution)/shard_map/pallas_call | solution.py:25
  47.3 0.5 %collective-permute-done.6.other_ref = f32[128,128]{1,0:T(8,128)S(1)} collective-permute-done((f32[128,128]{1,0:T(8,128)S(1)}, f32[128,128]{1,0:T(8,128)S(1)}, u32[]{:S(2)}, u32[]{:S(2)}) %collective-permute-start.6) | collective-permute-done | bytes 65568 | tf_op jit(solution)/shard_map/ppermute | solution.py:279
  47.8 0.7 %shard_map.110 = f32[128,256]{1,0:T(8,128)} custom-call(s32[1]{0:T(128)} %bitcast.2.half_ref, f32[128,128]{1,0:T(8,128)S(1)} %shard_map.109.own_ref, f32[128,128]{1,0:T(8,128)S(1)} %collective-permute-done.6.other_ref), custom_call_target="tpu_custom_call" | custom-call | flops 1048576 | bytes 1048576 | tf_op jit(solution)/shard_map/pallas_call | solution.py:25
  (1 shorter events, 0.0 us)
Async XLA Ops:
  0.6 0.7 %copy-start.4 = (bf16[128]{0:T(256)(128)(2,1)S(1)}, bf16[128]{0:T(256)(128)(2,1)}, u32[]{:S(2)}) copy-start(bf16[128]{0:T(256)(128)(2,1)} %param.9) | copy-start | bytes 772
  1.3 0.8 %copy-start.3 = (bf16[128,128]{1,0:T(8,128)(2,1)S(1)}, bf16[128,128]{1,0:T(8,128)(2,1)}, u32[]{:S(2)}) copy-start(bf16[128,128]{1,0:T(8,128)(2,1)} %features_hbm.1) | copy-start | bytes 98308
  2.2 8.1 %collective-permute-start.2 = (bf16[128,128]{1,0:T(8,128)(2,1)S(1)}, bf16[128,128]{1,0:T(8,128)(2,1)S(1)}, u32[]{:S(2)}, u32[]{:S(2)}) collective-permute-start(bf16[128,128]{1,0:T(8,128)(2,1)S(1)} %get-tuple-element.12.refs_0_), channel_id=1, source_target_pairs={{0,24},{8,0},{16,8},{24,16},{1,25},{9,1},{17,9},{25,17},{2,26},{10... | collective-permute-start | bytes 98312 | tf_op jit(solution)/shard_map/ppermute | solution.py:189
  7.3 4.8 %collective-permute-start.1 = (bf16[128,128]{1,0:T(8,128)(2,1)S(1)}, bf16[128,128]{1,0:T(8,128)(2,1)S(1)}, u32[]{:S(2)}, u32[]{:S(2)}) collective-permute-start(bf16[128,128]{1,0:T(8,128)(2,1)S(1)} %get-tuple-element.12.refs_0_), channel_id=1, source_target_pairs={{0,16},{8,24},{16,0},{24,8},{1,17},{9,25},{17,1},{25,9},{2,18},{10... | collective-permute-start | bytes 98312 | tf_op jit(solution)/shard_map/ppermute | solution.py:189
  7.3 5.7 %collective-permute-start = (bf16[128,128]{1,0:T(8,128)(2,1)S(1)}, bf16[128,128]{1,0:T(8,128)(2,1)S(1)}, u32[]{:S(2)}, u32[]{:S(2)}) collective-permute-start(bf16[128,128]{1,0:T(8,128)(2,1)S(1)} %get-tuple-element.12.refs_0_), channel_id=1, source_target_pairs={{0,8},{8,16},{16,24},{24,0},{1,9},{9,17},{17,25},{25,1},{2,10},{10... | collective-permute-start | bytes 98312 | tf_op jit(solution)/shard_map/ppermute | solution.py:189
  9.0 1.0 %copy-start = (s32[1,1,8,32,256]{4,3,2,1,0:T(8,128)S(1)}, s32[1,1,8,32,256]{4,3,2,1,0:T(8,128)}, u32[]{:S(2)}) copy-start(s32[1,1,8,32,256]{4,3,2,1,0:T(8,128)} %bits_ref.1) | copy-start | bytes 786436
  10.3 2.7 %copy-start.5 = (s32[1,1,8]{2,1,0:T(1,128)S(1)}, s32[1,1,8]{2,1,0:T(1,128)}, u32[]{:S(2)}) copy-start(s32[1,1,8]{2,1,0:T(1,128)} %rows_ref.3) | copy-start | bytes 100
  10.3 2.7 %copy-start.6 = (s32[1,1,8]{2,1,0:T(1,128)S(1)}, s32[1,1,8]{2,1,0:T(1,128)}, u32[]{:S(2)}) copy-start(s32[1,1,8]{2,1,0:T(1,128)} %cols_ref.3) | copy-start | bytes 100
  14.1 10.6 %copy-start.1 = (bf16[128,256]{1,0:T(8,128)(2,1)S(1)}, bf16[128,256]{1,0:T(8,128)(2,1)}, u32[]{:S(2)}) copy-start(bf16[128,256]{1,0:T(8,128)(2,1)} %weight_ref.1) | copy-start | bytes 196612
  14.1 10.6 %copy-start.2 = (bf16[128,256]{1,0:T(8,128)(2,1)S(1)}, bf16[128,256]{1,0:T(8,128)(2,1)}, u32[]{:S(2)}) copy-start(bf16[128,256]{1,0:T(8,128)(2,1)} %cotangent_ref.1) | copy-start | bytes 196612
  38.7 6.6 %collective-permute-start.3 = (bf16[2,128,128]{2,1,0:T(8,128)(2,1)S(1)}, bf16[2,128,128]{2,1,0:T(8,128)(2,1)S(1)}, u32[]{:S(2)}, u32[]{:S(2)}) collective-permute-start(bf16[2,128,128]{2,1,0:T(8,128)(2,1)S(1)} %get-tuple-element.16), channel_id=1, source_target_pairs={{0,8},{8,16},{16,24},{24,0},{1,9},{9,17},{17,25},{25,1},{2,10},{10... | collective-permute-start | bytes 196616 | tf_op jit(solution)/shard_map/ppermute | solution.py:189
  39.1 7.3 %collective-permute-start.4 = (bf16[2,128,128]{2,1,0:T(8,128)(2,1)S(1)}, bf16[2,128,128]{2,1,0:T(8,128)(2,1)S(1)}, u32[]{:S(2)}, u32[]{:S(2)}) collective-permute-start(bf16[2,128,128]{2,1,0:T(8,128)(2,1)S(1)} %get-tuple-element.17), channel_id=1, source_target_pairs={{0,16},{8,24},{16,0},{24,8},{1,17},{9,25},{17,1},{25,9},{2,18},{10... | collective-permute-start | bytes 196616 | tf_op jit(solution)/shard_map/ppermute | solution.py:189
  40.0 6.4 %collective-permute-start.5 = (bf16[2,128,128]{2,1,0:T(8,128)(2,1)S(1)}, bf16[2,128,128]{2,1,0:T(8,128)(2,1)S(1)}, u32[]{:S(2)}, u32[]{:S(2)}) collective-permute-start(bf16[2,128,128]{2,1,0:T(8,128)(2,1)S(1)} %get-tuple-element.18), channel_id=1, source_target_pairs={{0,24},{8,0},{16,8},{24,16},{1,25},{9,1},{17,9},{25,17},{2,26},{10... | collective-permute-start | bytes 196616 | tf_op jit(solution)/shard_map/ppermute | solution.py:189
  46.5 1.3 %collective-permute-start.6 = (f32[128,128]{1,0:T(8,128)S(1)}, f32[128,128]{1,0:T(8,128)S(1)}, u32[]{:S(2)}, u32[]{:S(2)}) collective-permute-start(f32[128,128]{1,0:T(8,128)S(1)} %shard_map.109.own_ref), channel_id=1, source_target_pairs={{0,1},{1,0},{2,3},{3,2},{4,5},{5,4},{6,7},{7,6},{8,9},{9,8},{10,11... | collective-permute-start | bytes 196616 | tf_op jit(solution)/shard_map/ppermute | solution.py:279

commit v3 on v0

v3 whole, which is shorter than its diff:
```python
import functools
import math

import jax
import jax.numpy as jnp
from jax import lax
from jax.experimental import pallas as pl
from jax.experimental.pallas import tpu as pltpu
from jax.sharding import PartitionSpec as P

VMEM = pl.BlockSpec(memory_space=pltpu.VMEM)
SMEM = pl.BlockSpec(memory_space=pltpu.SMEM)
ANY = pl.BlockSpec(memory_space=pl.ANY)
LIMIT = pltpu.CompilerParams(vmem_limit_bytes=40 * 1024 * 1024)
FIRST_FLOPS = 1 << 32
bf16, f32 = jnp.bfloat16, jnp.float32


def struct(shape, dtype):
    return jax.ShapeDtypeStruct(shape, dtype)


def call(body, out_shape, scalars, operands, scratch=(), flops=1 << 20, after=()):
    single = not isinstance(out_shape, (tuple, list))
    return pl.pallas_call(
        body,
        out_shape=out_shape,
        in_specs=[SMEM] * len(scalars) + [VMEM] * len(operands) + [ANY] * len(after),
        out_specs=VMEM if single else [VMEM] * len(out_shape),
        scratch_shapes=list(scratch),
        compiler_params=LIMIT,
        cost_estimate=pl.CostEstimate(flops=flops, bytes_accessed=1 << 20, transcendentals=0),
    )(*scalars, *operands, *after)


def block_at(index, size):
    return pl.ds(pl.multiple_of(index * size, size), size)


def unpack_tiles(count_ref, bits_ref, deg_ref, features_ref, scaled_ref, column_ref, masks_ref):
    column = spread_scale(deg_ref[...], column_ref.shape[0])
    column_ref[...] = column
    scaled_ref[...] = (features_ref[...].astype(f32) * column).astype(bf16)

    def one(slot):
        masks_ref[slot] = unpacked(jnp.where(slot < count_ref[0, 0], bits_ref[0, 0, slot], 0))

    pl.loop(0, masks_ref.shape[0])(one)


def forward_total(rows_ref, cols_ref, masks_ref, source, total):
    slots, tile_size = masks_ref.shape[:2]
    total[...] = jnp.zeros_like(total)

    def one(slot):
        place = block_at(rows_ref[0, 0, slot], tile_size)
        pick = block_at(cols_ref[0, 0, slot], tile_size)
        total[place, :] += jnp.dot(masks_ref[slot], source[pick, :], preferred_element_type=f32)

    pl.loop(0, slots)(one)


def backward_total(rows_ref, cols_ref, masks_ref, source, total):
    slots, tile_size = masks_ref.shape[:2]
    total[...] = jnp.zeros_like(total)

    def one(slot):
        pick = block_at(rows_ref[0, 0, slot], tile_size)
        place = block_at(cols_ref[0, 0, slot], tile_size)
        total[:, place] += jnp.dot(source[:, pick], masks_ref[slot], preferred_element_type=f32)

    pl.loop(0, slots)(one)


def unpacked(packed):
    words, tile_size = packed.shape
    repeated = jnp.broadcast_to(packed[:, None, :], (words, 8, tile_size))
    shifts = lax.broadcasted_iota(jnp.int32, (words, 8, tile_size), 1)
    bit_values = jnp.bitwise_and(jnp.right_shift(repeated, shifts), 1)
    return bit_values.reshape(words * 8, tile_size).astype(f32).astype(bf16)


def spread_scale(deg, size):
    rows = lax.broadcasted_iota(jnp.int32, (size, size), 0)
    columns = lax.broadcasted_iota(jnp.int32, (size, size), 1)
    diagonal = jnp.where(rows == columns, deg.astype(f32).reshape(1, size), 0.0).astype(bf16)
    return jnp.dot(diagonal, jnp.ones((size, size), bf16), preferred_element_type=f32)


def scale_column(deg_ref, column_ref):
    column_ref[...] = spread_scale(deg_ref[...], column_ref.shape[0])


def scale_rows(column_ref, features_ref, rows_ref, cols_ref, scaled_ref):
    scaled_ref[...] = (features_ref[...].astype(f32) * column_ref[...]).astype(bf16)


def build_adjacency(count_ref, rows_ref, cols_ref, bits_ref, after_ref, adjacency_ref):
    slots, words, tile_size = bits_ref.shape[2:]
    count = count_ref[0, 0]
    for slot in range(slots):
        packed = jnp.where(slot < count, bits_ref[0, 0, slot], 0)
        place = block_at(rows_ref[0, 0, slot], tile_size), block_at(cols_ref[0, 0, slot], tile_size)
        adjacency_ref[place] = unpacked(packed)


def forward_pair(row_ref, core_ref, adjacency_ref, *refs):
    *blocks, mine_ref, other_ref, source, total = refs
    size = blocks[0].shape[0]
    for step, block in enumerate(blocks):
        source[block_at(row_ref[0] ^ step, size), :] = block[...]
    total[...] = jnp.dot(adjacency_ref[...], source[...], preferred_element_type=f32)
    core = core_ref[0]
    for chip in range(mine_ref.shape[0]):
        mine_ref[chip] = total[block_at(2 * chip + core, size), :]
        other_ref[chip] = total[block_at(2 * chip + 1 - core, size), :].astype(bf16)


def forward_chips(chip_ref, mine_ref, received_ref, own_ref, *pieces):
    chip = chip_ref[0]
    own_ref[...] = mine_ref[chip] + received_ref[chip].astype(f32)
    for step, piece in zip((3, 2, 1), pieces):
        peer = chip ^ step
        piece[...] = (mine_ref[peer] + received_ref[peer].astype(f32)).astype(bf16)


def vertex_values(summed, column_ref, deg_ref, weight_ref, cotangent_ref):
    hidden = (summed * column_ref[...]).astype(bf16)
    weight = weight_ref[...]
    pre_act = jnp.dot(hidden, weight, preferred_element_type=f32)
    sigmoid_value = 1.0 / (1.0 + jnp.exp(-pre_act))
    slope = sigmoid_value * (1.0 + pre_act * (1.0 - sigmoid_value))
    slope_term = (cotangent_ref[...].astype(f32) * slope).astype(bf16)
    spread = lax.dot_general(
        weight, slope_term, (((1,), (1,)), ((), ())), preferred_element_type=f32
    )
    back = (spread * deg_ref[...].astype(f32).reshape(1, -1)).astype(bf16)
    local_grad = lax.dot_general(
        hidden, slope_term, (((0,), (0,)), ((), ())), preferred_element_type=f32
    )
    return back, local_grad, pre_act * sigmoid_value


def vertex_chips(column_ref, deg_ref, weight_ref, cotangent_ref, own_ref, *refs):
    *received, sent_ref, active_ref = refs
    summed = own_ref[...] + sum(piece[...].astype(f32) for piece in received)
    sent_ref[0], local_grad, active_ref[...] = vertex_values(
        summed, column_ref, deg_ref, weight_ref, cotangent_ref
    )
    half = sent_ref.shape[2]
    for core in range(2):
        sent_ref[1 + core] = local_grad[:, core * half : (core + 1) * half].astype(bf16)


def write_out(active_ref, out_ref, written_ref):
    out_ref[...] = active_ref[...].astype(bf16)
    written_ref[...] = jnp.zeros_like(written_ref)


def join_chips(chip_ref, core_ref, *refs):
    *blocks, _, joined_ref, own_grad_ref, ordered = refs
    chips = len(blocks)
    for step, block in enumerate(blocks):
        joined_ref[step] = block[0]
        ordered[chip_ref[0] ^ step] = block[1:]
    grad = jnp.sum(ordered[...].astype(f32), axis=0).astype(bf16)
    second = core_ref[0] == 1
    own_grad_ref[...] = jnp.where(second, grad[1], grad[0])
    joined_ref[chips] = jnp.where(second, grad[0], grad[1])


def backward_rows(row_ref, chip_ref, core_ref, adjacency_ref, own_ref, grad_ref, received_ref, *refs):
    *pieces, source, total = refs
    chips = own_ref.shape[0] - 1
    size = own_ref.shape[2]
    chip, core = chip_ref[0], core_ref[0]
    for step in range(chips):
        peer = 2 * (chip ^ step)
        source[:, block_at(peer + core, size)] = own_ref[step]
        source[:, block_at(peer + 1 - core, size)] = received_ref[step]
    total[...] = jnp.dot(source[...], adjacency_ref[...], preferred_element_type=f32)
    grad = (grad_ref[...].astype(f32) + received_ref[chips].astype(f32)).astype(bf16)
    for step, piece in zip((3, 2, 1, 0), pieces):
        piece[0] = total[:, block_at(row_ref[0] ^ step, size)].astype(bf16)
        piece[1] = grad


def sum_grad(factor, row_ref, *refs):
    *pieces, out_ref, ordered = refs
    for step, piece in zip((3, 2, 1, 0), pieces):
        ordered[row_ref[0] ^ step] = piece[1]
    total = jnp.sum(ordered[...].astype(f32), axis=0) * factor
    out_ref[...] = total.astype(out_ref.dtype)


def input_rows(deg_ref, *refs):
    *pieces, out_ref = refs
    total = sum(piece[0].astype(f32) for piece in pieces)
    out_ref[...] = (total * deg_ref[...].astype(f32).reshape(1, -1)).T.astype(bf16)


def join_halves(core_ref, own_ref, other_ref, out_ref):
    size = own_ref.shape[1]
    half = core_ref[0]
    out_ref[:, block_at(half, size)] = own_ref[...].astype(f32)
    out_ref[:, block_at(1 - half, size)] = other_ref[...].astype(f32)


def forward_all(rows_ref, cols_ref, masks_ref, source_ref, partial_ref, total):
    forward_total(rows_ref, cols_ref, masks_ref, source_ref, total)
    partial_ref[...] = total[...].astype(bf16).reshape(partial_ref.shape)


def vertex_all(column_ref, deg_ref, weight_ref, cotangent_ref, received_ref, act_ref, back_ref, grad_ref):
    summed = jnp.sum(received_ref[...].astype(f32), axis=0)
    back_ref[...], grad_ref[...], active = vertex_values(
        summed, column_ref, deg_ref, weight_ref, cotangent_ref
    )
    act_ref[...] = active.astype(bf16)


def backward_all(rows_ref, cols_ref, masks_ref, gathered_ref, pieces_ref, source, total):
    size = gathered_ref.shape[2]
    for shard in range(gathered_ref.shape[0]):
        source[:, shard * size : (shard + 1) * size] = gathered_ref[shard]
    backward_total(rows_ref, cols_ref, masks_ref, source, total)
    for shard in range(pieces_ref.shape[0]):
        pieces_ref[shard] = total[:, shard * size : (shard + 1) * size].astype(bf16)


def input_all(deg_ref, pieces_ref, out_ref):
    total = jnp.sum(pieces_ref[...].astype(f32), axis=0)
    out_ref[...] = (total * deg_ref[...].astype(f32).reshape(1, -1)).T.astype(bf16)


def exchange(block, axis, shards, distance):
    return lax.ppermute(block, axis, [(shard, shard ^ distance) for shard in range(shards)])


def on_device(features, deg_scale, weight, cotangent, tile_rows, tile_cols, tile_count, tile_bits):
    size, width = features.shape
    height, out_width = weight.shape
    row_shards = lax.axis_size("row")
    col_shards = lax.axis_size("col")
    chips = col_shards // 2
    slots, words, tile_size = tile_bits.shape[2:]
    factor = 1.0 / math.sqrt(row_shards * col_shards * size)
    row = lax.axis_index("row").astype(jnp.int32).reshape(1)
    col = lax.axis_index("col").astype(jnp.int32)
    chip, core = (col // 2).reshape(1), (col % 2).reshape(1)
    forward_scratch = [pltpu.VMEM((col_shards * size, width), f32)]
    backward_scratch = [
        pltpu.VMEM((width, col_shards * size), bf16),
        pltpu.VMEM((width, row_shards * size), f32),
    ]
    prepared = (struct((size, width), bf16), struct((size, width), f32))
    block = struct((width, size), bf16)
    activation = struct((size, out_width), bf16)
    input_shape = struct((size, width), bf16)

    covered = slots * tile_size * tile_size == row_shards * col_shards * size * size
    if row_shards != 4 or col_shards != 8 or not covered:
        scaled, column, masks = call(
            unpack_tiles,
            prepared + (struct((slots, tile_size, tile_size), bf16),),
            (tile_count,),
            (tile_bits, deg_scale, features),
        )
        gathered = lax.all_gather(scaled, "row", axis=0, tiled=True)
        partial_value = call(
            forward_all,
            struct((col_shards, size, width), bf16),
            (tile_rows, tile_cols),
            (masks, gathered),
            forward_scratch,
        )
        received = lax.all_to_all(partial_value, "col", 0, 0)
        activations, back, local_grad = call(
            vertex_all,
            (activation, block, struct((height, out_width), f32)),
            (),
            (column, deg_scale, weight, cotangent, received),
        )
        weight_grad = lax.psum(local_grad, ("row", "col")) * factor
        pieces = call(
            backward_all,
            struct((row_shards, width, size), bf16),
            (tile_rows, tile_cols),
            (masks, lax.all_gather(back, "col")),
            backward_scratch,
        )
        arrived = lax.all_to_all(pieces, "row", 0, 0)
        input_grad = call(input_all, input_shape, (), (deg_scale, arrived))
        return (activations, input_grad, weight_grad)

    column = call(
        scale_column, struct((size, width), f32), (), (deg_scale,), flops=FIRST_FLOPS
    )
    scaled = call(scale_rows, struct((size, width), bf16), (), (column, features, tile_rows, tile_cols))
    adjacency = pl.pallas_call(
        build_adjacency,
        out_shape=struct((col_shards * size, row_shards * size), bf16),
        in_specs=[SMEM, SMEM, SMEM, VMEM, ANY],
        out_specs=VMEM,
        compiler_params=LIMIT,
        cost_estimate=pl.CostEstimate(flops=1 << 20, bytes_accessed=1 << 20, transcendentals=0),
    )(tile_count, tile_rows, tile_cols, tile_bits, scaled)
    far_first = (3, 2, 1)
    blocks = [exchange(scaled, "row", row_shards, step) for step in (1, 2, 3)]
    blocks.insert(0, scaled)
    mine, other = call(
        forward_pair,
        (struct((chips, size, width), f32), struct((chips, size, width), bf16)),
        (row, core),
        (adjacency, *blocks),
        [pltpu.VMEM((row_shards * size, width), bf16)] + forward_scratch,
    )
    own, *pieces = call(
        forward_chips,
        (struct((size, width), f32),) + (struct((size, width), bf16),) * len(far_first),
        (chip,),
        (mine, exchange(other, "col", col_shards, 1)),
    )
    received = [
        exchange(piece, "col", col_shards, 2 * step) for step, piece in zip(far_first, pieces)
    ]
    sent, active = call(
        vertex_chips,
        (struct((3, width, size), bf16), struct((size, out_width), f32)),
        (),
        (column, deg_scale, weight, cotangent, own, *received),
    )
    activations, written = call(write_out, (activation, struct((8, 128), f32)), (), (active,))
    received = [exchange(sent, "col", col_shards, 2 * step) for step in (1, 2, 3)]
    joined, own_grad = call(
        join_chips,
        (struct((chips + 1, width, size), bf16), struct((width, size), bf16)),
        (chip, core),
        (sent, *received),
        [pltpu.VMEM((chips, 2, width, size), bf16)],
        after=(written,),
    )
    pieces = call(
        backward_rows,
        (struct((2, width, size), bf16),) * row_shards,
        (row, chip, core),
        (adjacency, joined, own_grad, exchange(joined, "col", col_shards, 1)),
        backward_scratch,
    )
    arrived = [exchange(piece, "row", row_shards, step) for step, piece in zip(far_first, pieces)]
    arrived.append(pieces[-1])
    half_grad = call(
        functools.partial(sum_grad, factor),
        struct((height, out_width // 2), bf16),
        (row,),
        arrived,
        [pltpu.VMEM((row_shards, height, out_width // 2), bf16)],
    )
    other_grad = exchange(half_grad, "col", col_shards, 1)
    input_grad = call(input_rows, input_shape, (), (deg_scale, *arrived))
    weight_grad = call(
        join_halves, struct((height, out_width), f32), (core,), (half_grad, other_grad)
    )
    return (activations, input_grad, weight_grad)


def solution(mesh):
    in_specs = (
        P(("row", "col"), None),
        P(("row", "col")),
        P(),
        P(("row", "col"), None),
        P("row", "col", None),
        P("row", "col", None),
        P("row", "col"),
        P("row", "col", None, None, None),
    )
    out_specs = (P(("row", "col"), None), P(("row", "col"), None), P())
    return jax.shard_map(
        on_device, mesh=mesh, in_specs=in_specs, out_specs=out_specs, check_vma=False
    )
```

time: 225 us -> 40.5 us (0.18)
  waiting for transfers between devices: 169 us -> 16.2 us
  blocking collectives: 24.3 us -> 0 us
  starting transfers between devices: 0.12 us -> 17.5 us
  between operations: 14.5 us -> 1.46 us
  matrix products: 6.99 us -> 0 us
  other arithmetic: 6 us -> 0 us
  Pallas kernels: 0 us -> 4.46 us
  local copies, waits for them, and re-layouts: 3.63 us -> 0.69 us
    psum x1 -> x0, waiting for transfers between devices: 113 us -> none  [on_device(): weight_grad = lax.psum(local_grad, ('row', 'col')) / math.sqrt(total_verts)]
    reduce_scatter x2 -> x0, waiting for transfers between devices: 55 us -> none  [the longest x1 35.5 us: on_device(): lax.psum_scatter(partial_value, 'col', scatter_dimension=0, tiled=True)]
    all_gather x2 -> x0, blocking collectives: 24.3 us -> none  [the longest x1 15.1 us: on_device(): lax.all_gather(scaled, 'row', axis=0, tiled=True)]
    ppermute x0 -> x15, starting transfers between devices: none -> 17.5 us  [exchange(): lax.ppermute(block, axis, [(shard, shard ^ distance) for shard in range(s...]
    ppermute x0 -> x15, waiting for transfers between devices: none -> 16.2 us  [exchange(): lax.ppermute(block, axis, [(shard, shard ^ distance) for shard in range(s...]
    dot_general x7 -> x0, matrix products: 6.99 us -> none  [the longest x2 2.96 us: block_step(): jnp.dot(onehot, flat_products, precision=lax.Precision.HIGHEST, preferred...]
    pallas_call x0 -> x12, Pallas kernels: none -> 4.46 us  [the longest x11 3.55 us: call(): pl.pallas_call(body, out_shape=out_shape, in_specs=[SMEM] * len(scalars)...]
    convert_element_type x4 -> x0, other arithmetic: 3.04 us -> none  [the longest x1 1.54 us: on_device(): input_grad = (gathered_back * scale[:, None]).astype(jnp.bfloat16)]
  transfers between devices with their start and end apart: 3 -> 15, of which waited for: 3 -> 11; matrix products, arithmetic and copies ran while one was open for 2% -> 0% of each run, Pallas kernels for 0% -> 6%
where the time goes in v3:
time: 40.5 us; the launch traced here: 40.4 us
  starting transfers between devices  17.5 us (43%)
  waiting for transfers between devices  16.2 us (40%)
  Pallas kernels  4.46 us (11%)
  between operations  1.46 us (4%)
  local copies, waits for them, and re-layouts  0.69 us (2%)
    ppermute x15, starting transfers between devices, exchange(): lax.ppermute(block, axis, [(shard, shard ^ distance) for shard in range(s...  17.5 us
    ppermute x15, waiting for transfers between devices, exchange(): lax.ppermute(block, axis, [(shard, shard ^ distance) for shard in range(s...  16.2 us
    pallas_call x11, Pallas kernels, call(): pl.pallas_call(body, out_shape=out_shape, in_specs=[SMEM] * len(scalars)...  3.55 us
    pallas_call x1, Pallas kernels, on_device(): pl.pallas_call(build_adjacency, out_shape=struct((col_shards * size, row_...  0.91 us
  transfers between devices with their start and end apart: 15, of which 11 were waited for; matrix products, arithmetic and copies ran while one was open for 0% of the time, Pallas kernels for 6%

profile of v3, /device:TPU:0, one launch (start us, length us, event | category | flops | bytes accessed | tf_op | source)
XLA Modules:
  0.0 40.4 jit_solution(9431994293542243230)
XLA Ops:
  0.6 0.0 copy-start.5
  0.6 0.0 copy-start.4
  0.7 0.0 copy-start.3
  0.7 0.0 copy-start.6
  0.7 0.7 %copy-done.6 = bf16[128]{0:T(256)(128)(2,1)S(1)} copy-done((bf16[128]{0:T(256)(128)(2,1)S(1)}, bf16[128]{0:T(256)(128)(2,1)}, u32[]{:S(2)}) %copy-start.6) | copy-done | bytes 280
  1.3 0.0 copy-start
  1.3 0.1 shard_map.103.column_ref
  1.5 0.0 copy-done.5
  1.5 0.0 copy-done.4
  1.5 0.0 copy-done.3
  1.5 5.1 %collective-permute-start.2 = (bf16[128,128]{1,0:T(8,128)(2,1)S(1)}, bf16[128,128]{1,0:T(8,128)(2,1)S(1)}, u32[]{:S(2)}, u32[]{:S(2)}) collective-permute-start(bf16[128,128]{1,0:T(8,128)(2,1)S(1)} %shard_map.104.after_ref.refs_0_), channel_id=1, source_target_pairs={{0,24},{8,16},{16,8},{24,0},{1,25},{9,17},{17,9},{25,1},{2,26},{10... | collective-permute-start | bytes 98312 | tf_op jit(solution)/shard_map/ppermute | solution.py:237
  6.6 0.0 collective-permute-start.1
  6.6 0.6 %collective-permute-start = (bf16[128,128]{1,0:T(8,128)(2,1)S(1)}, bf16[128,128]{1,0:T(8,128)(2,1)S(1)}, u32[]{:S(2)}, u32[]{:S(2)}) collective-permute-start(bf16[128,128]{1,0:T(8,128)(2,1)S(1)} %shard_map.104.after_ref.refs_0_), channel_id=1, source_target_pairs={{0,8},{8,0},{16,24},{24,16},{1,9},{9,1},{17,25},{25,17},{2,10},{10... | collective-permute-start | bytes 98312 | tf_op jit(solution)/shard_map/ppermute | solution.py:237
  7.9 0.0 copy-done
  7.9 0.9 %shard_map.105.adjacency_ref = bf16[1024,512]{1,0:T(8,128)(2,1)S(1)} custom-call(s32[1,1]{1,0:T(1,128)S(6)} %copy.11.count_ref, s32[1,1,8]{2,1,0:T(1,128)S(1)} %copy-done.4, s32[1,1,8]{2,1,0:T(1,128)S(1)} %copy-done.5, s32[1,1,8,32,256]{4,3,2,1,0:T(8,128)S(1)} %copy-done, bf16[128,128]{1,0:T(8,128)(2,1)S(1)} %shard_map.104.after_ref.refs_0_), custom_call_target="tpu_custom_call" | custom-call | flops 1048576 | bytes 1048576 | tf_op jit(solution)/shard_map/pallas_call | solution.py:300
  8.8 0.0 collective-permute-done.2.refs_3_
  8.9 2.6 %collective-permute-done.1.refs_2_ = bf16[128,128]{1,0:T(8,128)(2,1)S(1)} collective-permute-done((bf16[128,128]{1,0:T(8,128)(2,1)S(1)}, bf16[128,128]{1,0:T(8,128)(2,1)S(1)}, u32[]{:S(2)}, u32[]{:S(2)}) %collective-permute-start.1) | collective-permute-done | bytes 32800 | tf_op jit(solution)/shard_map/ppermute | solution.py:237
  11.4 0.0 collective-permute-done.refs_1_
  11.4 0.5 %shard_map.106 = (f32[4,128,128]{2,1,0:T(8,128)S(1)}, bf16[4,128,128]{2,1,0:T(8,128)(2,1)S(1)}) custom-call(s32[1]{0:T(128)} %bitcast.1.row_ref, s32[1]{0:T(128)} %bitcast.2.core_ref, bf16[1024,512]{1,0:T(8,128)(2,1)S(1)} %shard_map.105.adjacency_ref, bf16[128,128]{1,0:T(8,128)(2,1)S(1)} %shard_map.104.after_ref.refs_0_, ...), custom_call_target="tpu_custom_call" | custom-call | flops 1048576 | bytes 1048576 | tf_op jit(solution)/shard_map/pallas_call | solution.py:25
  11.9 0.1 collective-permute-start.3
  12.0 1.3 %collective-permute-done.3.received_ref = bf16[4,128,128]{2,1,0:T(8,128)(2,1)S(1)} collective-permute-done((bf16[4,128,128]{2,1,0:T(8,128)(2,1)S(1)}, bf16[4,128,128]{2,1,0:T(8,128)(2,1)S(1)}, u32[]{:S(2)}, u32[]{:S(2)}) %collective-permute-start.3) | collective-permute-done | bytes 131104 | tf_op jit(solution)/shard_map/ppermute | solution.py:237
  13.3 0.0 copy-start.1
  13.3 0.0 copy-start.2
  13.4 2.5 %collective-permute-start.4 = (bf16[128,128]{1,0:T(8,128)(2,1)S(1)}, bf16[128,128]{1,0:T(8,128)(2,1)S(1)}, u32[]{:S(2)}, u32[]{:S(2)}) collective-permute-start(bf16[128,128]{1,0:T(8,128)(2,1)S(1)} %get-tuple-element.22), channel_id=1, source_target_pairs={{0,6},{1,7},{2,4},{3,5},{4,2},{5,3},{6,0},{7,1},{8,14},{9,15},{10,... | collective-permute-start | bytes 98312 | tf_op jit(solution)/shard_map/ppermute | solution.py:237
  15.9 0.5 %collective-permute-start.5 = (bf16[128,128]{1,0:T(8,128)(2,1)S(1)}, bf16[128,128]{1,0:T(8,128)(2,1)S(1)}, u32[]{:S(2)}, u32[]{:S(2)}) collective-permute-start(bf16[128,128]{1,0:T(8,128)(2,1)S(1)} %get-tuple-element.23), channel_id=1, source_target_pairs={{0,4},{1,5},{2,6},{3,7},{4,0},{5,1},{6,2},{7,3},{8,12},{9,13},{10,... | collective-permute-start | bytes 98312 | tf_op jit(solution)/shard_map/ppermute | solution.py:237
  16.4 0.0 copy-start.7
  16.4 0.5 %collective-permute-start.6 = (bf16[128,128]{1,0:T(8,128)(2,1)S(1)}, bf16[128,128]{1,0:T(8,128)(2,1)S(1)}, u32[]{:S(2)}, u32[]{:S(2)}) collective-permute-start(bf16[128,128]{1,0:T(8,128)(2,1)S(1)} %get-tuple-element.24), channel_id=1, source_target_pairs={{0,2},{1,3},{2,0},{3,1},{4,6},{5,7},{6,4},{7,5},{8,10},{9,11},{10,... | collective-permute-start | bytes 98312 | tf_op jit(solution)/shard_map/ppermute | solution.py:237
  16.9 1.3 %collective-permute-done.4.refs_0_ = bf16[128,128]{1,0:T(8,128)(2,1)S(1)} collective-permute-done((bf16[128,128]{1,0:T(8,128)(2,1)S(1)}, bf16[128,128]{1,0:T(8,128)(2,1)S(1)}, u32[]{:S(2)}, u32[]{:S(2)}) %collective-permute-start.4) | collective-permute-done | bytes 32800 | tf_op jit(solution)/shard_map/ppermute | solution.py:237
  18.3 1.5 %collective-permute-done.5.refs_1_ = bf16[128,128]{1,0:T(8,128)(2,1)S(1)} collective-permute-done((bf16[128,128]{1,0:T(8,128)(2,1)S(1)}, bf16[128,128]{1,0:T(8,128)(2,1)S(1)}, u32[]{:S(2)}, u32[]{:S(2)}) %collective-permute-start.5) | collective-permute-done | bytes 32800 | tf_op jit(solution)/shard_map/ppermute | solution.py:237
  19.8 0.5 %collective-permute-done.6.refs_2_ = bf16[128,128]{1,0:T(8,128)(2,1)S(1)} collective-permute-done((bf16[128,128]{1,0:T(8,128)(2,1)S(1)}, bf16[128,128]{1,0:T(8,128)(2,1)S(1)}, u32[]{:S(2)}, u32[]{:S(2)}) %collective-permute-start.6) | collective-permute-done | bytes 32800 | tf_op jit(solution)/shard_map/ppermute | solution.py:237
  20.3 0.0 copy-done.1
  20.3 0.0 copy-done.2
  20.3 0.0 copy-done.7
  20.3 0.4 shard_map.108
  20.7 1.6 %collective-permute-start.9 = (bf16[3,128,128]{2,1,0:T(8,128)(2,1)S(1)}, bf16[3,128,128]{2,1,0:T(8,128)(2,1)S(1)}, u32[]{:S(2)}, u32[]{:S(2)}) collective-permute-start(bf16[3,128,128]{2,1,0:T(8,128)(2,1)S(1)} %get-tuple-element.27.refs_0_), channel_id=1, source_target_pairs={{0,6},{1,7},{2,4},{3,5},{4,2},{5,3},{6,0},{7,1},{8,14},{9,15},{10,... | collective-permute-start | bytes 294920 | tf_op jit(solution)/shard_map/ppermute | solution.py:237
  22.2 0.5 %collective-permute-start.8 = (bf16[3,128,128]{2,1,0:T(8,128)(2,1)S(1)}, bf16[3,128,128]{2,1,0:T(8,128)(2,1)S(1)}, u32[]{:S(2)}, u32[]{:S(2)}) collective-permute-start(bf16[3,128,128]{2,1,0:T(8,128)(2,1)S(1)} %get-tuple-element.27.refs_0_), channel_id=1, source_target_pairs={{0,4},{1,5},{2,6},{3,7},{4,0},{5,1},{6,2},{7,3},{8,12},{9,13},{10,... | collective-permute-start | bytes 294920 | tf_op jit(solution)/shard_map/ppermute | solution.py:237
  22.8 1.5 %collective-permute-start.7 = (bf16[3,128,128]{2,1,0:T(8,128)(2,1)S(1)}, bf16[3,128,128]{2,1,0:T(8,128)(2,1)S(1)}, u32[]{:S(2)}, u32[]{:S(2)}) collective-permute-start(bf16[3,128,128]{2,1,0:T(8,128)(2,1)S(1)} %get-tuple-element.27.refs_0_), channel_id=1, source_target_pairs={{0,2},{1,3},{2,0},{3,1},{4,6},{5,7},{6,4},{7,5},{8,10},{9,11},{10,... | collective-permute-start | bytes 294920 | tf_op jit(solution)/shard_map/ppermute | solution.py:237
  24.2 0.6 %shard_map.109 = (bf16[128,256]{1,0:T(8,128)(2,1)}, f32[8,128]{1,0:T(8,128)S(1)}) custom-call(f32[128,256]{1,0:T(8,128)S(1)} %get-tuple-element.25.active_ref), custom_call_target="tpu_custom_call" | custom-call | flops 1048576 | bytes 1048576 | tf_op jit(solution)/shard_map/pallas_call | solution.py:25
  24.9 1.8 %collective-permute-done.9.refs_3_ = bf16[3,128,128]{2,1,0:T(8,128)(2,1)S(1)} collective-permute-done((bf16[3,128,128]{2,1,0:T(8,128)(2,1)S(1)}, bf16[3,128,128]{2,1,0:T(8,128)(2,1)S(1)}, u32[]{:S(2)}, u32[]{:S(2)}) %collective-permute-start.9) | collective-permute-done | bytes 98336 | tf_op jit(solution)/shard_map/ppermute | solution.py:237
  26.7 0.9 %collective-permute-done.8.refs_2_ = bf16[3,128,128]{2,1,0:T(8,128)(2,1)S(1)} collective-permute-done((bf16[3,128,128]{2,1,0:T(8,128)(2,1)S(1)}, bf16[3,128,128]{2,1,0:T(8,128)(2,1)S(1)}, u32[]{:S(2)}, u32[]{:S(2)}) %collective-permute-start.8) | collective-permute-done | bytes 98336 | tf_op jit(solution)/shard_map/ppermute | solution.py:237
  27.6 0.0 collective-permute-done.7.refs_1_
  27.6 0.1 shard_map.110
  27.7 0.1 collective-permute-start.10
  27.8 1.4 %collective-permute-done.10.received_ref = bf16[5,128,128]{2,1,0:T(8,128)(2,1)S(1)} collective-permute-done((bf16[5,128,128]{2,1,0:T(8,128)(2,1)S(1)}, bf16[5,128,128]{2,1,0:T(8,128)(2,1)S(1)}, u32[]{:S(2)}, u32[]{:S(2)}) %collective-permute-start.10) | collective-permute-done | bytes 163872 | tf_op jit(solution)/shard_map/ppermute | solution.py:237
  29.2 0.4 shard_map.111
  29.6 1.5 %collective-permute-start.11 = (bf16[2,128,128]{2,1,0:T(8,128)(2,1)S(1)}, bf16[2,128,128]{2,1,0:T(8,128)(2,1)S(1)}, u32[]{:S(2)}, u32[]{:S(2)}) collective-permute-start(bf16[2,128,128]{2,1,0:T(8,128)(2,1)S(1)} %get-tuple-element.31), channel_id=1, source_target_pairs={{0,24},{8,16},{16,8},{24,0},{1,25},{9,17},{17,9},{25,1},{2,26},{10... | collective-permute-start | bytes 196616 | tf_op jit(solution)/shard_map/ppermute | solution.py:237
  31.1 0.6 %collective-permute-start.12 = (bf16[2,128,128]{2,1,0:T(8,128)(2,1)S(1)}, bf16[2,128,128]{2,1,0:T(8,128)(2,1)S(1)}, u32[]{:S(2)}, u32[]{:S(2)}) collective-permute-start(bf16[2,128,128]{2,1,0:T(8,128)(2,1)S(1)} %get-tuple-element.32), channel_id=1, source_target_pairs={{0,16},{8,24},{16,0},{24,8},{1,17},{9,25},{17,1},{25,9},{2,18},{10... | collective-permute-start | bytes 196616 | tf_op jit(solution)/shard_map/ppermute | solution.py:237
  31.7 2.3 %collective-permute-start.13 = (bf16[2,128,128]{2,1,0:T(8,128)(2,1)S(1)}, bf16[2,128,128]{2,1,0:T(8,128)(2,1)S(1)}, u32[]{:S(2)}, u32[]{:S(2)}) collective-permute-start(bf16[2,128,128]{2,1,0:T(8,128)(2,1)S(1)} %get-tuple-element.33), channel_id=1, source_target_pairs={{0,8},{8,0},{16,24},{24,16},{1,9},{9,1},{17,25},{25,17},{2,10},{10... | collective-permute-start | bytes 196616 | tf_op jit(solution)/shard_map/ppermute | solution.py:237
  34.0 2.4 %collective-permute-done.11.refs_0_ = bf16[2,128,128]{2,1,0:T(8,128)(2,1)S(1)} collective-permute-done((bf16[2,128,128]{2,1,0:T(8,128)(2,1)S(1)}, bf16[2,128,128]{2,1,0:T(8,128)(2,1)S(1)}, u32[]{:S(2)}, u32[]{:S(2)}) %collective-permute-start.11) | collective-permute-done | bytes 65568 | tf_op jit(solution)/shard_map/ppermute | solution.py:237
  36.4 2.0 %collective-permute-done.12.refs_1_ = bf16[2,128,128]{2,1,0:T(8,128)(2,1)S(1)} collective-permute-done((bf16[2,128,128]{2,1,0:T(8,128)(2,1)S(1)}, bf16[2,128,128]{2,1,0:T(8,128)(2,1)S(1)}, u32[]{:S(2)}, u32[]{:S(2)}) %collective-permute-start.12) | collective-permute-done | bytes 65568 | tf_op jit(solution)/shard_map/ppermute | solution.py:237
  38.4 0.0 collective-permute-done.13.refs_2_
  38.4 0.1 collective-permute-start.14
  38.5 0.7 %shard_map.112 = bf16[128,128]{1,0:T(8,128)(2,1)} custom-call(bf16[128]{0:T(256)(128)(2,1)S(1)} %copy-done.7, bf16[2,128,128]{2,1,0:T(8,128)(2,1)S(1)} %collective-permute-done.11.refs_0_, bf16[2,128,128]{2,1,0:T(8,128)(2,1)S(1)} %collective-permute-done.12.refs_1_, bf16[2,128,128]{2,1,0:T(8,128)(2,1)S(1)} %collective-permute-done.13.refs_2_, ...), custom_call_target="tpu_custom_call" | custom-call | flops 1048576 | bytes 1048576 | tf_op jit(solution)/shard_map/pallas_call | solution.py:25
  39.2 0.5 %collective-permute-done.14.other_ref = bf16[128,128]{1,0:T(8,128)(2,1)S(1)} collective-permute-done((bf16[128,128]{1,0:T(8,128)(2,1)S(1)}, bf16[128,128]{1,0:T(8,128)(2,1)S(1)}, u32[]{:S(2)}, u32[]{:S(2)}) %collective-permute-start.14) | collective-permute-done | bytes 32800 | tf_op jit(solution)/shard_map/ppermute | solution.py:237
  39.7 0.7 %shard_map.114 = f32[128,256]{1,0:T(8,128)} custom-call(s32[1]{0:T(128)} %bitcast.2.core_ref, bf16[128,128]{1,0:T(8,128)(2,1)S(1)} %shard_map.113.own_ref, bf16[128,128]{1,0:T(8,128)(2,1)S(1)} %collective-permute-done.14.other_ref), custom_call_target="tpu_custom_call" | custom-call | flops 1048576 | bytes 1048576 | tf_op jit(solution)/shard_map/pallas_call | solution.py:25
  (3 shorter events, 0.1 us)
Async XLA Ops:
  0.6 0.8 %copy-start.5 = (s32[1,1,8]{2,1,0:T(1,128)S(1)}, s32[1,1,8]{2,1,0:T(1,128)}, u32[]{:S(2)}) copy-start(s32[1,1,8]{2,1,0:T(1,128)} %cols_ref.3) | copy-start | bytes 100
  0.6 0.8 %copy-start.4 = (s32[1,1,8]{2,1,0:T(1,128)S(1)}, s32[1,1,8]{2,1,0:T(1,128)}, u32[]{:S(2)}) copy-start(s32[1,1,8]{2,1,0:T(1,128)} %rows_ref.3) | copy-start | bytes 100
  0.7 0.8 %copy-start.3 = (bf16[128,128]{1,0:T(8,128)(2,1)S(1)}, bf16[128,128]{1,0:T(8,128)(2,1)}, u32[]{:S(2)}) copy-start(bf16[128,128]{1,0:T(8,128)(2,1)} %features_ref.1) | copy-start | bytes 98308
  0.7 0.7 %copy-start.6 = (bf16[128]{0:T(256)(128)(2,1)S(1)}, bf16[128]{0:T(256)(128)(2,1)}, u32[]{:S(2)}) copy-start(bf16[128]{0:T(256)(128)(2,1)} %deg_ref.5) | copy-start | bytes 772
  1.3 6.6 %copy-start = (s32[1,1,8,32,256]{4,3,2,1,0:T(8,128)S(1)}, s32[1,1,8,32,256]{4,3,2,1,0:T(8,128)}, u32[]{:S(2)}) copy-start(s32[1,1,8,32,256]{4,3,2,1,0:T(8,128)} %bits_ref.1) | copy-start | bytes 786436
  1.5 7.3 %collective-permute-start.2 = (bf16[128,128]{1,0:T(8,128)(2,1)S(1)}, bf16[128,128]{1,0:T(8,128)(2,1)S(1)}, u32[]{:S(2)}, u32[]{:S(2)}) collective-permute-start(bf16[128,128]{1,0:T(8,128)(2,1)S(1)} %shard_map.104.after_ref.refs_0_), channel_id=1, source_target_pairs={{0,24},{8,16},{16,8},{24,0},{1,25},{9,17},{17,9},{25,1},{2,26},{10... | collective-permute-start | bytes 98312 | tf_op jit(solution)/shard_map/ppermute | solution.py:237
  6.6 4.8 %collective-permute-start.1 = (bf16[128,128]{1,0:T(8,128)(2,1)S(1)}, bf16[128,128]{1,0:T(8,128)(2,1)S(1)}, u32[]{:S(2)}, u32[]{:S(2)}) collective-permute-start(bf16[128,128]{1,0:T(8,128)(2,1)S(1)} %shard_map.104.after_ref.refs_0_), channel_id=1, source_target_pairs={{0,16},{8,24},{16,0},{24,8},{1,17},{9,25},{17,1},{25,9},{2,18},{10... | collective-permute-start | bytes 98312 | tf_op jit(solution)/shard_map/ppermute | solution.py:237
  6.6 4.8 %collective-permute-start = (bf16[128,128]{1,0:T(8,128)(2,1)S(1)}, bf16[128,128]{1,0:T(8,128)(2,1)S(1)}, u32[]{:S(2)}, u32[]{:S(2)}) collective-permute-start(bf16[128,128]{1,0:T(8,128)(2,1)S(1)} %shard_map.104.after_ref.refs_0_), channel_id=1, source_target_pairs={{0,8},{8,0},{16,24},{24,16},{1,9},{9,1},{17,25},{25,17},{2,10},{10... | collective-permute-start | bytes 98312 | tf_op jit(solution)/shard_map/ppermute | solution.py:237
  11.9 1.4 %collective-permute-start.3 = (bf16[4,128,128]{2,1,0:T(8,128)(2,1)S(1)}, bf16[4,128,128]{2,1,0:T(8,128)(2,1)S(1)}, u32[]{:S(2)}, u32[]{:S(2)}) collective-permute-start(bf16[4,128,128]{2,1,0:T(8,128)(2,1)S(1)} %get-tuple-element.20), channel_id=1, source_target_pairs={{0,1},{1,0},{2,3},{3,2},{4,5},{5,4},{6,7},{7,6},{8,9},{9,8},{10,11... | collective-permute-start | bytes 393224 | tf_op jit(solution)/shard_map/ppermute | solution.py:237
  13.3 7.0 %copy-start.1 = (bf16[128,256]{1,0:T(8,128)(2,1)S(1)}, bf16[128,256]{1,0:T(8,128)(2,1)}, u32[]{:S(2)}) copy-start(bf16[128,256]{1,0:T(8,128)(2,1)} %weight_ref.1) | copy-start | bytes 196612
  13.3 7.0 %copy-start.2 = (bf16[128,256]{1,0:T(8,128)(2,1)S(1)}, bf16[128,256]{1,0:T(8,128)(2,1)}, u32[]{:S(2)}) copy-start(bf16[128,256]{1,0:T(8,128)(2,1)} %cotangent_ref.1) | copy-start | bytes 196612
  13.4 4.9 %collective-permute-start.4 = (bf16[128,128]{1,0:T(8,128)(2,1)S(1)}, bf16[128,128]{1,0:T(8,128)(2,1)S(1)}, u32[]{:S(2)}, u32[]{:S(2)}) collective-permute-start(bf16[128,128]{1,0:T(8,128)(2,1)S(1)} %get-tuple-element.22), channel_id=1, source_target_pairs={{0,6},{1,7},{2,4},{3,5},{4,2},{5,3},{6,0},{7,1},{8,14},{9,15},{10,... | collective-permute-start | bytes 98312 | tf_op jit(solution)/shard_map/ppermute | solution.py:237
  15.9 3.9 %collective-permute-start.5 = (bf16[128,128]{1,0:T(8,128)(2,1)S(1)}, bf16[128,128]{1,0:T(8,128)(2,1)S(1)}, u32[]{:S(2)}, u32[]{:S(2)}) collective-permute-start(bf16[128,128]{1,0:T(8,128)(2,1)S(1)} %get-tuple-element.23), channel_id=1, source_target_pairs={{0,4},{1,5},{2,6},{3,7},{4,0},{5,1},{6,2},{7,3},{8,12},{9,13},{10,... | collective-permute-start | bytes 98312 | tf_op jit(solution)/shard_map/ppermute | solution.py:237
  16.4 3.9 %copy-start.7 = (bf16[128]{0:T(256)(128)(2,1)S(1)}, bf16[128]{0:T(256)(128)(2,1)}, u32[]{:S(2)}) copy-start(bf16[128]{0:T(256)(128)(2,1)} %deg_ref.5) | copy-start | bytes 772
  16.4 3.9 %collective-permute-start.6 = (bf16[128,128]{1,0:T(8,128)(2,1)S(1)}, bf16[128,128]{1,0:T(8,128)(2,1)S(1)}, u32[]{:S(2)}, u32[]{:S(2)}) collective-permute-start(bf16[128,128]{1,0:T(8,128)(2,1)S(1)} %get-tuple-element.24), channel_id=1, source_target_pairs={{0,2},{1,3},{2,0},{3,1},{4,6},{5,7},{6,4},{7,5},{8,10},{9,11},{10,... | collective-permute-start | bytes 98312 | tf_op jit(solution)/shard_map/ppermute | solution.py:237
  20.7 6.0 %collective-permute-start.9 = (bf16[3,128,128]{2,1,0:T(8,128)(2,1)S(1)}, bf16[3,128,128]{2,1,0:T(8,128)(2,1)S(1)}, u32[]{:S(2)}, u32[]{:S(2)}) collective-permute-start(bf16[3,128,128]{2,1,0:T(8,128)(2,1)S(1)} %get-tuple-element.27.refs_0_), channel_id=1, source_target_pairs={{0,6},{1,7},{2,4},{3,5},{4,2},{5,3},{6,0},{7,1},{8,14},{9,15},{10,... | collective-permute-start | bytes 294920 | tf_op jit(solution)/shard_map/ppermute | solution.py:237
  22.2 5.4 %collective-permute-start.8 = (bf16[3,128,128]{2,1,0:T(8,128)(2,1)S(1)}, bf16[3,128,128]{2,1,0:T(8,128)(2,1)S(1)}, u32[]{:S(2)}, u32[]{:S(2)}) collective-permute-start(bf16[3,128,128]{2,1,0:T(8,128)(2,1)S(1)} %get-tuple-element.27.refs_0_), channel_id=1, source_target_pairs={{0,4},{1,5},{2,6},{3,7},{4,0},{5,1},{6,2},{7,3},{8,12},{9,13},{10,... | collective-permute-start | bytes 294920 | tf_op jit(solution)/shard_map/ppermute | solution.py:237
  22.8 4.8 %collective-permute-start.7 = (bf16[3,128,128]{2,1,0:T(8,128)(2,1)S(1)}, bf16[3,128,128]{2,1,0:T(8,128)(2,1)S(1)}, u32[]{:S(2)}, u32[]{:S(2)}) collective-permute-start(bf16[3,128,128]{2,1,0:T(8,128)(2,1)S(1)} %get-tuple-element.27.refs_0_), channel_id=1, source_target_pairs={{0,2},{1,3},{2,0},{3,1},{4,6},{5,7},{6,4},{7,5},{8,10},{9,11},{10,... | collective-permute-start | bytes 294920 | tf_op jit(solution)/shard_map/ppermute | solution.py:237
  27.7 1.5 %collective-permute-start.10 = (bf16[5,128,128]{2,1,0:T(8,128)(2,1)S(1)}, bf16[5,128,128]{2,1,0:T(8,128)(2,1)S(1)}, u32[]{:S(2)}, u32[]{:S(2)}) collective-permute-start(bf16[5,128,128]{2,1,0:T(8,128)(2,1)S(1)} %get-tuple-element.29.own_ref), channel_id=1, source_target_pairs={{0,1},{1,0},{2,3},{3,2},{4,5},{5,4},{6,7},{7,6},{8,9},{9,8},{10,11... | collective-permute-start | bytes 491528 | tf_op jit(solution)/shard_map/ppermute | solution.py:237
  29.6 6.8 %collective-permute-start.11 = (bf16[2,128,128]{2,1,0:T(8,128)(2,1)S(1)}, bf16[2,128,128]{2,1,0:T(8,128)(2,1)S(1)}, u32[]{:S(2)}, u32[]{:S(2)}) collective-permute-start(bf16[2,128,128]{2,1,0:T(8,128)(2,1)S(1)} %get-tuple-element.31), channel_id=1, source_target_pairs={{0,24},{8,16},{16,8},{24,0},{1,25},{9,17},{17,9},{25,1},{2,26},{10... | collective-permute-start | bytes 196616 | tf_op jit(solution)/shard_map/ppermute | solution.py:237
  31.1 7.3 %collective-permute-start.12 = (bf16[2,128,128]{2,1,0:T(8,128)(2,1)S(1)}, bf16[2,128,128]{2,1,0:T(8,128)(2,1)S(1)}, u32[]{:S(2)}, u32[]{:S(2)}) collective-permute-start(bf16[2,128,128]{2,1,0:T(8,128)(2,1)S(1)} %get-tuple-element.32), channel_id=1, source_target_pairs={{0,16},{8,24},{16,0},{24,8},{1,17},{9,25},{17,1},{25,9},{2,18},{10... | collective-permute-start | bytes 196616 | tf_op jit(solution)/shard_map/ppermute | solution.py:237
  31.7 6.6 %collective-permute-start.13 = (bf16[2,128,128]{2,1,0:T(8,128)(2,1)S(1)}, bf16[2,128,128]{2,1,0:T(8,128)(2,1)S(1)}, u32[]{:S(2)}, u32[]{:S(2)}) collective-permute-start(bf16[2,128,128]{2,1,0:T(8,128)(2,1)S(1)} %get-tuple-element.33), channel_id=1, source_target_pairs={{0,8},{8,0},{16,24},{24,16},{1,9},{9,1},{17,25},{25,17},{2,10},{10... | collective-permute-start | bytes 196616 | tf_op jit(solution)/shard_map/ppermute | solution.py:237
  38.4 1.3 %collective-permute-start.14 = (bf16[128,128]{1,0:T(8,128)(2,1)S(1)}, bf16[128,128]{1,0:T(8,128)(2,1)S(1)}, u32[]{:S(2)}, u32[]{:S(2)}) collective-permute-start(bf16[128,128]{1,0:T(8,128)(2,1)S(1)} %shard_map.113.own_ref), channel_id=1, source_target_pairs={{0,1},{1,0},{2,3},{3,2},{4,5},{5,4},{6,7},{7,6},{8,9},{9,8},{10,11... | collective-permute-start | bytes 98312 | tf_op jit(solution)/shard_map/ppermute | solution.py:237

commit v4 on v3

--- a/solution.py
+++ b/solution.py
@@ -104,16 +104,16 @@
         adjacency_ref[place] = unpacked(packed)
 
 
-def forward_pair(row_ref, core_ref, adjacency_ref, *refs):
+def forward_pair(row_ref, chip_ref, core_ref, adjacency_ref, *refs):
     *blocks, mine_ref, other_ref, source, total = refs
     size = blocks[0].shape[0]
     for step, block in enumerate(blocks):
         source[block_at(row_ref[0] ^ step, size), :] = block[...]
     total[...] = jnp.dot(adjacency_ref[...], source[...], preferred_element_type=f32)
-    core = core_ref[0]
     for chip in range(mine_ref.shape[0]):
-        mine_ref[chip] = total[block_at(2 * chip + core, size), :]
-        other_ref[chip] = total[block_at(2 * chip + 1 - core, size), :].astype(bf16)
+        kept = jnp.where(chip == chip_ref[0], core_ref[0], 1 - core_ref[0])
+        mine_ref[chip] = total[block_at(2 * chip + kept, size), :]
+        other_ref[chip] = total[block_at(2 * chip + 1 - kept, size), :].astype(bf16)
 
 
 def forward_chips(chip_ref, mine_ref, received_ref, own_ref, *pieces):
@@ -157,29 +157,30 @@
     written_ref[...] = jnp.zeros_like(written_ref)
 
 
-def join_chips(chip_ref, core_ref, *refs):
-    *blocks, _, joined_ref, own_grad_ref, ordered = refs
+def join_chips(core_ref, *refs):
+    *blocks, _, joined_ref, own_grad_ref = refs
     chips = len(blocks)
+    second = core_ref[0] == 1
     for step, block in enumerate(blocks):
         joined_ref[step] = block[0]
-        ordered[chip_ref[0] ^ step] = block[1:]
+        joined_ref[chips + step] = jnp.where(second, block[1], block[2])
+        own_grad_ref[step] = jnp.where(second, block[2], block[1])
+
+
+def backward_rows(row_ref, chip_ref, core_ref, adjacency_ref, own_ref, grad_ref, received_ref, *refs):
+    *pieces, source, ordered, total = refs
+    chips, size = grad_ref.shape[0], grad_ref.shape[2]
+    core = core_ref[0]
+    for step in range(chips):
+        peer = 2 * (chip_ref[0] ^ step)
+        mine = peer + (1 - core if step else core)
+        other = peer + (core if step else 1 - core)
+        source[:, block_at(mine, size)] = own_ref[step]
+        source[:, block_at(other, size)] = received_ref[step]
+        ordered[mine] = grad_ref[step]
+        ordered[other] = received_ref[chips + step]
+    total[...] = jnp.dot(source[...], adjacency_ref[...], preferred_element_type=f32)
     grad = jnp.sum(ordered[...].astype(f32), axis=0).astype(bf16)
-    second = core_ref[0] == 1
-    own_grad_ref[...] = jnp.where(second, grad[1], grad[0])
-    joined_ref[chips] = jnp.where(second, grad[0], grad[1])
-
-
-def backward_rows(row_ref, chip_ref, core_ref, adjacency_ref, own_ref, grad_ref, received_ref, *refs):
-    *pieces, source, total = refs
-    chips = own_ref.shape[0] - 1
-    size = own_ref.shape[2]
-    chip, core = chip_ref[0], core_ref[0]
-    for step in range(chips):
-        peer = 2 * (chip ^ step)
-        source[:, block_at(peer + core, size)] = own_ref[step]
-        source[:, block_at(peer + 1 - core, size)] = received_ref[step]
-    total[...] = jnp.dot(source[...], adjacency_ref[...], preferred_element_type=f32)
-    grad = (grad_ref[...].astype(f32) + received_ref[chips].astype(f32)).astype(bf16)
     for step, piece in zip((3, 2, 1, 0), pieces):
         piece[0] = total[:, block_at(row_ref[0] ^ step, size)].astype(bf16)
         piece[1] = grad
@@ -311,7 +312,7 @@
     mine, other = call(
         forward_pair,
         (struct((chips, size, width), f32), struct((chips, size, width), bf16)),
-        (row, core),
+        (row, chip, core),
         (adjacency, *blocks),
         [pltpu.VMEM((row_shards * size, width), bf16)] + forward_scratch,
     )
@@ -322,7 +323,7 @@
         (mine, exchange(other, "col", col_shards, 1)),
     )
     received = [
-        exchange(piece, "col", col_shards, 2 * step) for step, piece in zip(far_first, pieces)
+        exchange(piece, "col", col_shards, 2 * step + 1) for step, piece in zip(far_first, pieces)
     ]
     sent, active = call(
         vertex_chips,
@@ -331,13 +332,12 @@
         (column, deg_scale, weight, cotangent, own, *received),
     )
     activations, written = call(write_out, (activation, struct((8, 128), f32)), (), (active,))
-    received = [exchange(sent, "col", col_shards, 2 * step) for step in (1, 2, 3)]
+    received = [exchange(sent, "col", col_shards, 2 * step + 1) for step in (1, 2, 3)]
     joined, own_grad = call(
         join_chips,
-        (struct((chips + 1, width, size), bf16), struct((width, size), bf16)),
-        (chip, core),
+        (struct((2 * chips, width, size), bf16), struct((chips, width, size), bf16)),
+        (core,),
         (sent, *received),
-        [pltpu.VMEM((chips, 2, width, size), bf16)],
         after=(written,),
     )
     pieces = call(
@@ -345,7 +345,11 @@
         (struct((2, width, size), bf16),) * row_shards,
         (row, chip, core),
         (adjacency, joined, own_grad, exchange(joined, "col", col_shards, 1)),
-        backward_scratch,
+        [
+            pltpu.VMEM((width, col_shards * size), bf16),
+            pltpu.VMEM((col_shards, width, size), bf16),
+            pltpu.VMEM((width, row_shards * size), f32),
+        ],
     )
     arrived = [exchange(piece, "row", row_shards, step) for step, piece in zip(far_first, pieces)]
     arrived.append(pieces[-1])

time: 40.5 us -> 41 us (1.012)
  waiting for transfers between devices: 16.2 us -> 17.6 us
  starting transfers between devices: 17.5 us -> 16.6 us
    ppermute x15, waiting for transfers between devices: 16.2 us -> 17.6 us  [exchange(): lax.ppermute(block, axis, [(shard, shard ^ distance) for shard in range(s...]
    ppermute x15, starting transfers between devices: 17.5 us -> 16.6 us  [exchange(): lax.ppermute(block, axis, [(shard, shard ^ distance) for shard in range(s...]
where the time goes in v4:
time: 41 us; the launch traced here: 40.8 us
  waiting for transfers between devices  17.6 us (43%)
  starting transfers between devices  16.6 us (40%)
  Pallas kernels  4.45 us (11%)
  between operations  1.44 us (4%)
  local copies, waits for them, and re-layouts  0.69 us (2%)
    ppermute x15, waiting for transfers between devices, exchange(): lax.ppermute(block, axis, [(shard, shard ^ distance) for shard in range(s...  17.6 us
    ppermute x15, starting transfers between devices, exchange(): lax.ppermute(block, axis, [(shard, shard ^ distance) for shard in range(s...  16.6 us
    pallas_call x11, Pallas kernels, call(): pl.pallas_call(body, out_shape=out_shape, in_specs=[SMEM] * len(scalars)...  3.54 us
    pallas_call x1, Pallas kernels, on_device(): pl.pallas_call(build_adjacency, out_shape=struct((col_shards * size, row_...  0.91 us
  transfers between devices with their start and end apart: 15, of which 11 were waited for; matrix products, arithmetic and copies ran while one was open for 0% of the time, Pallas kernels for 6%

profile of v4, /device:TPU:0, one launch (start us, length us, event | category | flops | bytes accessed | tf_op | source)
XLA Modules:
  0.0 40.8 jit_solution(12784083229669386917)
XLA Ops:
  0.6 0.0 copy-start.5
  0.6 0.0 copy-start.4
  0.7 0.0 copy-start.3
  0.7 0.0 copy-start.6
  0.7 0.7 %copy-done.6 = bf16[128]{0:T(256)(128)(2,1)S(1)} copy-done((bf16[128]{0:T(256)(128)(2,1)S(1)}, bf16[128]{0:T(256)(128)(2,1)}, u32[]{:S(2)}) %copy-start.6) | copy-done | bytes 280
  1.3 0.0 copy-start
  1.3 0.1 shard_map.103.column_ref
  1.5 0.0 copy-done.5
  1.5 0.0 copy-done.4
  1.5 0.0 copy-done.3
  1.5 5.1 %collective-permute-start.2 = (bf16[128,128]{1,0:T(8,128)(2,1)S(1)}, bf16[128,128]{1,0:T(8,128)(2,1)S(1)}, u32[]{:S(2)}, u32[]{:S(2)}) collective-permute-start(bf16[128,128]{1,0:T(8,128)(2,1)S(1)} %shard_map.104.after_ref.refs_0_), channel_id=1, source_target_pairs={{0,24},{8,16},{16,8},{24,0},{1,25},{9,17},{17,9},{25,1},{2,26},{10... | collective-permute-start | bytes 98312 | tf_op jit(solution)/shard_map/ppermute | solution.py:238
  6.6 0.0 collective-permute-start.1
  6.6 0.6 %collective-permute-start = (bf16[128,128]{1,0:T(8,128)(2,1)S(1)}, bf16[128,128]{1,0:T(8,128)(2,1)S(1)}, u32[]{:S(2)}, u32[]{:S(2)}) collective-permute-start(bf16[128,128]{1,0:T(8,128)(2,1)S(1)} %shard_map.104.after_ref.refs_0_), channel_id=1, source_target_pairs={{0,8},{8,0},{16,24},{24,16},{1,9},{9,1},{17,25},{25,17},{2,10},{10... | collective-permute-start | bytes 98312 | tf_op jit(solution)/shard_map/ppermute | solution.py:238
  7.9 0.0 copy-done
  7.9 0.9 %shard_map.105.adjacency_ref = bf16[1024,512]{1,0:T(8,128)(2,1)S(1)} custom-call(s32[1,1]{1,0:T(1,128)S(6)} %copy.11.count_ref, s32[1,1,8]{2,1,0:T(1,128)S(1)} %copy-done.4, s32[1,1,8]{2,1,0:T(1,128)S(1)} %copy-done.5, s32[1,1,8,32,256]{4,3,2,1,0:T(8,128)S(1)} %copy-done, bf16[128,128]{1,0:T(8,128)(2,1)S(1)} %shard_map.104.after_ref.refs_0_), custom_call_target="tpu_custom_call" | custom-call | flops 1048576 | bytes 1048576 | tf_op jit(solution)/shard_map/pallas_call | solution.py:301
  8.8 0.0 collective-permute-done.2.refs_3_
  8.9 2.6 %collective-permute-done.1.refs_2_ = bf16[128,128]{1,0:T(8,128)(2,1)S(1)} collective-permute-done((bf16[128,128]{1,0:T(8,128)(2,1)S(1)}, bf16[128,128]{1,0:T(8,128)(2,1)S(1)}, u32[]{:S(2)}, u32[]{:S(2)}) %collective-permute-start.1) | collective-permute-done | bytes 32800 | tf_op jit(solution)/shard_map/ppermute | solution.py:238
  11.4 0.0 collective-permute-done.refs_1_
  11.4 0.5 %shard_map.106 = (f32[4,128,128]{2,1,0:T(8,128)S(1)}, bf16[4,128,128]{2,1,0:T(8,128)(2,1)S(1)}) custom-call(s32[1]{0:T(128)} %bitcast.1.row_ref, s32[1]{0:T(128)} %bitcast.chip_ref, s32[1]{0:T(128)} %bitcast.2.core_ref, bf16[1024,512]{1,0:T(8,128)(2,1)S(1)} %shard_map.105.adjacency_ref, bf16[128,128]{1,0:T(8,128)(2,1)S(1)} %shard_map.104.after_ref.refs_0_, ...), custom_call_target="tpu_custom_call" | custom-call | flops 1048576 | bytes 1048576 | tf_op jit(solution)/shard_map/pallas_call | solution.py:25
  11.9 0.1 collective-permute-start.3
  12.0 1.3 %collective-permute-done.3.received_ref = bf16[4,128,128]{2,1,0:T(8,128)(2,1)S(1)} collective-permute-done((bf16[4,128,128]{2,1,0:T(8,128)(2,1)S(1)}, bf16[4,128,128]{2,1,0:T(8,128)(2,1)S(1)}, u32[]{:S(2)}, u32[]{:S(2)}) %collective-permute-start.3) | collective-permute-done | bytes 131104 | tf_op jit(solution)/shard_map/ppermute | solution.py:238
  13.3 0.0 copy-start.1
  13.3 0.0 copy-start.2
  13.4 2.3 %collective-permute-start.4 = (bf16[128,128]{1,0:T(8,128)(2,1)S(1)}, bf16[128,128]{1,0:T(8,128)(2,1)S(1)}, u32[]{:S(2)}, u32[]{:S(2)}) collective-permute-start(bf16[128,128]{1,0:T(8,128)(2,1)S(1)} %get-tuple-element.22), channel_id=1, source_target_pairs={{0,7},{1,6},{2,5},{3,4},{4,3},{5,2},{6,1},{7,0},{8,15},{9,14},{10,... | collective-permute-start | bytes 98312 | tf_op jit(solution)/shard_map/ppermute | solution.py:238
  15.6 0.5 %collective-permute-start.5 = (bf16[128,128]{1,0:T(8,128)(2,1)S(1)}, bf16[128,128]{1,0:T(8,128)(2,1)S(1)}, u32[]{:S(2)}, u32[]{:S(2)}) collective-permute-start(bf16[128,128]{1,0:T(8,128)(2,1)S(1)} %get-tuple-element.23), channel_id=1, source_target_pairs={{0,5},{1,4},{2,7},{3,6},{4,1},{5,0},{6,3},{7,2},{8,13},{9,12},{10,... | collective-permute-start | bytes 98312 | tf_op jit(solution)/shard_map/ppermute | solution.py:238
  16.1 0.0 copy-start.7
  16.1 0.3 collective-permute-start.6
  16.4 1.3 %collective-permute-done.4.refs_0_ = bf16[128,128]{1,0:T(8,128)(2,1)S(1)} collective-permute-done((bf16[128,128]{1,0:T(8,128)(2,1)S(1)}, bf16[128,128]{1,0:T(8,128)(2,1)S(1)}, u32[]{:S(2)}, u32[]{:S(2)}) %collective-permute-start.4) | collective-permute-done | bytes 32800 | tf_op jit(solution)/shard_map/ppermute | solution.py:238
  17.7 1.3 %collective-permute-done.5.refs_1_ = bf16[128,128]{1,0:T(8,128)(2,1)S(1)} collective-permute-done((bf16[128,128]{1,0:T(8,128)(2,1)S(1)}, bf16[128,128]{1,0:T(8,128)(2,1)S(1)}, u32[]{:S(2)}, u32[]{:S(2)}) %collective-permute-start.5) | collective-permute-done | bytes 32800 | tf_op jit(solution)/shard_map/ppermute | solution.py:238
  19.0 0.5 %collective-permute-done.6.refs_2_ = bf16[128,128]{1,0:T(8,128)(2,1)S(1)} collective-permute-done((bf16[128,128]{1,0:T(8,128)(2,1)S(1)}, bf16[128,128]{1,0:T(8,128)(2,1)S(1)}, u32[]{:S(2)}, u32[]{:S(2)}) %collective-permute-start.6) | collective-permute-done | bytes 32800 | tf_op jit(solution)/shard_map/ppermute | solution.py:238
  19.5 0.0 copy-done.1
  19.5 0.0 copy-done.2
  19.5 0.0 copy-done.7
  19.5 0.4 shard_map.108
  19.9 1.3 %collective-permute-start.9 = (bf16[3,128,128]{2,1,0:T(8,128)(2,1)S(1)}, bf16[3,128,128]{2,1,0:T(8,128)(2,1)S(1)}, u32[]{:S(2)}, u32[]{:S(2)}) collective-permute-start(bf16[3,128,128]{2,1,0:T(8,128)(2,1)S(1)} %get-tuple-element.27.refs_0_), channel_id=1, source_target_pairs={{0,7},{1,6},{2,5},{3,4},{4,3},{5,2},{6,1},{7,0},{8,15},{9,14},{10,... | collective-permute-start | bytes 294920 | tf_op jit(solution)/shard_map/ppermute | solution.py:238
  21.2 0.5 %collective-permute-start.8 = (bf16[3,128,128]{2,1,0:T(8,128)(2,1)S(1)}, bf16[3,128,128]{2,1,0:T(8,128)(2,1)S(1)}, u32[]{:S(2)}, u32[]{:S(2)}) collective-permute-start(bf16[3,128,128]{2,1,0:T(8,128)(2,1)S(1)} %get-tuple-element.27.refs_0_), channel_id=1, source_target_pairs={{0,5},{1,4},{2,7},{3,6},{4,1},{5,0},{6,3},{7,2},{8,13},{9,12},{10,... | collective-permute-start | bytes 294920 | tf_op jit(solution)/shard_map/ppermute | solution.py:238
  21.7 1.2 %collective-permute-start.7 = (bf16[3,128,128]{2,1,0:T(8,128)(2,1)S(1)}, bf16[3,128,128]{2,1,0:T(8,128)(2,1)S(1)}, u32[]{:S(2)}, u32[]{:S(2)}) collective-permute-start(bf16[3,128,128]{2,1,0:T(8,128)(2,1)S(1)} %get-tuple-element.27.refs_0_), channel_id=1, source_target_pairs={{0,3},{1,2},{2,1},{3,0},{4,7},{5,6},{6,5},{7,4},{8,11},{9,10},{10,... | collective-permute-start | bytes 294920 | tf_op jit(solution)/shard_map/ppermute | solution.py:238
  22.9 0.6 %shard_map.109 = (bf16[128,256]{1,0:T(8,128)(2,1)}, f32[8,128]{1,0:T(8,128)S(1)}) custom-call(f32[128,256]{1,0:T(8,128)S(1)} %get-tuple-element.25.active_ref), custom_call_target="tpu_custom_call" | custom-call | flops 1048576 | bytes 1048576 | tf_op jit(solution)/shard_map/pallas_call | solution.py:25
  23.5 2.2 %collective-permute-done.9.refs_3_ = bf16[3,128,128]{2,1,0:T(8,128)(2,1)S(1)} collective-permute-done((bf16[3,128,128]{2,1,0:T(8,128)(2,1)S(1)}, bf16[3,128,128]{2,1,0:T(8,128)(2,1)S(1)}, u32[]{:S(2)}, u32[]{:S(2)}) %collective-permute-start.9) | collective-permute-done | bytes 98336 | tf_op jit(solution)/shard_map/ppermute | solution.py:238
  25.8 2.2 %collective-permute-done.8.refs_2_ = bf16[3,128,128]{2,1,0:T(8,128)(2,1)S(1)} collective-permute-done((bf16[3,128,128]{2,1,0:T(8,128)(2,1)S(1)}, bf16[3,128,128]{2,1,0:T(8,128)(2,1)S(1)}, u32[]{:S(2)}, u32[]{:S(2)}) %collective-permute-start.8) | collective-permute-done | bytes 98336 | tf_op jit(solution)/shard_map/ppermute | solution.py:238
  28.0 0.0 collective-permute-done.7.refs_1_
  28.0 0.1 shard_map.110
  28.0 0.2 collective-permute-start.10
  28.2 1.4 %collective-permute-done.10.received_ref = bf16[8,128,128]{2,1,0:T(8,128)(2,1)S(1)} collective-permute-done((bf16[8,128,128]{2,1,0:T(8,128)(2,1)S(1)}, bf16[8,128,128]{2,1,0:T(8,128)(2,1)S(1)}, u32[]{:S(2)}, u32[]{:S(2)}) %collective-permute-start.10) | collective-permute-done | bytes 262176 | tf_op jit(solution)/shard_map/ppermute | solution.py:238
  29.6 0.4 %shard_map.111 = (bf16[2,128,128]{2,1,0:T(8,128)(2,1)S(1)}, bf16[2,128,128]{2,1,0:T(8,128)(2,1)S(1)}, bf16[2,128,128]{2,1,0:T(8,128)(2,1)S(1)}, bf16[2,128,128]{2,1,0:T(8,128)(2,1)S(1)}) custom-call(s32[1]{0:T(128)} %bitcast.1.row_ref, s32[1]{0:T(128)} %bitcast.chip_ref, s32[1]{0:T(128)} %bitcast.2.core_ref, bf16[1024,512]{1,0:T(8,128)(2,1)S(1)} %shard_map.105.adjacency_ref, ...), custom_call_target="tpu_custom_call" | custom-call | flops 1048576 | bytes 1048576 | tf_op jit(solution)/shard_map/pallas_call | solution.py:25
  30.1 1.5 %collective-permute-start.11 = (bf16[2,128,128]{2,1,0:T(8,128)(2,1)S(1)}, bf16[2,128,128]{2,1,0:T(8,128)(2,1)S(1)}, u32[]{:S(2)}, u32[]{:S(2)}) collective-permute-start(bf16[2,128,128]{2,1,0:T(8,128)(2,1)S(1)} %get-tuple-element.31), channel_id=1, source_target_pairs={{0,24},{8,16},{16,8},{24,0},{1,25},{9,17},{17,9},{25,1},{2,26},{10... | collective-permute-start | bytes 196616 | tf_op jit(solution)/shard_map/ppermute | solution.py:238
  31.6 0.6 %collective-permute-start.12 = (bf16[2,128,128]{2,1,0:T(8,128)(2,1)S(1)}, bf16[2,128,128]{2,1,0:T(8,128)(2,1)S(1)}, u32[]{:S(2)}, u32[]{:S(2)}) collective-permute-start(bf16[2,128,128]{2,1,0:T(8,128)(2,1)S(1)} %get-tuple-element.32), channel_id=1, source_target_pairs={{0,16},{8,24},{16,0},{24,8},{1,17},{9,25},{17,1},{25,9},{2,18},{10... | collective-permute-start | bytes 196616 | tf_op jit(solution)/shard_map/ppermute | solution.py:238
  32.2 2.3 %collective-permute-start.13 = (bf16[2,128,128]{2,1,0:T(8,128)(2,1)S(1)}, bf16[2,128,128]{2,1,0:T(8,128)(2,1)S(1)}, u32[]{:S(2)}, u32[]{:S(2)}) collective-permute-start(bf16[2,128,128]{2,1,0:T(8,128)(2,1)S(1)} %get-tuple-element.33), channel_id=1, source_target_pairs={{0,8},{8,0},{16,24},{24,16},{1,9},{9,1},{17,25},{25,17},{2,10},{10... | collective-permute-start | bytes 196616 | tf_op jit(solution)/shard_map/ppermute | solution.py:238
  34.5 2.4 %collective-permute-done.11.refs_0_ = bf16[2,128,128]{2,1,0:T(8,128)(2,1)S(1)} collective-permute-done((bf16[2,128,128]{2,1,0:T(8,128)(2,1)S(1)}, bf16[2,128,128]{2,1,0:T(8,128)(2,1)S(1)}, u32[]{:S(2)}, u32[]{:S(2)}) %collective-permute-start.11) | collective-permute-done | bytes 65568 | tf_op jit(solution)/shard_map/ppermute | solution.py:238
  36.9 2.0 %collective-permute-done.12.refs_1_ = bf16[2,128,128]{2,1,0:T(8,128)(2,1)S(1)} collective-permute-done((bf16[2,128,128]{2,1,0:T(8,128)(2,1)S(1)}, bf16[2,128,128]{2,1,0:T(8,128)(2,1)S(1)}, u32[]{:S(2)}, u32[]{:S(2)}) %collective-permute-start.12) | collective-permute-done | bytes 65568 | tf_op jit(solution)/shard_map/ppermute | solution.py:238
  38.9 0.0 collective-permute-done.13.refs_2_
  38.9 0.1 collective-permute-start.14
  39.0 0.7 %shard_map.112 = bf16[128,128]{1,0:T(8,128)(2,1)} custom-call(bf16[128]{0:T(256)(128)(2,1)S(1)} %copy-done.7, bf16[2,128,128]{2,1,0:T(8,128)(2,1)S(1)} %collective-permute-done.11.refs_0_, bf16[2,128,128]{2,1,0:T(8,128)(2,1)S(1)} %collective-permute-done.12.refs_1_, bf16[2,128,128]{2,1,0:T(8,128)(2,1)S(1)} %collective-permute-done.13.refs_2_, ...), custom_call_target="tpu_custom_call" | custom-call | flops 1048576 | bytes 1048576 | tf_op jit(solution)/shard_map/pallas_call | solution.py:25
  39.7 0.5 %collective-permute-done.14.other_ref = bf16[128,128]{1,0:T(8,128)(2,1)S(1)} collective-permute-done((bf16[128,128]{1,0:T(8,128)(2,1)S(1)}, bf16[128,128]{1,0:T(8,128)(2,1)S(1)}, u32[]{:S(2)}, u32[]{:S(2)}) %collective-permute-start.14) | collective-permute-done | bytes 32800 | tf_op jit(solution)/shard_map/ppermute | solution.py:238
  40.2 0.7 %shard_map.114 = f32[128,256]{1,0:T(8,128)} custom-call(s32[1]{0:T(128)} %bitcast.2.core_ref, bf16[128,128]{1,0:T(8,128)(2,1)S(1)} %shard_map.113.own_ref, bf16[128,128]{1,0:T(8,128)(2,1)S(1)} %collective-permute-done.14.other_ref), custom_call_target="tpu_custom_call" | custom-call | flops 1048576 | bytes 1048576 | tf_op jit(solution)/shard_map/pallas_call | solution.py:25
  (3 shorter events, 0.1 us)
Async XLA Ops:
  0.6 0.8 %copy-start.5 = (s32[1,1,8]{2,1,0:T(1,128)S(1)}, s32[1,1,8]{2,1,0:T(1,128)}, u32[]{:S(2)}) copy-start(s32[1,1,8]{2,1,0:T(1,128)} %cols_ref.3) | copy-start | bytes 100
  0.6 0.8 %copy-start.4 = (s32[1,1,8]{2,1,0:T(1,128)S(1)}, s32[1,1,8]{2,1,0:T(1,128)}, u32[]{:S(2)}) copy-start(s32[1,1,8]{2,1,0:T(1,128)} %rows_ref.3) | copy-start | bytes 100
  0.7 0.8 %copy-start.3 = (bf16[128,128]{1,0:T(8,128)(2,1)S(1)}, bf16[128,128]{1,0:T(8,128)(2,1)}, u32[]{:S(2)}) copy-start(bf16[128,128]{1,0:T(8,128)(2,1)} %features_ref.1) | copy-start | bytes 98308
  0.7 0.7 %copy-start.6 = (bf16[128]{0:T(256)(128)(2,1)S(1)}, bf16[128]{0:T(256)(128)(2,1)}, u32[]{:S(2)}) copy-start(bf16[128]{0:T(256)(128)(2,1)} %deg_ref.5) | copy-start | bytes 772
  1.3 6.6 %copy-start = (s32[1,1,8,32,256]{4,3,2,1,0:T(8,128)S(1)}, s32[1,1,8,32,256]{4,3,2,1,0:T(8,128)}, u32[]{:S(2)}) copy-start(s32[1,1,8,32,256]{4,3,2,1,0:T(8,128)} %bits_ref.1) | copy-start | bytes 786436
  1.5 7.3 %collective-permute-start.2 = (bf16[128,128]{1,0:T(8,128)(2,1)S(1)}, bf16[128,128]{1,0:T(8,128)(2,1)S(1)}, u32[]{:S(2)}, u32[]{:S(2)}) collective-permute-start(bf16[128,128]{1,0:T(8,128)(2,1)S(1)} %shard_map.104.after_ref.refs_0_), channel_id=1, source_target_pairs={{0,24},{8,16},{16,8},{24,0},{1,25},{9,17},{17,9},{25,1},{2,26},{10... | collective-permute-start | bytes 98312 | tf_op jit(solution)/shard_map/ppermute | solution.py:238
  6.6 4.8 %collective-permute-start.1 = (bf16[128,128]{1,0:T(8,128)(2,1)S(1)}, bf16[128,128]{1,0:T(8,128)(2,1)S(1)}, u32[]{:S(2)}, u32[]{:S(2)}) collective-permute-start(bf16[128,128]{1,0:T(8,128)(2,1)S(1)} %shard_map.104.after_ref.refs_0_), channel_id=1, source_target_pairs={{0,16},{8,24},{16,0},{24,8},{1,17},{9,25},{17,1},{25,9},{2,18},{10... | collective-permute-start | bytes 98312 | tf_op jit(solution)/shard_map/ppermute | solution.py:238
  6.6 4.8 %collective-permute-start = (bf16[128,128]{1,0:T(8,128)(2,1)S(1)}, bf16[128,128]{1,0:T(8,128)(2,1)S(1)}, u32[]{:S(2)}, u32[]{:S(2)}) collective-permute-start(bf16[128,128]{1,0:T(8,128)(2,1)S(1)} %shard_map.104.after_ref.refs_0_), channel_id=1, source_target_pairs={{0,8},{8,0},{16,24},{24,16},{1,9},{9,1},{17,25},{25,17},{2,10},{10... | collective-permute-start | bytes 98312 | tf_op jit(solution)/shard_map/ppermute | solution.py:238
  11.9 1.4 %collective-permute-start.3 = (bf16[4,128,128]{2,1,0:T(8,128)(2,1)S(1)}, bf16[4,128,128]{2,1,0:T(8,128)(2,1)S(1)}, u32[]{:S(2)}, u32[]{:S(2)}) collective-permute-start(bf16[4,128,128]{2,1,0:T(8,128)(2,1)S(1)} %get-tuple-element.20), channel_id=1, source_target_pairs={{0,1},{1,0},{2,3},{3,2},{4,5},{5,4},{6,7},{7,6},{8,9},{9,8},{10,11... | collective-permute-start | bytes 393224 | tf_op jit(solution)/shard_map/ppermute | solution.py:238
  13.3 6.1 %copy-start.1 = (bf16[128,256]{1,0:T(8,128)(2,1)S(1)}, bf16[128,256]{1,0:T(8,128)(2,1)}, u32[]{:S(2)}) copy-start(bf16[128,256]{1,0:T(8,128)(2,1)} %weight_ref.1) | copy-start | bytes 196612
  13.3 6.1 %copy-start.2 = (bf16[128,256]{1,0:T(8,128)(2,1)S(1)}, bf16[128,256]{1,0:T(8,128)(2,1)}, u32[]{:S(2)}) copy-start(bf16[128,256]{1,0:T(8,128)(2,1)} %cotangent_ref.1) | copy-start | bytes 196612
  13.4 4.3 %collective-permute-start.4 = (bf16[128,128]{1,0:T(8,128)(2,1)S(1)}, bf16[128,128]{1,0:T(8,128)(2,1)S(1)}, u32[]{:S(2)}, u32[]{:S(2)}) collective-permute-start(bf16[128,128]{1,0:T(8,128)(2,1)S(1)} %get-tuple-element.22), channel_id=1, source_target_pairs={{0,7},{1,6},{2,5},{3,4},{4,3},{5,2},{6,1},{7,0},{8,15},{9,14},{10,... | collective-permute-start | bytes 98312 | tf_op jit(solution)/shard_map/ppermute | solution.py:238
  15.6 3.4 %collective-permute-start.5 = (bf16[128,128]{1,0:T(8,128)(2,1)S(1)}, bf16[128,128]{1,0:T(8,128)(2,1)S(1)}, u32[]{:S(2)}, u32[]{:S(2)}) collective-permute-start(bf16[128,128]{1,0:T(8,128)(2,1)S(1)} %get-tuple-element.23), channel_id=1, source_target_pairs={{0,5},{1,4},{2,7},{3,6},{4,1},{5,0},{6,3},{7,2},{8,13},{9,12},{10,... | collective-permute-start | bytes 98312 | tf_op jit(solution)/shard_map/ppermute | solution.py:238
  16.1 3.4 %copy-start.7 = (bf16[128]{0:T(256)(128)(2,1)S(1)}, bf16[128]{0:T(256)(128)(2,1)}, u32[]{:S(2)}) copy-start(bf16[128]{0:T(256)(128)(2,1)} %deg_ref.5) | copy-start | bytes 772
  16.1 3.3 %collective-permute-start.6 = (bf16[128,128]{1,0:T(8,128)(2,1)S(1)}, bf16[128,128]{1,0:T(8,128)(2,1)S(1)}, u32[]{:S(2)}, u32[]{:S(2)}) collective-permute-start(bf16[128,128]{1,0:T(8,128)(2,1)S(1)} %get-tuple-element.24), channel_id=1, source_target_pairs={{0,3},{1,2},{2,1},{3,0},{4,7},{5,6},{6,5},{7,4},{8,11},{9,10},{10,... | collective-permute-start | bytes 98312 | tf_op jit(solution)/shard_map/ppermute | solution.py:238
  19.9 5.9 %collective-permute-start.9 = (bf16[3,128,128]{2,1,0:T(8,128)(2,1)S(1)}, bf16[3,128,128]{2,1,0:T(8,128)(2,1)S(1)}, u32[]{:S(2)}, u32[]{:S(2)}) collective-permute-start(bf16[3,128,128]{2,1,0:T(8,128)(2,1)S(1)} %get-tuple-element.27.refs_0_), channel_id=1, source_target_pairs={{0,7},{1,6},{2,5},{3,4},{4,3},{5,2},{6,1},{7,0},{8,15},{9,14},{10,... | collective-permute-start | bytes 294920 | tf_op jit(solution)/shard_map/ppermute | solution.py:238
  21.2 6.8 %collective-permute-start.8 = (bf16[3,128,128]{2,1,0:T(8,128)(2,1)S(1)}, bf16[3,128,128]{2,1,0:T(8,128)(2,1)S(1)}, u32[]{:S(2)}, u32[]{:S(2)}) collective-permute-start(bf16[3,128,128]{2,1,0:T(8,128)(2,1)S(1)} %get-tuple-element.27.refs_0_), channel_id=1, source_target_pairs={{0,5},{1,4},{2,7},{3,6},{4,1},{5,0},{6,3},{7,2},{8,13},{9,12},{10,... | collective-permute-start | bytes 294920 | tf_op jit(solution)/shard_map/ppermute | solution.py:238
  21.7 6.2 %collective-permute-start.7 = (bf16[3,128,128]{2,1,0:T(8,128)(2,1)S(1)}, bf16[3,128,128]{2,1,0:T(8,128)(2,1)S(1)}, u32[]{:S(2)}, u32[]{:S(2)}) collective-permute-start(bf16[3,128,128]{2,1,0:T(8,128)(2,1)S(1)} %get-tuple-element.27.refs_0_), channel_id=1, source_target_pairs={{0,3},{1,2},{2,1},{3,0},{4,7},{5,6},{6,5},{7,4},{8,11},{9,10},{10,... | collective-permute-start | bytes 294920 | tf_op jit(solution)/shard_map/ppermute | solution.py:238
  28.0 1.6 %collective-permute-start.10 = (bf16[8,128,128]{2,1,0:T(8,128)(2,1)S(1)}, bf16[8,128,128]{2,1,0:T(8,128)(2,1)S(1)}, u32[]{:S(2)}, u32[]{:S(2)}) collective-permute-start(bf16[8,128,128]{2,1,0:T(8,128)(2,1)S(1)} %get-tuple-element.29.own_ref), channel_id=1, source_target_pairs={{0,1},{1,0},{2,3},{3,2},{4,5},{5,4},{6,7},{7,6},{8,9},{9,8},{10,11... | collective-permute-start | bytes 786440 | tf_op jit(solution)/shard_map/ppermute | solution.py:238
  30.1 6.8 %collective-permute-start.11 = (bf16[2,128,128]{2,1,0:T(8,128)(2,1)S(1)}, bf16[2,128,128]{2,1,0:T(8,128)(2,1)S(1)}, u32[]{:S(2)}, u32[]{:S(2)}) collective-permute-start(bf16[2,128,128]{2,1,0:T(8,128)(2,1)S(1)} %get-tuple-element.31), channel_id=1, source_target_pairs={{0,24},{8,16},{16,8},{24,0},{1,25},{9,17},{17,9},{25,1},{2,26},{10... | collective-permute-start | bytes 196616 | tf_op jit(solution)/shard_map/ppermute | solution.py:238
  31.6 7.3 %collective-permute-start.12 = (bf16[2,128,128]{2,1,0:T(8,128)(2,1)S(1)}, bf16[2,128,128]{2,1,0:T(8,128)(2,1)S(1)}, u32[]{:S(2)}, u32[]{:S(2)}) collective-permute-start(bf16[2,128,128]{2,1,0:T(8,128)(2,1)S(1)} %get-tuple-element.32), channel_id=1, source_target_pairs={{0,16},{8,24},{16,0},{24,8},{1,17},{9,25},{17,1},{25,9},{2,18},{10... | collective-permute-start | bytes 196616 | tf_op jit(solution)/shard_map/ppermute | solution.py:238
  32.2 6.6 %collective-permute-start.13 = (bf16[2,128,128]{2,1,0:T(8,128)(2,1)S(1)}, bf16[2,128,128]{2,1,0:T(8,128)(2,1)S(1)}, u32[]{:S(2)}, u32[]{:S(2)}) collective-permute-start(bf16[2,128,128]{2,1,0:T(8,128)(2,1)S(1)} %get-tuple-element.33), channel_id=1, source_target_pairs={{0,8},{8,0},{16,24},{24,16},{1,9},{9,1},{17,25},{25,17},{2,10},{10... | collective-permute-start | bytes 196616 | tf_op jit(solution)/shard_map/ppermute | solution.py:238
  38.9 1.3 %collective-permute-start.14 = (bf16[128,128]{1,0:T(8,128)(2,1)S(1)}, bf16[128,128]{1,0:T(8,128)(2,1)S(1)}, u32[]{:S(2)}, u32[]{:S(2)}) collective-permute-start(bf16[128,128]{1,0:T(8,128)(2,1)S(1)} %shard_map.113.own_ref), channel_id=1, source_target_pairs={{0,1},{1,0},{2,3},{3,2},{4,5},{5,4},{6,7},{7,6},{8,9},{9,8},{10,11... | collective-permute-start | bytes 98312 | tf_op jit(solution)/shard_map/ppermute | solution.py:238

commit v5 on v4

--- a/solution.py
+++ b/solution.py
@@ -107,7 +107,7 @@
 def forward_pair(row_ref, chip_ref, core_ref, adjacency_ref, *refs):
     *blocks, mine_ref, other_ref, source, total = refs
     size = blocks[0].shape[0]
-    for step, block in enumerate(blocks):
+    for step, block in zip((0, 1, 3, 2), blocks):
         source[block_at(row_ref[0] ^ step, size), :] = block[...]
     total[...] = jnp.dot(adjacency_ref[...], source[...], preferred_element_type=f32)
     for chip in range(mine_ref.shape[0]):
@@ -141,15 +141,20 @@
     return back, local_grad, pre_act * sigmoid_value
 
 
-def vertex_chips(column_ref, deg_ref, weight_ref, cotangent_ref, own_ref, *refs):
-    *received, sent_ref, active_ref = refs
+def vertex_chips(chip_ref, column_ref, deg_ref, weight_ref, cotangent_ref, own_ref, *refs):
+    *received, far_ref, same_ref, near_ref, active_ref = refs
     summed = own_ref[...] + sum(piece[...].astype(f32) for piece in received)
-    sent_ref[0], local_grad, active_ref[...] = vertex_values(
+    back, local_grad, active_ref[...] = vertex_values(
         summed, column_ref, deg_ref, weight_ref, cotangent_ref
     )
-    half = sent_ref.shape[2]
-    for core in range(2):
-        sent_ref[1 + core] = local_grad[:, core * half : (core + 1) * half].astype(bf16)
+    local_grad = local_grad.astype(bf16)
+    half = same_ref.shape[2]
+    low, high = local_grad[:, :half], local_grad[:, half:]
+    first = lax.rem(chip_ref[0], 2) == 0
+    for sent_ref in (far_ref, same_ref, near_ref):
+        sent_ref[0] = back
+    same_ref[1] = jnp.where(first, low, high)
+    far_ref[1] = near_ref[1] = jnp.where(first, high, low)
 
 
 def write_out(active_ref, out_ref, written_ref):
@@ -157,19 +162,17 @@
     written_ref[...] = jnp.zeros_like(written_ref)
 
 
-def join_chips(core_ref, *refs):
-    *blocks, _, joined_ref, own_grad_ref = refs
+def join_chips(*refs):
+    *blocks, _, joined_ref = refs
     chips = len(blocks)
-    second = core_ref[0] == 1
-    for step, block in enumerate(blocks):
+    for step, block in zip((0, 3, 2, 1), blocks):
         joined_ref[step] = block[0]
-        joined_ref[chips + step] = jnp.where(second, block[1], block[2])
-        own_grad_ref[step] = jnp.where(second, block[2], block[1])
-
-
-def backward_rows(row_ref, chip_ref, core_ref, adjacency_ref, own_ref, grad_ref, received_ref, *refs):
+        joined_ref[chips + step] = block[1]
+
+
+def backward_rows(row_ref, chip_ref, core_ref, adjacency_ref, own_ref, received_ref, *refs):
     *pieces, source, ordered, total = refs
-    chips, size = grad_ref.shape[0], grad_ref.shape[2]
+    chips, size = own_ref.shape[0] // 2, own_ref.shape[2]
     core = core_ref[0]
     for step in range(chips):
         peer = 2 * (chip_ref[0] ^ step)
@@ -177,7 +180,7 @@
         other = peer + (core if step else 1 - core)
         source[:, block_at(mine, size)] = own_ref[step]
         source[:, block_at(other, size)] = received_ref[step]
-        ordered[mine] = grad_ref[step]
+        ordered[mine] = own_ref[chips + step]
         ordered[other] = received_ref[chips + step]
     total[...] = jnp.dot(source[...], adjacency_ref[...], preferred_element_type=f32)
     grad = jnp.sum(ordered[...].astype(f32), axis=0).astype(bf16)
@@ -200,9 +203,9 @@
     out_ref[...] = (total * deg_ref[...].astype(f32).reshape(1, -1)).T.astype(bf16)
 
 
-def join_halves(core_ref, own_ref, other_ref, out_ref):
+def join_halves(chip_ref, own_ref, other_ref, out_ref):
     size = own_ref.shape[1]
-    half = core_ref[0]
+    half = lax.rem(chip_ref[0], 2)
     out_ref[:, block_at(half, size)] = own_ref[...].astype(f32)
     out_ref[:, block_at(1 - half, size)] = other_ref[...].astype(f32)
 
@@ -307,7 +310,7 @@
         cost_estimate=pl.CostEstimate(flops=1 << 20, bytes_accessed=1 << 20, transcendentals=0),
     )(tile_count, tile_rows, tile_cols, tile_bits, scaled)
     far_first = (3, 2, 1)
-    blocks = [exchange(scaled, "row", row_shards, step) for step in (1, 2, 3)]
+    blocks = [exchange(scaled, "row", row_shards, step) for step in (1, 3, 2)]
     blocks.insert(0, scaled)
     mine, other = call(
         forward_pair,
@@ -325,26 +328,30 @@
     received = [
         exchange(piece, "col", col_shards, 2 * step + 1) for step, piece in zip(far_first, pieces)
     ]
-    sent, active = call(
+    message = struct((2, width, size), bf16)
+    far, same, near, active = call(
         vertex_chips,
-        (struct((3, width, size), bf16), struct((size, out_width), f32)),
+        (message, message, message, struct((size, out_width), f32)),
+        (chip,),
+        (column, deg_scale, weight, cotangent, own, *received),
+    )
+    activations, written = call(write_out, (activation, struct((8, 128), f32)), (), (active,))
+    received = [
+        exchange(sent, "col", col_shards, 2 * step + 1)
+        for step, sent in zip(far_first, (far, same, near))
+    ]
+    joined = call(
+        join_chips,
+        struct((2 * chips, width, size), bf16),
         (),
-        (column, deg_scale, weight, cotangent, own, *received),
-    )
-    activations, written = call(write_out, (activation, struct((8, 128), f32)), (), (active,))
-    received = [exchange(sent, "col", col_shards, 2 * step + 1) for step in (1, 2, 3)]
-    joined, own_grad = call(
-        join_chips,
-        (struct((2 * chips, width, size), bf16), struct((chips, width, size), bf16)),
-        (core,),
-        (sent, *received),
+        (same, *received),
         after=(written,),
     )
     pieces = call(
         backward_rows,
-        (struct((2, width, size), bf16),) * row_shards,
+        (message,) * row_shards,
         (row, chip, core),
-        (adjacency, joined, own_grad, exchange(joined, "col", col_shards, 1)),
+        (adjacency, joined, exchange(joined, "col", col_shards, 1)),
         [
             pltpu.VMEM((width, col_shards * size), bf16),
             pltpu.VMEM((col_shards, width, size), bf16),
@@ -360,10 +367,10 @@
         arrived,
         [pltpu.VMEM((row_shards, height, out_width // 2), bf16)],
     )
-    other_grad = exchange(half_grad, "col", col_shards, 1)
+    other_grad = exchange(half_grad, "col", col_shards, 3)
     input_grad = call(input_rows, input_shape, (), (deg_scale, *arrived))
     weight_grad = call(
-        join_halves, struct((height, out_width), f32), (core,), (half_grad, other_grad)
+        join_halves, struct((height, out_width), f32), (chip,), (half_grad, other_grad)
     )
     return (activations, input_grad, weight_grad)
 

time: 41 us -> 41.9 us (1.022)
  waiting for transfers between devices: 17.6 us -> 18.4 us
    ppermute x15, waiting for transfers between devices: 17.6 us -> 18.4 us  [exchange(): lax.ppermute(block, axis, [(shard, shard ^ distance) for shard in range(s...]
  transfers between devices with their start and end apart: 15 -> 15, of which waited for: 11 -> 12; matrix products, arithmetic and copies ran while one was open for 0% -> 0% of each run, Pallas kernels for 6% -> 5%
where the time goes in v5:
time: 41.9 us; the launch traced here: 41.7 us
  waiting for transfers between devices  18.4 us (44%)
  starting transfers between devices  16.7 us (40%)
  Pallas kernels  4.44 us (11%)
  between operations  1.43 us (3%)
  local copies, waits for them, and re-layouts  0.69 us (2%)
    ppermute x15, waiting for transfers between devices, exchange(): lax.ppermute(block, axis, [(shard, shard ^ distance) for shard in range(s...  18.4 us
    ppermute x15, starting transfers between devices, exchange(): lax.ppermute(block, axis, [(shard, shard ^ distance) for shard in range(s...  16.7 us
    pallas_call x11, Pallas kernels, call(): pl.pallas_call(body, out_shape=out_shape, in_specs=[SMEM] * len(scalars)...  3.53 us
    pallas_call x1, Pallas kernels, on_device(): pl.pallas_call(build_adjacency, out_shape=struct((col_shards * size, row_...  0.91 us
  transfers between devices with their start and end apart: 15, of which 12 were waited for; matrix products, arithmetic and copies ran while one was open for 0% of the time, Pallas kernels for 5%

profile of v5, /device:TPU:0, one launch (start us, length us, event | category | flops | bytes accessed | tf_op | source)
XLA Modules:
  0.0 41.7 jit_solution(5301477762050575168)
XLA Ops:
  0.6 0.0 copy-start.5
  0.6 0.0 copy-start.4
  0.7 0.0 copy-start.3
  0.7 0.0 copy-start.6
  0.7 0.7 %copy-done.6 = bf16[128]{0:T(256)(128)(2,1)S(1)} copy-done((bf16[128]{0:T(256)(128)(2,1)S(1)}, bf16[128]{0:T(256)(128)(2,1)}, u32[]{:S(2)}) %copy-start.6) | copy-done | bytes 280
  1.3 0.0 copy-start
  1.3 0.1 shard_map.103.column_ref
  1.5 0.0 copy-done.5
  1.5 0.0 copy-done.4
  1.5 0.0 copy-done.3
  1.5 4.1 %collective-permute-start.2 = (bf16[128,128]{1,0:T(8,128)(2,1)S(1)}, bf16[128,128]{1,0:T(8,128)(2,1)S(1)}, u32[]{:S(2)}, u32[]{:S(2)}) collective-permute-start(bf16[128,128]{1,0:T(8,128)(2,1)S(1)} %shard_map.104.after_ref.refs_0_), channel_id=1, source_target_pairs={{0,16},{8,24},{16,0},{24,8},{1,17},{9,25},{17,1},{25,9},{2,18},{10... | collective-permute-start | bytes 98312 | tf_op jit(solution)/shard_map/ppermute | solution.py:241
  5.6 1.3 %collective-permute-start.1 = (bf16[128,128]{1,0:T(8,128)(2,1)S(1)}, bf16[128,128]{1,0:T(8,128)(2,1)S(1)}, u32[]{:S(2)}, u32[]{:S(2)}) collective-permute-start(bf16[128,128]{1,0:T(8,128)(2,1)S(1)} %shard_map.104.after_ref.refs_0_), channel_id=1, source_target_pairs={{0,24},{8,16},{16,8},{24,0},{1,25},{9,17},{17,9},{25,1},{2,26},{10... | collective-permute-start | bytes 98312 | tf_op jit(solution)/shard_map/ppermute | solution.py:241
  7.0 0.2 collective-permute-start
  7.8 0.0 copy-done
  7.9 0.9 %shard_map.105.adjacency_ref = bf16[1024,512]{1,0:T(8,128)(2,1)S(1)} custom-call(s32[1,1]{1,0:T(1,128)S(6)} %copy.11.count_ref, s32[1,1,8]{2,1,0:T(1,128)S(1)} %copy-done.4, s32[1,1,8]{2,1,0:T(1,128)S(1)} %copy-done.5, s32[1,1,8,32,256]{4,3,2,1,0:T(8,128)S(1)} %copy-done, bf16[128,128]{1,0:T(8,128)(2,1)S(1)} %shard_map.104.after_ref.refs_0_), custom_call_target="tpu_custom_call" | custom-call | flops 1048576 | bytes 1048576 | tf_op jit(solution)/shard_map/pallas_call | solution.py:304
  8.8 0.0 collective-permute-done.2.refs_3_
  8.8 2.5 %collective-permute-done.1.refs_2_ = bf16[128,128]{1,0:T(8,128)(2,1)S(1)} collective-permute-done((bf16[128,128]{1,0:T(8,128)(2,1)S(1)}, bf16[128,128]{1,0:T(8,128)(2,1)S(1)}, u32[]{:S(2)}, u32[]{:S(2)}) %collective-permute-start.1) | collective-permute-done | bytes 32800 | tf_op jit(solution)/shard_map/ppermute | solution.py:241
  11.3 0.0 collective-permute-done.refs_1_
  11.3 0.5 %shard_map.106 = (f32[4,128,128]{2,1,0:T(8,128)S(1)}, bf16[4,128,128]{2,1,0:T(8,128)(2,1)S(1)}) custom-call(s32[1]{0:T(128)} %bitcast.1.row_ref, s32[1]{0:T(128)} %bitcast.chip_ref, s32[1]{0:T(128)} %bitcast.2.core_ref, bf16[1024,512]{1,0:T(8,128)(2,1)S(1)} %shard_map.105.adjacency_ref, bf16[128,128]{1,0:T(8,128)(2,1)S(1)} %shard_map.104.after_ref.refs_0_, ...), custom_call_target="tpu_custom_call" | custom-call | flops 1048576 | bytes 1048576 | tf_op jit(solution)/shard_map/pallas_call | solution.py:25
  11.8 0.1 collective-permute-start.3
  11.9 1.3 %collective-permute-done.3.received_ref = bf16[4,128,128]{2,1,0:T(8,128)(2,1)S(1)} collective-permute-done((bf16[4,128,128]{2,1,0:T(8,128)(2,1)S(1)}, bf16[4,128,128]{2,1,0:T(8,128)(2,1)S(1)}, u32[]{:S(2)}, u32[]{:S(2)}) %collective-permute-start.3) | collective-permute-done | bytes 131104 | tf_op jit(solution)/shard_map/ppermute | solution.py:241
  13.2 0.0 copy-start.1
  13.2 0.0 copy-start.2
  13.3 2.3 %collective-permute-start.4 = (bf16[128,128]{1,0:T(8,128)(2,1)S(1)}, bf16[128,128]{1,0:T(8,128)(2,1)S(1)}, u32[]{:S(2)}, u32[]{:S(2)}) collective-permute-start(bf16[128,128]{1,0:T(8,128)(2,1)S(1)} %get-tuple-element.22), channel_id=1, source_target_pairs={{0,7},{1,6},{2,5},{3,4},{4,3},{5,2},{6,1},{7,0},{8,15},{9,14},{10,... | collective-permute-start | bytes 98312 | tf_op jit(solution)/shard_map/ppermute | solution.py:241
  15.5 0.5 %collective-permute-start.5 = (bf16[128,128]{1,0:T(8,128)(2,1)S(1)}, bf16[128,128]{1,0:T(8,128)(2,1)S(1)}, u32[]{:S(2)}, u32[]{:S(2)}) collective-permute-start(bf16[128,128]{1,0:T(8,128)(2,1)S(1)} %get-tuple-element.23), channel_id=1, source_target_pairs={{0,5},{1,4},{2,7},{3,6},{4,1},{5,0},{6,3},{7,2},{8,13},{9,12},{10,... | collective-permute-start | bytes 98312 | tf_op jit(solution)/shard_map/ppermute | solution.py:241
  16.0 0.0 copy-start.7
  16.0 0.3 collective-permute-start.6
  16.3 1.3 %collective-permute-done.4.refs_0_ = bf16[128,128]{1,0:T(8,128)(2,1)S(1)} collective-permute-done((bf16[128,128]{1,0:T(8,128)(2,1)S(1)}, bf16[128,128]{1,0:T(8,128)(2,1)S(1)}, u32[]{:S(2)}, u32[]{:S(2)}) %collective-permute-start.4) | collective-permute-done | bytes 32800 | tf_op jit(solution)/shard_map/ppermute | solution.py:241
  17.6 1.3 %collective-permute-done.5.refs_1_ = bf16[128,128]{1,0:T(8,128)(2,1)S(1)} collective-permute-done((bf16[128,128]{1,0:T(8,128)(2,1)S(1)}, bf16[128,128]{1,0:T(8,128)(2,1)S(1)}, u32[]{:S(2)}, u32[]{:S(2)}) %collective-permute-start.5) | collective-permute-done | bytes 32800 | tf_op jit(solution)/shard_map/ppermute | solution.py:241
  18.9 0.5 %collective-permute-done.6.refs_2_ = bf16[128,128]{1,0:T(8,128)(2,1)S(1)} collective-permute-done((bf16[128,128]{1,0:T(8,128)(2,1)S(1)}, bf16[128,128]{1,0:T(8,128)(2,1)S(1)}, u32[]{:S(2)}, u32[]{:S(2)}) %collective-permute-start.6) | collective-permute-done | bytes 32800 | tf_op jit(solution)/shard_map/ppermute | solution.py:241
  19.3 0.0 copy-done.1
  19.3 0.0 copy-done.2
  19.4 0.0 copy-done.7
  19.4 0.4 shard_map.108
  19.7 1.3 %collective-permute-start.7 = (bf16[2,128,128]{2,1,0:T(8,128)(2,1)S(1)}, bf16[2,128,128]{2,1,0:T(8,128)(2,1)S(1)}, u32[]{:S(2)}, u32[]{:S(2)}) collective-permute-start(bf16[2,128,128]{2,1,0:T(8,128)(2,1)S(1)} %get-tuple-element.28), channel_id=1, source_target_pairs={{0,7},{1,6},{2,5},{3,4},{4,3},{5,2},{6,1},{7,0},{8,15},{9,14},{10,... | collective-permute-start | bytes 196616 | tf_op jit(solution)/shard_map/ppermute | solution.py:241
  21.1 1.4 %collective-permute-start.9 = (bf16[2,128,128]{2,1,0:T(8,128)(2,1)S(1)}, bf16[2,128,128]{2,1,0:T(8,128)(2,1)S(1)}, u32[]{:S(2)}, u32[]{:S(2)}) collective-permute-start(bf16[2,128,128]{2,1,0:T(8,128)(2,1)S(1)} %get-tuple-element.29), channel_id=1, source_target_pairs={{0,3},{1,2},{2,1},{3,0},{4,7},{5,6},{6,5},{7,4},{8,11},{9,10},{10,... | collective-permute-start | bytes 196616 | tf_op jit(solution)/shard_map/ppermute | solution.py:241
  22.5 0.3 collective-permute-start.8
  22.8 0.6 %shard_map.109 = (bf16[128,256]{1,0:T(8,128)(2,1)}, f32[8,128]{1,0:T(8,128)S(1)}) custom-call(f32[128,256]{1,0:T(8,128)S(1)} %get-tuple-element.25.active_ref), custom_call_target="tpu_custom_call" | custom-call | flops 1048576 | bytes 1048576 | tf_op jit(solution)/shard_map/pallas_call | solution.py:25
  23.4 1.3 %collective-permute-done.7.refs_1_ = bf16[2,128,128]{2,1,0:T(8,128)(2,1)S(1)} collective-permute-done((bf16[2,128,128]{2,1,0:T(8,128)(2,1)S(1)}, bf16[2,128,128]{2,1,0:T(8,128)(2,1)S(1)}, u32[]{:S(2)}, u32[]{:S(2)}) %collective-permute-start.7) | collective-permute-done | bytes 65568 | tf_op jit(solution)/shard_map/ppermute | solution.py:241
  24.8 1.5 %collective-permute-done.9.refs_3_ = bf16[2,128,128]{2,1,0:T(8,128)(2,1)S(1)} collective-permute-done((bf16[2,128,128]{2,1,0:T(8,128)(2,1)S(1)}, bf16[2,128,128]{2,1,0:T(8,128)(2,1)S(1)}, u32[]{:S(2)}, u32[]{:S(2)}) %collective-permute-start.9) | collective-permute-done | bytes 65568 | tf_op jit(solution)/shard_map/ppermute | solution.py:241
  26.2 0.3 collective-permute-done.8.refs_2_
  26.6 0.2 collective-permute-start.10
  26.8 1.4 %collective-permute-done.10.received_ref = bf16[8,128,128]{2,1,0:T(8,128)(2,1)S(1)} collective-permute-done((bf16[8,128,128]{2,1,0:T(8,128)(2,1)S(1)}, bf16[8,128,128]{2,1,0:T(8,128)(2,1)S(1)}, u32[]{:S(2)}, u32[]{:S(2)}) %collective-permute-start.10) | collective-permute-done | bytes 262176 | tf_op jit(solution)/shard_map/ppermute | solution.py:241
  28.2 0.4 shard_map.111
  28.6 2.2 %collective-permute-start.11 = (bf16[2,128,128]{2,1,0:T(8,128)(2,1)S(1)}, bf16[2,128,128]{2,1,0:T(8,128)(2,1)S(1)}, u32[]{:S(2)}, u32[]{:S(2)}) collective-permute-start(bf16[2,128,128]{2,1,0:T(8,128)(2,1)S(1)} %get-tuple-element.31), channel_id=1, source_target_pairs={{0,24},{8,16},{16,8},{24,0},{1,25},{9,17},{17,9},{25,1},{2,26},{10... | collective-permute-start | bytes 196616 | tf_op jit(solution)/shard_map/ppermute | solution.py:241
  30.8 0.0 collective-permute-start.12
  30.8 2.3 %collective-permute-start.13 = (bf16[2,128,128]{2,1,0:T(8,128)(2,1)S(1)}, bf16[2,128,128]{2,1,0:T(8,128)(2,1)S(1)}, u32[]{:S(2)}, u32[]{:S(2)}) collective-permute-start(bf16[2,128,128]{2,1,0:T(8,128)(2,1)S(1)} %get-tuple-element.33), channel_id=1, source_target_pairs={{0,8},{8,0},{16,24},{24,16},{1,9},{9,1},{17,25},{25,17},{2,10},{10... | collective-permute-start | bytes 196616 | tf_op jit(solution)/shard_map/ppermute | solution.py:241
  33.1 2.4 %collective-permute-done.11.refs_0_ = bf16[2,128,128]{2,1,0:T(8,128)(2,1)S(1)} collective-permute-done((bf16[2,128,128]{2,1,0:T(8,128)(2,1)S(1)}, bf16[2,128,128]{2,1,0:T(8,128)(2,1)S(1)}, u32[]{:S(2)}, u32[]{:S(2)}) %collective-permute-start.11) | collective-permute-done | bytes 65568 | tf_op jit(solution)/shard_map/ppermute | solution.py:241
  35.4 2.0 %collective-permute-done.12.refs_1_ = bf16[2,128,128]{2,1,0:T(8,128)(2,1)S(1)} collective-permute-done((bf16[2,128,128]{2,1,0:T(8,128)(2,1)S(1)}, bf16[2,128,128]{2,1,0:T(8,128)(2,1)S(1)}, u32[]{:S(2)}, u32[]{:S(2)}) %collective-permute-start.12) | collective-permute-done | bytes 65568 | tf_op jit(solution)/shard_map/ppermute | solution.py:241
  37.4 0.0 collective-permute-done.13.refs_2_
  37.5 0.2 collective-permute-start.14
  37.7 0.7 %shard_map.112 = bf16[128,128]{1,0:T(8,128)(2,1)} custom-call(bf16[128]{0:T(256)(128)(2,1)S(1)} %copy-done.7, bf16[2,128,128]{2,1,0:T(8,128)(2,1)S(1)} %collective-permute-done.11.refs_0_, bf16[2,128,128]{2,1,0:T(8,128)(2,1)S(1)} %collective-permute-done.12.refs_1_, bf16[2,128,128]{2,1,0:T(8,128)(2,1)S(1)} %collective-permute-done.13.refs_2_, ...), custom_call_target="tpu_custom_call" | custom-call | flops 1048576 | bytes 1048576 | tf_op jit(solution)/shard_map/pallas_call | solution.py:25
  38.4 2.6 %collective-permute-done.14.other_ref = bf16[128,128]{1,0:T(8,128)(2,1)S(1)} collective-permute-done((bf16[128,128]{1,0:T(8,128)(2,1)S(1)}, bf16[128,128]{1,0:T(8,128)(2,1)S(1)}, u32[]{:S(2)}, u32[]{:S(2)}) %collective-permute-start.14) | collective-permute-done | bytes 32800 | tf_op jit(solution)/shard_map/ppermute | solution.py:241
  41.0 0.7 %shard_map.114 = f32[128,256]{1,0:T(8,128)} custom-call(s32[1]{0:T(128)} %bitcast.chip_ref, bf16[128,128]{1,0:T(8,128)(2,1)S(1)} %shard_map.113.own_ref, bf16[128,128]{1,0:T(8,128)(2,1)S(1)} %collective-permute-done.14.other_ref), custom_call_target="tpu_custom_call" | custom-call | flops 1048576 | bytes 1048576 | tf_op jit(solution)/shard_map/pallas_call | solution.py:25
  (4 shorter events, 0.1 us)
Async XLA Ops:
  0.6 0.8 %copy-start.5 = (s32[1,1,8]{2,1,0:T(1,128)S(1)}, s32[1,1,8]{2,1,0:T(1,128)}, u32[]{:S(2)}) copy-start(s32[1,1,8]{2,1,0:T(1,128)} %cols_ref.3) | copy-start | bytes 100
  0.6 0.8 %copy-start.4 = (s32[1,1,8]{2,1,0:T(1,128)S(1)}, s32[1,1,8]{2,1,0:T(1,128)}, u32[]{:S(2)}) copy-start(s32[1,1,8]{2,1,0:T(1,128)} %rows_ref.3) | copy-start | bytes 100
  0.7 0.8 %copy-start.3 = (bf16[128,128]{1,0:T(8,128)(2,1)S(1)}, bf16[128,128]{1,0:T(8,128)(2,1)}, u32[]{:S(2)}) copy-start(bf16[128,128]{1,0:T(8,128)(2,1)} %features_ref.1) | copy-start | bytes 98308
  0.7 0.7 %copy-start.6 = (bf16[128]{0:T(256)(128)(2,1)S(1)}, bf16[128]{0:T(256)(128)(2,1)}, u32[]{:S(2)}) copy-start(bf16[128]{0:T(256)(128)(2,1)} %deg_ref.5) | copy-start | bytes 772
  1.3 6.5 %copy-start = (s32[1,1,8,32,256]{4,3,2,1,0:T(8,128)S(1)}, s32[1,1,8,32,256]{4,3,2,1,0:T(8,128)}, u32[]{:S(2)}) copy-start(s32[1,1,8,32,256]{4,3,2,1,0:T(8,128)} %bits_ref.1) | copy-start | bytes 786436
  1.5 7.3 %collective-permute-start.2 = (bf16[128,128]{1,0:T(8,128)(2,1)S(1)}, bf16[128,128]{1,0:T(8,128)(2,1)S(1)}, u32[]{:S(2)}, u32[]{:S(2)}) collective-permute-start(bf16[128,128]{1,0:T(8,128)(2,1)S(1)} %shard_map.104.after_ref.refs_0_), channel_id=1, source_target_pairs={{0,16},{8,24},{16,0},{24,8},{1,17},{9,25},{17,1},{25,9},{2,18},{10... | collective-permute-start | bytes 98312 | tf_op jit(solution)/shard_map/ppermute | solution.py:241
  5.6 5.7 %collective-permute-start.1 = (bf16[128,128]{1,0:T(8,128)(2,1)S(1)}, bf16[128,128]{1,0:T(8,128)(2,1)S(1)}, u32[]{:S(2)}, u32[]{:S(2)}) collective-permute-start(bf16[128,128]{1,0:T(8,128)(2,1)S(1)} %shard_map.104.after_ref.refs_0_), channel_id=1, source_target_pairs={{0,24},{8,16},{16,8},{24,0},{1,25},{9,17},{17,9},{25,1},{2,26},{10... | collective-permute-start | bytes 98312 | tf_op jit(solution)/shard_map/ppermute | solution.py:241
  7.0 4.4 %collective-permute-start = (bf16[128,128]{1,0:T(8,128)(2,1)S(1)}, bf16[128,128]{1,0:T(8,128)(2,1)S(1)}, u32[]{:S(2)}, u32[]{:S(2)}) collective-permute-start(bf16[128,128]{1,0:T(8,128)(2,1)S(1)} %shard_map.104.after_ref.refs_0_), channel_id=1, source_target_pairs={{0,8},{8,0},{16,24},{24,16},{1,9},{9,1},{17,25},{25,17},{2,10},{10... | collective-permute-start | bytes 98312 | tf_op jit(solution)/shard_map/ppermute | solution.py:241
  11.8 1.4 %collective-permute-start.3 = (bf16[4,128,128]{2,1,0:T(8,128)(2,1)S(1)}, bf16[4,128,128]{2,1,0:T(8,128)(2,1)S(1)}, u32[]{:S(2)}, u32[]{:S(2)}) collective-permute-start(bf16[4,128,128]{2,1,0:T(8,128)(2,1)S(1)} %get-tuple-element.20), channel_id=1, source_target_pairs={{0,1},{1,0},{2,3},{3,2},{4,5},{5,4},{6,7},{7,6},{8,9},{9,8},{10,11... | collective-permute-start | bytes 393224 | tf_op jit(solution)/shard_map/ppermute | solution.py:241
  13.2 6.1 %copy-start.1 = (bf16[128,256]{1,0:T(8,128)(2,1)S(1)}, bf16[128,256]{1,0:T(8,128)(2,1)}, u32[]{:S(2)}) copy-start(bf16[128,256]{1,0:T(8,128)(2,1)} %weight_ref.1) | copy-start | bytes 196612
  13.2 6.1 %copy-start.2 = (bf16[128,256]{1,0:T(8,128)(2,1)S(1)}, bf16[128,256]{1,0:T(8,128)(2,1)}, u32[]{:S(2)}) copy-start(bf16[128,256]{1,0:T(8,128)(2,1)} %cotangent_ref.1) | copy-start | bytes 196612
  13.3 4.3 %collective-permute-start.4 = (bf16[128,128]{1,0:T(8,128)(2,1)S(1)}, bf16[128,128]{1,0:T(8,128)(2,1)S(1)}, u32[]{:S(2)}, u32[]{:S(2)}) collective-permute-start(bf16[128,128]{1,0:T(8,128)(2,1)S(1)} %get-tuple-element.22), channel_id=1, source_target_pairs={{0,7},{1,6},{2,5},{3,4},{4,3},{5,2},{6,1},{7,0},{8,15},{9,14},{10,... | collective-permute-start | bytes 98312 | tf_op jit(solution)/shard_map/ppermute | solution.py:241
  15.5 3.4 %collective-permute-start.5 = (bf16[128,128]{1,0:T(8,128)(2,1)S(1)}, bf16[128,128]{1,0:T(8,128)(2,1)S(1)}, u32[]{:S(2)}, u32[]{:S(2)}) collective-permute-start(bf16[128,128]{1,0:T(8,128)(2,1)S(1)} %get-tuple-element.23), channel_id=1, source_target_pairs={{0,5},{1,4},{2,7},{3,6},{4,1},{5,0},{6,3},{7,2},{8,13},{9,12},{10,... | collective-permute-start | bytes 98312 | tf_op jit(solution)/shard_map/ppermute | solution.py:241
  16.0 3.4 %copy-start.7 = (bf16[128]{0:T(256)(128)(2,1)S(1)}, bf16[128]{0:T(256)(128)(2,1)}, u32[]{:S(2)}) copy-start(bf16[128]{0:T(256)(128)(2,1)} %deg_ref.5) | copy-start | bytes 772
  16.0 3.3 %collective-permute-start.6 = (bf16[128,128]{1,0:T(8,128)(2,1)S(1)}, bf16[128,128]{1,0:T(8,128)(2,1)S(1)}, u32[]{:S(2)}, u32[]{:S(2)}) collective-permute-start(bf16[128,128]{1,0:T(8,128)(2,1)S(1)} %get-tuple-element.24), channel_id=1, source_target_pairs={{0,3},{1,2},{2,1},{3,0},{4,7},{5,6},{6,5},{7,4},{8,11},{9,10},{10,... | collective-permute-start | bytes 98312 | tf_op jit(solution)/shard_map/ppermute | solution.py:241
  19.7 5.0 %collective-permute-start.7 = (bf16[2,128,128]{2,1,0:T(8,128)(2,1)S(1)}, bf16[2,128,128]{2,1,0:T(8,128)(2,1)S(1)}, u32[]{:S(2)}, u32[]{:S(2)}) collective-permute-start(bf16[2,128,128]{2,1,0:T(8,128)(2,1)S(1)} %get-tuple-element.28), channel_id=1, source_target_pairs={{0,7},{1,6},{2,5},{3,4},{4,3},{5,2},{6,1},{7,0},{8,15},{9,14},{10,... | collective-permute-start | bytes 196616 | tf_op jit(solution)/shard_map/ppermute | solution.py:241
  21.1 5.1 %collective-permute-start.9 = (bf16[2,128,128]{2,1,0:T(8,128)(2,1)S(1)}, bf16[2,128,128]{2,1,0:T(8,128)(2,1)S(1)}, u32[]{:S(2)}, u32[]{:S(2)}) collective-permute-start(bf16[2,128,128]{2,1,0:T(8,128)(2,1)S(1)} %get-tuple-element.29), channel_id=1, source_target_pairs={{0,3},{1,2},{2,1},{3,0},{4,7},{5,6},{6,5},{7,4},{8,11},{9,10},{10,... | collective-permute-start | bytes 196616 | tf_op jit(solution)/shard_map/ppermute | solution.py:241
  22.5 4.0 %collective-permute-start.8 = (bf16[2,128,128]{2,1,0:T(8,128)(2,1)S(1)}, bf16[2,128,128]{2,1,0:T(8,128)(2,1)S(1)}, u32[]{:S(2)}, u32[]{:S(2)}) collective-permute-start(bf16[2,128,128]{2,1,0:T(8,128)(2,1)S(1)} %get-tuple-element.27.refs_0_), channel_id=1, source_target_pairs={{0,5},{1,4},{2,7},{3,6},{4,1},{5,0},{6,3},{7,2},{8,13},{9,12},{10,... | collective-permute-start | bytes 196616 | tf_op jit(solution)/shard_map/ppermute | solution.py:241
  26.6 1.6 %collective-permute-start.10 = (bf16[8,128,128]{2,1,0:T(8,128)(2,1)S(1)}, bf16[8,128,128]{2,1,0:T(8,128)(2,1)S(1)}, u32[]{:S(2)}, u32[]{:S(2)}) collective-permute-start(bf16[8,128,128]{2,1,0:T(8,128)(2,1)S(1)} %shard_map.110.own_ref), channel_id=1, source_target_pairs={{0,1},{1,0},{2,3},{3,2},{4,5},{5,4},{6,7},{7,6},{8,9},{9,8},{10,11... | collective-permute-start | bytes 786440 | tf_op jit(solution)/shard_map/ppermute | solution.py:241
  28.6 6.8 %collective-permute-start.11 = (bf16[2,128,128]{2,1,0:T(8,128)(2,1)S(1)}, bf16[2,128,128]{2,1,0:T(8,128)(2,1)S(1)}, u32[]{:S(2)}, u32[]{:S(2)}) collective-permute-start(bf16[2,128,128]{2,1,0:T(8,128)(2,1)S(1)} %get-tuple-element.31), channel_id=1, source_target_pairs={{0,24},{8,16},{16,8},{24,0},{1,25},{9,17},{17,9},{25,1},{2,26},{10... | collective-permute-start | bytes 196616 | tf_op jit(solution)/shard_map/ppermute | solution.py:241
  30.8 6.7 %collective-permute-start.12 = (bf16[2,128,128]{2,1,0:T(8,128)(2,1)S(1)}, bf16[2,128,128]{2,1,0:T(8,128)(2,1)S(1)}, u32[]{:S(2)}, u32[]{:S(2)}) collective-permute-start(bf16[2,128,128]{2,1,0:T(8,128)(2,1)S(1)} %get-tuple-element.32), channel_id=1, source_target_pairs={{0,16},{8,24},{16,0},{24,8},{1,17},{9,25},{17,1},{25,9},{2,18},{10... | collective-permute-start | bytes 196616 | tf_op jit(solution)/shard_map/ppermute | solution.py:241
  30.8 6.7 %collective-permute-start.13 = (bf16[2,128,128]{2,1,0:T(8,128)(2,1)S(1)}, bf16[2,128,128]{2,1,0:T(8,128)(2,1)S(1)}, u32[]{:S(2)}, u32[]{:S(2)}) collective-permute-start(bf16[2,128,128]{2,1,0:T(8,128)(2,1)S(1)} %get-tuple-element.33), channel_id=1, source_target_pairs={{0,8},{8,0},{16,24},{24,16},{1,9},{9,1},{17,25},{25,17},{2,10},{10... | collective-permute-start | bytes 196616 | tf_op jit(solution)/shard_map/ppermute | solution.py:241
  37.5 3.6 %collective-permute-start.14 = (bf16[128,128]{1,0:T(8,128)(2,1)S(1)}, bf16[128,128]{1,0:T(8,128)(2,1)S(1)}, u32[]{:S(2)}, u32[]{:S(2)}) collective-permute-start(bf16[128,128]{1,0:T(8,128)(2,1)S(1)} %shard_map.113.own_ref), channel_id=1, source_target_pairs={{0,3},{1,2},{2,1},{3,0},{4,7},{5,6},{6,5},{7,4},{8,11},{9,10},{10,... | collective-permute-start | bytes 98312 | tf_op jit(solution)/shard_map/ppermute | solution.py:241

commit v6 on v3

--- a/solution.py
+++ b/solution.py
@@ -107,7 +107,7 @@
 def forward_pair(row_ref, core_ref, adjacency_ref, *refs):
     *blocks, mine_ref, other_ref, source, total = refs
     size = blocks[0].shape[0]
-    for step, block in enumerate(blocks):
+    for step, block in zip((0, 1, 3, 2), blocks):
         source[block_at(row_ref[0] ^ step, size), :] = block[...]
     total[...] = jnp.dot(adjacency_ref[...], source[...], preferred_element_type=f32)
     core = core_ref[0]
@@ -180,14 +180,14 @@
         source[:, block_at(peer + 1 - core, size)] = received_ref[step]
     total[...] = jnp.dot(source[...], adjacency_ref[...], preferred_element_type=f32)
     grad = (grad_ref[...].astype(f32) + received_ref[chips].astype(f32)).astype(bf16)
-    for step, piece in zip((3, 2, 1, 0), pieces):
+    for step, piece in zip((2, 3, 1, 0), pieces):
         piece[0] = total[:, block_at(row_ref[0] ^ step, size)].astype(bf16)
         piece[1] = grad
 
 
 def sum_grad(factor, row_ref, *refs):
     *pieces, out_ref, ordered = refs
-    for step, piece in zip((3, 2, 1, 0), pieces):
+    for step, piece in zip((2, 3, 1, 0), pieces):
         ordered[row_ref[0] ^ step] = piece[1]
     total = jnp.sum(ordered[...].astype(f32), axis=0) * factor
     out_ref[...] = total.astype(out_ref.dtype)
@@ -306,7 +306,7 @@
         cost_estimate=pl.CostEstimate(flops=1 << 20, bytes_accessed=1 << 20, transcendentals=0),
     )(tile_count, tile_rows, tile_cols, tile_bits, scaled)
     far_first = (3, 2, 1)
-    blocks = [exchange(scaled, "row", row_shards, step) for step in (1, 2, 3)]
+    blocks = [exchange(scaled, "row", row_shards, step) for step in (1, 3, 2)]
     blocks.insert(0, scaled)
     mine, other = call(
         forward_pair,
@@ -347,7 +347,7 @@
         (adjacency, joined, own_grad, exchange(joined, "col", col_shards, 1)),
         backward_scratch,
     )
-    arrived = [exchange(piece, "row", row_shards, step) for step, piece in zip(far_first, pieces)]
+    arrived = [exchange(piece, "row", row_shards, step) for step, piece in zip((2, 3, 1), pieces)]
     arrived.append(pieces[-1])
     half_grad = call(
         functools.partial(sum_grad, factor),

time: 40.5 us -> 40.3 us (level)
  starting transfers between devices: 17.5 us -> 16.6 us
  waiting for transfers between devices: 16.2 us -> 17 us
    ppermute x15, starting transfers between devices: 17.5 us -> 16.6 us  [exchange(): lax.ppermute(block, axis, [(shard, shard ^ distance) for shard in range(s...]
    ppermute x15, waiting for transfers between devices: 16.2 us -> 17 us  [exchange(): lax.ppermute(block, axis, [(shard, shard ^ distance) for shard in range(s...]
  transfers between devices with their start and end apart: 15 -> 15, of which waited for: 11 -> 12; matrix products, arithmetic and copies ran while one was open for 0% -> 0% of each run, Pallas kernels for 6% -> 6%
where the time goes in v6:
time: 40.3 us; the launch traced here: 40.1 us
  waiting for transfers between devices  17 us (42%)
  starting transfers between devices  16.6 us (41%)
  Pallas kernels  4.46 us (11%)
  between operations  1.45 us (4%)
  local copies, waits for them, and re-layouts  0.69 us (2%)
    ppermute x15, waiting for transfers between devices, exchange(): lax.ppermute(block, axis, [(shard, shard ^ distance) for shard in range(s...  17 us
    ppermute x15, starting transfers between devices, exchange(): lax.ppermute(block, axis, [(shard, shard ^ distance) for shard in range(s...  16.6 us
    pallas_call x11, Pallas kernels, call(): pl.pallas_call(body, out_shape=out_shape, in_specs=[SMEM] * len(scalars)...  3.56 us
    pallas_call x1, Pallas kernels, on_device(): pl.pallas_call(build_adjacency, out_shape=struct((col_shards * size, row_...  0.91 us
  transfers between devices with their start and end apart: 15, of which 12 were waited for; matrix products, arithmetic and copies ran while one was open for 0% of the time, Pallas kernels for 6%

profile of v6, /device:TPU:0, one launch (start us, length us, event | category | flops | bytes accessed | tf_op | source)
XLA Modules:
  0.0 40.1 jit_solution(2977422709651717097)
XLA Ops:
  0.6 0.0 copy-start.5
  0.6 0.0 copy-start.4
  0.7 0.0 copy-start.3
  0.7 0.0 copy-start.6
  0.7 0.7 %copy-done.6 = bf16[128]{0:T(256)(128)(2,1)S(1)} copy-done((bf16[128]{0:T(256)(128)(2,1)S(1)}, bf16[128]{0:T(256)(128)(2,1)}, u32[]{:S(2)}) %copy-start.6) | copy-done | bytes 280
  1.3 0.0 copy-start
  1.3 0.1 shard_map.103.column_ref
  1.5 0.0 copy-done.5
  1.5 0.0 copy-done.4
  1.5 0.0 copy-done.3
  1.5 4.1 %collective-permute-start.2 = (bf16[128,128]{1,0:T(8,128)(2,1)S(1)}, bf16[128,128]{1,0:T(8,128)(2,1)S(1)}, u32[]{:S(2)}, u32[]{:S(2)}) collective-permute-start(bf16[128,128]{1,0:T(8,128)(2,1)S(1)} %shard_map.104.after_ref.refs_0_), channel_id=1, source_target_pairs={{0,16},{8,24},{16,0},{24,8},{1,17},{9,25},{17,1},{25,9},{2,18},{10... | collective-permute-start | bytes 98312 | tf_op jit(solution)/shard_map/ppermute | solution.py:237
  5.6 1.3 %collective-permute-start.1 = (bf16[128,128]{1,0:T(8,128)(2,1)S(1)}, bf16[128,128]{1,0:T(8,128)(2,1)S(1)}, u32[]{:S(2)}, u32[]{:S(2)}) collective-permute-start(bf16[128,128]{1,0:T(8,128)(2,1)S(1)} %shard_map.104.after_ref.refs_0_), channel_id=1, source_target_pairs={{0,24},{8,16},{16,8},{24,0},{1,25},{9,17},{17,9},{25,1},{2,26},{10... | collective-permute-start | bytes 98312 | tf_op jit(solution)/shard_map/ppermute | solution.py:237
  7.0 0.2 collective-permute-start
  7.8 0.0 copy-done
  7.9 0.9 %shard_map.105.adjacency_ref = bf16[1024,512]{1,0:T(8,128)(2,1)S(1)} custom-call(s32[1,1]{1,0:T(1,128)S(6)} %copy.11.count_ref, s32[1,1,8]{2,1,0:T(1,128)S(1)} %copy-done.4, s32[1,1,8]{2,1,0:T(1,128)S(1)} %copy-done.5, s32[1,1,8,32,256]{4,3,2,1,0:T(8,128)S(1)} %copy-done, bf16[128,128]{1,0:T(8,128)(2,1)S(1)} %shard_map.104.after_ref.refs_0_), custom_call_target="tpu_custom_call" | custom-call | flops 1048576 | bytes 1048576 | tf_op jit(solution)/shard_map/pallas_call | solution.py:300
  8.8 0.0 collective-permute-done.2.refs_3_
  8.8 2.5 %collective-permute-done.1.refs_2_ = bf16[128,128]{1,0:T(8,128)(2,1)S(1)} collective-permute-done((bf16[128,128]{1,0:T(8,128)(2,1)S(1)}, bf16[128,128]{1,0:T(8,128)(2,1)S(1)}, u32[]{:S(2)}, u32[]{:S(2)}) %collective-permute-start.1) | collective-permute-done | bytes 32800 | tf_op jit(solution)/shard_map/ppermute | solution.py:237
  11.3 0.0 collective-permute-done.refs_1_
  11.3 0.5 %shard_map.106 = (f32[4,128,128]{2,1,0:T(8,128)S(1)}, bf16[4,128,128]{2,1,0:T(8,128)(2,1)S(1)}) custom-call(s32[1]{0:T(128)} %bitcast.1.row_ref, s32[1]{0:T(128)} %bitcast.2.core_ref, bf16[1024,512]{1,0:T(8,128)(2,1)S(1)} %shard_map.105.adjacency_ref, bf16[128,128]{1,0:T(8,128)(2,1)S(1)} %shard_map.104.after_ref.refs_0_, ...), custom_call_target="tpu_custom_call" | custom-call | flops 1048576 | bytes 1048576 | tf_op jit(solution)/shard_map/pallas_call | solution.py:25
  11.8 0.1 collective-permute-start.3
  11.9 1.3 %collective-permute-done.3.received_ref = bf16[4,128,128]{2,1,0:T(8,128)(2,1)S(1)} collective-permute-done((bf16[4,128,128]{2,1,0:T(8,128)(2,1)S(1)}, bf16[4,128,128]{2,1,0:T(8,128)(2,1)S(1)}, u32[]{:S(2)}, u32[]{:S(2)}) %collective-permute-start.3) | collective-permute-done | bytes 131104 | tf_op jit(solution)/shard_map/ppermute | solution.py:237
  13.2 0.0 copy-start.1
  13.2 0.0 copy-start.2
  13.3 2.5 %collective-permute-start.4 = (bf16[128,128]{1,0:T(8,128)(2,1)S(1)}, bf16[128,128]{1,0:T(8,128)(2,1)S(1)}, u32[]{:S(2)}, u32[]{:S(2)}) collective-permute-start(bf16[128,128]{1,0:T(8,128)(2,1)S(1)} %get-tuple-element.22), channel_id=1, source_target_pairs={{0,6},{1,7},{2,4},{3,5},{4,2},{5,3},{6,0},{7,1},{8,14},{9,15},{10,... | collective-permute-start | bytes 98312 | tf_op jit(solution)/shard_map/ppermute | solution.py:237
  15.8 0.5 %collective-permute-start.5 = (bf16[128,128]{1,0:T(8,128)(2,1)S(1)}, bf16[128,128]{1,0:T(8,128)(2,1)S(1)}, u32[]{:S(2)}, u32[]{:S(2)}) collective-permute-start(bf16[128,128]{1,0:T(8,128)(2,1)S(1)} %get-tuple-element.23), channel_id=1, source_target_pairs={{0,4},{1,5},{2,6},{3,7},{4,0},{5,1},{6,2},{7,3},{8,12},{9,13},{10,... | collective-permute-start | bytes 98312 | tf_op jit(solution)/shard_map/ppermute | solution.py:237
  16.3 0.0 copy-start.7
  16.3 0.5 %collective-permute-start.6 = (bf16[128,128]{1,0:T(8,128)(2,1)S(1)}, bf16[128,128]{1,0:T(8,128)(2,1)S(1)}, u32[]{:S(2)}, u32[]{:S(2)}) collective-permute-start(bf16[128,128]{1,0:T(8,128)(2,1)S(1)} %get-tuple-element.24), channel_id=1, source_target_pairs={{0,2},{1,3},{2,0},{3,1},{4,6},{5,7},{6,4},{7,5},{8,10},{9,11},{10,... | collective-permute-start | bytes 98312 | tf_op jit(solution)/shard_map/ppermute | solution.py:237
  16.8 1.3 %collective-permute-done.4.refs_0_ = bf16[128,128]{1,0:T(8,128)(2,1)S(1)} collective-permute-done((bf16[128,128]{1,0:T(8,128)(2,1)S(1)}, bf16[128,128]{1,0:T(8,128)(2,1)S(1)}, u32[]{:S(2)}, u32[]{:S(2)}) %collective-permute-start.4) | collective-permute-done | bytes 32800 | tf_op jit(solution)/shard_map/ppermute | solution.py:237
  18.1 1.5 %collective-permute-done.5.refs_1_ = bf16[128,128]{1,0:T(8,128)(2,1)S(1)} collective-permute-done((bf16[128,128]{1,0:T(8,128)(2,1)S(1)}, bf16[128,128]{1,0:T(8,128)(2,1)S(1)}, u32[]{:S(2)}, u32[]{:S(2)}) %collective-permute-start.5) | collective-permute-done | bytes 32800 | tf_op jit(solution)/shard_map/ppermute | solution.py:237
  19.7 0.5 %collective-permute-done.6.refs_2_ = bf16[128,128]{1,0:T(8,128)(2,1)S(1)} collective-permute-done((bf16[128,128]{1,0:T(8,128)(2,1)S(1)}, bf16[128,128]{1,0:T(8,128)(2,1)S(1)}, u32[]{:S(2)}, u32[]{:S(2)}) %collective-permute-start.6) | collective-permute-done | bytes 32800 | tf_op jit(solution)/shard_map/ppermute | solution.py:237
  20.2 0.0 copy-done.1
  20.2 0.0 copy-done.2
  20.2 0.0 copy-done.7
  20.2 0.4 shard_map.108
  20.6 1.6 %collective-permute-start.9 = (bf16[3,128,128]{2,1,0:T(8,128)(2,1)S(1)}, bf16[3,128,128]{2,1,0:T(8,128)(2,1)S(1)}, u32[]{:S(2)}, u32[]{:S(2)}) collective-permute-start(bf16[3,128,128]{2,1,0:T(8,128)(2,1)S(1)} %get-tuple-element.27.refs_0_), channel_id=1, source_target_pairs={{0,6},{1,7},{2,4},{3,5},{4,2},{5,3},{6,0},{7,1},{8,14},{9,15},{10,... | collective-permute-start | bytes 294920 | tf_op jit(solution)/shard_map/ppermute | solution.py:237
  22.1 0.5 %collective-permute-start.8 = (bf16[3,128,128]{2,1,0:T(8,128)(2,1)S(1)}, bf16[3,128,128]{2,1,0:T(8,128)(2,1)S(1)}, u32[]{:S(2)}, u32[]{:S(2)}) collective-permute-start(bf16[3,128,128]{2,1,0:T(8,128)(2,1)S(1)} %get-tuple-element.27.refs_0_), channel_id=1, source_target_pairs={{0,4},{1,5},{2,6},{3,7},{4,0},{5,1},{6,2},{7,3},{8,12},{9,13},{10,... | collective-permute-start | bytes 294920 | tf_op jit(solution)/shard_map/ppermute | solution.py:237
  22.7 1.5 %collective-permute-start.7 = (bf16[3,128,128]{2,1,0:T(8,128)(2,1)S(1)}, bf16[3,128,128]{2,1,0:T(8,128)(2,1)S(1)}, u32[]{:S(2)}, u32[]{:S(2)}) collective-permute-start(bf16[3,128,128]{2,1,0:T(8,128)(2,1)S(1)} %get-tuple-element.27.refs_0_), channel_id=1, source_target_pairs={{0,2},{1,3},{2,0},{3,1},{4,6},{5,7},{6,4},{7,5},{8,10},{9,11},{10,... | collective-permute-start | bytes 294920 | tf_op jit(solution)/shard_map/ppermute | solution.py:237
  24.1 0.6 %shard_map.109 = (bf16[128,256]{1,0:T(8,128)(2,1)}, f32[8,128]{1,0:T(8,128)S(1)}) custom-call(f32[128,256]{1,0:T(8,128)S(1)} %get-tuple-element.25.active_ref), custom_call_target="tpu_custom_call" | custom-call | flops 1048576 | bytes 1048576 | tf_op jit(solution)/shard_map/pallas_call | solution.py:25
  24.8 1.8 %collective-permute-done.9.refs_3_ = bf16[3,128,128]{2,1,0:T(8,128)(2,1)S(1)} collective-permute-done((bf16[3,128,128]{2,1,0:T(8,128)(2,1)S(1)}, bf16[3,128,128]{2,1,0:T(8,128)(2,1)S(1)}, u32[]{:S(2)}, u32[]{:S(2)}) %collective-permute-start.9) | collective-permute-done | bytes 98336 | tf_op jit(solution)/shard_map/ppermute | solution.py:237
  26.6 0.9 %collective-permute-done.8.refs_2_ = bf16[3,128,128]{2,1,0:T(8,128)(2,1)S(1)} collective-permute-done((bf16[3,128,128]{2,1,0:T(8,128)(2,1)S(1)}, bf16[3,128,128]{2,1,0:T(8,128)(2,1)S(1)}, u32[]{:S(2)}, u32[]{:S(2)}) %collective-permute-start.8) | collective-permute-done | bytes 98336 | tf_op jit(solution)/shard_map/ppermute | solution.py:237
  27.5 0.0 collective-permute-done.7.refs_1_
  27.5 0.1 shard_map.110
  27.6 0.1 collective-permute-start.10
  27.7 1.4 %collective-permute-done.10.received_ref = bf16[5,128,128]{2,1,0:T(8,128)(2,1)S(1)} collective-permute-done((bf16[5,128,128]{2,1,0:T(8,128)(2,1)S(1)}, bf16[5,128,128]{2,1,0:T(8,128)(2,1)S(1)}, u32[]{:S(2)}, u32[]{:S(2)}) %collective-permute-start.10) | collective-permute-done | bytes 163872 | tf_op jit(solution)/shard_map/ppermute | solution.py:237
  29.0 0.4 %shard_map.111 = (bf16[2,128,128]{2,1,0:T(8,128)(2,1)S(1)}, bf16[2,128,128]{2,1,0:T(8,128)(2,1)S(1)}, bf16[2,128,128]{2,1,0:T(8,128)(2,1)S(1)}, bf16[2,128,128]{2,1,0:T(8,128)(2,1)S(1)}) custom-call(s32[1]{0:T(128)} %bitcast.1.row_ref, s32[1]{0:T(128)} %bitcast.chip_ref, s32[1]{0:T(128)} %bitcast.2.core_ref, bf16[1024,512]{1,0:T(8,128)(2,1)S(1)} %shard_map.105.adjacency_ref, ...), custom_call_target="tpu_custom_call" | custom-call | flops 1048576 | bytes 1048576 | tf_op jit(solution)/shard_map/pallas_call | solution.py:25
  29.5 1.3 %collective-permute-start.11 = (bf16[2,128,128]{2,1,0:T(8,128)(2,1)S(1)}, bf16[2,128,128]{2,1,0:T(8,128)(2,1)S(1)}, u32[]{:S(2)}, u32[]{:S(2)}) collective-permute-start(bf16[2,128,128]{2,1,0:T(8,128)(2,1)S(1)} %get-tuple-element.31), channel_id=1, source_target_pairs={{0,16},{8,24},{16,0},{24,8},{1,17},{9,25},{17,1},{25,9},{2,18},{10... | collective-permute-start | bytes 196616 | tf_op jit(solution)/shard_map/ppermute | solution.py:237
  30.8 1.0 %collective-permute-start.12 = (bf16[2,128,128]{2,1,0:T(8,128)(2,1)S(1)}, bf16[2,128,128]{2,1,0:T(8,128)(2,1)S(1)}, u32[]{:S(2)}, u32[]{:S(2)}) collective-permute-start(bf16[2,128,128]{2,1,0:T(8,128)(2,1)S(1)} %get-tuple-element.32), channel_id=1, source_target_pairs={{0,24},{8,16},{16,8},{24,0},{1,25},{9,17},{17,9},{25,1},{2,26},{10... | collective-permute-start | bytes 196616 | tf_op jit(solution)/shard_map/ppermute | solution.py:237
  31.8 1.2 %collective-permute-start.13 = (bf16[2,128,128]{2,1,0:T(8,128)(2,1)S(1)}, bf16[2,128,128]{2,1,0:T(8,128)(2,1)S(1)}, u32[]{:S(2)}, u32[]{:S(2)}) collective-permute-start(bf16[2,128,128]{2,1,0:T(8,128)(2,1)S(1)} %get-tuple-element.33), channel_id=1, source_target_pairs={{0,8},{8,0},{16,24},{24,16},{1,9},{9,1},{17,25},{25,17},{2,10},{10... | collective-permute-start | bytes 196616 | tf_op jit(solution)/shard_map/ppermute | solution.py:237
  33.0 3.2 %collective-permute-done.11.refs_0_ = bf16[2,128,128]{2,1,0:T(8,128)(2,1)S(1)} collective-permute-done((bf16[2,128,128]{2,1,0:T(8,128)(2,1)S(1)}, bf16[2,128,128]{2,1,0:T(8,128)(2,1)S(1)}, u32[]{:S(2)}, u32[]{:S(2)}) %collective-permute-start.11) | collective-permute-done | bytes 65568 | tf_op jit(solution)/shard_map/ppermute | solution.py:237
  36.2 0.9 %collective-permute-done.12.refs_1_ = bf16[2,128,128]{2,1,0:T(8,128)(2,1)S(1)} collective-permute-done((bf16[2,128,128]{2,1,0:T(8,128)(2,1)S(1)}, bf16[2,128,128]{2,1,0:T(8,128)(2,1)S(1)}, u32[]{:S(2)}, u32[]{:S(2)}) %collective-permute-start.12) | collective-permute-done | bytes 65568 | tf_op jit(solution)/shard_map/ppermute | solution.py:237
  37.2 1.0 %collective-permute-done.13.refs_2_ = bf16[2,128,128]{2,1,0:T(8,128)(2,1)S(1)} collective-permute-done((bf16[2,128,128]{2,1,0:T(8,128)(2,1)S(1)}, bf16[2,128,128]{2,1,0:T(8,128)(2,1)S(1)}, u32[]{:S(2)}, u32[]{:S(2)}) %collective-permute-start.13) | collective-permute-done | bytes 65568 | tf_op jit(solution)/shard_map/ppermute | solution.py:237
  38.2 0.1 collective-permute-start.14
  38.3 0.7 %shard_map.112 = bf16[128,128]{1,0:T(8,128)(2,1)} custom-call(bf16[128]{0:T(256)(128)(2,1)S(1)} %copy-done.7, bf16[2,128,128]{2,1,0:T(8,128)(2,1)S(1)} %collective-permute-done.11.refs_0_, bf16[2,128,128]{2,1,0:T(8,128)(2,1)S(1)} %collective-permute-done.12.refs_1_, bf16[2,128,128]{2,1,0:T(8,128)(2,1)S(1)} %collective-permute-done.13.refs_2_, ...), custom_call_target="tpu_custom_call" | custom-call | flops 1048576 | bytes 1048576 | tf_op jit(solution)/shard_map/pallas_call | solution.py:25
  39.0 0.5 %collective-permute-done.14.other_ref = bf16[128,128]{1,0:T(8,128)(2,1)S(1)} collective-permute-done((bf16[128,128]{1,0:T(8,128)(2,1)S(1)}, bf16[128,128]{1,0:T(8,128)(2,1)S(1)}, u32[]{:S(2)}, u32[]{:S(2)}) %collective-permute-start.14) | collective-permute-done | bytes 32800 | tf_op jit(solution)/shard_map/ppermute | solution.py:237
  39.5 0.7 %shard_map.114 = f32[128,256]{1,0:T(8,128)} custom-call(s32[1]{0:T(128)} %bitcast.2.core_ref, bf16[128,128]{1,0:T(8,128)(2,1)S(1)} %shard_map.113.own_ref, bf16[128,128]{1,0:T(8,128)(2,1)S(1)} %collective-permute-done.14.other_ref), custom_call_target="tpu_custom_call" | custom-call | flops 1048576 | bytes 1048576 | tf_op jit(solution)/shard_map/pallas_call | solution.py:25
  (3 shorter events, 0.1 us)
Async XLA Ops:
  0.6 0.8 %copy-start.5 = (s32[1,1,8]{2,1,0:T(1,128)S(1)}, s32[1,1,8]{2,1,0:T(1,128)}, u32[]{:S(2)}) copy-start(s32[1,1,8]{2,1,0:T(1,128)} %cols_ref.3) | copy-start | bytes 100
  0.6 0.8 %copy-start.4 = (s32[1,1,8]{2,1,0:T(1,128)S(1)}, s32[1,1,8]{2,1,0:T(1,128)}, u32[]{:S(2)}) copy-start(s32[1,1,8]{2,1,0:T(1,128)} %rows_ref.3) | copy-start | bytes 100
  0.7 0.8 %copy-start.3 = (bf16[128,128]{1,0:T(8,128)(2,1)S(1)}, bf16[128,128]{1,0:T(8,128)(2,1)}, u32[]{:S(2)}) copy-start(bf16[128,128]{1,0:T(8,128)(2,1)} %features_ref.1) | copy-start | bytes 98308
  0.7 0.7 %copy-start.6 = (bf16[128]{0:T(256)(128)(2,1)S(1)}, bf16[128]{0:T(256)(128)(2,1)}, u32[]{:S(2)}) copy-start(bf16[128]{0:T(256)(128)(2,1)} %deg_ref.5) | copy-start | bytes 772
  1.3 6.5 %copy-start = (s32[1,1,8,32,256]{4,3,2,1,0:T(8,128)S(1)}, s32[1,1,8,32,256]{4,3,2,1,0:T(8,128)}, u32[]{:S(2)}) copy-start(s32[1,1,8,32,256]{4,3,2,1,0:T(8,128)} %bits_ref.1) | copy-start | bytes 786436
  1.5 7.3 %collective-permute-start.2 = (bf16[128,128]{1,0:T(8,128)(2,1)S(1)}, bf16[128,128]{1,0:T(8,128)(2,1)S(1)}, u32[]{:S(2)}, u32[]{:S(2)}) collective-permute-start(bf16[128,128]{1,0:T(8,128)(2,1)S(1)} %shard_map.104.after_ref.refs_0_), channel_id=1, source_target_pairs={{0,16},{8,24},{16,0},{24,8},{1,17},{9,25},{17,1},{25,9},{2,18},{10... | collective-permute-start | bytes 98312 | tf_op jit(solution)/shard_map/ppermute | solution.py:237
  5.6 5.7 %collective-permute-start.1 = (bf16[128,128]{1,0:T(8,128)(2,1)S(1)}, bf16[128,128]{1,0:T(8,128)(2,1)S(1)}, u32[]{:S(2)}, u32[]{:S(2)}) collective-permute-start(bf16[128,128]{1,0:T(8,128)(2,1)S(1)} %shard_map.104.after_ref.refs_0_), channel_id=1, source_target_pairs={{0,24},{8,16},{16,8},{24,0},{1,25},{9,17},{17,9},{25,1},{2,26},{10... | collective-permute-start | bytes 98312 | tf_op jit(solution)/shard_map/ppermute | solution.py:237
  7.0 4.4 %collective-permute-start = (bf16[128,128]{1,0:T(8,128)(2,1)S(1)}, bf16[128,128]{1,0:T(8,128)(2,1)S(1)}, u32[]{:S(2)}, u32[]{:S(2)}) collective-permute-start(bf16[128,128]{1,0:T(8,128)(2,1)S(1)} %shard_map.104.after_ref.refs_0_), channel_id=1, source_target_pairs={{0,8},{8,0},{16,24},{24,16},{1,9},{9,1},{17,25},{25,17},{2,10},{10... | collective-permute-start | bytes 98312 | tf_op jit(solution)/shard_map/ppermute | solution.py:237
  11.8 1.4 %collective-permute-start.3 = (bf16[4,128,128]{2,1,0:T(8,128)(2,1)S(1)}, bf16[4,128,128]{2,1,0:T(8,128)(2,1)S(1)}, u32[]{:S(2)}, u32[]{:S(2)}) collective-permute-start(bf16[4,128,128]{2,1,0:T(8,128)(2,1)S(1)} %get-tuple-element.20), channel_id=1, source_target_pairs={{0,1},{1,0},{2,3},{3,2},{4,5},{5,4},{6,7},{7,6},{8,9},{9,8},{10,11... | collective-permute-start | bytes 393224 | tf_op jit(solution)/shard_map/ppermute | solution.py:237
  13.2 7.0 %copy-start.1 = (bf16[128,256]{1,0:T(8,128)(2,1)S(1)}, bf16[128,256]{1,0:T(8,128)(2,1)}, u32[]{:S(2)}) copy-start(bf16[128,256]{1,0:T(8,128)(2,1)} %weight_ref.1) | copy-start | bytes 196612
  13.2 7.0 %copy-start.2 = (bf16[128,256]{1,0:T(8,128)(2,1)S(1)}, bf16[128,256]{1,0:T(8,128)(2,1)}, u32[]{:S(2)}) copy-start(bf16[128,256]{1,0:T(8,128)(2,1)} %cotangent_ref.1) | copy-start | bytes 196612
  13.3 4.9 %collective-permute-start.4 = (bf16[128,128]{1,0:T(8,128)(2,1)S(1)}, bf16[128,128]{1,0:T(8,128)(2,1)S(1)}, u32[]{:S(2)}, u32[]{:S(2)}) collective-permute-start(bf16[128,128]{1,0:T(8,128)(2,1)S(1)} %get-tuple-element.22), channel_id=1, source_target_pairs={{0,6},{1,7},{2,4},{3,5},{4,2},{5,3},{6,0},{7,1},{8,14},{9,15},{10,... | collective-permute-start | bytes 98312 | tf_op jit(solution)/shard_map/ppermute | solution.py:237
  15.8 3.9 %collective-permute-start.5 = (bf16[128,128]{1,0:T(8,128)(2,1)S(1)}, bf16[128,128]{1,0:T(8,128)(2,1)S(1)}, u32[]{:S(2)}, u32[]{:S(2)}) collective-permute-start(bf16[128,128]{1,0:T(8,128)(2,1)S(1)} %get-tuple-element.23), channel_id=1, source_target_pairs={{0,4},{1,5},{2,6},{3,7},{4,0},{5,1},{6,2},{7,3},{8,12},{9,13},{10,... | collective-permute-start | bytes 98312 | tf_op jit(solution)/shard_map/ppermute | solution.py:237
  16.3 3.9 %copy-start.7 = (bf16[128]{0:T(256)(128)(2,1)S(1)}, bf16[128]{0:T(256)(128)(2,1)}, u32[]{:S(2)}) copy-start(bf16[128]{0:T(256)(128)(2,1)} %deg_ref.5) | copy-start | bytes 772
  16.3 3.9 %collective-permute-start.6 = (bf16[128,128]{1,0:T(8,128)(2,1)S(1)}, bf16[128,128]{1,0:T(8,128)(2,1)S(1)}, u32[]{:S(2)}, u32[]{:S(2)}) collective-permute-start(bf16[128,128]{1,0:T(8,128)(2,1)S(1)} %get-tuple-element.24), channel_id=1, source_target_pairs={{0,2},{1,3},{2,0},{3,1},{4,6},{5,7},{6,4},{7,5},{8,10},{9,11},{10,... | collective-permute-start | bytes 98312 | tf_op jit(solution)/shard_map/ppermute | solution.py:237
  20.6 6.0 %collective-permute-start.9 = (bf16[3,128,128]{2,1,0:T(8,128)(2,1)S(1)}, bf16[3,128,128]{2,1,0:T(8,128)(2,1)S(1)}, u32[]{:S(2)}, u32[]{:S(2)}) collective-permute-start(bf16[3,128,128]{2,1,0:T(8,128)(2,1)S(1)} %get-tuple-element.27.refs_0_), channel_id=1, source_target_pairs={{0,6},{1,7},{2,4},{3,5},{4,2},{5,3},{6,0},{7,1},{8,14},{9,15},{10,... | collective-permute-start | bytes 294920 | tf_op jit(solution)/shard_map/ppermute | solution.py:237
  22.1 5.4 %collective-permute-start.8 = (bf16[3,128,128]{2,1,0:T(8,128)(2,1)S(1)}, bf16[3,128,128]{2,1,0:T(8,128)(2,1)S(1)}, u32[]{:S(2)}, u32[]{:S(2)}) collective-permute-start(bf16[3,128,128]{2,1,0:T(8,128)(2,1)S(1)} %get-tuple-element.27.refs_0_), channel_id=1, source_target_pairs={{0,4},{1,5},{2,6},{3,7},{4,0},{5,1},{6,2},{7,3},{8,12},{9,13},{10,... | collective-permute-start | bytes 294920 | tf_op jit(solution)/shard_map/ppermute | solution.py:237
  22.7 4.8 %collective-permute-start.7 = (bf16[3,128,128]{2,1,0:T(8,128)(2,1)S(1)}, bf16[3,128,128]{2,1,0:T(8,128)(2,1)S(1)}, u32[]{:S(2)}, u32[]{:S(2)}) collective-permute-start(bf16[3,128,128]{2,1,0:T(8,128)(2,1)S(1)} %get-tuple-element.27.refs_0_), channel_id=1, source_target_pairs={{0,2},{1,3},{2,0},{3,1},{4,6},{5,7},{6,4},{7,5},{8,10},{9,11},{10,... | collective-permute-start | bytes 294920 | tf_op jit(solution)/shard_map/ppermute | solution.py:237
  27.6 1.5 %collective-permute-start.10 = (bf16[5,128,128]{2,1,0:T(8,128)(2,1)S(1)}, bf16[5,128,128]{2,1,0:T(8,128)(2,1)S(1)}, u32[]{:S(2)}, u32[]{:S(2)}) collective-permute-start(bf16[5,128,128]{2,1,0:T(8,128)(2,1)S(1)} %get-tuple-element.29.own_ref), channel_id=1, source_target_pairs={{0,1},{1,0},{2,3},{3,2},{4,5},{5,4},{6,7},{7,6},{8,9},{9,8},{10,11... | collective-permute-start | bytes 491528 | tf_op jit(solution)/shard_map/ppermute | solution.py:237
  29.5 6.8 %collective-permute-start.11 = (bf16[2,128,128]{2,1,0:T(8,128)(2,1)S(1)}, bf16[2,128,128]{2,1,0:T(8,128)(2,1)S(1)}, u32[]{:S(2)}, u32[]{:S(2)}) collective-permute-start(bf16[2,128,128]{2,1,0:T(8,128)(2,1)S(1)} %get-tuple-element.31), channel_id=1, source_target_pairs={{0,16},{8,24},{16,0},{24,8},{1,17},{9,25},{17,1},{25,9},{2,18},{10... | collective-permute-start | bytes 196616 | tf_op jit(solution)/shard_map/ppermute | solution.py:237
  30.8 6.4 %collective-permute-start.12 = (bf16[2,128,128]{2,1,0:T(8,128)(2,1)S(1)}, bf16[2,128,128]{2,1,0:T(8,128)(2,1)S(1)}, u32[]{:S(2)}, u32[]{:S(2)}) collective-permute-start(bf16[2,128,128]{2,1,0:T(8,128)(2,1)S(1)} %get-tuple-element.32), channel_id=1, source_target_pairs={{0,24},{8,16},{16,8},{24,0},{1,25},{9,17},{17,9},{25,1},{2,26},{10... | collective-permute-start | bytes 196616 | tf_op jit(solution)/shard_map/ppermute | solution.py:237
  31.8 6.4 %collective-permute-start.13 = (bf16[2,128,128]{2,1,0:T(8,128)(2,1)S(1)}, bf16[2,128,128]{2,1,0:T(8,128)(2,1)S(1)}, u32[]{:S(2)}, u32[]{:S(2)}) collective-permute-start(bf16[2,128,128]{2,1,0:T(8,128)(2,1)S(1)} %get-tuple-element.33), channel_id=1, source_target_pairs={{0,8},{8,0},{16,24},{24,16},{1,9},{9,1},{17,25},{25,17},{2,10},{10... | collective-permute-start | bytes 196616 | tf_op jit(solution)/shard_map/ppermute | solution.py:237
  38.2 1.3 %collective-permute-start.14 = (bf16[128,128]{1,0:T(8,128)(2,1)S(1)}, bf16[128,128]{1,0:T(8,128)(2,1)S(1)}, u32[]{:S(2)}, u32[]{:S(2)}) collective-permute-start(bf16[128,128]{1,0:T(8,128)(2,1)S(1)} %shard_map.113.own_ref), channel_id=1, source_target_pairs={{0,1},{1,0},{2,3},{3,2},{4,5},{5,4},{6,7},{7,6},{8,9},{9,8},{10,11... | collective-permute-start | bytes 98312 | tf_op jit(solution)/shard_map/ppermute | solution.py:237

commit v7 on v6

--- a/solution.py
+++ b/solution.py
@@ -104,16 +104,28 @@
         adjacency_ref[place] = unpacked(packed)
 
 
-def forward_pair(row_ref, core_ref, adjacency_ref, *refs):
-    *blocks, mine_ref, other_ref, source, total = refs
+def rows_of(core, adjacency_ref, size):
+    blocks = [
+        adjacency_ref[block_at(2 * chip + core, size), :]
+        for chip in range(adjacency_ref.shape[0] // (2 * size))
+    ]
+    return jnp.concatenate(blocks, axis=0)
+
+
+def forward_other(row_ref, core_ref, adjacency_ref, *refs):
+    *blocks, source_ref, other_ref = refs
     size = blocks[0].shape[0]
     for step, block in zip((0, 1, 3, 2), blocks):
-        source[block_at(row_ref[0] ^ step, size), :] = block[...]
-    total[...] = jnp.dot(adjacency_ref[...], source[...], preferred_element_type=f32)
-    core = core_ref[0]
-    for chip in range(mine_ref.shape[0]):
-        mine_ref[chip] = total[block_at(2 * chip + core, size), :]
-        other_ref[chip] = total[block_at(2 * chip + 1 - core, size), :].astype(bf16)
+        source_ref[block_at(row_ref[0] ^ step, size), :] = block[...]
+    rows = rows_of(1 - core_ref[0], adjacency_ref, size)
+    total = jnp.dot(rows, source_ref[...], preferred_element_type=f32)
+    other_ref[...] = total.astype(bf16).reshape(other_ref.shape)
+
+
+def forward_mine(core_ref, adjacency_ref, source_ref, mine_ref):
+    rows = rows_of(core_ref[0], adjacency_ref, mine_ref.shape[1])
+    total = jnp.dot(rows, source_ref[...], preferred_element_type=f32)
+    mine_ref[...] = total.reshape(mine_ref.shape)
 
 
 def forward_chips(chip_ref, mine_ref, received_ref, own_ref, *pieces):
@@ -163,10 +175,10 @@
     for step, block in enumerate(blocks):
         joined_ref[step] = block[0]
         ordered[chip_ref[0] ^ step] = block[1:]
-    grad = jnp.sum(ordered[...].astype(f32), axis=0).astype(bf16)
+    grad = jnp.sum(ordered[...].astype(f32), axis=0)
     second = core_ref[0] == 1
     own_grad_ref[...] = jnp.where(second, grad[1], grad[0])
-    joined_ref[chips] = jnp.where(second, grad[0], grad[1])
+    joined_ref[chips] = jnp.where(second, grad[0], grad[1]).astype(bf16)
 
 
 def backward_rows(row_ref, chip_ref, core_ref, adjacency_ref, own_ref, grad_ref, received_ref, *refs):
@@ -179,7 +191,7 @@
         source[:, block_at(peer + core, size)] = own_ref[step]
         source[:, block_at(peer + 1 - core, size)] = received_ref[step]
     total[...] = jnp.dot(source[...], adjacency_ref[...], preferred_element_type=f32)
-    grad = (grad_ref[...].astype(f32) + received_ref[chips].astype(f32)).astype(bf16)
+    grad = (grad_ref[...] + received_ref[chips].astype(f32)).astype(bf16)
     for step, piece in zip((2, 3, 1, 0), pieces):
         piece[0] = total[:, block_at(row_ref[0] ^ step, size)].astype(bf16)
         piece[1] = grad
@@ -308,12 +320,14 @@
     far_first = (3, 2, 1)
     blocks = [exchange(scaled, "row", row_shards, step) for step in (1, 3, 2)]
     blocks.insert(0, scaled)
-    mine, other = call(
-        forward_pair,
-        (struct((chips, size, width), f32), struct((chips, size, width), bf16)),
+    source, other = call(
+        forward_other,
+        (struct((row_shards * size, width), bf16), struct((chips, size, width), bf16)),
         (row, core),
         (adjacency, *blocks),
-        [pltpu.VMEM((row_shards * size, width), bf16)] + forward_scratch,
+    )
+    mine = call(
+        forward_mine, struct((chips, size, width), f32), (core,), (adjacency, source)
     )
     own, *pieces = call(
         forward_chips,
@@ -334,7 +348,7 @@
     received = [exchange(sent, "col", col_shards, 2 * step) for step in (1, 2, 3)]
     joined, own_grad = call(
         join_chips,
-        (struct((chips + 1, width, size), bf16), struct((width, size), bf16)),
+        (struct((chips + 1, width, size), bf16), struct((width, size), f32)),
         (chip, core),
         (sent, *received),
         [pltpu.VMEM((chips, 2, width, size), bf16)],
@@ -351,7 +365,7 @@
     arrived.append(pieces[-1])
     half_grad = call(
         functools.partial(sum_grad, factor),
-        struct((height, out_width // 2), bf16),
+        struct((height, out_width // 2), f32),
         (row,),
         arrived,
         [pltpu.VMEM((row_shards, height, out_width // 2), bf16)],

time: 40.3 us -> 40.2 us (level)
    pallas_call x11 -> x12, Pallas kernels: 3.56 us -> 3.68 us  [call(): pl.pallas_call(body, out_shape=out_shape, in_specs=[SMEM] * len(scalars)...]
where the time goes in v7:
time: 40.2 us; the launch traced here: 40 us
  waiting for transfers between devices  16.7 us (42%)
  starting transfers between devices  16.6 us (41%)
  Pallas kernels  4.59 us (11%)
  between operations  1.46 us (4%)
  local copies, waits for them, and re-layouts  0.69 us (2%)
    ppermute x15, waiting for transfers between devices, exchange(): lax.ppermute(block, axis, [(shard, shard ^ distance) for shard in range(s...  16.7 us
    ppermute x15, starting transfers between devices, exchange(): lax.ppermute(block, axis, [(shard, shard ^ distance) for shard in range(s...  16.6 us
    pallas_call x12, Pallas kernels, call(): pl.pallas_call(body, out_shape=out_shape, in_specs=[SMEM] * len(scalars)...  3.68 us
    pallas_call x1, Pallas kernels, on_device(): pl.pallas_call(build_adjacency, out_shape=struct((col_shards * size, row_...  0.91 us
  transfers between devices with their start and end apart: 15, of which 12 were waited for; matrix products, arithmetic and copies ran while one was open for 0% of the time, Pallas kernels for 6%

profile of v7, /device:TPU:0, one launch (start us, length us, event | category | flops | bytes accessed | tf_op | source)
XLA Modules:
  0.0 40.0 jit_solution(9027475102805566085)
XLA Ops:
  0.6 0.0 copy-start.5
  0.6 0.0 copy-start.4
  0.7 0.0 copy-start.3
  0.7 0.0 copy-start.6
  0.7 0.7 %copy-done.6 = bf16[128]{0:T(256)(128)(2,1)S(1)} copy-done((bf16[128]{0:T(256)(128)(2,1)S(1)}, bf16[128]{0:T(256)(128)(2,1)}, u32[]{:S(2)}) %copy-start.6) | copy-done | bytes 280
  1.3 0.0 copy-start
  1.3 0.1 shard_map.103.column_ref
  1.5 0.0 copy-done.5
  1.5 0.0 copy-done.4
  1.5 0.0 copy-done.3
  1.5 4.1 %collective-permute-start.2 = (bf16[128,128]{1,0:T(8,128)(2,1)S(1)}, bf16[128,128]{1,0:T(8,128)(2,1)S(1)}, u32[]{:S(2)}, u32[]{:S(2)}) collective-permute-start(bf16[128,128]{1,0:T(8,128)(2,1)S(1)} %shard_map.104.after_ref.refs_0_), channel_id=1, source_target_pairs={{0,16},{8,24},{16,0},{24,8},{1,17},{9,25},{17,1},{25,9},{2,18},{10... | collective-permute-start | bytes 98312 | tf_op jit(solution)/shard_map/ppermute | solution.py:249
  5.6 1.3 %collective-permute-start.1 = (bf16[128,128]{1,0:T(8,128)(2,1)S(1)}, bf16[128,128]{1,0:T(8,128)(2,1)S(1)}, u32[]{:S(2)}, u32[]{:S(2)}) collective-permute-start(bf16[128,128]{1,0:T(8,128)(2,1)S(1)} %shard_map.104.after_ref.refs_0_), channel_id=1, source_target_pairs={{0,24},{8,16},{16,8},{24,0},{1,25},{9,17},{17,9},{25,1},{2,26},{10... | collective-permute-start | bytes 98312 | tf_op jit(solution)/shard_map/ppermute | solution.py:249
  7.0 0.2 collective-permute-start
  7.8 0.0 copy-done
  7.9 0.9 %shard_map.105.adjacency_ref = bf16[1024,512]{1,0:T(8,128)(2,1)S(1)} custom-call(s32[1,1]{1,0:T(1,128)S(6)} %copy.11.count_ref, s32[1,1,8]{2,1,0:T(1,128)S(1)} %copy-done.4, s32[1,1,8]{2,1,0:T(1,128)S(1)} %copy-done.5, s32[1,1,8,32,256]{4,3,2,1,0:T(8,128)S(1)} %copy-done, bf16[128,128]{1,0:T(8,128)(2,1)S(1)} %shard_map.104.after_ref.refs_0_), custom_call_target="tpu_custom_call" | custom-call | flops 1048576 | bytes 1048576 | tf_op jit(solution)/shard_map/pallas_call | solution.py:312
  8.8 0.0 collective-permute-done.2.refs_3_
  8.8 2.5 %collective-permute-done.1.refs_2_ = bf16[128,128]{1,0:T(8,128)(2,1)S(1)} collective-permute-done((bf16[128,128]{1,0:T(8,128)(2,1)S(1)}, bf16[128,128]{1,0:T(8,128)(2,1)S(1)}, u32[]{:S(2)}, u32[]{:S(2)}) %collective-permute-start.1) | collective-permute-done | bytes 32800 | tf_op jit(solution)/shard_map/ppermute | solution.py:249
  11.3 0.0 collective-permute-done.refs_1_
  11.3 0.3 shard_map.106
  11.6 0.1 collective-permute-start.3
  11.7 0.3 shard_map.107.mine_ref
  12.0 1.0 %collective-permute-done.3.received_ref = bf16[4,128,128]{2,1,0:T(8,128)(2,1)S(1)} collective-permute-done((bf16[4,128,128]{2,1,0:T(8,128)(2,1)S(1)}, bf16[4,128,128]{2,1,0:T(8,128)(2,1)S(1)}, u32[]{:S(2)}, u32[]{:S(2)}) %collective-permute-start.3) | collective-permute-done | bytes 131104 | tf_op jit(solution)/shard_map/ppermute | solution.py:249
  13.1 0.0 copy-start.1
  13.1 0.0 copy-start.2
  13.1 2.5 %collective-permute-start.4 = (bf16[128,128]{1,0:T(8,128)(2,1)S(1)}, bf16[128,128]{1,0:T(8,128)(2,1)S(1)}, u32[]{:S(2)}, u32[]{:S(2)}) collective-permute-start(bf16[128,128]{1,0:T(8,128)(2,1)S(1)} %get-tuple-element.22), channel_id=1, source_target_pairs={{0,6},{1,7},{2,4},{3,5},{4,2},{5,3},{6,0},{7,1},{8,14},{9,15},{10,... | collective-permute-start | bytes 98312 | tf_op jit(solution)/shard_map/ppermute | solution.py:249
  15.6 0.5 %collective-permute-start.5 = (bf16[128,128]{1,0:T(8,128)(2,1)S(1)}, bf16[128,128]{1,0:T(8,128)(2,1)S(1)}, u32[]{:S(2)}, u32[]{:S(2)}) collective-permute-start(bf16[128,128]{1,0:T(8,128)(2,1)S(1)} %get-tuple-element.23), channel_id=1, source_target_pairs={{0,4},{1,5},{2,6},{3,7},{4,0},{5,1},{6,2},{7,3},{8,12},{9,13},{10,... | collective-permute-start | bytes 98312 | tf_op jit(solution)/shard_map/ppermute | solution.py:249
  16.1 0.0 copy-start.7
  16.1 0.5 %collective-permute-start.6 = (bf16[128,128]{1,0:T(8,128)(2,1)S(1)}, bf16[128,128]{1,0:T(8,128)(2,1)S(1)}, u32[]{:S(2)}, u32[]{:S(2)}) collective-permute-start(bf16[128,128]{1,0:T(8,128)(2,1)S(1)} %get-tuple-element.24), channel_id=1, source_target_pairs={{0,2},{1,3},{2,0},{3,1},{4,6},{5,7},{6,4},{7,5},{8,10},{9,11},{10,... | collective-permute-start | bytes 98312 | tf_op jit(solution)/shard_map/ppermute | solution.py:249
  16.6 1.3 %collective-permute-done.4.refs_0_ = bf16[128,128]{1,0:T(8,128)(2,1)S(1)} collective-permute-done((bf16[128,128]{1,0:T(8,128)(2,1)S(1)}, bf16[128,128]{1,0:T(8,128)(2,1)S(1)}, u32[]{:S(2)}, u32[]{:S(2)}) %collective-permute-start.4) | collective-permute-done | bytes 32800 | tf_op jit(solution)/shard_map/ppermute | solution.py:249
  18.0 1.5 %collective-permute-done.5.refs_1_ = bf16[128,128]{1,0:T(8,128)(2,1)S(1)} collective-permute-done((bf16[128,128]{1,0:T(8,128)(2,1)S(1)}, bf16[128,128]{1,0:T(8,128)(2,1)S(1)}, u32[]{:S(2)}, u32[]{:S(2)}) %collective-permute-start.5) | collective-permute-done | bytes 32800 | tf_op jit(solution)/shard_map/ppermute | solution.py:249
  19.5 0.5 %collective-permute-done.6.refs_2_ = bf16[128,128]{1,0:T(8,128)(2,1)S(1)} collective-permute-done((bf16[128,128]{1,0:T(8,128)(2,1)S(1)}, bf16[128,128]{1,0:T(8,128)(2,1)S(1)}, u32[]{:S(2)}, u32[]{:S(2)}) %collective-permute-start.6) | collective-permute-done | bytes 32800 | tf_op jit(solution)/shard_map/ppermute | solution.py:249
  20.0 0.0 copy-done.1
  20.0 0.0 copy-done.2
  20.0 0.0 copy-done.7
  20.0 0.4 shard_map.109
  20.4 1.6 %collective-permute-start.9 = (bf16[3,128,128]{2,1,0:T(8,128)(2,1)S(1)}, bf16[3,128,128]{2,1,0:T(8,128)(2,1)S(1)}, u32[]{:S(2)}, u32[]{:S(2)}) collective-permute-start(bf16[3,128,128]{2,1,0:T(8,128)(2,1)S(1)} %get-tuple-element.27.refs_0_), channel_id=1, source_target_pairs={{0,6},{1,7},{2,4},{3,5},{4,2},{5,3},{6,0},{7,1},{8,14},{9,15},{10,... | collective-permute-start | bytes 294920 | tf_op jit(solution)/shard_map/ppermute | solution.py:249
  22.0 0.5 %collective-permute-start.8 = (bf16[3,128,128]{2,1,0:T(8,128)(2,1)S(1)}, bf16[3,128,128]{2,1,0:T(8,128)(2,1)S(1)}, u32[]{:S(2)}, u32[]{:S(2)}) collective-permute-start(bf16[3,128,128]{2,1,0:T(8,128)(2,1)S(1)} %get-tuple-element.27.refs_0_), channel_id=1, source_target_pairs={{0,4},{1,5},{2,6},{3,7},{4,0},{5,1},{6,2},{7,3},{8,12},{9,13},{10,... | collective-permute-start | bytes 294920 | tf_op jit(solution)/shard_map/ppermute | solution.py:249
  22.5 1.5 %collective-permute-start.7 = (bf16[3,128,128]{2,1,0:T(8,128)(2,1)S(1)}, bf16[3,128,128]{2,1,0:T(8,128)(2,1)S(1)}, u32[]{:S(2)}, u32[]{:S(2)}) collective-permute-start(bf16[3,128,128]{2,1,0:T(8,128)(2,1)S(1)} %get-tuple-element.27.refs_0_), channel_id=1, source_target_pairs={{0,2},{1,3},{2,0},{3,1},{4,6},{5,7},{6,4},{7,5},{8,10},{9,11},{10,... | collective-permute-start | bytes 294920 | tf_op jit(solution)/shard_map/ppermute | solution.py:249
  24.0 0.6 %shard_map.110 = (bf16[128,256]{1,0:T(8,128)(2,1)}, f32[8,128]{1,0:T(8,128)S(1)}) custom-call(f32[128,256]{1,0:T(8,128)S(1)} %get-tuple-element.25.active_ref), custom_call_target="tpu_custom_call" | custom-call | flops 1048576 | bytes 1048576 | tf_op jit(solution)/shard_map/pallas_call | solution.py:25
  24.6 1.8 %collective-permute-done.9.refs_3_ = bf16[3,128,128]{2,1,0:T(8,128)(2,1)S(1)} collective-permute-done((bf16[3,128,128]{2,1,0:T(8,128)(2,1)S(1)}, bf16[3,128,128]{2,1,0:T(8,128)(2,1)S(1)}, u32[]{:S(2)}, u32[]{:S(2)}) %collective-permute-start.9) | collective-permute-done | bytes 98336 | tf_op jit(solution)/shard_map/ppermute | solution.py:249
  26.4 0.9 %collective-permute-done.8.refs_2_ = bf16[3,128,128]{2,1,0:T(8,128)(2,1)S(1)} collective-permute-done((bf16[3,128,128]{2,1,0:T(8,128)(2,1)S(1)}, bf16[3,128,128]{2,1,0:T(8,128)(2,1)S(1)}, u32[]{:S(2)}, u32[]{:S(2)}) %collective-permute-start.8) | collective-permute-done | bytes 98336 | tf_op jit(solution)/shard_map/ppermute | solution.py:249
  27.3 0.0 collective-permute-done.7.refs_1_
  27.3 0.1 shard_map.111
  27.4 0.1 collective-permute-start.10
  27.5 1.4 %collective-permute-done.10.received_ref = bf16[5,128,128]{2,1,0:T(8,128)(2,1)S(1)} collective-permute-done((bf16[5,128,128]{2,1,0:T(8,128)(2,1)S(1)}, bf16[5,128,128]{2,1,0:T(8,128)(2,1)S(1)}, u32[]{:S(2)}, u32[]{:S(2)}) %collective-permute-start.10) | collective-permute-done | bytes 163872 | tf_op jit(solution)/shard_map/ppermute | solution.py:249
  28.9 0.4 %shard_map.112 = (bf16[2,128,128]{2,1,0:T(8,128)(2,1)S(1)}, bf16[2,128,128]{2,1,0:T(8,128)(2,1)S(1)}, bf16[2,128,128]{2,1,0:T(8,128)(2,1)S(1)}, bf16[2,128,128]{2,1,0:T(8,128)(2,1)S(1)}) custom-call(s32[1]{0:T(128)} %bitcast.2.row_ref, s32[1]{0:T(128)} %bitcast.chip_ref, s32[1]{0:T(128)} %bitcast.1.core_ref, bf16[1024,512]{1,0:T(8,128)(2,1)S(1)} %shard_map.105.adjacency_ref, ...), custom_call_target="tpu_custom_call" | custom-call | flops 1048576 | bytes 1048576 | tf_op jit(solution)/shard_map/pallas_call | solution.py:25
  29.3 1.3 %collective-permute-start.11 = (bf16[2,128,128]{2,1,0:T(8,128)(2,1)S(1)}, bf16[2,128,128]{2,1,0:T(8,128)(2,1)S(1)}, u32[]{:S(2)}, u32[]{:S(2)}) collective-permute-start(bf16[2,128,128]{2,1,0:T(8,128)(2,1)S(1)} %get-tuple-element.31), channel_id=1, source_target_pairs={{0,16},{8,24},{16,0},{24,8},{1,17},{9,25},{17,1},{25,9},{2,18},{10... | collective-permute-start | bytes 196616 | tf_op jit(solution)/shard_map/ppermute | solution.py:249
  30.6 1.0 %collective-permute-start.12 = (bf16[2,128,128]{2,1,0:T(8,128)(2,1)S(1)}, bf16[2,128,128]{2,1,0:T(8,128)(2,1)S(1)}, u32[]{:S(2)}, u32[]{:S(2)}) collective-permute-start(bf16[2,128,128]{2,1,0:T(8,128)(2,1)S(1)} %get-tuple-element.32), channel_id=1, source_target_pairs={{0,24},{8,16},{16,8},{24,0},{1,25},{9,17},{17,9},{25,1},{2,26},{10... | collective-permute-start | bytes 196616 | tf_op jit(solution)/shard_map/ppermute | solution.py:249
  31.6 1.2 %collective-permute-start.13 = (bf16[2,128,128]{2,1,0:T(8,128)(2,1)S(1)}, bf16[2,128,128]{2,1,0:T(8,128)(2,1)S(1)}, u32[]{:S(2)}, u32[]{:S(2)}) collective-permute-start(bf16[2,128,128]{2,1,0:T(8,128)(2,1)S(1)} %get-tuple-element.33), channel_id=1, source_target_pairs={{0,8},{8,0},{16,24},{24,16},{1,9},{9,1},{17,25},{25,17},{2,10},{10... | collective-permute-start | bytes 196616 | tf_op jit(solution)/shard_map/ppermute | solution.py:249
  32.8 3.2 %collective-permute-done.11.refs_0_ = bf16[2,128,128]{2,1,0:T(8,128)(2,1)S(1)} collective-permute-done((bf16[2,128,128]{2,1,0:T(8,128)(2,1)S(1)}, bf16[2,128,128]{2,1,0:T(8,128)(2,1)S(1)}, u32[]{:S(2)}, u32[]{:S(2)}) %collective-permute-start.11) | collective-permute-done | bytes 65568 | tf_op jit(solution)/shard_map/ppermute | solution.py:249
  36.1 0.9 %collective-permute-done.12.refs_1_ = bf16[2,128,128]{2,1,0:T(8,128)(2,1)S(1)} collective-permute-done((bf16[2,128,128]{2,1,0:T(8,128)(2,1)S(1)}, bf16[2,128,128]{2,1,0:T(8,128)(2,1)S(1)}, u32[]{:S(2)}, u32[]{:S(2)}) %collective-permute-start.12) | collective-permute-done | bytes 65568 | tf_op jit(solution)/shard_map/ppermute | solution.py:249
  37.0 1.0 %collective-permute-done.13.refs_2_ = bf16[2,128,128]{2,1,0:T(8,128)(2,1)S(1)} collective-permute-done((bf16[2,128,128]{2,1,0:T(8,128)(2,1)S(1)}, bf16[2,128,128]{2,1,0:T(8,128)(2,1)S(1)}, u32[]{:S(2)}, u32[]{:S(2)}) %collective-permute-start.13) | collective-permute-done | bytes 65568 | tf_op jit(solution)/shard_map/ppermute | solution.py:249
  38.0 0.1 collective-permute-start.14
  38.1 0.7 %shard_map.113 = bf16[128,128]{1,0:T(8,128)(2,1)} custom-call(bf16[128]{0:T(256)(128)(2,1)S(1)} %copy-done.7, bf16[2,128,128]{2,1,0:T(8,128)(2,1)S(1)} %collective-permute-done.11.refs_0_, bf16[2,128,128]{2,1,0:T(8,128)(2,1)S(1)} %collective-permute-done.12.refs_1_, bf16[2,128,128]{2,1,0:T(8,128)(2,1)S(1)} %collective-permute-done.13.refs_2_, ...), custom_call_target="tpu_custom_call" | custom-call | flops 1048576 | bytes 1048576 | tf_op jit(solution)/shard_map/pallas_call | solution.py:25
  38.8 0.5 %collective-permute-done.14.other_ref = f32[128,128]{1,0:T(8,128)S(1)} collective-permute-done((f32[128,128]{1,0:T(8,128)S(1)}, f32[128,128]{1,0:T(8,128)S(1)}, u32[]{:S(2)}, u32[]{:S(2)}) %collective-permute-start.14) | collective-permute-done | bytes 65568 | tf_op jit(solution)/shard_map/ppermute | solution.py:249
  39.3 0.7 %shard_map.115 = f32[128,256]{1,0:T(8,128)} custom-call(s32[1]{0:T(128)} %bitcast.1.core_ref, f32[128,128]{1,0:T(8,128)S(1)} %shard_map.114.own_ref, f32[128,128]{1,0:T(8,128)S(1)} %collective-permute-done.14.other_ref), custom_call_target="tpu_custom_call" | custom-call | flops 1048576 | bytes 1048576 | tf_op jit(solution)/shard_map/pallas_call | solution.py:25
  (3 shorter events, 0.1 us)
Async XLA Ops:
  0.6 0.8 %copy-start.5 = (s32[1,1,8]{2,1,0:T(1,128)S(1)}, s32[1,1,8]{2,1,0:T(1,128)}, u32[]{:S(2)}) copy-start(s32[1,1,8]{2,1,0:T(1,128)} %cols_ref.3) | copy-start | bytes 100
  0.6 0.8 %copy-start.4 = (s32[1,1,8]{2,1,0:T(1,128)S(1)}, s32[1,1,8]{2,1,0:T(1,128)}, u32[]{:S(2)}) copy-start(s32[1,1,8]{2,1,0:T(1,128)} %rows_ref.3) | copy-start | bytes 100
  0.7 0.8 %copy-start.3 = (bf16[128,128]{1,0:T(8,128)(2,1)S(1)}, bf16[128,128]{1,0:T(8,128)(2,1)}, u32[]{:S(2)}) copy-start(bf16[128,128]{1,0:T(8,128)(2,1)} %features_ref.1) | copy-start | bytes 98308
  0.7 0.7 %copy-start.6 = (bf16[128]{0:T(256)(128)(2,1)S(1)}, bf16[128]{0:T(256)(128)(2,1)}, u32[]{:S(2)}) copy-start(bf16[128]{0:T(256)(128)(2,1)} %deg_ref.5) | copy-start | bytes 772
  1.3 6.5 %copy-start = (s32[1,1,8,32,256]{4,3,2,1,0:T(8,128)S(1)}, s32[1,1,8,32,256]{4,3,2,1,0:T(8,128)}, u32[]{:S(2)}) copy-start(s32[1,1,8,32,256]{4,3,2,1,0:T(8,128)} %bits_ref.1) | copy-start | bytes 786436
  1.5 7.3 %collective-permute-start.2 = (bf16[128,128]{1,0:T(8,128)(2,1)S(1)}, bf16[128,128]{1,0:T(8,128)(2,1)S(1)}, u32[]{:S(2)}, u32[]{:S(2)}) collective-permute-start(bf16[128,128]{1,0:T(8,128)(2,1)S(1)} %shard_map.104.after_ref.refs_0_), channel_id=1, source_target_pairs={{0,16},{8,24},{16,0},{24,8},{1,17},{9,25},{17,1},{25,9},{2,18},{10... | collective-permute-start | bytes 98312 | tf_op jit(solution)/shard_map/ppermute | solution.py:249
  5.6 5.7 %collective-permute-start.1 = (bf16[128,128]{1,0:T(8,128)(2,1)S(1)}, bf16[128,128]{1,0:T(8,128)(2,1)S(1)}, u32[]{:S(2)}, u32[]{:S(2)}) collective-permute-start(bf16[128,128]{1,0:T(8,128)(2,1)S(1)} %shard_map.104.after_ref.refs_0_), channel_id=1, source_target_pairs={{0,24},{8,16},{16,8},{24,0},{1,25},{9,17},{17,9},{25,1},{2,26},{10... | collective-permute-start | bytes 98312 | tf_op jit(solution)/shard_map/ppermute | solution.py:249
  7.0 4.4 %collective-permute-start = (bf16[128,128]{1,0:T(8,128)(2,1)S(1)}, bf16[128,128]{1,0:T(8,128)(2,1)S(1)}, u32[]{:S(2)}, u32[]{:S(2)}) collective-permute-start(bf16[128,128]{1,0:T(8,128)(2,1)S(1)} %shard_map.104.after_ref.refs_0_), channel_id=1, source_target_pairs={{0,8},{8,0},{16,24},{24,16},{1,9},{9,1},{17,25},{25,17},{2,10},{10... | collective-permute-start | bytes 98312 | tf_op jit(solution)/shard_map/ppermute | solution.py:249
  11.6 1.4 %collective-permute-start.3 = (bf16[4,128,128]{2,1,0:T(8,128)(2,1)S(1)}, bf16[4,128,128]{2,1,0:T(8,128)(2,1)S(1)}, u32[]{:S(2)}, u32[]{:S(2)}) collective-permute-start(bf16[4,128,128]{2,1,0:T(8,128)(2,1)S(1)} %get-tuple-element.20), channel_id=1, source_target_pairs={{0,1},{1,0},{2,3},{3,2},{4,5},{5,4},{6,7},{7,6},{8,9},{9,8},{10,11... | collective-permute-start | bytes 393224 | tf_op jit(solution)/shard_map/ppermute | solution.py:249
  13.1 7.0 %copy-start.1 = (bf16[128,256]{1,0:T(8,128)(2,1)S(1)}, bf16[128,256]{1,0:T(8,128)(2,1)}, u32[]{:S(2)}) copy-start(bf16[128,256]{1,0:T(8,128)(2,1)} %weight_ref.1) | copy-start | bytes 196612
  13.1 7.0 %copy-start.2 = (bf16[128,256]{1,0:T(8,128)(2,1)S(1)}, bf16[128,256]{1,0:T(8,128)(2,1)}, u32[]{:S(2)}) copy-start(bf16[128,256]{1,0:T(8,128)(2,1)} %cotangent_ref.1) | copy-start | bytes 196612
  13.1 4.9 %collective-permute-start.4 = (bf16[128,128]{1,0:T(8,128)(2,1)S(1)}, bf16[128,128]{1,0:T(8,128)(2,1)S(1)}, u32[]{:S(2)}, u32[]{:S(2)}) collective-permute-start(bf16[128,128]{1,0:T(8,128)(2,1)S(1)} %get-tuple-element.22), channel_id=1, source_target_pairs={{0,6},{1,7},{2,4},{3,5},{4,2},{5,3},{6,0},{7,1},{8,14},{9,15},{10,... | collective-permute-start | bytes 98312 | tf_op jit(solution)/shard_map/ppermute | solution.py:249
  15.6 3.9 %collective-permute-start.5 = (bf16[128,128]{1,0:T(8,128)(2,1)S(1)}, bf16[128,128]{1,0:T(8,128)(2,1)S(1)}, u32[]{:S(2)}, u32[]{:S(2)}) collective-permute-start(bf16[128,128]{1,0:T(8,128)(2,1)S(1)} %get-tuple-element.23), channel_id=1, source_target_pairs={{0,4},{1,5},{2,6},{3,7},{4,0},{5,1},{6,2},{7,3},{8,12},{9,13},{10,... | collective-permute-start | bytes 98312 | tf_op jit(solution)/shard_map/ppermute | solution.py:249
  16.1 3.9 %copy-start.7 = (bf16[128]{0:T(256)(128)(2,1)S(1)}, bf16[128]{0:T(256)(128)(2,1)}, u32[]{:S(2)}) copy-start(bf16[128]{0:T(256)(128)(2,1)} %deg_ref.5) | copy-start | bytes 772
  16.1 3.9 %collective-permute-start.6 = (bf16[128,128]{1,0:T(8,128)(2,1)S(1)}, bf16[128,128]{1,0:T(8,128)(2,1)S(1)}, u32[]{:S(2)}, u32[]{:S(2)}) collective-permute-start(bf16[128,128]{1,0:T(8,128)(2,1)S(1)} %get-tuple-element.24), channel_id=1, source_target_pairs={{0,2},{1,3},{2,0},{3,1},{4,6},{5,7},{6,4},{7,5},{8,10},{9,11},{10,... | collective-permute-start | bytes 98312 | tf_op jit(solution)/shard_map/ppermute | solution.py:249
  20.4 6.0 %collective-permute-start.9 = (bf16[3,128,128]{2,1,0:T(8,128)(2,1)S(1)}, bf16[3,128,128]{2,1,0:T(8,128)(2,1)S(1)}, u32[]{:S(2)}, u32[]{:S(2)}) collective-permute-start(bf16[3,128,128]{2,1,0:T(8,128)(2,1)S(1)} %get-tuple-element.27.refs_0_), channel_id=1, source_target_pairs={{0,6},{1,7},{2,4},{3,5},{4,2},{5,3},{6,0},{7,1},{8,14},{9,15},{10,... | collective-permute-start | bytes 294920 | tf_op jit(solution)/shard_map/ppermute | solution.py:249
  22.0 5.4 %collective-permute-start.8 = (bf16[3,128,128]{2,1,0:T(8,128)(2,1)S(1)}, bf16[3,128,128]{2,1,0:T(8,128)(2,1)S(1)}, u32[]{:S(2)}, u32[]{:S(2)}) collective-permute-start(bf16[3,128,128]{2,1,0:T(8,128)(2,1)S(1)} %get-tuple-element.27.refs_0_), channel_id=1, source_target_pairs={{0,4},{1,5},{2,6},{3,7},{4,0},{5,1},{6,2},{7,3},{8,12},{9,13},{10,... | collective-permute-start | bytes 294920 | tf_op jit(solution)/shard_map/ppermute | solution.py:249
  22.5 4.8 %collective-permute-start.7 = (bf16[3,128,128]{2,1,0:T(8,128)(2,1)S(1)}, bf16[3,128,128]{2,1,0:T(8,128)(2,1)S(1)}, u32[]{:S(2)}, u32[]{:S(2)}) collective-permute-start(bf16[3,128,128]{2,1,0:T(8,128)(2,1)S(1)} %get-tuple-element.27.refs_0_), channel_id=1, source_target_pairs={{0,2},{1,3},{2,0},{3,1},{4,6},{5,7},{6,4},{7,5},{8,10},{9,11},{10,... | collective-permute-start | bytes 294920 | tf_op jit(solution)/shard_map/ppermute | solution.py:249
  27.4 1.5 %collective-permute-start.10 = (bf16[5,128,128]{2,1,0:T(8,128)(2,1)S(1)}, bf16[5,128,128]{2,1,0:T(8,128)(2,1)S(1)}, u32[]{:S(2)}, u32[]{:S(2)}) collective-permute-start(bf16[5,128,128]{2,1,0:T(8,128)(2,1)S(1)} %get-tuple-element.29.own_ref), channel_id=1, source_target_pairs={{0,1},{1,0},{2,3},{3,2},{4,5},{5,4},{6,7},{7,6},{8,9},{9,8},{10,11... | collective-permute-start | bytes 491528 | tf_op jit(solution)/shard_map/ppermute | solution.py:249
  29.3 6.8 %collective-permute-start.11 = (bf16[2,128,128]{2,1,0:T(8,128)(2,1)S(1)}, bf16[2,128,128]{2,1,0:T(8,128)(2,1)S(1)}, u32[]{:S(2)}, u32[]{:S(2)}) collective-permute-start(bf16[2,128,128]{2,1,0:T(8,128)(2,1)S(1)} %get-tuple-element.31), channel_id=1, source_target_pairs={{0,16},{8,24},{16,0},{24,8},{1,17},{9,25},{17,1},{25,9},{2,18},{10... | collective-permute-start | bytes 196616 | tf_op jit(solution)/shard_map/ppermute | solution.py:249
  30.6 6.4 %collective-permute-start.12 = (bf16[2,128,128]{2,1,0:T(8,128)(2,1)S(1)}, bf16[2,128,128]{2,1,0:T(8,128)(2,1)S(1)}, u32[]{:S(2)}, u32[]{:S(2)}) collective-permute-start(bf16[2,128,128]{2,1,0:T(8,128)(2,1)S(1)} %get-tuple-element.32), channel_id=1, source_target_pairs={{0,24},{8,16},{16,8},{24,0},{1,25},{9,17},{17,9},{25,1},{2,26},{10... | collective-permute-start | bytes 196616 | tf_op jit(solution)/shard_map/ppermute | solution.py:249
  31.6 6.4 %collective-permute-start.13 = (bf16[2,128,128]{2,1,0:T(8,128)(2,1)S(1)}, bf16[2,128,128]{2,1,0:T(8,128)(2,1)S(1)}, u32[]{:S(2)}, u32[]{:S(2)}) collective-permute-start(bf16[2,128,128]{2,1,0:T(8,128)(2,1)S(1)} %get-tuple-element.33), channel_id=1, source_target_pairs={{0,8},{8,0},{16,24},{24,16},{1,9},{9,1},{17,25},{25,17},{2,10},{10... | collective-permute-start | bytes 196616 | tf_op jit(solution)/shard_map/ppermute | solution.py:249
  38.0 1.3 %collective-permute-start.14 = (f32[128,128]{1,0:T(8,128)S(1)}, f32[128,128]{1,0:T(8,128)S(1)}, u32[]{:S(2)}, u32[]{:S(2)}) collective-permute-start(f32[128,128]{1,0:T(8,128)S(1)} %shard_map.114.own_ref), channel_id=1, source_target_pairs={{0,1},{1,0},{2,3},{3,2},{4,5},{5,4},{6,7},{7,6},{8,9},{9,8},{10,11... | collective-permute-start | bytes 196616 | tf_op jit(solution)/shard_map/ppermute | solution.py:249

commit v8 on v7

--- a/solution.py
+++ b/solution.py
@@ -192,14 +192,14 @@
         source[:, block_at(peer + 1 - core, size)] = received_ref[step]
     total[...] = jnp.dot(source[...], adjacency_ref[...], preferred_element_type=f32)
     grad = (grad_ref[...] + received_ref[chips].astype(f32)).astype(bf16)
-    for step, piece in zip((2, 3, 1, 0), pieces):
+    for step, piece in zip((3, 1, 2, 0), pieces):
         piece[0] = total[:, block_at(row_ref[0] ^ step, size)].astype(bf16)
         piece[1] = grad
 
 
 def sum_grad(factor, row_ref, *refs):
     *pieces, out_ref, ordered = refs
-    for step, piece in zip((2, 3, 1, 0), pieces):
+    for step, piece in zip((3, 1, 2, 0), pieces):
         ordered[row_ref[0] ^ step] = piece[1]
     total = jnp.sum(ordered[...].astype(f32), axis=0) * factor
     out_ref[...] = total.astype(out_ref.dtype)
@@ -361,7 +361,7 @@
         (adjacency, joined, own_grad, exchange(joined, "col", col_shards, 1)),
         backward_scratch,
     )
-    arrived = [exchange(piece, "row", row_shards, step) for step, piece in zip((2, 3, 1), pieces)]
+    arrived = [exchange(piece, "row", row_shards, step) for step, piece in zip((3, 1, 2), pieces)]
     arrived.append(pieces[-1])
     half_grad = call(
         functools.partial(sum_grad, factor),

time: 40.2 us -> 40.4 us (level)
  starting transfers between devices: 16.6 us -> 17.5 us
  waiting for transfers between devices: 16.7 us -> 16 us
    ppermute x15, starting transfers between devices: 16.6 us -> 17.5 us  [exchange(): lax.ppermute(block, axis, [(shard, shard ^ distance) for shard in range(s...]
    ppermute x15, waiting for transfers between devices: 16.7 us -> 16 us  [exchange(): lax.ppermute(block, axis, [(shard, shard ^ distance) for shard in range(s...]
where the time goes in v8:
time: 40.4 us; the launch traced here: 40.2 us
  starting transfers between devices  17.5 us (43%)
  waiting for transfers between devices  16 us (40%)
  Pallas kernels  4.59 us (11%)
  between operations  1.46 us (4%)
  local copies, waits for them, and re-layouts  0.69 us (2%)
    ppermute x15, starting transfers between devices, exchange(): lax.ppermute(block, axis, [(shard, shard ^ distance) for shard in range(s...  17.5 us
    ppermute x15, waiting for transfers between devices, exchange(): lax.ppermute(block, axis, [(shard, shard ^ distance) for shard in range(s...  16 us
    pallas_call x12, Pallas kernels, call(): pl.pallas_call(body, out_shape=out_shape, in_specs=[SMEM] * len(scalars)...  3.68 us
    pallas_call x1, Pallas kernels, on_device(): pl.pallas_call(build_adjacency, out_shape=struct((col_shards * size, row_...  0.91 us
  transfers between devices with their start and end apart: 15, of which 12 were waited for; matrix products, arithmetic and copies ran while one was open for 0% of the time, Pallas kernels for 6%

profile of v8, /device:TPU:0, one launch (start us, length us, event | category | flops | bytes accessed | tf_op | source)
XLA Modules:
  0.0 40.2 jit_solution(12319844080032352832)
XLA Ops:
  0.6 0.0 copy-start.5
  0.6 0.0 copy-start.4
  0.7 0.0 copy-start.3
  0.7 0.0 copy-start.6
  0.7 0.7 %copy-done.6 = bf16[128]{0:T(256)(128)(2,1)S(1)} copy-done((bf16[128]{0:T(256)(128)(2,1)S(1)}, bf16[128]{0:T(256)(128)(2,1)}, u32[]{:S(2)}) %copy-start.6) | copy-done | bytes 280
  1.3 0.0 copy-start
  1.3 0.1 shard_map.103.column_ref
  1.5 0.0 copy-done.5
  1.5 0.0 copy-done.4
  1.5 0.0 copy-done.3
  1.5 4.1 %collective-permute-start.2 = (bf16[128,128]{1,0:T(8,128)(2,1)S(1)}, bf16[128,128]{1,0:T(8,128)(2,1)S(1)}, u32[]{:S(2)}, u32[]{:S(2)}) collective-permute-start(bf16[128,128]{1,0:T(8,128)(2,1)S(1)} %shard_map.104.after_ref.refs_0_), channel_id=1, source_target_pairs={{0,16},{8,24},{16,0},{24,8},{1,17},{9,25},{17,1},{25,9},{2,18},{10... | collective-permute-start | bytes 98312 | tf_op jit(solution)/shard_map/ppermute | solution.py:249
  5.6 1.3 %collective-permute-start.1 = (bf16[128,128]{1,0:T(8,128)(2,1)S(1)}, bf16[128,128]{1,0:T(8,128)(2,1)S(1)}, u32[]{:S(2)}, u32[]{:S(2)}) collective-permute-start(bf16[128,128]{1,0:T(8,128)(2,1)S(1)} %shard_map.104.after_ref.refs_0_), channel_id=1, source_target_pairs={{0,24},{8,16},{16,8},{24,0},{1,25},{9,17},{17,9},{25,1},{2,26},{10... | collective-permute-start | bytes 98312 | tf_op jit(solution)/shard_map/ppermute | solution.py:249
  7.0 0.2 collective-permute-start
  7.8 0.0 copy-done
  7.9 0.9 %shard_map.105.adjacency_ref = bf16[1024,512]{1,0:T(8,128)(2,1)S(1)} custom-call(s32[1,1]{1,0:T(1,128)S(6)} %copy.11.count_ref, s32[1,1,8]{2,1,0:T(1,128)S(1)} %copy-done.4, s32[1,1,8]{2,1,0:T(1,128)S(1)} %copy-done.5, s32[1,1,8,32,256]{4,3,2,1,0:T(8,128)S(1)} %copy-done, bf16[128,128]{1,0:T(8,128)(2,1)S(1)} %shard_map.104.after_ref.refs_0_), custom_call_target="tpu_custom_call" | custom-call | flops 1048576 | bytes 1048576 | tf_op jit(solution)/shard_map/pallas_call | solution.py:312
  8.8 0.0 collective-permute-done.2.refs_3_
  8.8 2.5 %collective-permute-done.1.refs_2_ = bf16[128,128]{1,0:T(8,128)(2,1)S(1)} collective-permute-done((bf16[128,128]{1,0:T(8,128)(2,1)S(1)}, bf16[128,128]{1,0:T(8,128)(2,1)S(1)}, u32[]{:S(2)}, u32[]{:S(2)}) %collective-permute-start.1) | collective-permute-done | bytes 32800 | tf_op jit(solution)/shard_map/ppermute | solution.py:249
  11.3 0.0 collective-permute-done.refs_1_
  11.3 0.3 shard_map.106
  11.6 0.1 collective-permute-start.3
  11.7 0.3 shard_map.107.mine_ref
  12.0 1.0 %collective-permute-done.3.received_ref = bf16[4,128,128]{2,1,0:T(8,128)(2,1)S(1)} collective-permute-done((bf16[4,128,128]{2,1,0:T(8,128)(2,1)S(1)}, bf16[4,128,128]{2,1,0:T(8,128)(2,1)S(1)}, u32[]{:S(2)}, u32[]{:S(2)}) %collective-permute-start.3) | collective-permute-done | bytes 131104 | tf_op jit(solution)/shard_map/ppermute | solution.py:249
  13.1 0.0 copy-start.1
  13.1 0.0 copy-start.2
  13.1 2.5 %collective-permute-start.4 = (bf16[128,128]{1,0:T(8,128)(2,1)S(1)}, bf16[128,128]{1,0:T(8,128)(2,1)S(1)}, u32[]{:S(2)}, u32[]{:S(2)}) collective-permute-start(bf16[128,128]{1,0:T(8,128)(2,1)S(1)} %get-tuple-element.22), channel_id=1, source_target_pairs={{0,6},{1,7},{2,4},{3,5},{4,2},{5,3},{6,0},{7,1},{8,14},{9,15},{10,... | collective-permute-start | bytes 98312 | tf_op jit(solution)/shard_map/ppermute | solution.py:249
  15.6 0.5 %collective-permute-start.5 = (bf16[128,128]{1,0:T(8,128)(2,1)S(1)}, bf16[128,128]{1,0:T(8,128)(2,1)S(1)}, u32[]{:S(2)}, u32[]{:S(2)}) collective-permute-start(bf16[128,128]{1,0:T(8,128)(2,1)S(1)} %get-tuple-element.23), channel_id=1, source_target_pairs={{0,4},{1,5},{2,6},{3,7},{4,0},{5,1},{6,2},{7,3},{8,12},{9,13},{10,... | collective-permute-start | bytes 98312 | tf_op jit(solution)/shard_map/ppermute | solution.py:249
  16.1 0.0 copy-start.7
  16.1 0.5 %collective-permute-start.6 = (bf16[128,128]{1,0:T(8,128)(2,1)S(1)}, bf16[128,128]{1,0:T(8,128)(2,1)S(1)}, u32[]{:S(2)}, u32[]{:S(2)}) collective-permute-start(bf16[128,128]{1,0:T(8,128)(2,1)S(1)} %get-tuple-element.24), channel_id=1, source_target_pairs={{0,2},{1,3},{2,0},{3,1},{4,6},{5,7},{6,4},{7,5},{8,10},{9,11},{10,... | collective-permute-start | bytes 98312 | tf_op jit(solution)/shard_map/ppermute | solution.py:249
  16.6 1.3 %collective-permute-done.4.refs_0_ = bf16[128,128]{1,0:T(8,128)(2,1)S(1)} collective-permute-done((bf16[128,128]{1,0:T(8,128)(2,1)S(1)}, bf16[128,128]{1,0:T(8,128)(2,1)S(1)}, u32[]{:S(2)}, u32[]{:S(2)}) %collective-permute-start.4) | collective-permute-done | bytes 32800 | tf_op jit(solution)/shard_map/ppermute | solution.py:249
  18.0 1.5 %collective-permute-done.5.refs_1_ = bf16[128,128]{1,0:T(8,128)(2,1)S(1)} collective-permute-done((bf16[128,128]{1,0:T(8,128)(2,1)S(1)}, bf16[128,128]{1,0:T(8,128)(2,1)S(1)}, u32[]{:S(2)}, u32[]{:S(2)}) %collective-permute-start.5) | collective-permute-done | bytes 32800 | tf_op jit(solution)/shard_map/ppermute | solution.py:249
  19.5 0.5 %collective-permute-done.6.refs_2_ = bf16[128,128]{1,0:T(8,128)(2,1)S(1)} collective-permute-done((bf16[128,128]{1,0:T(8,128)(2,1)S(1)}, bf16[128,128]{1,0:T(8,128)(2,1)S(1)}, u32[]{:S(2)}, u32[]{:S(2)}) %collective-permute-start.6) | collective-permute-done | bytes 32800 | tf_op jit(solution)/shard_map/ppermute | solution.py:249
  20.0 0.0 copy-done.1
  20.0 0.0 copy-done.2
  20.0 0.0 copy-done.7
  20.0 0.4 shard_map.109
  20.4 1.6 %collective-permute-start.9 = (bf16[3,128,128]{2,1,0:T(8,128)(2,1)S(1)}, bf16[3,128,128]{2,1,0:T(8,128)(2,1)S(1)}, u32[]{:S(2)}, u32[]{:S(2)}) collective-permute-start(bf16[3,128,128]{2,1,0:T(8,128)(2,1)S(1)} %get-tuple-element.27.refs_0_), channel_id=1, source_target_pairs={{0,6},{1,7},{2,4},{3,5},{4,2},{5,3},{6,0},{7,1},{8,14},{9,15},{10,... | collective-permute-start | bytes 294920 | tf_op jit(solution)/shard_map/ppermute | solution.py:249
  22.0 0.5 %collective-permute-start.8 = (bf16[3,128,128]{2,1,0:T(8,128)(2,1)S(1)}, bf16[3,128,128]{2,1,0:T(8,128)(2,1)S(1)}, u32[]{:S(2)}, u32[]{:S(2)}) collective-permute-start(bf16[3,128,128]{2,1,0:T(8,128)(2,1)S(1)} %get-tuple-element.27.refs_0_), channel_id=1, source_target_pairs={{0,4},{1,5},{2,6},{3,7},{4,0},{5,1},{6,2},{7,3},{8,12},{9,13},{10,... | collective-permute-start | bytes 294920 | tf_op jit(solution)/shard_map/ppermute | solution.py:249
  22.5 1.5 %collective-permute-start.7 = (bf16[3,128,128]{2,1,0:T(8,128)(2,1)S(1)}, bf16[3,128,128]{2,1,0:T(8,128)(2,1)S(1)}, u32[]{:S(2)}, u32[]{:S(2)}) collective-permute-start(bf16[3,128,128]{2,1,0:T(8,128)(2,1)S(1)} %get-tuple-element.27.refs_0_), channel_id=1, source_target_pairs={{0,2},{1,3},{2,0},{3,1},{4,6},{5,7},{6,4},{7,5},{8,10},{9,11},{10,... | collective-permute-start | bytes 294920 | tf_op jit(solution)/shard_map/ppermute | solution.py:249
  24.0 0.6 %shard_map.110 = (bf16[128,256]{1,0:T(8,128)(2,1)}, f32[8,128]{1,0:T(8,128)S(1)}) custom-call(f32[128,256]{1,0:T(8,128)S(1)} %get-tuple-element.25.active_ref), custom_call_target="tpu_custom_call" | custom-call | flops 1048576 | bytes 1048576 | tf_op jit(solution)/shard_map/pallas_call | solution.py:25
  24.6 1.8 %collective-permute-done.9.refs_3_ = bf16[3,128,128]{2,1,0:T(8,128)(2,1)S(1)} collective-permute-done((bf16[3,128,128]{2,1,0:T(8,128)(2,1)S(1)}, bf16[3,128,128]{2,1,0:T(8,128)(2,1)S(1)}, u32[]{:S(2)}, u32[]{:S(2)}) %collective-permute-start.9) | collective-permute-done | bytes 98336 | tf_op jit(solution)/shard_map/ppermute | solution.py:249
  26.4 0.9 %collective-permute-done.8.refs_2_ = bf16[3,128,128]{2,1,0:T(8,128)(2,1)S(1)} collective-permute-done((bf16[3,128,128]{2,1,0:T(8,128)(2,1)S(1)}, bf16[3,128,128]{2,1,0:T(8,128)(2,1)S(1)}, u32[]{:S(2)}, u32[]{:S(2)}) %collective-permute-start.8) | collective-permute-done | bytes 98336 | tf_op jit(solution)/shard_map/ppermute | solution.py:249
  27.3 0.0 collective-permute-done.7.refs_1_
  27.3 0.1 shard_map.111
  27.4 0.1 collective-permute-start.10
  27.5 1.4 %collective-permute-done.10.received_ref = bf16[5,128,128]{2,1,0:T(8,128)(2,1)S(1)} collective-permute-done((bf16[5,128,128]{2,1,0:T(8,128)(2,1)S(1)}, bf16[5,128,128]{2,1,0:T(8,128)(2,1)S(1)}, u32[]{:S(2)}, u32[]{:S(2)}) %collective-permute-start.10) | collective-permute-done | bytes 163872 | tf_op jit(solution)/shard_map/ppermute | solution.py:249
  28.9 0.4 shard_map.112
  29.3 2.1 %collective-permute-start.11 = (bf16[2,128,128]{2,1,0:T(8,128)(2,1)S(1)}, bf16[2,128,128]{2,1,0:T(8,128)(2,1)S(1)}, u32[]{:S(2)}, u32[]{:S(2)}) collective-permute-start(bf16[2,128,128]{2,1,0:T(8,128)(2,1)S(1)} %get-tuple-element.31), channel_id=1, source_target_pairs={{0,24},{8,16},{16,8},{24,0},{1,25},{9,17},{17,9},{25,1},{2,26},{10... | collective-permute-start | bytes 196616 | tf_op jit(solution)/shard_map/ppermute | solution.py:249
  31.4 0.0 collective-permute-start.12
  31.4 2.4 %collective-permute-start.13 = (bf16[2,128,128]{2,1,0:T(8,128)(2,1)S(1)}, bf16[2,128,128]{2,1,0:T(8,128)(2,1)S(1)}, u32[]{:S(2)}, u32[]{:S(2)}) collective-permute-start(bf16[2,128,128]{2,1,0:T(8,128)(2,1)S(1)} %get-tuple-element.33), channel_id=1, source_target_pairs={{0,16},{8,24},{16,0},{24,8},{1,17},{9,25},{17,1},{25,9},{2,18},{10... | collective-permute-start | bytes 196616 | tf_op jit(solution)/shard_map/ppermute | solution.py:249
  33.7 2.3 %collective-permute-done.11.refs_0_ = bf16[2,128,128]{2,1,0:T(8,128)(2,1)S(1)} collective-permute-done((bf16[2,128,128]{2,1,0:T(8,128)(2,1)S(1)}, bf16[2,128,128]{2,1,0:T(8,128)(2,1)S(1)}, u32[]{:S(2)}, u32[]{:S(2)}) %collective-permute-start.11) | collective-permute-done | bytes 65568 | tf_op jit(solution)/shard_map/ppermute | solution.py:249
  36.0 1.9 %collective-permute-done.12.refs_1_ = bf16[2,128,128]{2,1,0:T(8,128)(2,1)S(1)} collective-permute-done((bf16[2,128,128]{2,1,0:T(8,128)(2,1)S(1)}, bf16[2,128,128]{2,1,0:T(8,128)(2,1)S(1)}, u32[]{:S(2)}, u32[]{:S(2)}) %collective-permute-start.12) | collective-permute-done | bytes 65568 | tf_op jit(solution)/shard_map/ppermute | solution.py:249
  37.9 0.3 collective-permute-done.13.refs_2_
  38.3 0.1 collective-permute-start.14
  38.3 0.7 %shard_map.113 = bf16[128,128]{1,0:T(8,128)(2,1)} custom-call(bf16[128]{0:T(256)(128)(2,1)S(1)} %copy-done.7, bf16[2,128,128]{2,1,0:T(8,128)(2,1)S(1)} %collective-permute-done.11.refs_0_, bf16[2,128,128]{2,1,0:T(8,128)(2,1)S(1)} %collective-permute-done.12.refs_1_, bf16[2,128,128]{2,1,0:T(8,128)(2,1)S(1)} %collective-permute-done.13.refs_2_, ...), custom_call_target="tpu_custom_call" | custom-call | flops 1048576 | bytes 1048576 | tf_op jit(solution)/shard_map/pallas_call | solution.py:25
  39.1 0.5 %collective-permute-done.14.other_ref = f32[128,128]{1,0:T(8,128)S(1)} collective-permute-done((f32[128,128]{1,0:T(8,128)S(1)}, f32[128,128]{1,0:T(8,128)S(1)}, u32[]{:S(2)}, u32[]{:S(2)}) %collective-permute-start.14) | collective-permute-done | bytes 65568 | tf_op jit(solution)/shard_map/ppermute | solution.py:249
  39.6 0.7 %shard_map.115 = f32[128,256]{1,0:T(8,128)} custom-call(s32[1]{0:T(128)} %bitcast.1.core_ref, f32[128,128]{1,0:T(8,128)S(1)} %shard_map.114.own_ref, f32[128,128]{1,0:T(8,128)S(1)} %collective-permute-done.14.other_ref), custom_call_target="tpu_custom_call" | custom-call | flops 1048576 | bytes 1048576 | tf_op jit(solution)/shard_map/pallas_call | solution.py:25
  (3 shorter events, 0.1 us)
Async XLA Ops:
  0.6 0.8 %copy-start.5 = (s32[1,1,8]{2,1,0:T(1,128)S(1)}, s32[1,1,8]{2,1,0:T(1,128)}, u32[]{:S(2)}) copy-start(s32[1,1,8]{2,1,0:T(1,128)} %cols_ref.3) | copy-start | bytes 100
  0.6 0.8 %copy-start.4 = (s32[1,1,8]{2,1,0:T(1,128)S(1)}, s32[1,1,8]{2,1,0:T(1,128)}, u32[]{:S(2)}) copy-start(s32[1,1,8]{2,1,0:T(1,128)} %rows_ref.3) | copy-start | bytes 100
  0.7 0.8 %copy-start.3 = (bf16[128,128]{1,0:T(8,128)(2,1)S(1)}, bf16[128,128]{1,0:T(8,128)(2,1)}, u32[]{:S(2)}) copy-start(bf16[128,128]{1,0:T(8,128)(2,1)} %features_ref.1) | copy-start | bytes 98308
  0.7 0.7 %copy-start.6 = (bf16[128]{0:T(256)(128)(2,1)S(1)}, bf16[128]{0:T(256)(128)(2,1)}, u32[]{:S(2)}) copy-start(bf16[128]{0:T(256)(128)(2,1)} %deg_ref.5) | copy-start | bytes 772
  1.3 6.5 %copy-start = (s32[1,1,8,32,256]{4,3,2,1,0:T(8,128)S(1)}, s32[1,1,8,32,256]{4,3,2,1,0:T(8,128)}, u32[]{:S(2)}) copy-start(s32[1,1,8,32,256]{4,3,2,1,0:T(8,128)} %bits_ref.1) | copy-start | bytes 786436
  1.5 7.3 %collective-permute-start.2 = (bf16[128,128]{1,0:T(8,128)(2,1)S(1)}, bf16[128,128]{1,0:T(8,128)(2,1)S(1)}, u32[]{:S(2)}, u32[]{:S(2)}) collective-permute-start(bf16[128,128]{1,0:T(8,128)(2,1)S(1)} %shard_map.104.after_ref.refs_0_), channel_id=1, source_target_pairs={{0,16},{8,24},{16,0},{24,8},{1,17},{9,25},{17,1},{25,9},{2,18},{10... | collective-permute-start | bytes 98312 | tf_op jit(solution)/shard_map/ppermute | solution.py:249
  5.6 5.7 %collective-permute-start.1 = (bf16[128,128]{1,0:T(8,128)(2,1)S(1)}, bf16[128,128]{1,0:T(8,128)(2,1)S(1)}, u32[]{:S(2)}, u32[]{:S(2)}) collective-permute-start(bf16[128,128]{1,0:T(8,128)(2,1)S(1)} %shard_map.104.after_ref.refs_0_), channel_id=1, source_target_pairs={{0,24},{8,16},{16,8},{24,0},{1,25},{9,17},{17,9},{25,1},{2,26},{10... | collective-permute-start | bytes 98312 | tf_op jit(solution)/shard_map/ppermute | solution.py:249
  7.0 4.4 %collective-permute-start = (bf16[128,128]{1,0:T(8,128)(2,1)S(1)}, bf16[128,128]{1,0:T(8,128)(2,1)S(1)}, u32[]{:S(2)}, u32[]{:S(2)}) collective-permute-start(bf16[128,128]{1,0:T(8,128)(2,1)S(1)} %shard_map.104.after_ref.refs_0_), channel_id=1, source_target_pairs={{0,8},{8,0},{16,24},{24,16},{1,9},{9,1},{17,25},{25,17},{2,10},{10... | collective-permute-start | bytes 98312 | tf_op jit(solution)/shard_map/ppermute | solution.py:249
  11.6 1.4 %collective-permute-start.3 = (bf16[4,128,128]{2,1,0:T(8,128)(2,1)S(1)}, bf16[4,128,128]{2,1,0:T(8,128)(2,1)S(1)}, u32[]{:S(2)}, u32[]{:S(2)}) collective-permute-start(bf16[4,128,128]{2,1,0:T(8,128)(2,1)S(1)} %get-tuple-element.20), channel_id=1, source_target_pairs={{0,1},{1,0},{2,3},{3,2},{4,5},{5,4},{6,7},{7,6},{8,9},{9,8},{10,11... | collective-permute-start | bytes 393224 | tf_op jit(solution)/shard_map/ppermute | solution.py:249
  13.1 7.0 %copy-start.1 = (bf16[128,256]{1,0:T(8,128)(2,1)S(1)}, bf16[128,256]{1,0:T(8,128)(2,1)}, u32[]{:S(2)}) copy-start(bf16[128,256]{1,0:T(8,128)(2,1)} %weight_ref.1) | copy-start | bytes 196612
  13.1 7.0 %copy-start.2 = (bf16[128,256]{1,0:T(8,128)(2,1)S(1)}, bf16[128,256]{1,0:T(8,128)(2,1)}, u32[]{:S(2)}) copy-start(bf16[128,256]{1,0:T(8,128)(2,1)} %cotangent_ref.1) | copy-start | bytes 196612
  13.1 4.9 %collective-permute-start.4 = (bf16[128,128]{1,0:T(8,128)(2,1)S(1)}, bf16[128,128]{1,0:T(8,128)(2,1)S(1)}, u32[]{:S(2)}, u32[]{:S(2)}) collective-permute-start(bf16[128,128]{1,0:T(8,128)(2,1)S(1)} %get-tuple-element.22), channel_id=1, source_target_pairs={{0,6},{1,7},{2,4},{3,5},{4,2},{5,3},{6,0},{7,1},{8,14},{9,15},{10,... | collective-permute-start | bytes 98312 | tf_op jit(solution)/shard_map/ppermute | solution.py:249
  15.6 3.9 %collective-permute-start.5 = (bf16[128,128]{1,0:T(8,128)(2,1)S(1)}, bf16[128,128]{1,0:T(8,128)(2,1)S(1)}, u32[]{:S(2)}, u32[]{:S(2)}) collective-permute-start(bf16[128,128]{1,0:T(8,128)(2,1)S(1)} %get-tuple-element.23), channel_id=1, source_target_pairs={{0,4},{1,5},{2,6},{3,7},{4,0},{5,1},{6,2},{7,3},{8,12},{9,13},{10,... | collective-permute-start | bytes 98312 | tf_op jit(solution)/shard_map/ppermute | solution.py:249
  16.1 3.9 %copy-start.7 = (bf16[128]{0:T(256)(128)(2,1)S(1)}, bf16[128]{0:T(256)(128)(2,1)}, u32[]{:S(2)}) copy-start(bf16[128]{0:T(256)(128)(2,1)} %deg_ref.5) | copy-start | bytes 772
  16.1 3.9 %collective-permute-start.6 = (bf16[128,128]{1,0:T(8,128)(2,1)S(1)}, bf16[128,128]{1,0:T(8,128)(2,1)S(1)}, u32[]{:S(2)}, u32[]{:S(2)}) collective-permute-start(bf16[128,128]{1,0:T(8,128)(2,1)S(1)} %get-tuple-element.24), channel_id=1, source_target_pairs={{0,2},{1,3},{2,0},{3,1},{4,6},{5,7},{6,4},{7,5},{8,10},{9,11},{10,... | collective-permute-start | bytes 98312 | tf_op jit(solution)/shard_map/ppermute | solution.py:249
  20.4 6.0 %collective-permute-start.9 = (bf16[3,128,128]{2,1,0:T(8,128)(2,1)S(1)}, bf16[3,128,128]{2,1,0:T(8,128)(2,1)S(1)}, u32[]{:S(2)}, u32[]{:S(2)}) collective-permute-start(bf16[3,128,128]{2,1,0:T(8,128)(2,1)S(1)} %get-tuple-element.27.refs_0_), channel_id=1, source_target_pairs={{0,6},{1,7},{2,4},{3,5},{4,2},{5,3},{6,0},{7,1},{8,14},{9,15},{10,... | collective-permute-start | bytes 294920 | tf_op jit(solution)/shard_map/ppermute | solution.py:249
  22.0 5.4 %collective-permute-start.8 = (bf16[3,128,128]{2,1,0:T(8,128)(2,1)S(1)}, bf16[3,128,128]{2,1,0:T(8,128)(2,1)S(1)}, u32[]{:S(2)}, u32[]{:S(2)}) collective-permute-start(bf16[3,128,128]{2,1,0:T(8,128)(2,1)S(1)} %get-tuple-element.27.refs_0_), channel_id=1, source_target_pairs={{0,4},{1,5},{2,6},{3,7},{4,0},{5,1},{6,2},{7,3},{8,12},{9,13},{10,... | collective-permute-start | bytes 294920 | tf_op jit(solution)/shard_map/ppermute | solution.py:249
  22.5 4.8 %collective-permute-start.7 = (bf16[3,128,128]{2,1,0:T(8,128)(2,1)S(1)}, bf16[3,128,128]{2,1,0:T(8,128)(2,1)S(1)}, u32[]{:S(2)}, u32[]{:S(2)}) collective-permute-start(bf16[3,128,128]{2,1,0:T(8,128)(2,1)S(1)} %get-tuple-element.27.refs_0_), channel_id=1, source_target_pairs={{0,2},{1,3},{2,0},{3,1},{4,6},{5,7},{6,4},{7,5},{8,10},{9,11},{10,... | collective-permute-start | bytes 294920 | tf_op jit(solution)/shard_map/ppermute | solution.py:249
  27.4 1.5 %collective-permute-start.10 = (bf16[5,128,128]{2,1,0:T(8,128)(2,1)S(1)}, bf16[5,128,128]{2,1,0:T(8,128)(2,1)S(1)}, u32[]{:S(2)}, u32[]{:S(2)}) collective-permute-start(bf16[5,128,128]{2,1,0:T(8,128)(2,1)S(1)} %get-tuple-element.29.own_ref), channel_id=1, source_target_pairs={{0,1},{1,0},{2,3},{3,2},{4,5},{5,4},{6,7},{7,6},{8,9},{9,8},{10,11... | collective-permute-start | bytes 491528 | tf_op jit(solution)/shard_map/ppermute | solution.py:249
  29.3 6.8 %collective-permute-start.11 = (bf16[2,128,128]{2,1,0:T(8,128)(2,1)S(1)}, bf16[2,128,128]{2,1,0:T(8,128)(2,1)S(1)}, u32[]{:S(2)}, u32[]{:S(2)}) collective-permute-start(bf16[2,128,128]{2,1,0:T(8,128)(2,1)S(1)} %get-tuple-element.31), channel_id=1, source_target_pairs={{0,24},{8,16},{16,8},{24,0},{1,25},{9,17},{17,9},{25,1},{2,26},{10... | collective-permute-start | bytes 196616 | tf_op jit(solution)/shard_map/ppermute | solution.py:249
  31.4 6.5 %collective-permute-start.12 = (bf16[2,128,128]{2,1,0:T(8,128)(2,1)S(1)}, bf16[2,128,128]{2,1,0:T(8,128)(2,1)S(1)}, u32[]{:S(2)}, u32[]{:S(2)}) collective-permute-start(bf16[2,128,128]{2,1,0:T(8,128)(2,1)S(1)} %get-tuple-element.32), channel_id=1, source_target_pairs={{0,8},{8,0},{16,24},{24,16},{1,9},{9,1},{17,25},{25,17},{2,10},{10... | collective-permute-start | bytes 196616 | tf_op jit(solution)/shard_map/ppermute | solution.py:249
  31.4 6.8 %collective-permute-start.13 = (bf16[2,128,128]{2,1,0:T(8,128)(2,1)S(1)}, bf16[2,128,128]{2,1,0:T(8,128)(2,1)S(1)}, u32[]{:S(2)}, u32[]{:S(2)}) collective-permute-start(bf16[2,128,128]{2,1,0:T(8,128)(2,1)S(1)} %get-tuple-element.33), channel_id=1, source_target_pairs={{0,16},{8,24},{16,0},{24,8},{1,17},{9,25},{17,1},{25,9},{2,18},{10... | collective-permute-start | bytes 196616 | tf_op jit(solution)/shard_map/ppermute | solution.py:249
  38.3 1.3 %collective-permute-start.14 = (f32[128,128]{1,0:T(8,128)S(1)}, f32[128,128]{1,0:T(8,128)S(1)}, u32[]{:S(2)}, u32[]{:S(2)}) collective-permute-start(f32[128,128]{1,0:T(8,128)S(1)} %shard_map.114.own_ref), channel_id=1, source_target_pairs={{0,1},{1,0},{2,3},{3,2},{4,5},{5,4},{6,7},{7,6},{8,9},{9,8},{10,11... | collective-permute-start | bytes 196616 | tf_op jit(solution)/shard_map/ppermute | solution.py:249

commit v9 on v8

--- a/solution.py
+++ b/solution.py
@@ -181,16 +181,27 @@
     joined_ref[chips] = jnp.where(second, grad[0], grad[1]).astype(bf16)
 
 
-def backward_rows(row_ref, chip_ref, core_ref, adjacency_ref, own_ref, grad_ref, received_ref, *refs):
+def chip_blocks(chip, blocks_ref, source):
+    size = source.shape[0]
+    for step in range(source.shape[1] // size):
+        source[:, block_at(chip ^ step, size)] = blocks_ref[step]
+    return source[...]
+
+
+def backward_own(chip_ref, core_ref, adjacency_ref, joined_ref, total_ref, source):
+    blocks = chip_blocks(chip_ref[0], joined_ref, source)
+    rows = rows_of(core_ref[0], adjacency_ref, source.shape[0])
+    total_ref[...] = jnp.dot(blocks, rows, preferred_element_type=f32)
+
+
+def backward_rows(
+    row_ref, chip_ref, core_ref, adjacency_ref, own_ref, grad_ref, received_ref, *refs
+):
     *pieces, source, total = refs
-    chips = own_ref.shape[0] - 1
-    size = own_ref.shape[2]
-    chip, core = chip_ref[0], core_ref[0]
-    for step in range(chips):
-        peer = 2 * (chip ^ step)
-        source[:, block_at(peer + core, size)] = own_ref[step]
-        source[:, block_at(peer + 1 - core, size)] = received_ref[step]
-    total[...] = jnp.dot(source[...], adjacency_ref[...], preferred_element_type=f32)
+    chips, size = received_ref.shape[0] - 1, received_ref.shape[2]
+    blocks = chip_blocks(chip_ref[0], received_ref, source)
+    rows = rows_of(1 - core_ref[0], adjacency_ref, size)
+    total[...] = own_ref[...] + jnp.dot(blocks, rows, preferred_element_type=f32)
     grad = (grad_ref[...] + received_ref[chips].astype(f32)).astype(bf16)
     for step, piece in zip((3, 1, 2, 0), pieces):
         piece[0] = total[:, block_at(row_ref[0] ^ step, size)].astype(bf16)
@@ -354,12 +365,20 @@
         [pltpu.VMEM((chips, 2, width, size), bf16)],
         after=(written,),
     )
+    half_source = pltpu.VMEM((width, chips * size), bf16)
+    own_total = call(
+        backward_own,
+        struct((width, row_shards * size), f32),
+        (chip, core),
+        (adjacency, joined),
+        [half_source],
+    )
     pieces = call(
         backward_rows,
         (struct((2, width, size), bf16),) * row_shards,
         (row, chip, core),
-        (adjacency, joined, own_grad, exchange(joined, "col", col_shards, 1)),
-        backward_scratch,
+        (adjacency, own_total, own_grad, exchange(joined, "col", col_shards, 1)),
+        [half_source, pltpu.VMEM((width, row_shards * size), f32)],
     )
     arrived = [exchange(piece, "row", row_shards, step) for step, piece in zip((3, 1, 2), pieces)]
     arrived.append(pieces[-1])

time: 40.4 us -> 40.3 us (level)
    pallas_call x12 -> x13, Pallas kernels: 3.68 us -> 3.8 us  [call(): pl.pallas_call(body, out_shape=out_shape, in_specs=[SMEM] * len(scalars)...]
  transfers between devices with their start and end apart: 15 -> 15, of which waited for: 12 -> 12; matrix products, arithmetic and copies ran while one was open for 0% -> 0% of each run, Pallas kernels for 6% -> 7%
where the time goes in v9:
time: 40.3 us; the launch traced here: 40.1 us
  starting transfers between devices  17.5 us (43%)
  waiting for transfers between devices  15.8 us (39%)
  Pallas kernels  4.71 us (12%)
  between operations  1.47 us (4%)
  local copies, waits for them, and re-layouts  0.69 us (2%)
    ppermute x15, starting transfers between devices, exchange(): lax.ppermute(block, axis, [(shard, shard ^ distance) for shard in range(s...  17.5 us
    ppermute x15, waiting for transfers between devices, exchange(): lax.ppermute(block, axis, [(shard, shard ^ distance) for shard in range(s...  15.8 us
    pallas_call x13, Pallas kernels, call(): pl.pallas_call(body, out_shape=out_shape, in_specs=[SMEM] * len(scalars)...  3.8 us
    pallas_call x1, Pallas kernels, on_device(): pl.pallas_call(build_adjacency, out_shape=struct((col_shards * size, row_...  0.91 us
  transfers between devices with their start and end apart: 15, of which 12 were waited for; matrix products, arithmetic and copies ran while one was open for 0% of the time, Pallas kernels for 7%

profile of v9, /device:TPU:0, one launch (start us, length us, event | category | flops | bytes accessed | tf_op | source)
XLA Modules:
  0.0 40.1 jit_solution(11833621493315260959)
XLA Ops:
  0.6 0.0 copy-start.5
  0.6 0.0 copy-start.4
  0.7 0.0 copy-start.3
  0.7 0.0 copy-start.6
  0.7 0.7 %copy-done.6 = bf16[128]{0:T(256)(128)(2,1)S(1)} copy-done((bf16[128]{0:T(256)(128)(2,1)S(1)}, bf16[128]{0:T(256)(128)(2,1)}, u32[]{:S(2)}) %copy-start.6) | copy-done | bytes 280
  1.3 0.0 copy-start
  1.3 0.1 shard_map.103.column_ref
  1.5 0.0 copy-done.5
  1.5 0.0 copy-done.4
  1.5 0.0 copy-done.3
  1.5 4.1 %collective-permute-start.2 = (bf16[128,128]{1,0:T(8,128)(2,1)S(1)}, bf16[128,128]{1,0:T(8,128)(2,1)S(1)}, u32[]{:S(2)}, u32[]{:S(2)}) collective-permute-start(bf16[128,128]{1,0:T(8,128)(2,1)S(1)} %shard_map.104.after_ref.refs_0_), channel_id=1, source_target_pairs={{0,16},{8,24},{16,0},{24,8},{1,17},{9,25},{17,1},{25,9},{2,18},{10... | collective-permute-start | bytes 98312 | tf_op jit(solution)/shard_map/ppermute | solution.py:260
  5.6 1.3 %collective-permute-start.1 = (bf16[128,128]{1,0:T(8,128)(2,1)S(1)}, bf16[128,128]{1,0:T(8,128)(2,1)S(1)}, u32[]{:S(2)}, u32[]{:S(2)}) collective-permute-start(bf16[128,128]{1,0:T(8,128)(2,1)S(1)} %shard_map.104.after_ref.refs_0_), channel_id=1, source_target_pairs={{0,24},{8,16},{16,8},{24,0},{1,25},{9,17},{17,9},{25,1},{2,26},{10... | collective-permute-start | bytes 98312 | tf_op jit(solution)/shard_map/ppermute | solution.py:260
  7.0 0.2 collective-permute-start
  7.8 0.0 copy-done
  7.9 0.9 %shard_map.105.adjacency_ref = bf16[1024,512]{1,0:T(8,128)(2,1)S(1)} custom-call(s32[1,1]{1,0:T(1,128)S(6)} %copy.11.count_ref, s32[1,1,8]{2,1,0:T(1,128)S(1)} %copy-done.4, s32[1,1,8]{2,1,0:T(1,128)S(1)} %copy-done.5, s32[1,1,8,32,256]{4,3,2,1,0:T(8,128)S(1)} %copy-done, bf16[128,128]{1,0:T(8,128)(2,1)S(1)} %shard_map.104.after_ref.refs_0_), custom_call_target="tpu_custom_call" | custom-call | flops 1048576 | bytes 1048576 | tf_op jit(solution)/shard_map/pallas_call | solution.py:323
  8.8 0.0 collective-permute-done.2.refs_3_
  8.8 2.5 %collective-permute-done.1.refs_2_ = bf16[128,128]{1,0:T(8,128)(2,1)S(1)} collective-permute-done((bf16[128,128]{1,0:T(8,128)(2,1)S(1)}, bf16[128,128]{1,0:T(8,128)(2,1)S(1)}, u32[]{:S(2)}, u32[]{:S(2)}) %collective-permute-start.1) | collective-permute-done | bytes 32800 | tf_op jit(solution)/shard_map/ppermute | solution.py:260
  11.3 0.0 collective-permute-done.refs_1_
  11.3 0.3 shard_map.106
  11.6 0.1 collective-permute-start.3
  11.7 0.3 shard_map.107.mine_ref
  12.0 1.0 %collective-permute-done.3.received_ref = bf16[4,128,128]{2,1,0:T(8,128)(2,1)S(1)} collective-permute-done((bf16[4,128,128]{2,1,0:T(8,128)(2,1)S(1)}, bf16[4,128,128]{2,1,0:T(8,128)(2,1)S(1)}, u32[]{:S(2)}, u32[]{:S(2)}) %collective-permute-start.3) | collective-permute-done | bytes 131104 | tf_op jit(solution)/shard_map/ppermute | solution.py:260
  13.1 0.0 copy-start.1
  13.1 0.0 copy-start.2
  13.1 2.5 %collective-permute-start.4 = (bf16[128,128]{1,0:T(8,128)(2,1)S(1)}, bf16[128,128]{1,0:T(8,128)(2,1)S(1)}, u32[]{:S(2)}, u32[]{:S(2)}) collective-permute-start(bf16[128,128]{1,0:T(8,128)(2,1)S(1)} %get-tuple-element.22), channel_id=1, source_target_pairs={{0,6},{1,7},{2,4},{3,5},{4,2},{5,3},{6,0},{7,1},{8,14},{9,15},{10,... | collective-permute-start | bytes 98312 | tf_op jit(solution)/shard_map/ppermute | solution.py:260
  15.6 0.5 %collective-permute-start.5 = (bf16[128,128]{1,0:T(8,128)(2,1)S(1)}, bf16[128,128]{1,0:T(8,128)(2,1)S(1)}, u32[]{:S(2)}, u32[]{:S(2)}) collective-permute-start(bf16[128,128]{1,0:T(8,128)(2,1)S(1)} %get-tuple-element.23), channel_id=1, source_target_pairs={{0,4},{1,5},{2,6},{3,7},{4,0},{5,1},{6,2},{7,3},{8,12},{9,13},{10,... | collective-permute-start | bytes 98312 | tf_op jit(solution)/shard_map/ppermute | solution.py:260
  16.1 0.0 copy-start.7
  16.1 0.5 %collective-permute-start.6 = (bf16[128,128]{1,0:T(8,128)(2,1)S(1)}, bf16[128,128]{1,0:T(8,128)(2,1)S(1)}, u32[]{:S(2)}, u32[]{:S(2)}) collective-permute-start(bf16[128,128]{1,0:T(8,128)(2,1)S(1)} %get-tuple-element.24), channel_id=1, source_target_pairs={{0,2},{1,3},{2,0},{3,1},{4,6},{5,7},{6,4},{7,5},{8,10},{9,11},{10,... | collective-permute-start | bytes 98312 | tf_op jit(solution)/shard_map/ppermute | solution.py:260
  16.6 1.3 %collective-permute-done.4.refs_0_ = bf16[128,128]{1,0:T(8,128)(2,1)S(1)} collective-permute-done((bf16[128,128]{1,0:T(8,128)(2,1)S(1)}, bf16[128,128]{1,0:T(8,128)(2,1)S(1)}, u32[]{:S(2)}, u32[]{:S(2)}) %collective-permute-start.4) | collective-permute-done | bytes 32800 | tf_op jit(solution)/shard_map/ppermute | solution.py:260
  18.0 1.5 %collective-permute-done.5.refs_1_ = bf16[128,128]{1,0:T(8,128)(2,1)S(1)} collective-permute-done((bf16[128,128]{1,0:T(8,128)(2,1)S(1)}, bf16[128,128]{1,0:T(8,128)(2,1)S(1)}, u32[]{:S(2)}, u32[]{:S(2)}) %collective-permute-start.5) | collective-permute-done | bytes 32800 | tf_op jit(solution)/shard_map/ppermute | solution.py:260
  19.5 0.5 %collective-permute-done.6.refs_2_ = bf16[128,128]{1,0:T(8,128)(2,1)S(1)} collective-permute-done((bf16[128,128]{1,0:T(8,128)(2,1)S(1)}, bf16[128,128]{1,0:T(8,128)(2,1)S(1)}, u32[]{:S(2)}, u32[]{:S(2)}) %collective-permute-start.6) | collective-permute-done | bytes 32800 | tf_op jit(solution)/shard_map/ppermute | solution.py:260
  20.0 0.0 copy-done.1
  20.0 0.0 copy-done.2
  20.0 0.0 copy-done.7
  20.0 0.4 shard_map.109
  20.4 1.6 %collective-permute-start.9 = (bf16[3,128,128]{2,1,0:T(8,128)(2,1)S(1)}, bf16[3,128,128]{2,1,0:T(8,128)(2,1)S(1)}, u32[]{:S(2)}, u32[]{:S(2)}) collective-permute-start(bf16[3,128,128]{2,1,0:T(8,128)(2,1)S(1)} %get-tuple-element.27.refs_0_), channel_id=1, source_target_pairs={{0,6},{1,7},{2,4},{3,5},{4,2},{5,3},{6,0},{7,1},{8,14},{9,15},{10,... | collective-permute-start | bytes 294920 | tf_op jit(solution)/shard_map/ppermute | solution.py:260
  22.0 0.5 %collective-permute-start.8 = (bf16[3,128,128]{2,1,0:T(8,128)(2,1)S(1)}, bf16[3,128,128]{2,1,0:T(8,128)(2,1)S(1)}, u32[]{:S(2)}, u32[]{:S(2)}) collective-permute-start(bf16[3,128,128]{2,1,0:T(8,128)(2,1)S(1)} %get-tuple-element.27.refs_0_), channel_id=1, source_target_pairs={{0,4},{1,5},{2,6},{3,7},{4,0},{5,1},{6,2},{7,3},{8,12},{9,13},{10,... | collective-permute-start | bytes 294920 | tf_op jit(solution)/shard_map/ppermute | solution.py:260
  22.5 1.5 %collective-permute-start.7 = (bf16[3,128,128]{2,1,0:T(8,128)(2,1)S(1)}, bf16[3,128,128]{2,1,0:T(8,128)(2,1)S(1)}, u32[]{:S(2)}, u32[]{:S(2)}) collective-permute-start(bf16[3,128,128]{2,1,0:T(8,128)(2,1)S(1)} %get-tuple-element.27.refs_0_), channel_id=1, source_target_pairs={{0,2},{1,3},{2,0},{3,1},{4,6},{5,7},{6,4},{7,5},{8,10},{9,11},{10,... | collective-permute-start | bytes 294920 | tf_op jit(solution)/shard_map/ppermute | solution.py:260
  24.0 0.6 %shard_map.110 = (bf16[128,256]{1,0:T(8,128)(2,1)}, f32[8,128]{1,0:T(8,128)S(1)}) custom-call(f32[128,256]{1,0:T(8,128)S(1)} %get-tuple-element.25.active_ref), custom_call_target="tpu_custom_call" | custom-call | flops 1048576 | bytes 1048576 | tf_op jit(solution)/shard_map/pallas_call | solution.py:25
  24.6 1.8 %collective-permute-done.9.refs_3_ = bf16[3,128,128]{2,1,0:T(8,128)(2,1)S(1)} collective-permute-done((bf16[3,128,128]{2,1,0:T(8,128)(2,1)S(1)}, bf16[3,128,128]{2,1,0:T(8,128)(2,1)S(1)}, u32[]{:S(2)}, u32[]{:S(2)}) %collective-permute-start.9) | collective-permute-done | bytes 98336 | tf_op jit(solution)/shard_map/ppermute | solution.py:260
  26.4 0.9 %collective-permute-done.8.refs_2_ = bf16[3,128,128]{2,1,0:T(8,128)(2,1)S(1)} collective-permute-done((bf16[3,128,128]{2,1,0:T(8,128)(2,1)S(1)}, bf16[3,128,128]{2,1,0:T(8,128)(2,1)S(1)}, u32[]{:S(2)}, u32[]{:S(2)}) %collective-permute-start.8) | collective-permute-done | bytes 98336 | tf_op jit(solution)/shard_map/ppermute | solution.py:260
  27.3 0.0 collective-permute-done.7.refs_1_
  27.3 0.1 shard_map.111
  27.4 0.1 collective-permute-start.10
  27.5 0.2 shard_map.112.own_ref
  27.7 1.1 %collective-permute-done.10.received_ref = bf16[5,128,128]{2,1,0:T(8,128)(2,1)S(1)} collective-permute-done((bf16[5,128,128]{2,1,0:T(8,128)(2,1)S(1)}, bf16[5,128,128]{2,1,0:T(8,128)(2,1)S(1)}, u32[]{:S(2)}, u32[]{:S(2)}) %collective-permute-start.10) | collective-permute-done | bytes 163872 | tf_op jit(solution)/shard_map/ppermute | solution.py:260
  28.9 0.3 shard_map.113
  29.2 2.1 %collective-permute-start.11 = (bf16[2,128,128]{2,1,0:T(8,128)(2,1)S(1)}, bf16[2,128,128]{2,1,0:T(8,128)(2,1)S(1)}, u32[]{:S(2)}, u32[]{:S(2)}) collective-permute-start(bf16[2,128,128]{2,1,0:T(8,128)(2,1)S(1)} %get-tuple-element.31), channel_id=1, source_target_pairs={{0,24},{8,16},{16,8},{24,0},{1,25},{9,17},{17,9},{25,1},{2,26},{10... | collective-permute-start | bytes 196616 | tf_op jit(solution)/shard_map/ppermute | solution.py:260
  31.2 0.0 collective-permute-start.12
  31.2 2.4 %collective-permute-start.13 = (bf16[2,128,128]{2,1,0:T(8,128)(2,1)S(1)}, bf16[2,128,128]{2,1,0:T(8,128)(2,1)S(1)}, u32[]{:S(2)}, u32[]{:S(2)}) collective-permute-start(bf16[2,128,128]{2,1,0:T(8,128)(2,1)S(1)} %get-tuple-element.33), channel_id=1, source_target_pairs={{0,16},{8,24},{16,0},{24,8},{1,17},{9,25},{17,1},{25,9},{2,18},{10... | collective-permute-start | bytes 196616 | tf_op jit(solution)/shard_map/ppermute | solution.py:260
  33.6 2.3 %collective-permute-done.11.refs_0_ = bf16[2,128,128]{2,1,0:T(8,128)(2,1)S(1)} collective-permute-done((bf16[2,128,128]{2,1,0:T(8,128)(2,1)S(1)}, bf16[2,128,128]{2,1,0:T(8,128)(2,1)S(1)}, u32[]{:S(2)}, u32[]{:S(2)}) %collective-permute-start.11) | collective-permute-done | bytes 65568 | tf_op jit(solution)/shard_map/ppermute | solution.py:260
  35.9 1.9 %collective-permute-done.12.refs_1_ = bf16[2,128,128]{2,1,0:T(8,128)(2,1)S(1)} collective-permute-done((bf16[2,128,128]{2,1,0:T(8,128)(2,1)S(1)}, bf16[2,128,128]{2,1,0:T(8,128)(2,1)S(1)}, u32[]{:S(2)}, u32[]{:S(2)}) %collective-permute-start.12) | collective-permute-done | bytes 65568 | tf_op jit(solution)/shard_map/ppermute | solution.py:260
  37.8 0.3 collective-permute-done.13.refs_2_
  38.1 0.1 collective-permute-start.14
  38.2 0.7 %shard_map.114 = bf16[128,128]{1,0:T(8,128)(2,1)} custom-call(bf16[128]{0:T(256)(128)(2,1)S(1)} %copy-done.7, bf16[2,128,128]{2,1,0:T(8,128)(2,1)S(1)} %collective-permute-done.11.refs_0_, bf16[2,128,128]{2,1,0:T(8,128)(2,1)S(1)} %collective-permute-done.12.refs_1_, bf16[2,128,128]{2,1,0:T(8,128)(2,1)S(1)} %collective-permute-done.13.refs_2_, ...), custom_call_target="tpu_custom_call" | custom-call | flops 1048576 | bytes 1048576 | tf_op jit(solution)/shard_map/pallas_call | solution.py:25
  38.9 0.5 %collective-permute-done.14.other_ref = f32[128,128]{1,0:T(8,128)S(1)} collective-permute-done((f32[128,128]{1,0:T(8,128)S(1)}, f32[128,128]{1,0:T(8,128)S(1)}, u32[]{:S(2)}, u32[]{:S(2)}) %collective-permute-start.14) | collective-permute-done | bytes 65568 | tf_op jit(solution)/shard_map/ppermute | solution.py:260
  39.5 0.7 %shard_map.116 = f32[128,256]{1,0:T(8,128)} custom-call(s32[1]{0:T(128)} %bitcast.1.core_ref, f32[128,128]{1,0:T(8,128)S(1)} %shard_map.115.own_ref, f32[128,128]{1,0:T(8,128)S(1)} %collective-permute-done.14.other_ref), custom_call_target="tpu_custom_call" | custom-call | flops 1048576 | bytes 1048576 | tf_op jit(solution)/shard_map/pallas_call | solution.py:25
  (3 shorter events, 0.1 us)
Async XLA Ops:
  0.6 0.8 %copy-start.5 = (s32[1,1,8]{2,1,0:T(1,128)S(1)}, s32[1,1,8]{2,1,0:T(1,128)}, u32[]{:S(2)}) copy-start(s32[1,1,8]{2,1,0:T(1,128)} %cols_ref.3) | copy-start | bytes 100
  0.6 0.8 %copy-start.4 = (s32[1,1,8]{2,1,0:T(1,128)S(1)}, s32[1,1,8]{2,1,0:T(1,128)}, u32[]{:S(2)}) copy-start(s32[1,1,8]{2,1,0:T(1,128)} %rows_ref.3) | copy-start | bytes 100
  0.7 0.8 %copy-start.3 = (bf16[128,128]{1,0:T(8,128)(2,1)S(1)}, bf16[128,128]{1,0:T(8,128)(2,1)}, u32[]{:S(2)}) copy-start(bf16[128,128]{1,0:T(8,128)(2,1)} %features_ref.1) | copy-start | bytes 98308
  0.7 0.7 %copy-start.6 = (bf16[128]{0:T(256)(128)(2,1)S(1)}, bf16[128]{0:T(256)(128)(2,1)}, u32[]{:S(2)}) copy-start(bf16[128]{0:T(256)(128)(2,1)} %deg_ref.5) | copy-start | bytes 772
  1.3 6.5 %copy-start = (s32[1,1,8,32,256]{4,3,2,1,0:T(8,128)S(1)}, s32[1,1,8,32,256]{4,3,2,1,0:T(8,128)}, u32[]{:S(2)}) copy-start(s32[1,1,8,32,256]{4,3,2,1,0:T(8,128)} %bits_ref.1) | copy-start | bytes 786436
  1.5 7.3 %collective-permute-start.2 = (bf16[128,128]{1,0:T(8,128)(2,1)S(1)}, bf16[128,128]{1,0:T(8,128)(2,1)S(1)}, u32[]{:S(2)}, u32[]{:S(2)}) collective-permute-start(bf16[128,128]{1,0:T(8,128)(2,1)S(1)} %shard_map.104.after_ref.refs_0_), channel_id=1, source_target_pairs={{0,16},{8,24},{16,0},{24,8},{1,17},{9,25},{17,1},{25,9},{2,18},{10... | collective-permute-start | bytes 98312 | tf_op jit(solution)/shard_map/ppermute | solution.py:260
  5.6 5.7 %collective-permute-start.1 = (bf16[128,128]{1,0:T(8,128)(2,1)S(1)}, bf16[128,128]{1,0:T(8,128)(2,1)S(1)}, u32[]{:S(2)}, u32[]{:S(2)}) collective-permute-start(bf16[128,128]{1,0:T(8,128)(2,1)S(1)} %shard_map.104.after_ref.refs_0_), channel_id=1, source_target_pairs={{0,24},{8,16},{16,8},{24,0},{1,25},{9,17},{17,9},{25,1},{2,26},{10... | collective-permute-start | bytes 98312 | tf_op jit(solution)/shard_map/ppermute | solution.py:260
  7.0 4.4 %collective-permute-start = (bf16[128,128]{1,0:T(8,128)(2,1)S(1)}, bf16[128,128]{1,0:T(8,128)(2,1)S(1)}, u32[]{:S(2)}, u32[]{:S(2)}) collective-permute-start(bf16[128,128]{1,0:T(8,128)(2,1)S(1)} %shard_map.104.after_ref.refs_0_), channel_id=1, source_target_pairs={{0,8},{8,0},{16,24},{24,16},{1,9},{9,1},{17,25},{25,17},{2,10},{10... | collective-permute-start | bytes 98312 | tf_op jit(solution)/shard_map/ppermute | solution.py:260
  11.6 1.4 %collective-permute-start.3 = (bf16[4,128,128]{2,1,0:T(8,128)(2,1)S(1)}, bf16[4,128,128]{2,1,0:T(8,128)(2,1)S(1)}, u32[]{:S(2)}, u32[]{:S(2)}) collective-permute-start(bf16[4,128,128]{2,1,0:T(8,128)(2,1)S(1)} %get-tuple-element.20), channel_id=1, source_target_pairs={{0,1},{1,0},{2,3},{3,2},{4,5},{5,4},{6,7},{7,6},{8,9},{9,8},{10,11... | collective-permute-start | bytes 393224 | tf_op jit(solution)/shard_map/ppermute | solution.py:260
  13.1 7.0 %copy-start.1 = (bf16[128,256]{1,0:T(8,128)(2,1)S(1)}, bf16[128,256]{1,0:T(8,128)(2,1)}, u32[]{:S(2)}) copy-start(bf16[128,256]{1,0:T(8,128)(2,1)} %weight_ref.1) | copy-start | bytes 196612
  13.1 7.0 %copy-start.2 = (bf16[128,256]{1,0:T(8,128)(2,1)S(1)}, bf16[128,256]{1,0:T(8,128)(2,1)}, u32[]{:S(2)}) copy-start(bf16[128,256]{1,0:T(8,128)(2,1)} %cotangent_ref.1) | copy-start | bytes 196612
  13.1 4.9 %collective-permute-start.4 = (bf16[128,128]{1,0:T(8,128)(2,1)S(1)}, bf16[128,128]{1,0:T(8,128)(2,1)S(1)}, u32[]{:S(2)}, u32[]{:S(2)}) collective-permute-start(bf16[128,128]{1,0:T(8,128)(2,1)S(1)} %get-tuple-element.22), channel_id=1, source_target_pairs={{0,6},{1,7},{2,4},{3,5},{4,2},{5,3},{6,0},{7,1},{8,14},{9,15},{10,... | collective-permute-start | bytes 98312 | tf_op jit(solution)/shard_map/ppermute | solution.py:260
  15.6 3.9 %collective-permute-start.5 = (bf16[128,128]{1,0:T(8,128)(2,1)S(1)}, bf16[128,128]{1,0:T(8,128)(2,1)S(1)}, u32[]{:S(2)}, u32[]{:S(2)}) collective-permute-start(bf16[128,128]{1,0:T(8,128)(2,1)S(1)} %get-tuple-element.23), channel_id=1, source_target_pairs={{0,4},{1,5},{2,6},{3,7},{4,0},{5,1},{6,2},{7,3},{8,12},{9,13},{10,... | collective-permute-start | bytes 98312 | tf_op jit(solution)/shard_map/ppermute | solution.py:260
  16.1 3.9 %copy-start.7 = (bf16[128]{0:T(256)(128)(2,1)S(1)}, bf16[128]{0:T(256)(128)(2,1)}, u32[]{:S(2)}) copy-start(bf16[128]{0:T(256)(128)(2,1)} %deg_ref.5) | copy-start | bytes 772
  16.1 3.9 %collective-permute-start.6 = (bf16[128,128]{1,0:T(8,128)(2,1)S(1)}, bf16[128,128]{1,0:T(8,128)(2,1)S(1)}, u32[]{:S(2)}, u32[]{:S(2)}) collective-permute-start(bf16[128,128]{1,0:T(8,128)(2,1)S(1)} %get-tuple-element.24), channel_id=1, source_target_pairs={{0,2},{1,3},{2,0},{3,1},{4,6},{5,7},{6,4},{7,5},{8,10},{9,11},{10,... | collective-permute-start | bytes 98312 | tf_op jit(solution)/shard_map/ppermute | solution.py:260
  20.4 6.0 %collective-permute-start.9 = (bf16[3,128,128]{2,1,0:T(8,128)(2,1)S(1)}, bf16[3,128,128]{2,1,0:T(8,128)(2,1)S(1)}, u32[]{:S(2)}, u32[]{:S(2)}) collective-permute-start(bf16[3,128,128]{2,1,0:T(8,128)(2,1)S(1)} %get-tuple-element.27.refs_0_), channel_id=1, source_target_pairs={{0,6},{1,7},{2,4},{3,5},{4,2},{5,3},{6,0},{7,1},{8,14},{9,15},{10,... | collective-permute-start | bytes 294920 | tf_op jit(solution)/shard_map/ppermute | solution.py:260
  22.0 5.4 %collective-permute-start.8 = (bf16[3,128,128]{2,1,0:T(8,128)(2,1)S(1)}, bf16[3,128,128]{2,1,0:T(8,128)(2,1)S(1)}, u32[]{:S(2)}, u32[]{:S(2)}) collective-permute-start(bf16[3,128,128]{2,1,0:T(8,128)(2,1)S(1)} %get-tuple-element.27.refs_0_), channel_id=1, source_target_pairs={{0,4},{1,5},{2,6},{3,7},{4,0},{5,1},{6,2},{7,3},{8,12},{9,13},{10,... | collective-permute-start | bytes 294920 | tf_op jit(solution)/shard_map/ppermute | solution.py:260
  22.5 4.8 %collective-permute-start.7 = (bf16[3,128,128]{2,1,0:T(8,128)(2,1)S(1)}, bf16[3,128,128]{2,1,0:T(8,128)(2,1)S(1)}, u32[]{:S(2)}, u32[]{:S(2)}) collective-permute-start(bf16[3,128,128]{2,1,0:T(8,128)(2,1)S(1)} %get-tuple-element.27.refs_0_), channel_id=1, source_target_pairs={{0,2},{1,3},{2,0},{3,1},{4,6},{5,7},{6,4},{7,5},{8,10},{9,11},{10,... | collective-permute-start | bytes 294920 | tf_op jit(solution)/shard_map/ppermute | solution.py:260
  27.4 1.5 %collective-permute-start.10 = (bf16[5,128,128]{2,1,0:T(8,128)(2,1)S(1)}, bf16[5,128,128]{2,1,0:T(8,128)(2,1)S(1)}, u32[]{:S(2)}, u32[]{:S(2)}) collective-permute-start(bf16[5,128,128]{2,1,0:T(8,128)(2,1)S(1)} %get-tuple-element.29.joined_ref), channel_id=1, source_target_pairs={{0,1},{1,0},{2,3},{3,2},{4,5},{5,4},{6,7},{7,6},{8,9},{9,8},{10,11... | collective-permute-start | bytes 491528 | tf_op jit(solution)/shard_map/ppermute | solution.py:260
  29.2 6.8 %collective-permute-start.11 = (bf16[2,128,128]{2,1,0:T(8,128)(2,1)S(1)}, bf16[2,128,128]{2,1,0:T(8,128)(2,1)S(1)}, u32[]{:S(2)}, u32[]{:S(2)}) collective-permute-start(bf16[2,128,128]{2,1,0:T(8,128)(2,1)S(1)} %get-tuple-element.31), channel_id=1, source_target_pairs={{0,24},{8,16},{16,8},{24,0},{1,25},{9,17},{17,9},{25,1},{2,26},{10... | collective-permute-start | bytes 196616 | tf_op jit(solution)/shard_map/ppermute | solution.py:260
  31.2 6.5 %collective-permute-start.12 = (bf16[2,128,128]{2,1,0:T(8,128)(2,1)S(1)}, bf16[2,128,128]{2,1,0:T(8,128)(2,1)S(1)}, u32[]{:S(2)}, u32[]{:S(2)}) collective-permute-start(bf16[2,128,128]{2,1,0:T(8,128)(2,1)S(1)} %get-tuple-element.32), channel_id=1, source_target_pairs={{0,8},{8,0},{16,24},{24,16},{1,9},{9,1},{17,25},{25,17},{2,10},{10... | collective-permute-start | bytes 196616 | tf_op jit(solution)/shard_map/ppermute | solution.py:260
  31.2 6.8 %collective-permute-start.13 = (bf16[2,128,128]{2,1,0:T(8,128)(2,1)S(1)}, bf16[2,128,128]{2,1,0:T(8,128)(2,1)S(1)}, u32[]{:S(2)}, u32[]{:S(2)}) collective-permute-start(bf16[2,128,128]{2,1,0:T(8,128)(2,1)S(1)} %get-tuple-element.33), channel_id=1, source_target_pairs={{0,16},{8,24},{16,0},{24,8},{1,17},{9,25},{17,1},{25,9},{2,18},{10... | collective-permute-start | bytes 196616 | tf_op jit(solution)/shard_map/ppermute | solution.py:260
  38.1 1.3 %collective-permute-start.14 = (f32[128,128]{1,0:T(8,128)S(1)}, f32[128,128]{1,0:T(8,128)S(1)}, u32[]{:S(2)}, u32[]{:S(2)}) collective-permute-start(f32[128,128]{1,0:T(8,128)S(1)} %shard_map.115.own_ref), channel_id=1, source_target_pairs={{0,1},{1,0},{2,3},{3,2},{4,5},{5,4},{6,7},{7,6},{8,9},{9,8},{10,11... | collective-permute-start | bytes 196616 | tf_op jit(solution)/shard_map/ppermute | solution.py:260

commit v10 on v9

--- a/solution.py
+++ b/solution.py
@@ -203,15 +203,16 @@
     rows = rows_of(1 - core_ref[0], adjacency_ref, size)
     total[...] = own_ref[...] + jnp.dot(blocks, rows, preferred_element_type=f32)
     grad = (grad_ref[...] + received_ref[chips].astype(f32)).astype(bf16)
-    for step, piece in zip((3, 1, 2, 0), pieces):
-        piece[0] = total[:, block_at(row_ref[0] ^ step, size)].astype(bf16)
+    for step, piece in zip((1, 2, 3, 0), pieces):
+        owner = lax.rem(row_ref[0] + step, len(pieces))
+        piece[0] = total[:, block_at(owner, size)].astype(bf16)
         piece[1] = grad
 
 
 def sum_grad(factor, row_ref, *refs):
     *pieces, out_ref, ordered = refs
-    for step, piece in zip((3, 1, 2, 0), pieces):
-        ordered[row_ref[0] ^ step] = piece[1]
+    for step, piece in zip((3, 2, 1, 0), pieces):
+        ordered[lax.rem(row_ref[0] + step, len(pieces))] = piece[1]
     total = jnp.sum(ordered[...].astype(f32), axis=0) * factor
     out_ref[...] = total.astype(out_ref.dtype)
 
@@ -258,6 +259,10 @@
 
 def exchange(block, axis, shards, distance):
     return lax.ppermute(block, axis, [(shard, shard ^ distance) for shard in range(shards)])
+
+
+def shifted(block, axis, shards, step):
+    return lax.ppermute(block, axis, [(shard, (shard + step) % shards) for shard in range(shards)])
 
 
 def on_device(features, deg_scale, weight, cotangent, tile_rows, tile_cols, tile_count, tile_bits):
@@ -380,7 +385,7 @@
         (adjacency, own_total, own_grad, exchange(joined, "col", col_shards, 1)),
         [half_source, pltpu.VMEM((width, row_shards * size), f32)],
     )
-    arrived = [exchange(piece, "row", row_shards, step) for step, piece in zip((3, 1, 2), pieces)]
+    arrived = [shifted(piece, "row", row_shards, step) for step, piece in zip((1, 2, 3), pieces)]
     arrived.append(pieces[-1])
     half_grad = call(
         functools.partial(sum_grad, factor),

time: 40.3 us -> 40.1 us (level)
    ppermute x0 -> x3, waiting for transfers between devices: none -> 4.49 us  [shifted(): lax.ppermute(block, axis, [(shard, (shard + step) % shards) for shard in...]
    ppermute x15 -> x12, waiting for transfers between devices: 15.8 us -> 11.3 us  [exchange(): lax.ppermute(block, axis, [(shard, shard ^ distance) for shard in range(s...]
    ppermute x15 -> x12, starting transfers between devices: 17.5 us -> 13 us  [exchange(): lax.ppermute(block, axis, [(shard, shard ^ distance) for shard in range(s...]
    ppermute x0 -> x3, starting transfers between devices: none -> 4.21 us  [shifted(): lax.ppermute(block, axis, [(shard, (shard + step) % shards) for shard in...]
  transfers between devices with their start and end apart: 15 -> 15, of which waited for: 12 -> 11; matrix products, arithmetic and copies ran while one was open for 0% -> 0% of each run, Pallas kernels for 7% -> 7%
where the time goes in v10:
time: 40.1 us; the launch traced here: 39.9 us
  starting transfers between devices  17.2 us (43%)
  waiting for transfers between devices  15.8 us (39%)
  Pallas kernels  4.72 us (12%)
  between operations  1.47 us (4%)
  local copies, waits for them, and re-layouts  0.69 us (2%)
    ppermute x12, starting transfers between devices, exchange(): lax.ppermute(block, axis, [(shard, shard ^ distance) for shard in range(s...  13 us
    ppermute x12, waiting for transfers between devices, exchange(): lax.ppermute(block, axis, [(shard, shard ^ distance) for shard in range(s...  11.3 us
    ppermute x3, waiting for transfers between devices, shifted(): lax.ppermute(block, axis, [(shard, (shard + step) % shards) for shard in...  4.49 us
    ppermute x3, starting transfers between devices, shifted(): lax.ppermute(block, axis, [(shard, (shard + step) % shards) for shard in...  4.21 us
    pallas_call x13, Pallas kernels, call(): pl.pallas_call(body, out_shape=out_shape, in_specs=[SMEM] * len(scalars)...  3.81 us
    pallas_call x1, Pallas kernels, on_device(): pl.pallas_call(build_adjacency, out_shape=struct((col_shards * size, row_...  0.91 us
  transfers between devices with their start and end apart: 15, of which 11 were waited for; matrix products, arithmetic and copies ran while one was open for 0% of the time, Pallas kernels for 7%

profile of v10, /device:TPU:0, one launch (start us, length us, event | category | flops | bytes accessed | tf_op | source)
XLA Modules:
  0.0 39.9 jit_solution(17378828620265920509)
XLA Ops:
  0.6 0.0 copy-start.5
  0.6 0.0 copy-start.4
  0.7 0.0 copy-start.3
  0.7 0.0 copy-start.6
  0.7 0.7 %copy-done.6 = bf16[128]{0:T(256)(128)(2,1)S(1)} copy-done((bf16[128]{0:T(256)(128)(2,1)S(1)}, bf16[128]{0:T(256)(128)(2,1)}, u32[]{:S(2)}) %copy-start.6) | copy-done | bytes 280
  1.3 0.0 copy-start
  1.3 0.1 shard_map.103.column_ref
  1.5 0.0 copy-done.5
  1.5 0.0 copy-done.4
  1.5 0.0 copy-done.3
  1.5 4.1 %collective-permute-start.2 = (bf16[128,128]{1,0:T(8,128)(2,1)S(1)}, bf16[128,128]{1,0:T(8,128)(2,1)S(1)}, u32[]{:S(2)}, u32[]{:S(2)}) collective-permute-start(bf16[128,128]{1,0:T(8,128)(2,1)S(1)} %shard_map.104.after_ref.refs_0_), channel_id=1, source_target_pairs={{0,16},{8,24},{16,0},{24,8},{1,17},{9,25},{17,1},{25,9},{2,18},{10... | collective-permute-start | bytes 98312 | tf_op jit(solution)/shard_map/ppermute | solution.py:261
  5.6 1.3 %collective-permute-start.1 = (bf16[128,128]{1,0:T(8,128)(2,1)S(1)}, bf16[128,128]{1,0:T(8,128)(2,1)S(1)}, u32[]{:S(2)}, u32[]{:S(2)}) collective-permute-start(bf16[128,128]{1,0:T(8,128)(2,1)S(1)} %shard_map.104.after_ref.refs_0_), channel_id=1, source_target_pairs={{0,24},{8,16},{16,8},{24,0},{1,25},{9,17},{17,9},{25,1},{2,26},{10... | collective-permute-start | bytes 98312 | tf_op jit(solution)/shard_map/ppermute | solution.py:261
  7.0 0.2 collective-permute-start
  7.8 0.0 copy-done
  7.9 0.9 %shard_map.105.adjacency_ref = bf16[1024,512]{1,0:T(8,128)(2,1)S(1)} custom-call(s32[1,1]{1,0:T(1,128)S(6)} %copy.11.count_ref, s32[1,1,8]{2,1,0:T(1,128)S(1)} %copy-done.4, s32[1,1,8]{2,1,0:T(1,128)S(1)} %copy-done.5, s32[1,1,8,32,256]{4,3,2,1,0:T(8,128)S(1)} %copy-done, bf16[128,128]{1,0:T(8,128)(2,1)S(1)} %shard_map.104.after_ref.refs_0_), custom_call_target="tpu_custom_call" | custom-call | flops 1048576 | bytes 1048576 | tf_op jit(solution)/shard_map/pallas_call | solution.py:328
  8.8 0.0 collective-permute-done.2.refs_3_
  8.8 2.5 %collective-permute-done.1.refs_2_ = bf16[128,128]{1,0:T(8,128)(2,1)S(1)} collective-permute-done((bf16[128,128]{1,0:T(8,128)(2,1)S(1)}, bf16[128,128]{1,0:T(8,128)(2,1)S(1)}, u32[]{:S(2)}, u32[]{:S(2)}) %collective-permute-start.1) | collective-permute-done | bytes 32800 | tf_op jit(solution)/shard_map/ppermute | solution.py:261
  11.3 0.0 collective-permute-done.refs_1_
  11.3 0.3 shard_map.106
  11.6 0.1 collective-permute-start.3
  11.7 0.3 shard_map.107.mine_ref
  12.0 1.0 %collective-permute-done.3.received_ref = bf16[4,128,128]{2,1,0:T(8,128)(2,1)S(1)} collective-permute-done((bf16[4,128,128]{2,1,0:T(8,128)(2,1)S(1)}, bf16[4,128,128]{2,1,0:T(8,128)(2,1)S(1)}, u32[]{:S(2)}, u32[]{:S(2)}) %collective-permute-start.3) | collective-permute-done | bytes 131104 | tf_op jit(solution)/shard_map/ppermute | solution.py:261
  13.1 0.0 copy-start.1
  13.1 0.0 copy-start.2
  13.1 2.5 %collective-permute-start.4 = (bf16[128,128]{1,0:T(8,128)(2,1)S(1)}, bf16[128,128]{1,0:T(8,128)(2,1)S(1)}, u32[]{:S(2)}, u32[]{:S(2)}) collective-permute-start(bf16[128,128]{1,0:T(8,128)(2,1)S(1)} %get-tuple-element.22), channel_id=1, source_target_pairs={{0,6},{1,7},{2,4},{3,5},{4,2},{5,3},{6,0},{7,1},{8,14},{9,15},{10,... | collective-permute-start | bytes 98312 | tf_op jit(solution)/shard_map/ppermute | solution.py:261
  15.6 0.5 %collective-permute-start.5 = (bf16[128,128]{1,0:T(8,128)(2,1)S(1)}, bf16[128,128]{1,0:T(8,128)(2,1)S(1)}, u32[]{:S(2)}, u32[]{:S(2)}) collective-permute-start(bf16[128,128]{1,0:T(8,128)(2,1)S(1)} %get-tuple-element.23), channel_id=1, source_target_pairs={{0,4},{1,5},{2,6},{3,7},{4,0},{5,1},{6,2},{7,3},{8,12},{9,13},{10,... | collective-permute-start | bytes 98312 | tf_op jit(solution)/shard_map/ppermute | solution.py:261
  16.1 0.0 copy-start.7
  16.1 0.5 %collective-permute-start.6 = (bf16[128,128]{1,0:T(8,128)(2,1)S(1)}, bf16[128,128]{1,0:T(8,128)(2,1)S(1)}, u32[]{:S(2)}, u32[]{:S(2)}) collective-permute-start(bf16[128,128]{1,0:T(8,128)(2,1)S(1)} %get-tuple-element.24), channel_id=1, source_target_pairs={{0,2},{1,3},{2,0},{3,1},{4,6},{5,7},{6,4},{7,5},{8,10},{9,11},{10,... | collective-permute-start | bytes 98312 | tf_op jit(solution)/shard_map/ppermute | solution.py:261
  16.6 1.3 %collective-permute-done.4.refs_0_ = bf16[128,128]{1,0:T(8,128)(2,1)S(1)} collective-permute-done((bf16[128,128]{1,0:T(8,128)(2,1)S(1)}, bf16[128,128]{1,0:T(8,128)(2,1)S(1)}, u32[]{:S(2)}, u32[]{:S(2)}) %collective-permute-start.4) | collective-permute-done | bytes 32800 | tf_op jit(solution)/shard_map/ppermute | solution.py:261
  18.0 1.5 %collective-permute-done.5.refs_1_ = bf16[128,128]{1,0:T(8,128)(2,1)S(1)} collective-permute-done((bf16[128,128]{1,0:T(8,128)(2,1)S(1)}, bf16[128,128]{1,0:T(8,128)(2,1)S(1)}, u32[]{:S(2)}, u32[]{:S(2)}) %collective-permute-start.5) | collective-permute-done | bytes 32800 | tf_op jit(solution)/shard_map/ppermute | solution.py:261
  19.5 0.5 %collective-permute-done.6.refs_2_ = bf16[128,128]{1,0:T(8,128)(2,1)S(1)} collective-permute-done((bf16[128,128]{1,0:T(8,128)(2,1)S(1)}, bf16[128,128]{1,0:T(8,128)(2,1)S(1)}, u32[]{:S(2)}, u32[]{:S(2)}) %collective-permute-start.6) | collective-permute-done | bytes 32800 | tf_op jit(solution)/shard_map/ppermute | solution.py:261
  20.0 0.0 copy-done.1
  20.0 0.0 copy-done.2
  20.0 0.0 copy-done.7
  20.0 0.4 shard_map.109
  20.4 1.6 %collective-permute-start.9 = (bf16[3,128,128]{2,1,0:T(8,128)(2,1)S(1)}, bf16[3,128,128]{2,1,0:T(8,128)(2,1)S(1)}, u32[]{:S(2)}, u32[]{:S(2)}) collective-permute-start(bf16[3,128,128]{2,1,0:T(8,128)(2,1)S(1)} %get-tuple-element.27.refs_0_), channel_id=1, source_target_pairs={{0,6},{1,7},{2,4},{3,5},{4,2},{5,3},{6,0},{7,1},{8,14},{9,15},{10,... | collective-permute-start | bytes 294920 | tf_op jit(solution)/shard_map/ppermute | solution.py:261
  22.0 0.5 %collective-permute-start.8 = (bf16[3,128,128]{2,1,0:T(8,128)(2,1)S(1)}, bf16[3,128,128]{2,1,0:T(8,128)(2,1)S(1)}, u32[]{:S(2)}, u32[]{:S(2)}) collective-permute-start(bf16[3,128,128]{2,1,0:T(8,128)(2,1)S(1)} %get-tuple-element.27.refs_0_), channel_id=1, source_target_pairs={{0,4},{1,5},{2,6},{3,7},{4,0},{5,1},{6,2},{7,3},{8,12},{9,13},{10,... | collective-permute-start | bytes 294920 | tf_op jit(solution)/shard_map/ppermute | solution.py:261
  22.5 1.5 %collective-permute-start.7 = (bf16[3,128,128]{2,1,0:T(8,128)(2,1)S(1)}, bf16[3,128,128]{2,1,0:T(8,128)(2,1)S(1)}, u32[]{:S(2)}, u32[]{:S(2)}) collective-permute-start(bf16[3,128,128]{2,1,0:T(8,128)(2,1)S(1)} %get-tuple-element.27.refs_0_), channel_id=1, source_target_pairs={{0,2},{1,3},{2,0},{3,1},{4,6},{5,7},{6,4},{7,5},{8,10},{9,11},{10,... | collective-permute-start | bytes 294920 | tf_op jit(solution)/shard_map/ppermute | solution.py:261
  24.0 0.6 %shard_map.110 = (bf16[128,256]{1,0:T(8,128)(2,1)}, f32[8,128]{1,0:T(8,128)S(1)}) custom-call(f32[128,256]{1,0:T(8,128)S(1)} %get-tuple-element.25.active_ref), custom_call_target="tpu_custom_call" | custom-call | flops 1048576 | bytes 1048576 | tf_op jit(solution)/shard_map/pallas_call | solution.py:25
  24.6 1.8 %collective-permute-done.9.refs_3_ = bf16[3,128,128]{2,1,0:T(8,128)(2,1)S(1)} collective-permute-done((bf16[3,128,128]{2,1,0:T(8,128)(2,1)S(1)}, bf16[3,128,128]{2,1,0:T(8,128)(2,1)S(1)}, u32[]{:S(2)}, u32[]{:S(2)}) %collective-permute-start.9) | collective-permute-done | bytes 98336 | tf_op jit(solution)/shard_map/ppermute | solution.py:261
  26.4 0.9 %collective-permute-done.8.refs_2_ = bf16[3,128,128]{2,1,0:T(8,128)(2,1)S(1)} collective-permute-done((bf16[3,128,128]{2,1,0:T(8,128)(2,1)S(1)}, bf16[3,128,128]{2,1,0:T(8,128)(2,1)S(1)}, u32[]{:S(2)}, u32[]{:S(2)}) %collective-permute-start.8) | collective-permute-done | bytes 98336 | tf_op jit(solution)/shard_map/ppermute | solution.py:261
  27.3 0.0 collective-permute-done.7.refs_1_
  27.3 0.1 shard_map.111
  27.4 0.1 collective-permute-start.10
  27.5 0.2 shard_map.112.own_ref
  27.7 1.1 %collective-permute-done.10.received_ref = bf16[5,128,128]{2,1,0:T(8,128)(2,1)S(1)} collective-permute-done((bf16[5,128,128]{2,1,0:T(8,128)(2,1)S(1)}, bf16[5,128,128]{2,1,0:T(8,128)(2,1)S(1)}, u32[]{:S(2)}, u32[]{:S(2)}) %collective-permute-start.10) | collective-permute-done | bytes 163872 | tf_op jit(solution)/shard_map/ppermute | solution.py:261
  28.9 0.3 shard_map.113
  29.2 0.1 collective-permute-start.11
  29.2 2.6 %collective-permute-start.12 = (bf16[2,128,128]{2,1,0:T(8,128)(2,1)S(1)}, bf16[2,128,128]{2,1,0:T(8,128)(2,1)S(1)}, u32[]{:S(2)}, u32[]{:S(2)}) collective-permute-start(bf16[2,128,128]{2,1,0:T(8,128)(2,1)S(1)} %get-tuple-element.32), channel_id=1, source_target_pairs={{0,16},{8,24},{16,0},{24,8},{1,17},{9,25},{17,1},{25,9},{2,18},{10... | collective-permute-start | bytes 196616 | tf_op jit(solution)/shard_map/ppermute | solution.py:265
  31.8 1.6 %collective-permute-start.13 = (bf16[2,128,128]{2,1,0:T(8,128)(2,1)S(1)}, bf16[2,128,128]{2,1,0:T(8,128)(2,1)S(1)}, u32[]{:S(2)}, u32[]{:S(2)}) collective-permute-start(bf16[2,128,128]{2,1,0:T(8,128)(2,1)S(1)} %get-tuple-element.33), channel_id=1, source_target_pairs={{0,24},{8,0},{16,8},{24,16},{1,25},{9,1},{17,9},{25,17},{2,26},{10... | collective-permute-start | bytes 196616 | tf_op jit(solution)/shard_map/ppermute | solution.py:265
  33.4 2.6 %collective-permute-done.11.refs_0_ = bf16[2,128,128]{2,1,0:T(8,128)(2,1)S(1)} collective-permute-done((bf16[2,128,128]{2,1,0:T(8,128)(2,1)S(1)}, bf16[2,128,128]{2,1,0:T(8,128)(2,1)S(1)}, u32[]{:S(2)}, u32[]{:S(2)}) %collective-permute-start.11) | collective-permute-done | bytes 65568 | tf_op jit(solution)/shard_map/ppermute | solution.py:265
  36.0 1.9 %collective-permute-done.12.refs_1_ = bf16[2,128,128]{2,1,0:T(8,128)(2,1)S(1)} collective-permute-done((bf16[2,128,128]{2,1,0:T(8,128)(2,1)S(1)}, bf16[2,128,128]{2,1,0:T(8,128)(2,1)S(1)}, u32[]{:S(2)}, u32[]{:S(2)}) %collective-permute-start.12) | collective-permute-done | bytes 65568 | tf_op jit(solution)/shard_map/ppermute | solution.py:265
  37.9 0.0 collective-permute-done.13.refs_2_
  37.9 0.1 collective-permute-start.14
  38.0 0.7 %shard_map.114 = bf16[128,128]{1,0:T(8,128)(2,1)} custom-call(bf16[128]{0:T(256)(128)(2,1)S(1)} %copy-done.7, bf16[2,128,128]{2,1,0:T(8,128)(2,1)S(1)} %collective-permute-done.11.refs_0_, bf16[2,128,128]{2,1,0:T(8,128)(2,1)S(1)} %collective-permute-done.12.refs_1_, bf16[2,128,128]{2,1,0:T(8,128)(2,1)S(1)} %collective-permute-done.13.refs_2_, ...), custom_call_target="tpu_custom_call" | custom-call | flops 1048576 | bytes 1048576 | tf_op jit(solution)/shard_map/pallas_call | solution.py:25
  38.7 0.5 %collective-permute-done.14.other_ref = f32[128,128]{1,0:T(8,128)S(1)} collective-permute-done((f32[128,128]{1,0:T(8,128)S(1)}, f32[128,128]{1,0:T(8,128)S(1)}, u32[]{:S(2)}, u32[]{:S(2)}) %collective-permute-start.14) | collective-permute-done | bytes 65568 | tf_op jit(solution)/shard_map/ppermute | solution.py:261
  39.2 0.7 %shard_map.116 = f32[128,256]{1,0:T(8,128)} custom-call(s32[1]{0:T(128)} %bitcast.1.core_ref, f32[128,128]{1,0:T(8,128)S(1)} %shard_map.115.own_ref, f32[128,128]{1,0:T(8,128)S(1)} %collective-permute-done.14.other_ref), custom_call_target="tpu_custom_call" | custom-call | flops 1048576 | bytes 1048576 | tf_op jit(solution)/shard_map/pallas_call | solution.py:25
  (3 shorter events, 0.1 us)
Async XLA Ops:
  0.6 0.8 %copy-start.5 = (s32[1,1,8]{2,1,0:T(1,128)S(1)}, s32[1,1,8]{2,1,0:T(1,128)}, u32[]{:S(2)}) copy-start(s32[1,1,8]{2,1,0:T(1,128)} %cols_ref.3) | copy-start | bytes 100
  0.6 0.8 %copy-start.4 = (s32[1,1,8]{2,1,0:T(1,128)S(1)}, s32[1,1,8]{2,1,0:T(1,128)}, u32[]{:S(2)}) copy-start(s32[1,1,8]{2,1,0:T(1,128)} %rows_ref.3) | copy-start | bytes 100
  0.7 0.8 %copy-start.3 = (bf16[128,128]{1,0:T(8,128)(2,1)S(1)}, bf16[128,128]{1,0:T(8,128)(2,1)}, u32[]{:S(2)}) copy-start(bf16[128,128]{1,0:T(8,128)(2,1)} %features_ref.1) | copy-start | bytes 98308
  0.7 0.7 %copy-start.6 = (bf16[128]{0:T(256)(128)(2,1)S(1)}, bf16[128]{0:T(256)(128)(2,1)}, u32[]{:S(2)}) copy-start(bf16[128]{0:T(256)(128)(2,1)} %deg_ref.5) | copy-start | bytes 772
  1.3 6.5 %copy-start = (s32[1,1,8,32,256]{4,3,2,1,0:T(8,128)S(1)}, s32[1,1,8,32,256]{4,3,2,1,0:T(8,128)}, u32[]{:S(2)}) copy-start(s32[1,1,8,32,256]{4,3,2,1,0:T(8,128)} %bits_ref.1) | copy-start | bytes 786436
  1.5 7.3 %collective-permute-start.2 = (bf16[128,128]{1,0:T(8,128)(2,1)S(1)}, bf16[128,128]{1,0:T(8,128)(2,1)S(1)}, u32[]{:S(2)}, u32[]{:S(2)}) collective-permute-start(bf16[128,128]{1,0:T(8,128)(2,1)S(1)} %shard_map.104.after_ref.refs_0_), channel_id=1, source_target_pairs={{0,16},{8,24},{16,0},{24,8},{1,17},{9,25},{17,1},{25,9},{2,18},{10... | collective-permute-start | bytes 98312 | tf_op jit(solution)/shard_map/ppermute | solution.py:261
  5.6 5.7 %collective-permute-start.1 = (bf16[128,128]{1,0:T(8,128)(2,1)S(1)}, bf16[128,128]{1,0:T(8,128)(2,1)S(1)}, u32[]{:S(2)}, u32[]{:S(2)}) collective-permute-start(bf16[128,128]{1,0:T(8,128)(2,1)S(1)} %shard_map.104.after_ref.refs_0_), channel_id=1, source_target_pairs={{0,24},{8,16},{16,8},{24,0},{1,25},{9,17},{17,9},{25,1},{2,26},{10... | collective-permute-start | bytes 98312 | tf_op jit(solution)/shard_map/ppermute | solution.py:261
  7.0 4.4 %collective-permute-start = (bf16[128,128]{1,0:T(8,128)(2,1)S(1)}, bf16[128,128]{1,0:T(8,128)(2,1)S(1)}, u32[]{:S(2)}, u32[]{:S(2)}) collective-permute-start(bf16[128,128]{1,0:T(8,128)(2,1)S(1)} %shard_map.104.after_ref.refs_0_), channel_id=1, source_target_pairs={{0,8},{8,0},{16,24},{24,16},{1,9},{9,1},{17,25},{25,17},{2,10},{10... | collective-permute-start | bytes 98312 | tf_op jit(solution)/shard_map/ppermute | solution.py:261
  11.6 1.4 %collective-permute-start.3 = (bf16[4,128,128]{2,1,0:T(8,128)(2,1)S(1)}, bf16[4,128,128]{2,1,0:T(8,128)(2,1)S(1)}, u32[]{:S(2)}, u32[]{:S(2)}) collective-permute-start(bf16[4,128,128]{2,1,0:T(8,128)(2,1)S(1)} %get-tuple-element.20), channel_id=1, source_target_pairs={{0,1},{1,0},{2,3},{3,2},{4,5},{5,4},{6,7},{7,6},{8,9},{9,8},{10,11... | collective-permute-start | bytes 393224 | tf_op jit(solution)/shard_map/ppermute | solution.py:261
  13.1 7.0 %copy-start.1 = (bf16[128,256]{1,0:T(8,128)(2,1)S(1)}, bf16[128,256]{1,0:T(8,128)(2,1)}, u32[]{:S(2)}) copy-start(bf16[128,256]{1,0:T(8,128)(2,1)} %weight_ref.1) | copy-start | bytes 196612
  13.1 7.0 %copy-start.2 = (bf16[128,256]{1,0:T(8,128)(2,1)S(1)}, bf16[128,256]{1,0:T(8,128)(2,1)}, u32[]{:S(2)}) copy-start(bf16[128,256]{1,0:T(8,128)(2,1)} %cotangent_ref.1) | copy-start | bytes 196612
  13.1 4.9 %collective-permute-start.4 = (bf16[128,128]{1,0:T(8,128)(2,1)S(1)}, bf16[128,128]{1,0:T(8,128)(2,1)S(1)}, u32[]{:S(2)}, u32[]{:S(2)}) collective-permute-start(bf16[128,128]{1,0:T(8,128)(2,1)S(1)} %get-tuple-element.22), channel_id=1, source_target_pairs={{0,6},{1,7},{2,4},{3,5},{4,2},{5,3},{6,0},{7,1},{8,14},{9,15},{10,... | collective-permute-start | bytes 98312 | tf_op jit(solution)/shard_map/ppermute | solution.py:261
  15.6 3.9 %collective-permute-start.5 = (bf16[128,128]{1,0:T(8,128)(2,1)S(1)}, bf16[128,128]{1,0:T(8,128)(2,1)S(1)}, u32[]{:S(2)}, u32[]{:S(2)}) collective-permute-start(bf16[128,128]{1,0:T(8,128)(2,1)S(1)} %get-tuple-element.23), channel_id=1, source_target_pairs={{0,4},{1,5},{2,6},{3,7},{4,0},{5,1},{6,2},{7,3},{8,12},{9,13},{10,... | collective-permute-start | bytes 98312 | tf_op jit(solution)/shard_map/ppermute | solution.py:261
  16.1 3.9 %copy-start.7 = (bf16[128]{0:T(256)(128)(2,1)S(1)}, bf16[128]{0:T(256)(128)(2,1)}, u32[]{:S(2)}) copy-start(bf16[128]{0:T(256)(128)(2,1)} %deg_ref.5) | copy-start | bytes 772
  16.1 3.9 %collective-permute-start.6 = (bf16[128,128]{1,0:T(8,128)(2,1)S(1)}, bf16[128,128]{1,0:T(8,128)(2,1)S(1)}, u32[]{:S(2)}, u32[]{:S(2)}) collective-permute-start(bf16[128,128]{1,0:T(8,128)(2,1)S(1)} %get-tuple-element.24), channel_id=1, source_target_pairs={{0,2},{1,3},{2,0},{3,1},{4,6},{5,7},{6,4},{7,5},{8,10},{9,11},{10,... | collective-permute-start | bytes 98312 | tf_op jit(solution)/shard_map/ppermute | solution.py:261
  20.4 6.0 %collective-permute-start.9 = (bf16[3,128,128]{2,1,0:T(8,128)(2,1)S(1)}, bf16[3,128,128]{2,1,0:T(8,128)(2,1)S(1)}, u32[]{:S(2)}, u32[]{:S(2)}) collective-permute-start(bf16[3,128,128]{2,1,0:T(8,128)(2,1)S(1)} %get-tuple-element.27.refs_0_), channel_id=1, source_target_pairs={{0,6},{1,7},{2,4},{3,5},{4,2},{5,3},{6,0},{7,1},{8,14},{9,15},{10,... | collective-permute-start | bytes 294920 | tf_op jit(solution)/shard_map/ppermute | solution.py:261
  22.0 5.4 %collective-permute-start.8 = (bf16[3,128,128]{2,1,0:T(8,128)(2,1)S(1)}, bf16[3,128,128]{2,1,0:T(8,128)(2,1)S(1)}, u32[]{:S(2)}, u32[]{:S(2)}) collective-permute-start(bf16[3,128,128]{2,1,0:T(8,128)(2,1)S(1)} %get-tuple-element.27.refs_0_), channel_id=1, source_target_pairs={{0,4},{1,5},{2,6},{3,7},{4,0},{5,1},{6,2},{7,3},{8,12},{9,13},{10,... | collective-permute-start | bytes 294920 | tf_op jit(solution)/shard_map/ppermute | solution.py:261
  22.5 4.8 %collective-permute-start.7 = (bf16[3,128,128]{2,1,0:T(8,128)(2,1)S(1)}, bf16[3,128,128]{2,1,0:T(8,128)(2,1)S(1)}, u32[]{:S(2)}, u32[]{:S(2)}) collective-permute-start(bf16[3,128,128]{2,1,0:T(8,128)(2,1)S(1)} %get-tuple-element.27.refs_0_), channel_id=1, source_target_pairs={{0,2},{1,3},{2,0},{3,1},{4,6},{5,7},{6,4},{7,5},{8,10},{9,11},{10,... | collective-permute-start | bytes 294920 | tf_op jit(solution)/shard_map/ppermute | solution.py:261
  27.4 1.5 %collective-permute-start.10 = (bf16[5,128,128]{2,1,0:T(8,128)(2,1)S(1)}, bf16[5,128,128]{2,1,0:T(8,128)(2,1)S(1)}, u32[]{:S(2)}, u32[]{:S(2)}) collective-permute-start(bf16[5,128,128]{2,1,0:T(8,128)(2,1)S(1)} %get-tuple-element.29.joined_ref), channel_id=1, source_target_pairs={{0,1},{1,0},{2,3},{3,2},{4,5},{5,4},{6,7},{7,6},{8,9},{9,8},{10,11... | collective-permute-start | bytes 491528 | tf_op jit(solution)/shard_map/ppermute | solution.py:261
  29.2 6.8 %collective-permute-start.11 = (bf16[2,128,128]{2,1,0:T(8,128)(2,1)S(1)}, bf16[2,128,128]{2,1,0:T(8,128)(2,1)S(1)}, u32[]{:S(2)}, u32[]{:S(2)}) collective-permute-start(bf16[2,128,128]{2,1,0:T(8,128)(2,1)S(1)} %get-tuple-element.31), channel_id=1, source_target_pairs={{0,8},{8,16},{16,24},{24,0},{1,9},{9,17},{17,25},{25,1},{2,10},{10... | collective-permute-start | bytes 196616 | tf_op jit(solution)/shard_map/ppermute | solution.py:265
  29.2 8.6 %collective-permute-start.12 = (bf16[2,128,128]{2,1,0:T(8,128)(2,1)S(1)}, bf16[2,128,128]{2,1,0:T(8,128)(2,1)S(1)}, u32[]{:S(2)}, u32[]{:S(2)}) collective-permute-start(bf16[2,128,128]{2,1,0:T(8,128)(2,1)S(1)} %get-tuple-element.32), channel_id=1, source_target_pairs={{0,16},{8,24},{16,0},{24,8},{1,17},{9,25},{17,1},{25,9},{2,18},{10... | collective-permute-start | bytes 196616 | tf_op jit(solution)/shard_map/ppermute | solution.py:265
  31.8 6.1 %collective-permute-start.13 = (bf16[2,128,128]{2,1,0:T(8,128)(2,1)S(1)}, bf16[2,128,128]{2,1,0:T(8,128)(2,1)S(1)}, u32[]{:S(2)}, u32[]{:S(2)}) collective-permute-start(bf16[2,128,128]{2,1,0:T(8,128)(2,1)S(1)} %get-tuple-element.33), channel_id=1, source_target_pairs={{0,24},{8,0},{16,8},{24,16},{1,25},{9,1},{17,9},{25,17},{2,26},{10... | collective-permute-start | bytes 196616 | tf_op jit(solution)/shard_map/ppermute | solution.py:265
  37.9 1.3 %collective-permute-start.14 = (f32[128,128]{1,0:T(8,128)S(1)}, f32[128,128]{1,0:T(8,128)S(1)}, u32[]{:S(2)}, u32[]{:S(2)}) collective-permute-start(f32[128,128]{1,0:T(8,128)S(1)} %shard_map.115.own_ref), channel_id=1, source_target_pairs={{0,1},{1,0},{2,3},{3,2},{4,5},{5,4},{6,7},{7,6},{8,9},{9,8},{10,11... | collective-permute-start | bytes 196616 | tf_op jit(solution)/shard_map/ppermute | solution.py:261

commit v11 on v10

--- a/solution.py
+++ b/solution.py
@@ -203,7 +203,7 @@
     rows = rows_of(1 - core_ref[0], adjacency_ref, size)
     total[...] = own_ref[...] + jnp.dot(blocks, rows, preferred_element_type=f32)
     grad = (grad_ref[...] + received_ref[chips].astype(f32)).astype(bf16)
-    for step, piece in zip((1, 2, 3, 0), pieces):
+    for step, piece in zip((2, 1, 3, 0), pieces):
         owner = lax.rem(row_ref[0] + step, len(pieces))
         piece[0] = total[:, block_at(owner, size)].astype(bf16)
         piece[1] = grad
@@ -211,7 +211,7 @@
 
 def sum_grad(factor, row_ref, *refs):
     *pieces, out_ref, ordered = refs
-    for step, piece in zip((3, 2, 1, 0), pieces):
+    for step, piece in zip((2, 3, 1, 0), pieces):
         ordered[lax.rem(row_ref[0] + step, len(pieces))] = piece[1]
     total = jnp.sum(ordered[...].astype(f32), axis=0) * factor
     out_ref[...] = total.astype(out_ref.dtype)
@@ -385,7 +385,7 @@
         (adjacency, own_total, own_grad, exchange(joined, "col", col_shards, 1)),
         [half_source, pltpu.VMEM((width, row_shards * size), f32)],
     )
-    arrived = [shifted(piece, "row", row_shards, step) for step, piece in zip((1, 2, 3), pieces)]
+    arrived = [shifted(piece, "row", row_shards, step) for step, piece in zip((2, 1, 3), pieces)]
     arrived.append(pieces[-1])
     half_grad = call(
         functools.partial(sum_grad, factor),

time: 40.1 us -> 40.1 us (level)
  starting transfers between devices: 17.2 us -> 18.1 us
  waiting for transfers between devices: 15.8 us -> 14.9 us
    ppermute x3, starting transfers between devices: 4.21 us -> 5.12 us  [shifted(): lax.ppermute(block, axis, [(shard, (shard + step) % shards) for shard in...]
    ppermute x3, waiting for transfers between devices: 4.49 us -> 3.58 us  [shifted(): lax.ppermute(block, axis, [(shard, (shard + step) % shards) for shard in...]
  transfers between devices with their start and end apart: 15 -> 15, of which waited for: 11 -> 12; matrix products, arithmetic and copies ran while one was open for 0% -> 0% of each run, Pallas kernels for 7% -> 7%
where the time goes in v11:
time: 40.1 us; the launch traced here: 39.9 us
  starting transfers between devices  18.1 us (45%)
  waiting for transfers between devices  14.9 us (37%)
  Pallas kernels  4.72 us (12%)
  between operations  1.46 us (4%)
  local copies, waits for them, and re-layouts  0.69 us (2%)
    ppermute x12, starting transfers between devices, exchange(): lax.ppermute(block, axis, [(shard, shard ^ distance) for shard in range(s...  13 us
    ppermute x12, waiting for transfers between devices, exchange(): lax.ppermute(block, axis, [(shard, shard ^ distance) for shard in range(s...  11.3 us
    ppermute x3, starting transfers between devices, shifted(): lax.ppermute(block, axis, [(shard, (shard + step) % shards) for shard in...  5.12 us
    pallas_call x13, Pallas kernels, call(): pl.pallas_call(body, out_shape=out_shape, in_specs=[SMEM] * len(scalars)...  3.81 us
    ppermute x3, waiting for transfers between devices, shifted(): lax.ppermute(block, axis, [(shard, (shard + step) % shards) for shard in...  3.58 us
    pallas_call x1, Pallas kernels, on_device(): pl.pallas_call(build_adjacency, out_shape=struct((col_shards * size, row_...  0.91 us
  transfers between devices with their start and end apart: 15, of which 12 were waited for; matrix products, arithmetic and copies ran while one was open for 0% of the time, Pallas kernels for 7%

profile of v11, /device:TPU:0, one launch (start us, length us, event | category | flops | bytes accessed | tf_op | source)
XLA Modules:
  0.0 39.9 jit_solution(10720708718027229814)
XLA Ops:
  0.6 0.0 copy-start.5
  0.6 0.0 copy-start.4
  0.7 0.0 copy-start.3
  0.7 0.0 copy-start.6
  0.7 0.7 %copy-done.6 = bf16[128]{0:T(256)(128)(2,1)S(1)} copy-done((bf16[128]{0:T(256)(128)(2,1)S(1)}, bf16[128]{0:T(256)(128)(2,1)}, u32[]{:S(2)}) %copy-start.6) | copy-done | bytes 280
  1.3 0.0 copy-start
  1.3 0.1 shard_map.103.column_ref
  1.5 0.0 copy-done.5
  1.5 0.0 copy-done.4
  1.5 0.0 copy-done.3
  1.5 4.1 %collective-permute-start.2 = (bf16[128,128]{1,0:T(8,128)(2,1)S(1)}, bf16[128,128]{1,0:T(8,128)(2,1)S(1)}, u32[]{:S(2)}, u32[]{:S(2)}) collective-permute-start(bf16[128,128]{1,0:T(8,128)(2,1)S(1)} %shard_map.104.after_ref.refs_0_), channel_id=1, source_target_pairs={{0,16},{8,24},{16,0},{24,8},{1,17},{9,25},{17,1},{25,9},{2,18},{10... | collective-permute-start | bytes 98312 | tf_op jit(solution)/shard_map/ppermute | solution.py:261
  5.6 1.3 %collective-permute-start.1 = (bf16[128,128]{1,0:T(8,128)(2,1)S(1)}, bf16[128,128]{1,0:T(8,128)(2,1)S(1)}, u32[]{:S(2)}, u32[]{:S(2)}) collective-permute-start(bf16[128,128]{1,0:T(8,128)(2,1)S(1)} %shard_map.104.after_ref.refs_0_), channel_id=1, source_target_pairs={{0,24},{8,16},{16,8},{24,0},{1,25},{9,17},{17,9},{25,1},{2,26},{10... | collective-permute-start | bytes 98312 | tf_op jit(solution)/shard_map/ppermute | solution.py:261
  7.0 0.2 collective-permute-start
  7.8 0.0 copy-done
  7.9 0.9 %shard_map.105.adjacency_ref = bf16[1024,512]{1,0:T(8,128)(2,1)S(1)} custom-call(s32[1,1]{1,0:T(1,128)S(6)} %copy.11.count_ref, s32[1,1,8]{2,1,0:T(1,128)S(1)} %copy-done.4, s32[1,1,8]{2,1,0:T(1,128)S(1)} %copy-done.5, s32[1,1,8,32,256]{4,3,2,1,0:T(8,128)S(1)} %copy-done, bf16[128,128]{1,0:T(8,128)(2,1)S(1)} %shard_map.104.after_ref.refs_0_), custom_call_target="tpu_custom_call" | custom-call | flops 1048576 | bytes 1048576 | tf_op jit(solution)/shard_map/pallas_call | solution.py:328
  8.8 0.0 collective-permute-done.2.refs_3_
  8.8 2.5 %collective-permute-done.1.refs_2_ = bf16[128,128]{1,0:T(8,128)(2,1)S(1)} collective-permute-done((bf16[128,128]{1,0:T(8,128)(2,1)S(1)}, bf16[128,128]{1,0:T(8,128)(2,1)S(1)}, u32[]{:S(2)}, u32[]{:S(2)}) %collective-permute-start.1) | collective-permute-done | bytes 32800 | tf_op jit(solution)/shard_map/ppermute | solution.py:261
  11.3 0.0 collective-permute-done.refs_1_
  11.3 0.3 shard_map.106
  11.6 0.1 collective-permute-start.3
  11.7 0.3 shard_map.107.mine_ref
  12.0 1.0 %collective-permute-done.3.received_ref = bf16[4,128,128]{2,1,0:T(8,128)(2,1)S(1)} collective-permute-done((bf16[4,128,128]{2,1,0:T(8,128)(2,1)S(1)}, bf16[4,128,128]{2,1,0:T(8,128)(2,1)S(1)}, u32[]{:S(2)}, u32[]{:S(2)}) %collective-permute-start.3) | collective-permute-done | bytes 131104 | tf_op jit(solution)/shard_map/ppermute | solution.py:261
  13.1 0.0 copy-start.1
  13.1 0.0 copy-start.2
  13.1 2.5 %collective-permute-start.4 = (bf16[128,128]{1,0:T(8,128)(2,1)S(1)}, bf16[128,128]{1,0:T(8,128)(2,1)S(1)}, u32[]{:S(2)}, u32[]{:S(2)}) collective-permute-start(bf16[128,128]{1,0:T(8,128)(2,1)S(1)} %get-tuple-element.22), channel_id=1, source_target_pairs={{0,6},{1,7},{2,4},{3,5},{4,2},{5,3},{6,0},{7,1},{8,14},{9,15},{10,... | collective-permute-start | bytes 98312 | tf_op jit(solution)/shard_map/ppermute | solution.py:261
  15.6 0.5 %collective-permute-start.5 = (bf16[128,128]{1,0:T(8,128)(2,1)S(1)}, bf16[128,128]{1,0:T(8,128)(2,1)S(1)}, u32[]{:S(2)}, u32[]{:S(2)}) collective-permute-start(bf16[128,128]{1,0:T(8,128)(2,1)S(1)} %get-tuple-element.23), channel_id=1, source_target_pairs={{0,4},{1,5},{2,6},{3,7},{4,0},{5,1},{6,2},{7,3},{8,12},{9,13},{10,... | collective-permute-start | bytes 98312 | tf_op jit(solution)/shard_map/ppermute | solution.py:261
  16.1 0.0 copy-start.7
  16.1 0.5 %collective-permute-start.6 = (bf16[128,128]{1,0:T(8,128)(2,1)S(1)}, bf16[128,128]{1,0:T(8,128)(2,1)S(1)}, u32[]{:S(2)}, u32[]{:S(2)}) collective-permute-start(bf16[128,128]{1,0:T(8,128)(2,1)S(1)} %get-tuple-element.24), channel_id=1, source_target_pairs={{0,2},{1,3},{2,0},{3,1},{4,6},{5,7},{6,4},{7,5},{8,10},{9,11},{10,... | collective-permute-start | bytes 98312 | tf_op jit(solution)/shard_map/ppermute | solution.py:261
  16.6 1.3 %collective-permute-done.4.refs_0_ = bf16[128,128]{1,0:T(8,128)(2,1)S(1)} collective-permute-done((bf16[128,128]{1,0:T(8,128)(2,1)S(1)}, bf16[128,128]{1,0:T(8,128)(2,1)S(1)}, u32[]{:S(2)}, u32[]{:S(2)}) %collective-permute-start.4) | collective-permute-done | bytes 32800 | tf_op jit(solution)/shard_map/ppermute | solution.py:261
  18.0 1.5 %collective-permute-done.5.refs_1_ = bf16[128,128]{1,0:T(8,128)(2,1)S(1)} collective-permute-done((bf16[128,128]{1,0:T(8,128)(2,1)S(1)}, bf16[128,128]{1,0:T(8,128)(2,1)S(1)}, u32[]{:S(2)}, u32[]{:S(2)}) %collective-permute-start.5) | collective-permute-done | bytes 32800 | tf_op jit(solution)/shard_map/ppermute | solution.py:261
  19.5 0.5 %collective-permute-done.6.refs_2_ = bf16[128,128]{1,0:T(8,128)(2,1)S(1)} collective-permute-done((bf16[128,128]{1,0:T(8,128)(2,1)S(1)}, bf16[128,128]{1,0:T(8,128)(2,1)S(1)}, u32[]{:S(2)}, u32[]{:S(2)}) %collective-permute-start.6) | collective-permute-done | bytes 32800 | tf_op jit(solution)/shard_map/ppermute | solution.py:261
  20.0 0.0 copy-done.1
  20.0 0.0 copy-done.2
  20.0 0.0 copy-done.7
  20.0 0.4 shard_map.109
  20.4 1.6 %collective-permute-start.9 = (bf16[3,128,128]{2,1,0:T(8,128)(2,1)S(1)}, bf16[3,128,128]{2,1,0:T(8,128)(2,1)S(1)}, u32[]{:S(2)}, u32[]{:S(2)}) collective-permute-start(bf16[3,128,128]{2,1,0:T(8,128)(2,1)S(1)} %get-tuple-element.27.refs_0_), channel_id=1, source_target_pairs={{0,6},{1,7},{2,4},{3,5},{4,2},{5,3},{6,0},{7,1},{8,14},{9,15},{10,... | collective-permute-start | bytes 294920 | tf_op jit(solution)/shard_map/ppermute | solution.py:261
  22.0 0.5 %collective-permute-start.8 = (bf16[3,128,128]{2,1,0:T(8,128)(2,1)S(1)}, bf16[3,128,128]{2,1,0:T(8,128)(2,1)S(1)}, u32[]{:S(2)}, u32[]{:S(2)}) collective-permute-start(bf16[3,128,128]{2,1,0:T(8,128)(2,1)S(1)} %get-tuple-element.27.refs_0_), channel_id=1, source_target_pairs={{0,4},{1,5},{2,6},{3,7},{4,0},{5,1},{6,2},{7,3},{8,12},{9,13},{10,... | collective-permute-start | bytes 294920 | tf_op jit(solution)/shard_map/ppermute | solution.py:261
  22.5 1.5 %collective-permute-start.7 = (bf16[3,128,128]{2,1,0:T(8,128)(2,1)S(1)}, bf16[3,128,128]{2,1,0:T(8,128)(2,1)S(1)}, u32[]{:S(2)}, u32[]{:S(2)}) collective-permute-start(bf16[3,128,128]{2,1,0:T(8,128)(2,1)S(1)} %get-tuple-element.27.refs_0_), channel_id=1, source_target_pairs={{0,2},{1,3},{2,0},{3,1},{4,6},{5,7},{6,4},{7,5},{8,10},{9,11},{10,... | collective-permute-start | bytes 294920 | tf_op jit(solution)/shard_map/ppermute | solution.py:261
  24.0 0.6 %shard_map.110 = (bf16[128,256]{1,0:T(8,128)(2,1)}, f32[8,128]{1,0:T(8,128)S(1)}) custom-call(f32[128,256]{1,0:T(8,128)S(1)} %get-tuple-element.25.active_ref), custom_call_target="tpu_custom_call" | custom-call | flops 1048576 | bytes 1048576 | tf_op jit(solution)/shard_map/pallas_call | solution.py:25
  24.6 1.8 %collective-permute-done.9.refs_3_ = bf16[3,128,128]{2,1,0:T(8,128)(2,1)S(1)} collective-permute-done((bf16[3,128,128]{2,1,0:T(8,128)(2,1)S(1)}, bf16[3,128,128]{2,1,0:T(8,128)(2,1)S(1)}, u32[]{:S(2)}, u32[]{:S(2)}) %collective-permute-start.9) | collective-permute-done | bytes 98336 | tf_op jit(solution)/shard_map/ppermute | solution.py:261
  26.4 0.9 %collective-permute-done.8.refs_2_ = bf16[3,128,128]{2,1,0:T(8,128)(2,1)S(1)} collective-permute-done((bf16[3,128,128]{2,1,0:T(8,128)(2,1)S(1)}, bf16[3,128,128]{2,1,0:T(8,128)(2,1)S(1)}, u32[]{:S(2)}, u32[]{:S(2)}) %collective-permute-start.8) | collective-permute-done | bytes 98336 | tf_op jit(solution)/shard_map/ppermute | solution.py:261
  27.3 0.0 collective-permute-done.7.refs_1_
  27.3 0.1 shard_map.111
  27.4 0.1 collective-permute-start.10
  27.5 0.2 shard_map.112.own_ref
  27.7 1.1 %collective-permute-done.10.received_ref = bf16[5,128,128]{2,1,0:T(8,128)(2,1)S(1)} collective-permute-done((bf16[5,128,128]{2,1,0:T(8,128)(2,1)S(1)}, bf16[5,128,128]{2,1,0:T(8,128)(2,1)S(1)}, u32[]{:S(2)}, u32[]{:S(2)}) %collective-permute-start.10) | collective-permute-done | bytes 163872 | tf_op jit(solution)/shard_map/ppermute | solution.py:261
  28.9 0.3 shard_map.113
  29.2 1.3 %collective-permute-start.11 = (bf16[2,128,128]{2,1,0:T(8,128)(2,1)S(1)}, bf16[2,128,128]{2,1,0:T(8,128)(2,1)S(1)}, u32[]{:S(2)}, u32[]{:S(2)}) collective-permute-start(bf16[2,128,128]{2,1,0:T(8,128)(2,1)S(1)} %get-tuple-element.31), channel_id=1, source_target_pairs={{0,16},{8,24},{16,0},{24,8},{1,17},{9,25},{17,1},{25,9},{2,18},{10... | collective-permute-start | bytes 196616 | tf_op jit(solution)/shard_map/ppermute | solution.py:265
  30.5 1.4 %collective-permute-start.12 = (bf16[2,128,128]{2,1,0:T(8,128)(2,1)S(1)}, bf16[2,128,128]{2,1,0:T(8,128)(2,1)S(1)}, u32[]{:S(2)}, u32[]{:S(2)}) collective-permute-start(bf16[2,128,128]{2,1,0:T(8,128)(2,1)S(1)} %get-tuple-element.32), channel_id=1, source_target_pairs={{0,8},{8,16},{16,24},{24,0},{1,9},{9,17},{17,25},{25,1},{2,10},{10... | collective-permute-start | bytes 196616 | tf_op jit(solution)/shard_map/ppermute | solution.py:265
  31.8 2.5 %collective-permute-start.13 = (bf16[2,128,128]{2,1,0:T(8,128)(2,1)S(1)}, bf16[2,128,128]{2,1,0:T(8,128)(2,1)S(1)}, u32[]{:S(2)}, u32[]{:S(2)}) collective-permute-start(bf16[2,128,128]{2,1,0:T(8,128)(2,1)S(1)} %get-tuple-element.33), channel_id=1, source_target_pairs={{0,24},{8,0},{16,8},{24,16},{1,25},{9,1},{17,9},{25,17},{2,26},{10... | collective-permute-start | bytes 196616 | tf_op jit(solution)/shard_map/ppermute | solution.py:265
  34.3 1.6 %collective-permute-done.11.refs_0_ = bf16[2,128,128]{2,1,0:T(8,128)(2,1)S(1)} collective-permute-done((bf16[2,128,128]{2,1,0:T(8,128)(2,1)S(1)}, bf16[2,128,128]{2,1,0:T(8,128)(2,1)S(1)}, u32[]{:S(2)}, u32[]{:S(2)}) %collective-permute-start.11) | collective-permute-done | bytes 65568 | tf_op jit(solution)/shard_map/ppermute | solution.py:265
  35.9 1.0 %collective-permute-done.12.refs_1_ = bf16[2,128,128]{2,1,0:T(8,128)(2,1)S(1)} collective-permute-done((bf16[2,128,128]{2,1,0:T(8,128)(2,1)S(1)}, bf16[2,128,128]{2,1,0:T(8,128)(2,1)S(1)}, u32[]{:S(2)}, u32[]{:S(2)}) %collective-permute-start.12) | collective-permute-done | bytes 65568 | tf_op jit(solution)/shard_map/ppermute | solution.py:265
  36.9 1.0 %collective-permute-done.13.refs_2_ = bf16[2,128,128]{2,1,0:T(8,128)(2,1)S(1)} collective-permute-done((bf16[2,128,128]{2,1,0:T(8,128)(2,1)S(1)}, bf16[2,128,128]{2,1,0:T(8,128)(2,1)S(1)}, u32[]{:S(2)}, u32[]{:S(2)}) %collective-permute-start.13) | collective-permute-done | bytes 65568 | tf_op jit(solution)/shard_map/ppermute | solution.py:265
  37.9 0.1 collective-permute-start.14
  38.0 0.7 %shard_map.114 = bf16[128,128]{1,0:T(8,128)(2,1)} custom-call(bf16[128]{0:T(256)(128)(2,1)S(1)} %copy-done.7, bf16[2,128,128]{2,1,0:T(8,128)(2,1)S(1)} %collective-permute-done.11.refs_0_, bf16[2,128,128]{2,1,0:T(8,128)(2,1)S(1)} %collective-permute-done.12.refs_1_, bf16[2,128,128]{2,1,0:T(8,128)(2,1)S(1)} %collective-permute-done.13.refs_2_, ...), custom_call_target="tpu_custom_call" | custom-call | flops 1048576 | bytes 1048576 | tf_op jit(solution)/shard_map/pallas_call | solution.py:25
  38.7 0.5 %collective-permute-done.14.other_ref = f32[128,128]{1,0:T(8,128)S(1)} collective-permute-done((f32[128,128]{1,0:T(8,128)S(1)}, f32[128,128]{1,0:T(8,128)S(1)}, u32[]{:S(2)}, u32[]{:S(2)}) %collective-permute-start.14) | collective-permute-done | bytes 65568 | tf_op jit(solution)/shard_map/ppermute | solution.py:261
  39.2 0.7 %shard_map.116 = f32[128,256]{1,0:T(8,128)} custom-call(s32[1]{0:T(128)} %bitcast.1.core_ref, f32[128,128]{1,0:T(8,128)S(1)} %shard_map.115.own_ref, f32[128,128]{1,0:T(8,128)S(1)} %collective-permute-done.14.other_ref), custom_call_target="tpu_custom_call" | custom-call | flops 1048576 | bytes 1048576 | tf_op jit(solution)/shard_map/pallas_call | solution.py:25
  (3 shorter events, 0.1 us)
Async XLA Ops:
  0.6 0.8 %copy-start.5 = (s32[1,1,8]{2,1,0:T(1,128)S(1)}, s32[1,1,8]{2,1,0:T(1,128)}, u32[]{:S(2)}) copy-start(s32[1,1,8]{2,1,0:T(1,128)} %cols_ref.3) | copy-start | bytes 100
  0.6 0.8 %copy-start.4 = (s32[1,1,8]{2,1,0:T(1,128)S(1)}, s32[1,1,8]{2,1,0:T(1,128)}, u32[]{:S(2)}) copy-start(s32[1,1,8]{2,1,0:T(1,128)} %rows_ref.3) | copy-start | bytes 100
  0.7 0.8 %copy-start.3 = (bf16[128,128]{1,0:T(8,128)(2,1)S(1)}, bf16[128,128]{1,0:T(8,128)(2,1)}, u32[]{:S(2)}) copy-start(bf16[128,128]{1,0:T(8,128)(2,1)} %features_ref.1) | copy-start | bytes 98308
  0.7 0.7 %copy-start.6 = (bf16[128]{0:T(256)(128)(2,1)S(1)}, bf16[128]{0:T(256)(128)(2,1)}, u32[]{:S(2)}) copy-start(bf16[128]{0:T(256)(128)(2,1)} %deg_ref.5) | copy-start | bytes 772
  1.3 6.5 %copy-start = (s32[1,1,8,32,256]{4,3,2,1,0:T(8,128)S(1)}, s32[1,1,8,32,256]{4,3,2,1,0:T(8,128)}, u32[]{:S(2)}) copy-start(s32[1,1,8,32,256]{4,3,2,1,0:T(8,128)} %bits_ref.1) | copy-start | bytes 786436
  1.5 7.3 %collective-permute-start.2 = (bf16[128,128]{1,0:T(8,128)(2,1)S(1)}, bf16[128,128]{1,0:T(8,128)(2,1)S(1)}, u32[]{:S(2)}, u32[]{:S(2)}) collective-permute-start(bf16[128,128]{1,0:T(8,128)(2,1)S(1)} %shard_map.104.after_ref.refs_0_), channel_id=1, source_target_pairs={{0,16},{8,24},{16,0},{24,8},{1,17},{9,25},{17,1},{25,9},{2,18},{10... | collective-permute-start | bytes 98312 | tf_op jit(solution)/shard_map/ppermute | solution.py:261
  5.6 5.7 %collective-permute-start.1 = (bf16[128,128]{1,0:T(8,128)(2,1)S(1)}, bf16[128,128]{1,0:T(8,128)(2,1)S(1)}, u32[]{:S(2)}, u32[]{:S(2)}) collective-permute-start(bf16[128,128]{1,0:T(8,128)(2,1)S(1)} %shard_map.104.after_ref.refs_0_), channel_id=1, source_target_pairs={{0,24},{8,16},{16,8},{24,0},{1,25},{9,17},{17,9},{25,1},{2,26},{10... | collective-permute-start | bytes 98312 | tf_op jit(solution)/shard_map/ppermute | solution.py:261
  7.0 4.4 %collective-permute-start = (bf16[128,128]{1,0:T(8,128)(2,1)S(1)}, bf16[128,128]{1,0:T(8,128)(2,1)S(1)}, u32[]{:S(2)}, u32[]{:S(2)}) collective-permute-start(bf16[128,128]{1,0:T(8,128)(2,1)S(1)} %shard_map.104.after_ref.refs_0_), channel_id=1, source_target_pairs={{0,8},{8,0},{16,24},{24,16},{1,9},{9,1},{17,25},{25,17},{2,10},{10... | collective-permute-start | bytes 98312 | tf_op jit(solution)/shard_map/ppermute | solution.py:261
  11.6 1.4 %collective-permute-start.3 = (bf16[4,128,128]{2,1,0:T(8,128)(2,1)S(1)}, bf16[4,128,128]{2,1,0:T(8,128)(2,1)S(1)}, u32[]{:S(2)}, u32[]{:S(2)}) collective-permute-start(bf16[4,128,128]{2,1,0:T(8,128)(2,1)S(1)} %get-tuple-element.20), channel_id=1, source_target_pairs={{0,1},{1,0},{2,3},{3,2},{4,5},{5,4},{6,7},{7,6},{8,9},{9,8},{10,11... | collective-permute-start | bytes 393224 | tf_op jit(solution)/shard_map/ppermute | solution.py:261
  13.1 7.0 %copy-start.1 = (bf16[128,256]{1,0:T(8,128)(2,1)S(1)}, bf16[128,256]{1,0:T(8,128)(2,1)}, u32[]{:S(2)}) copy-start(bf16[128,256]{1,0:T(8,128)(2,1)} %weight_ref.1) | copy-start | bytes 196612
  13.1 7.0 %copy-start.2 = (bf16[128,256]{1,0:T(8,128)(2,1)S(1)}, bf16[128,256]{1,0:T(8,128)(2,1)}, u32[]{:S(2)}) copy-start(bf16[128,256]{1,0:T(8,128)(2,1)} %cotangent_ref.1) | copy-start | bytes 196612
  13.1 4.9 %collective-permute-start.4 = (bf16[128,128]{1,0:T(8,128)(2,1)S(1)}, bf16[128,128]{1,0:T(8,128)(2,1)S(1)}, u32[]{:S(2)}, u32[]{:S(2)}) collective-permute-start(bf16[128,128]{1,0:T(8,128)(2,1)S(1)} %get-tuple-element.22), channel_id=1, source_target_pairs={{0,6},{1,7},{2,4},{3,5},{4,2},{5,3},{6,0},{7,1},{8,14},{9,15},{10,... | collective-permute-start | bytes 98312 | tf_op jit(solution)/shard_map/ppermute | solution.py:261
  15.6 3.9 %collective-permute-start.5 = (bf16[128,128]{1,0:T(8,128)(2,1)S(1)}, bf16[128,128]{1,0:T(8,128)(2,1)S(1)}, u32[]{:S(2)}, u32[]{:S(2)}) collective-permute-start(bf16[128,128]{1,0:T(8,128)(2,1)S(1)} %get-tuple-element.23), channel_id=1, source_target_pairs={{0,4},{1,5},{2,6},{3,7},{4,0},{5,1},{6,2},{7,3},{8,12},{9,13},{10,... | collective-permute-start | bytes 98312 | tf_op jit(solution)/shard_map/ppermute | solution.py:261
  16.1 3.9 %copy-start.7 = (bf16[128]{0:T(256)(128)(2,1)S(1)}, bf16[128]{0:T(256)(128)(2,1)}, u32[]{:S(2)}) copy-start(bf16[128]{0:T(256)(128)(2,1)} %deg_ref.5) | copy-start | bytes 772
  16.1 3.9 %collective-permute-start.6 = (bf16[128,128]{1,0:T(8,128)(2,1)S(1)}, bf16[128,128]{1,0:T(8,128)(2,1)S(1)}, u32[]{:S(2)}, u32[]{:S(2)}) collective-permute-start(bf16[128,128]{1,0:T(8,128)(2,1)S(1)} %get-tuple-element.24), channel_id=1, source_target_pairs={{0,2},{1,3},{2,0},{3,1},{4,6},{5,7},{6,4},{7,5},{8,10},{9,11},{10,... | collective-permute-start | bytes 98312 | tf_op jit(solution)/shard_map/ppermute | solution.py:261
  20.4 6.0 %collective-permute-start.9 = (bf16[3,128,128]{2,1,0:T(8,128)(2,1)S(1)}, bf16[3,128,128]{2,1,0:T(8,128)(2,1)S(1)}, u32[]{:S(2)}, u32[]{:S(2)}) collective-permute-start(bf16[3,128,128]{2,1,0:T(8,128)(2,1)S(1)} %get-tuple-element.27.refs_0_), channel_id=1, source_target_pairs={{0,6},{1,7},{2,4},{3,5},{4,2},{5,3},{6,0},{7,1},{8,14},{9,15},{10,... | collective-permute-start | bytes 294920 | tf_op jit(solution)/shard_map/ppermute | solution.py:261
  22.0 5.4 %collective-permute-start.8 = (bf16[3,128,128]{2,1,0:T(8,128)(2,1)S(1)}, bf16[3,128,128]{2,1,0:T(8,128)(2,1)S(1)}, u32[]{:S(2)}, u32[]{:S(2)}) collective-permute-start(bf16[3,128,128]{2,1,0:T(8,128)(2,1)S(1)} %get-tuple-element.27.refs_0_), channel_id=1, source_target_pairs={{0,4},{1,5},{2,6},{3,7},{4,0},{5,1},{6,2},{7,3},{8,12},{9,13},{10,... | collective-permute-start | bytes 294920 | tf_op jit(solution)/shard_map/ppermute | solution.py:261
  22.5 4.8 %collective-permute-start.7 = (bf16[3,128,128]{2,1,0:T(8,128)(2,1)S(1)}, bf16[3,128,128]{2,1,0:T(8,128)(2,1)S(1)}, u32[]{:S(2)}, u32[]{:S(2)}) collective-permute-start(bf16[3,128,128]{2,1,0:T(8,128)(2,1)S(1)} %get-tuple-element.27.refs_0_), channel_id=1, source_target_pairs={{0,2},{1,3},{2,0},{3,1},{4,6},{5,7},{6,4},{7,5},{8,10},{9,11},{10,... | collective-permute-start | bytes 294920 | tf_op jit(solution)/shard_map/ppermute | solution.py:261
  27.4 1.5 %collective-permute-start.10 = (bf16[5,128,128]{2,1,0:T(8,128)(2,1)S(1)}, bf16[5,128,128]{2,1,0:T(8,128)(2,1)S(1)}, u32[]{:S(2)}, u32[]{:S(2)}) collective-permute-start(bf16[5,128,128]{2,1,0:T(8,128)(2,1)S(1)} %get-tuple-element.29.joined_ref), channel_id=1, source_target_pairs={{0,1},{1,0},{2,3},{3,2},{4,5},{5,4},{6,7},{7,6},{8,9},{9,8},{10,11... | collective-permute-start | bytes 491528 | tf_op jit(solution)/shard_map/ppermute | solution.py:261
  29.2 6.7 %collective-permute-start.11 = (bf16[2,128,128]{2,1,0:T(8,128)(2,1)S(1)}, bf16[2,128,128]{2,1,0:T(8,128)(2,1)S(1)}, u32[]{:S(2)}, u32[]{:S(2)}) collective-permute-start(bf16[2,128,128]{2,1,0:T(8,128)(2,1)S(1)} %get-tuple-element.31), channel_id=1, source_target_pairs={{0,16},{8,24},{16,0},{24,8},{1,17},{9,25},{17,1},{25,9},{2,18},{10... | collective-permute-start | bytes 196616 | tf_op jit(solution)/shard_map/ppermute | solution.py:265
  30.5 6.4 %collective-permute-start.12 = (bf16[2,128,128]{2,1,0:T(8,128)(2,1)S(1)}, bf16[2,128,128]{2,1,0:T(8,128)(2,1)S(1)}, u32[]{:S(2)}, u32[]{:S(2)}) collective-permute-start(bf16[2,128,128]{2,1,0:T(8,128)(2,1)S(1)} %get-tuple-element.32), channel_id=1, source_target_pairs={{0,8},{8,16},{16,24},{24,0},{1,9},{9,17},{17,25},{25,1},{2,10},{10... | collective-permute-start | bytes 196616 | tf_op jit(solution)/shard_map/ppermute | solution.py:265
  31.8 6.0 %collective-permute-start.13 = (bf16[2,128,128]{2,1,0:T(8,128)(2,1)S(1)}, bf16[2,128,128]{2,1,0:T(8,128)(2,1)S(1)}, u32[]{:S(2)}, u32[]{:S(2)}) collective-permute-start(bf16[2,128,128]{2,1,0:T(8,128)(2,1)S(1)} %get-tuple-element.33), channel_id=1, source_target_pairs={{0,24},{8,0},{16,8},{24,16},{1,25},{9,1},{17,9},{25,17},{2,26},{10... | collective-permute-start | bytes 196616 | tf_op jit(solution)/shard_map/ppermute | solution.py:265
  37.9 1.3 %collective-permute-start.14 = (f32[128,128]{1,0:T(8,128)S(1)}, f32[128,128]{1,0:T(8,128)S(1)}, u32[]{:S(2)}, u32[]{:S(2)}) collective-permute-start(f32[128,128]{1,0:T(8,128)S(1)} %shard_map.115.own_ref), channel_id=1, source_target_pairs={{0,1},{1,0},{2,3},{3,2},{4,5},{5,4},{6,7},{7,6},{8,9},{9,8},{10,11... | collective-permute-start | bytes 196616 | tf_op jit(solution)/shard_map/ppermute | solution.py:261

commit v12 on v10

--- a/solution.py
+++ b/solution.py
@@ -209,25 +209,29 @@
         piece[1] = grad
 
 
-def sum_grad(factor, row_ref, *refs):
-    *pieces, out_ref, ordered = refs
-    for step, piece in zip((3, 2, 1, 0), pieces):
-        ordered[lax.rem(row_ref[0] + step, len(pieces))] = piece[1]
-    total = jnp.sum(ordered[...].astype(f32), axis=0) * factor
-    out_ref[...] = total.astype(out_ref.dtype)
-
-
-def input_rows(deg_ref, *refs):
-    *pieces, out_ref = refs
-    total = sum(piece[0].astype(f32) for piece in pieces)
-    out_ref[...] = (total * deg_ref[...].astype(f32).reshape(1, -1)).T.astype(bf16)
-
-
-def join_halves(core_ref, own_ref, other_ref, out_ref):
-    size = own_ref.shape[1]
-    half = core_ref[0]
-    out_ref[:, block_at(half, size)] = own_ref[...].astype(f32)
-    out_ref[:, block_at(1 - half, size)] = other_ref[...].astype(f32)
+def pack_pieces(*refs):
+    *pieces, own_ref, sent_ref = refs
+    count = len(pieces)
+    for index, piece in enumerate(pieces):
+        sent_ref[index] = piece[0]
+        sent_ref[count + index] = piece[1]
+    sent_ref[2 * count] = own_ref[1]
+
+
+def finish(factor, row_ref, core_ref, deg_ref, own_ref, received_ref, *refs):
+    *pieces, input_ref, grad_ref, ordered = refs
+    count, size = len(pieces), own_ref.shape[1]
+    total = sum(received_ref[index].astype(f32) for index in range(count)) + own_ref[0].astype(f32)
+    input_ref[...] = (total * deg_ref[...].astype(f32).reshape(1, -1)).T.astype(bf16)
+    for index, piece in enumerate(pieces):
+        plane = lax.rem(row_ref[0] + count - index, count + 1)
+        ordered[0, plane] = received_ref[count + index]
+        ordered[1, plane] = piece[1]
+    ordered[0, row_ref[0]] = own_ref[1]
+    ordered[1, row_ref[0]] = received_ref[2 * count]
+    for index, half in enumerate((core_ref[0], 1 - core_ref[0])):
+        half_grad = jnp.sum(ordered[index].astype(f32), axis=0) * factor
+        grad_ref[:, block_at(half, size)] = half_grad
 
 
 def forward_all(rows_ref, cols_ref, masks_ref, source_ref, partial_ref, total):
@@ -261,8 +265,13 @@
     return lax.ppermute(block, axis, [(shard, shard ^ distance) for shard in range(shards)])
 
 
-def shifted(block, axis, shards, step):
-    return lax.ppermute(block, axis, [(shard, (shard + step) % shards) for shard in range(shards)])
+def crossed(block, rows, cols, step):
+    pairs = [
+        (row * cols + col, (row + step) % rows * cols + (col ^ 1))
+        for row in range(rows)
+        for col in range(cols)
+    ]
+    return lax.ppermute(block, ("row", "col"), pairs)
 
 
 def on_device(features, deg_scale, weight, cotangent, tile_rows, tile_cols, tile_count, tile_bits):
@@ -385,19 +394,22 @@
         (adjacency, own_total, own_grad, exchange(joined, "col", col_shards, 1)),
         [half_source, pltpu.VMEM((width, row_shards * size), f32)],
     )
-    arrived = [shifted(piece, "row", row_shards, step) for step, piece in zip((1, 2, 3), pieces)]
-    arrived.append(pieces[-1])
-    half_grad = call(
-        functools.partial(sum_grad, factor),
-        struct((height, out_width // 2), f32),
-        (row,),
-        arrived,
-        [pltpu.VMEM((row_shards, height, out_width // 2), bf16)],
-    )
-    other_grad = exchange(half_grad, "col", col_shards, 1)
-    input_grad = call(input_rows, input_shape, (), (deg_scale, *arrived))
-    weight_grad = call(
-        join_halves, struct((height, out_width), f32), (core,), (half_grad, other_grad)
+    own_piece = pieces[-1]
+    arrived = [
+        crossed(piece, row_shards, col_shards, step) for step, piece in zip((1, 2, 3), pieces)
+    ]
+    packed = call(
+        pack_pieces,
+        struct((2 * len(arrived) + 1, width, size), bf16),
+        (),
+        (*arrived, own_piece),
+    )
+    input_grad, weight_grad = call(
+        functools.partial(finish, factor),
+        (input_shape, struct((height, out_width), f32)),
+        (row, core),
+        (deg_scale, own_piece, exchange(packed, "col", col_shards, 1), *arrived),
+        [pltpu.VMEM((2, row_shards, height, out_width // 2), bf16)],
     )
     return (activations, input_grad, weight_grad)
 

time: 40.1 us -> 39.7 us (0.990)
  Pallas kernels: 4.72 us -> 4.05 us
    pallas_call x13 -> x12, Pallas kernels: 3.81 us -> 3.14 us  [call(): pl.pallas_call(body, out_shape=out_shape, in_specs=[SMEM] * len(scalars)...]
    ppermute x12, waiting for transfers between devices: 11.3 us -> 11.9 us  [exchange(): lax.ppermute(block, axis, [(shard, shard ^ distance) for shard in range(s...]
    ppermute x3, starting transfers between devices: 4.21 us -> 3.69 us  [crossed(): return lax.ppermute(block, ('row', 'col'), pairs)]
    ppermute x12, starting transfers between devices: 13 us -> 13.5 us  [exchange(): lax.ppermute(block, axis, [(shard, shard ^ distance) for shard in range(s...]
  transfers between devices with their start and end apart: 15 -> 15, of which waited for: 11 -> 12; matrix products, arithmetic and copies ran while one was open for 0% -> 0% of each run, Pallas kernels for 7% -> 5%
where the time goes in v12:
time: 39.7 us; the launch traced here: 39.5 us
  starting transfers between devices  17.2 us (43%)
  waiting for transfers between devices  16.1 us (41%)
  Pallas kernels  4.05 us (10%)
  between operations  1.47 us (4%)
  local copies, waits for them, and re-layouts  0.69 us (2%)
    ppermute x12, starting transfers between devices, exchange(): lax.ppermute(block, axis, [(shard, shard ^ distance) for shard in range(s...  13.5 us
    ppermute x12, waiting for transfers between devices, exchange(): lax.ppermute(block, axis, [(shard, shard ^ distance) for shard in range(s...  11.9 us
    ppermute x3, waiting for transfers between devices, crossed(): return lax.ppermute(block, ('row', 'col'), pairs)  4.21 us
    ppermute x3, starting transfers between devices, crossed(): return lax.ppermute(block, ('row', 'col'), pairs)  3.69 us
    pallas_call x12, Pallas kernels, call(): pl.pallas_call(body, out_shape=out_shape, in_specs=[SMEM] * len(scalars)...  3.14 us
    pallas_call x1, Pallas kernels, on_device(): pl.pallas_call(build_adjacency, out_shape=struct((col_shards * size, row_...  0.91 us
  transfers between devices with their start and end apart: 15, of which 12 were waited for; matrix products, arithmetic and copies ran while one was open for 0% of the time, Pallas kernels for 5%

profile of v12, /device:TPU:0, one launch (start us, length us, event | category | flops | bytes accessed | tf_op | source)
XLA Modules:
  0.0 39.5 jit_solution(14281691493307158912)
XLA Ops:
  0.6 0.0 copy-start.5
  0.6 0.0 copy-start.4
  0.7 0.0 copy-start.3
  0.7 0.0 copy-start.6
  0.7 0.7 %copy-done.6 = bf16[128]{0:T(256)(128)(2,1)S(1)} copy-done((bf16[128]{0:T(256)(128)(2,1)S(1)}, bf16[128]{0:T(256)(128)(2,1)}, u32[]{:S(2)}) %copy-start.6) | copy-done | bytes 280
  1.3 0.0 copy-start
  1.3 0.1 shard_map.103.column_ref
  1.5 0.0 copy-done.5
  1.5 0.0 copy-done.4
  1.5 0.0 copy-done.3
  1.5 4.1 %collective-permute-start.2 = (bf16[128,128]{1,0:T(8,128)(2,1)S(1)}, bf16[128,128]{1,0:T(8,128)(2,1)S(1)}, u32[]{:S(2)}, u32[]{:S(2)}) collective-permute-start(bf16[128,128]{1,0:T(8,128)(2,1)S(1)} %shard_map.104.after_ref.refs_0_), channel_id=1, source_target_pairs={{0,16},{8,24},{16,0},{24,8},{1,17},{9,25},{17,1},{25,9},{2,18},{10... | collective-permute-start | bytes 98312 | tf_op jit(solution)/shard_map/ppermute | solution.py:265
  5.6 1.3 %collective-permute-start.1 = (bf16[128,128]{1,0:T(8,128)(2,1)S(1)}, bf16[128,128]{1,0:T(8,128)(2,1)S(1)}, u32[]{:S(2)}, u32[]{:S(2)}) collective-permute-start(bf16[128,128]{1,0:T(8,128)(2,1)S(1)} %shard_map.104.after_ref.refs_0_), channel_id=1, source_target_pairs={{0,24},{8,16},{16,8},{24,0},{1,25},{9,17},{17,9},{25,1},{2,26},{10... | collective-permute-start | bytes 98312 | tf_op jit(solution)/shard_map/ppermute | solution.py:265
  7.0 0.2 collective-permute-start
  7.8 0.0 copy-done
  7.9 0.9 %shard_map.105.adjacency_ref = bf16[1024,512]{1,0:T(8,128)(2,1)S(1)} custom-call(s32[1,1]{1,0:T(1,128)S(6)} %copy.11.count_ref, s32[1,1,8]{2,1,0:T(1,128)S(1)} %copy-done.4, s32[1,1,8]{2,1,0:T(1,128)S(1)} %copy-done.5, s32[1,1,8,32,256]{4,3,2,1,0:T(8,128)S(1)} %copy-done, bf16[128,128]{1,0:T(8,128)(2,1)S(1)} %shard_map.104.after_ref.refs_0_), custom_call_target="tpu_custom_call" | custom-call | flops 1048576 | bytes 1048576 | tf_op jit(solution)/shard_map/pallas_call | solution.py:337
  8.8 0.0 collective-permute-done.2.refs_3_
  8.8 2.5 %collective-permute-done.1.refs_2_ = bf16[128,128]{1,0:T(8,128)(2,1)S(1)} collective-permute-done((bf16[128,128]{1,0:T(8,128)(2,1)S(1)}, bf16[128,128]{1,0:T(8,128)(2,1)S(1)}, u32[]{:S(2)}, u32[]{:S(2)}) %collective-permute-start.1) | collective-permute-done | bytes 32800 | tf_op jit(solution)/shard_map/ppermute | solution.py:265
  11.3 0.0 collective-permute-done.refs_1_
  11.3 0.3 shard_map.106
  11.6 0.1 collective-permute-start.3
  11.7 0.3 shard_map.107.mine_ref
  12.0 1.0 %collective-permute-done.3.received_ref = bf16[4,128,128]{2,1,0:T(8,128)(2,1)S(1)} collective-permute-done((bf16[4,128,128]{2,1,0:T(8,128)(2,1)S(1)}, bf16[4,128,128]{2,1,0:T(8,128)(2,1)S(1)}, u32[]{:S(2)}, u32[]{:S(2)}) %collective-permute-start.3) | collective-permute-done | bytes 131104 | tf_op jit(solution)/shard_map/ppermute | solution.py:265
  13.1 0.0 copy-start.1
  13.1 0.0 copy-start.2
  13.1 2.5 %collective-permute-start.4 = (bf16[128,128]{1,0:T(8,128)(2,1)S(1)}, bf16[128,128]{1,0:T(8,128)(2,1)S(1)}, u32[]{:S(2)}, u32[]{:S(2)}) collective-permute-start(bf16[128,128]{1,0:T(8,128)(2,1)S(1)} %get-tuple-element.24), channel_id=1, source_target_pairs={{0,6},{1,7},{2,4},{3,5},{4,2},{5,3},{6,0},{7,1},{8,14},{9,15},{10,... | collective-permute-start | bytes 98312 | tf_op jit(solution)/shard_map/ppermute | solution.py:265
  15.6 0.5 %collective-permute-start.5 = (bf16[128,128]{1,0:T(8,128)(2,1)S(1)}, bf16[128,128]{1,0:T(8,128)(2,1)S(1)}, u32[]{:S(2)}, u32[]{:S(2)}) collective-permute-start(bf16[128,128]{1,0:T(8,128)(2,1)S(1)} %get-tuple-element.25), channel_id=1, source_target_pairs={{0,4},{1,5},{2,6},{3,7},{4,0},{5,1},{6,2},{7,3},{8,12},{9,13},{10,... | collective-permute-start | bytes 98312 | tf_op jit(solution)/shard_map/ppermute | solution.py:265
  16.1 0.0 copy-start.7
  16.1 0.5 %collective-permute-start.6 = (bf16[128,128]{1,0:T(8,128)(2,1)S(1)}, bf16[128,128]{1,0:T(8,128)(2,1)S(1)}, u32[]{:S(2)}, u32[]{:S(2)}) collective-permute-start(bf16[128,128]{1,0:T(8,128)(2,1)S(1)} %get-tuple-element.26), channel_id=1, source_target_pairs={{0,2},{1,3},{2,0},{3,1},{4,6},{5,7},{6,4},{7,5},{8,10},{9,11},{10,... | collective-permute-start | bytes 98312 | tf_op jit(solution)/shard_map/ppermute | solution.py:265
  16.6 1.3 %collective-permute-done.4.refs_0_ = bf16[128,128]{1,0:T(8,128)(2,1)S(1)} collective-permute-done((bf16[128,128]{1,0:T(8,128)(2,1)S(1)}, bf16[128,128]{1,0:T(8,128)(2,1)S(1)}, u32[]{:S(2)}, u32[]{:S(2)}) %collective-permute-start.4) | collective-permute-done | bytes 32800 | tf_op jit(solution)/shard_map/ppermute | solution.py:265
  18.0 1.5 %collective-permute-done.5.refs_1_ = bf16[128,128]{1,0:T(8,128)(2,1)S(1)} collective-permute-done((bf16[128,128]{1,0:T(8,128)(2,1)S(1)}, bf16[128,128]{1,0:T(8,128)(2,1)S(1)}, u32[]{:S(2)}, u32[]{:S(2)}) %collective-permute-start.5) | collective-permute-done | bytes 32800 | tf_op jit(solution)/shard_map/ppermute | solution.py:265
  19.5 0.5 %collective-permute-done.6.refs_2_ = bf16[128,128]{1,0:T(8,128)(2,1)S(1)} collective-permute-done((bf16[128,128]{1,0:T(8,128)(2,1)S(1)}, bf16[128,128]{1,0:T(8,128)(2,1)S(1)}, u32[]{:S(2)}, u32[]{:S(2)}) %collective-permute-start.6) | collective-permute-done | bytes 32800 | tf_op jit(solution)/shard_map/ppermute | solution.py:265
  20.0 0.0 copy-done.1
  20.0 0.0 copy-done.2
  20.0 0.0 copy-done.7
  20.0 0.4 shard_map.109
  20.4 1.6 %collective-permute-start.9 = (bf16[3,128,128]{2,1,0:T(8,128)(2,1)S(1)}, bf16[3,128,128]{2,1,0:T(8,128)(2,1)S(1)}, u32[]{:S(2)}, u32[]{:S(2)}) collective-permute-start(bf16[3,128,128]{2,1,0:T(8,128)(2,1)S(1)} %get-tuple-element.29.refs_0_), channel_id=1, source_target_pairs={{0,6},{1,7},{2,4},{3,5},{4,2},{5,3},{6,0},{7,1},{8,14},{9,15},{10,... | collective-permute-start | bytes 294920 | tf_op jit(solution)/shard_map/ppermute | solution.py:265
  22.0 0.5 %collective-permute-start.8 = (bf16[3,128,128]{2,1,0:T(8,128)(2,1)S(1)}, bf16[3,128,128]{2,1,0:T(8,128)(2,1)S(1)}, u32[]{:S(2)}, u32[]{:S(2)}) collective-permute-start(bf16[3,128,128]{2,1,0:T(8,128)(2,1)S(1)} %get-tuple-element.29.refs_0_), channel_id=1, source_target_pairs={{0,4},{1,5},{2,6},{3,7},{4,0},{5,1},{6,2},{7,3},{8,12},{9,13},{10,... | collective-permute-start | bytes 294920 | tf_op jit(solution)/shard_map/ppermute | solution.py:265
  22.5 1.5 %collective-permute-start.7 = (bf16[3,128,128]{2,1,0:T(8,128)(2,1)S(1)}, bf16[3,128,128]{2,1,0:T(8,128)(2,1)S(1)}, u32[]{:S(2)}, u32[]{:S(2)}) collective-permute-start(bf16[3,128,128]{2,1,0:T(8,128)(2,1)S(1)} %get-tuple-element.29.refs_0_), channel_id=1, source_target_pairs={{0,2},{1,3},{2,0},{3,1},{4,6},{5,7},{6,4},{7,5},{8,10},{9,11},{10,... | collective-permute-start | bytes 294920 | tf_op jit(solution)/shard_map/ppermute | solution.py:265
  24.0 0.6 %shard_map.110 = (bf16[128,256]{1,0:T(8,128)(2,1)}, f32[8,128]{1,0:T(8,128)S(1)}) custom-call(f32[128,256]{1,0:T(8,128)S(1)} %get-tuple-element.27.active_ref), custom_call_target="tpu_custom_call" | custom-call | flops 1048576 | bytes 1048576 | tf_op jit(solution)/shard_map/pallas_call | solution.py:25
  24.6 1.8 %collective-permute-done.9.refs_3_ = bf16[3,128,128]{2,1,0:T(8,128)(2,1)S(1)} collective-permute-done((bf16[3,128,128]{2,1,0:T(8,128)(2,1)S(1)}, bf16[3,128,128]{2,1,0:T(8,128)(2,1)S(1)}, u32[]{:S(2)}, u32[]{:S(2)}) %collective-permute-start.9) | collective-permute-done | bytes 98336 | tf_op jit(solution)/shard_map/ppermute | solution.py:265
  26.4 0.9 %collective-permute-done.8.refs_2_ = bf16[3,128,128]{2,1,0:T(8,128)(2,1)S(1)} collective-permute-done((bf16[3,128,128]{2,1,0:T(8,128)(2,1)S(1)}, bf16[3,128,128]{2,1,0:T(8,128)(2,1)S(1)}, u32[]{:S(2)}, u32[]{:S(2)}) %collective-permute-start.8) | collective-permute-done | bytes 98336 | tf_op jit(solution)/shard_map/ppermute | solution.py:265
  27.3 0.0 collective-permute-done.7.refs_1_
  27.3 0.1 shard_map.111
  27.4 0.1 collective-permute-start.10
  27.5 0.2 shard_map.112.own_ref
  27.7 1.1 %collective-permute-done.10.received_ref = bf16[5,128,128]{2,1,0:T(8,128)(2,1)S(1)} collective-permute-done((bf16[5,128,128]{2,1,0:T(8,128)(2,1)S(1)}, bf16[5,128,128]{2,1,0:T(8,128)(2,1)S(1)}, u32[]{:S(2)}, u32[]{:S(2)}) %collective-permute-start.10) | collective-permute-done | bytes 163872 | tf_op jit(solution)/shard_map/ppermute | solution.py:265
  28.9 0.3 shard_map.113
  29.2 0.1 collective-permute-start.11
  29.2 2.3 %collective-permute-start.12 = (bf16[2,128,128]{2,1,0:T(8,128)(2,1)S(1)}, bf16[2,128,128]{2,1,0:T(8,128)(2,1)S(1)}, u32[]{:S(2)}, u32[]{:S(2)}) collective-permute-start(bf16[2,128,128]{2,1,0:T(8,128)(2,1)S(1)} %get-tuple-element.35), channel_id=1, source_target_pairs={{0,17},{1,16},{2,19},{3,18},{4,21},{5,20},{6,23},{7,22},{8,25},{9,... | collective-permute-start | bytes 196616 | tf_op jit(solution)/shard_map/ppermute | solution.py:274
  31.5 1.3 %collective-permute-start.13 = (bf16[2,128,128]{2,1,0:T(8,128)(2,1)S(1)}, bf16[2,128,128]{2,1,0:T(8,128)(2,1)S(1)}, u32[]{:S(2)}, u32[]{:S(2)}) collective-permute-start(bf16[2,128,128]{2,1,0:T(8,128)(2,1)S(1)} %get-tuple-element.36), channel_id=1, source_target_pairs={{0,25},{1,24},{2,27},{3,26},{4,29},{5,28},{6,31},{7,30},{8,1},{9,0... | collective-permute-start | bytes 196616 | tf_op jit(solution)/shard_map/ppermute | solution.py:274
  32.9 2.4 %collective-permute-done.11.refs_0_ = bf16[2,128,128]{2,1,0:T(8,128)(2,1)S(1)} collective-permute-done((bf16[2,128,128]{2,1,0:T(8,128)(2,1)S(1)}, bf16[2,128,128]{2,1,0:T(8,128)(2,1)S(1)}, u32[]{:S(2)}, u32[]{:S(2)}) %collective-permute-start.11) | collective-permute-done | bytes 65568 | tf_op jit(solution)/shard_map/ppermute | solution.py:274
  35.3 1.7 %collective-permute-done.12.refs_1_ = bf16[2,128,128]{2,1,0:T(8,128)(2,1)S(1)} collective-permute-done((bf16[2,128,128]{2,1,0:T(8,128)(2,1)S(1)}, bf16[2,128,128]{2,1,0:T(8,128)(2,1)S(1)}, u32[]{:S(2)}, u32[]{:S(2)}) %collective-permute-start.12) | collective-permute-done | bytes 65568 | tf_op jit(solution)/shard_map/ppermute | solution.py:274
  37.0 0.1 collective-permute-done.13.refs_2_
  37.1 0.5 %collective-permute-start.14 = (bf16[7,128,128]{2,1,0:T(8,128)(2,1)S(1)}, bf16[7,128,128]{2,1,0:T(8,128)(2,1)S(1)}, u32[]{:S(2)}, u32[]{:S(2)}) collective-permute-start(bf16[7,128,128]{2,1,0:T(8,128)(2,1)S(1)} %shard_map.114), channel_id=1, source_target_pairs={{0,1},{1,0},{2,3},{3,2},{4,5},{5,4},{6,7},{7,6},{8,9},{9,8},{10,11... | collective-permute-start | bytes 688136 | tf_op jit(solution)/shard_map/ppermute | solution.py:265
  37.6 1.1 %collective-permute-done.14.received_ref = bf16[7,128,128]{2,1,0:T(8,128)(2,1)S(1)} collective-permute-done((bf16[7,128,128]{2,1,0:T(8,128)(2,1)S(1)}, bf16[7,128,128]{2,1,0:T(8,128)(2,1)S(1)}, u32[]{:S(2)}, u32[]{:S(2)}) %collective-permute-start.14) | collective-permute-done | bytes 229408 | tf_op jit(solution)/shard_map/ppermute | solution.py:265
  38.7 0.7 %shard_map.115 = (bf16[128,128]{1,0:T(8,128)(2,1)}, f32[128,256]{1,0:T(8,128)}) custom-call(s32[1]{0:T(128)} %bitcast.2.row_ref, s32[1]{0:T(128)} %bitcast.1.core_ref, bf16[128]{0:T(256)(128)(2,1)S(1)} %copy-done.7, bf16[2,128,128]{2,1,0:T(8,128)(2,1)S(1)} %get-tuple-element.33.refs_3_.own_ref, ...), custom_call_target="tpu_custom_call" | custom-call | flops 1048576 | bytes 1048576 | tf_op jit(solution)/shard_map/pallas_call | solution.py:25
  (3 shorter events, 0.1 us)
Async XLA Ops:
  0.6 0.8 %copy-start.5 = (s32[1,1,8]{2,1,0:T(1,128)S(1)}, s32[1,1,8]{2,1,0:T(1,128)}, u32[]{:S(2)}) copy-start(s32[1,1,8]{2,1,0:T(1,128)} %cols_ref.3) | copy-start | bytes 100
  0.6 0.8 %copy-start.4 = (s32[1,1,8]{2,1,0:T(1,128)S(1)}, s32[1,1,8]{2,1,0:T(1,128)}, u32[]{:S(2)}) copy-start(s32[1,1,8]{2,1,0:T(1,128)} %rows_ref.3) | copy-start | bytes 100
  0.7 0.8 %copy-start.3 = (bf16[128,128]{1,0:T(8,128)(2,1)S(1)}, bf16[128,128]{1,0:T(8,128)(2,1)}, u32[]{:S(2)}) copy-start(bf16[128,128]{1,0:T(8,128)(2,1)} %features_ref.1) | copy-start | bytes 98308
  0.7 0.7 %copy-start.6 = (bf16[128]{0:T(256)(128)(2,1)S(1)}, bf16[128]{0:T(256)(128)(2,1)}, u32[]{:S(2)}) copy-start(bf16[128]{0:T(256)(128)(2,1)} %deg_ref.5) | copy-start | bytes 772
  1.3 6.5 %copy-start = (s32[1,1,8,32,256]{4,3,2,1,0:T(8,128)S(1)}, s32[1,1,8,32,256]{4,3,2,1,0:T(8,128)}, u32[]{:S(2)}) copy-start(s32[1,1,8,32,256]{4,3,2,1,0:T(8,128)} %bits_ref.1) | copy-start | bytes 786436
  1.5 7.3 %collective-permute-start.2 = (bf16[128,128]{1,0:T(8,128)(2,1)S(1)}, bf16[128,128]{1,0:T(8,128)(2,1)S(1)}, u32[]{:S(2)}, u32[]{:S(2)}) collective-permute-start(bf16[128,128]{1,0:T(8,128)(2,1)S(1)} %shard_map.104.after_ref.refs_0_), channel_id=1, source_target_pairs={{0,16},{8,24},{16,0},{24,8},{1,17},{9,25},{17,1},{25,9},{2,18},{10... | collective-permute-start | bytes 98312 | tf_op jit(solution)/shard_map/ppermute | solution.py:265
  5.6 5.7 %collective-permute-start.1 = (bf16[128,128]{1,0:T(8,128)(2,1)S(1)}, bf16[128,128]{1,0:T(8,128)(2,1)S(1)}, u32[]{:S(2)}, u32[]{:S(2)}) collective-permute-start(bf16[128,128]{1,0:T(8,128)(2,1)S(1)} %shard_map.104.after_ref.refs_0_), channel_id=1, source_target_pairs={{0,24},{8,16},{16,8},{24,0},{1,25},{9,17},{17,9},{25,1},{2,26},{10... | collective-permute-start | bytes 98312 | tf_op jit(solution)/shard_map/ppermute | solution.py:265
  7.0 4.4 %collective-permute-start = (bf16[128,128]{1,0:T(8,128)(2,1)S(1)}, bf16[128,128]{1,0:T(8,128)(2,1)S(1)}, u32[]{:S(2)}, u32[]{:S(2)}) collective-permute-start(bf16[128,128]{1,0:T(8,128)(2,1)S(1)} %shard_map.104.after_ref.refs_0_), channel_id=1, source_target_pairs={{0,8},{8,0},{16,24},{24,16},{1,9},{9,1},{17,25},{25,17},{2,10},{10... | collective-permute-start | bytes 98312 | tf_op jit(solution)/shard_map/ppermute | solution.py:265
  11.6 1.4 %collective-permute-start.3 = (bf16[4,128,128]{2,1,0:T(8,128)(2,1)S(1)}, bf16[4,128,128]{2,1,0:T(8,128)(2,1)S(1)}, u32[]{:S(2)}, u32[]{:S(2)}) collective-permute-start(bf16[4,128,128]{2,1,0:T(8,128)(2,1)S(1)} %get-tuple-element.22), channel_id=1, source_target_pairs={{0,1},{1,0},{2,3},{3,2},{4,5},{5,4},{6,7},{7,6},{8,9},{9,8},{10,11... | collective-permute-start | bytes 393224 | tf_op jit(solution)/shard_map/ppermute | solution.py:265
  13.1 7.0 %copy-start.1 = (bf16[128,256]{1,0:T(8,128)(2,1)S(1)}, bf16[128,256]{1,0:T(8,128)(2,1)}, u32[]{:S(2)}) copy-start(bf16[128,256]{1,0:T(8,128)(2,1)} %weight_ref.1) | copy-start | bytes 196612
  13.1 7.0 %copy-start.2 = (bf16[128,256]{1,0:T(8,128)(2,1)S(1)}, bf16[128,256]{1,0:T(8,128)(2,1)}, u32[]{:S(2)}) copy-start(bf16[128,256]{1,0:T(8,128)(2,1)} %cotangent_ref.1) | copy-start | bytes 196612
  13.1 4.9 %collective-permute-start.4 = (bf16[128,128]{1,0:T(8,128)(2,1)S(1)}, bf16[128,128]{1,0:T(8,128)(2,1)S(1)}, u32[]{:S(2)}, u32[]{:S(2)}) collective-permute-start(bf16[128,128]{1,0:T(8,128)(2,1)S(1)} %get-tuple-element.24), channel_id=1, source_target_pairs={{0,6},{1,7},{2,4},{3,5},{4,2},{5,3},{6,0},{7,1},{8,14},{9,15},{10,... | collective-permute-start | bytes 98312 | tf_op jit(solution)/shard_map/ppermute | solution.py:265
  15.6 3.9 %collective-permute-start.5 = (bf16[128,128]{1,0:T(8,128)(2,1)S(1)}, bf16[128,128]{1,0:T(8,128)(2,1)S(1)}, u32[]{:S(2)}, u32[]{:S(2)}) collective-permute-start(bf16[128,128]{1,0:T(8,128)(2,1)S(1)} %get-tuple-element.25), channel_id=1, source_target_pairs={{0,4},{1,5},{2,6},{3,7},{4,0},{5,1},{6,2},{7,3},{8,12},{9,13},{10,... | collective-permute-start | bytes 98312 | tf_op jit(solution)/shard_map/ppermute | solution.py:265
  16.1 3.9 %copy-start.7 = (bf16[128]{0:T(256)(128)(2,1)S(1)}, bf16[128]{0:T(256)(128)(2,1)}, u32[]{:S(2)}) copy-start(bf16[128]{0:T(256)(128)(2,1)} %deg_ref.5) | copy-start | bytes 772
  16.1 3.9 %collective-permute-start.6 = (bf16[128,128]{1,0:T(8,128)(2,1)S(1)}, bf16[128,128]{1,0:T(8,128)(2,1)S(1)}, u32[]{:S(2)}, u32[]{:S(2)}) collective-permute-start(bf16[128,128]{1,0:T(8,128)(2,1)S(1)} %get-tuple-element.26), channel_id=1, source_target_pairs={{0,2},{1,3},{2,0},{3,1},{4,6},{5,7},{6,4},{7,5},{8,10},{9,11},{10,... | collective-permute-start | bytes 98312 | tf_op jit(solution)/shard_map/ppermute | solution.py:265
  20.4 6.0 %collective-permute-start.9 = (bf16[3,128,128]{2,1,0:T(8,128)(2,1)S(1)}, bf16[3,128,128]{2,1,0:T(8,128)(2,1)S(1)}, u32[]{:S(2)}, u32[]{:S(2)}) collective-permute-start(bf16[3,128,128]{2,1,0:T(8,128)(2,1)S(1)} %get-tuple-element.29.refs_0_), channel_id=1, source_target_pairs={{0,6},{1,7},{2,4},{3,5},{4,2},{5,3},{6,0},{7,1},{8,14},{9,15},{10,... | collective-permute-start | bytes 294920 | tf_op jit(solution)/shard_map/ppermute | solution.py:265
  22.0 5.4 %collective-permute-start.8 = (bf16[3,128,128]{2,1,0:T(8,128)(2,1)S(1)}, bf16[3,128,128]{2,1,0:T(8,128)(2,1)S(1)}, u32[]{:S(2)}, u32[]{:S(2)}) collective-permute-start(bf16[3,128,128]{2,1,0:T(8,128)(2,1)S(1)} %get-tuple-element.29.refs_0_), channel_id=1, source_target_pairs={{0,4},{1,5},{2,6},{3,7},{4,0},{5,1},{6,2},{7,3},{8,12},{9,13},{10,... | collective-permute-start | bytes 294920 | tf_op jit(solution)/shard_map/ppermute | solution.py:265
  22.5 4.8 %collective-permute-start.7 = (bf16[3,128,128]{2,1,0:T(8,128)(2,1)S(1)}, bf16[3,128,128]{2,1,0:T(8,128)(2,1)S(1)}, u32[]{:S(2)}, u32[]{:S(2)}) collective-permute-start(bf16[3,128,128]{2,1,0:T(8,128)(2,1)S(1)} %get-tuple-element.29.refs_0_), channel_id=1, source_target_pairs={{0,2},{1,3},{2,0},{3,1},{4,6},{5,7},{6,4},{7,5},{8,10},{9,11},{10,... | collective-permute-start | bytes 294920 | tf_op jit(solution)/shard_map/ppermute | solution.py:265
  27.4 1.5 %collective-permute-start.10 = (bf16[5,128,128]{2,1,0:T(8,128)(2,1)S(1)}, bf16[5,128,128]{2,1,0:T(8,128)(2,1)S(1)}, u32[]{:S(2)}, u32[]{:S(2)}) collective-permute-start(bf16[5,128,128]{2,1,0:T(8,128)(2,1)S(1)} %get-tuple-element.31.joined_ref), channel_id=1, source_target_pairs={{0,1},{1,0},{2,3},{3,2},{4,5},{5,4},{6,7},{7,6},{8,9},{9,8},{10,11... | collective-permute-start | bytes 491528 | tf_op jit(solution)/shard_map/ppermute | solution.py:265
  29.2 6.1 %collective-permute-start.11 = (bf16[2,128,128]{2,1,0:T(8,128)(2,1)S(1)}, bf16[2,128,128]{2,1,0:T(8,128)(2,1)S(1)}, u32[]{:S(2)}, u32[]{:S(2)}) collective-permute-start(bf16[2,128,128]{2,1,0:T(8,128)(2,1)S(1)} %get-tuple-element.34), channel_id=1, source_target_pairs={{0,9},{1,8},{2,11},{3,10},{4,13},{5,12},{6,15},{7,14},{8,17},{9,16... | collective-permute-start | bytes 196616 | tf_op jit(solution)/shard_map/ppermute | solution.py:274
  29.2 7.7 %collective-permute-start.12 = (bf16[2,128,128]{2,1,0:T(8,128)(2,1)S(1)}, bf16[2,128,128]{2,1,0:T(8,128)(2,1)S(1)}, u32[]{:S(2)}, u32[]{:S(2)}) collective-permute-start(bf16[2,128,128]{2,1,0:T(8,128)(2,1)S(1)} %get-tuple-element.35), channel_id=1, source_target_pairs={{0,17},{1,16},{2,19},{3,18},{4,21},{5,20},{6,23},{7,22},{8,25},{9,... | collective-permute-start | bytes 196616 | tf_op jit(solution)/shard_map/ppermute | solution.py:274
  31.5 5.5 %collective-permute-start.13 = (bf16[2,128,128]{2,1,0:T(8,128)(2,1)S(1)}, bf16[2,128,128]{2,1,0:T(8,128)(2,1)S(1)}, u32[]{:S(2)}, u32[]{:S(2)}) collective-permute-start(bf16[2,128,128]{2,1,0:T(8,128)(2,1)S(1)} %get-tuple-element.36), channel_id=1, source_target_pairs={{0,25},{1,24},{2,27},{3,26},{4,29},{5,28},{6,31},{7,30},{8,1},{9,0... | collective-permute-start | bytes 196616 | tf_op jit(solution)/shard_map/ppermute | solution.py:274
  37.1 1.7 %collective-permute-start.14 = (bf16[7,128,128]{2,1,0:T(8,128)(2,1)S(1)}, bf16[7,128,128]{2,1,0:T(8,128)(2,1)S(1)}, u32[]{:S(2)}, u32[]{:S(2)}) collective-permute-start(bf16[7,128,128]{2,1,0:T(8,128)(2,1)S(1)} %shard_map.114), channel_id=1, source_target_pairs={{0,1},{1,0},{2,3},{3,2},{4,5},{5,4},{6,7},{7,6},{8,9},{9,8},{10,11... | collective-permute-start | bytes 688136 | tf_op jit(solution)/shard_map/ppermute | solution.py:265

commit v13 on v12

--- a/solution.py
+++ b/solution.py
@@ -203,7 +203,7 @@
     rows = rows_of(1 - core_ref[0], adjacency_ref, size)
     total[...] = own_ref[...] + jnp.dot(blocks, rows, preferred_element_type=f32)
     grad = (grad_ref[...] + received_ref[chips].astype(f32)).astype(bf16)
-    for step, piece in zip((1, 2, 3, 0), pieces):
+    for step, piece in zip((2, 1, 3, 0), pieces):
         owner = lax.rem(row_ref[0] + step, len(pieces))
         piece[0] = total[:, block_at(owner, size)].astype(bf16)
         piece[1] = grad
@@ -223,8 +223,8 @@
     count, size = len(pieces), own_ref.shape[1]
     total = sum(received_ref[index].astype(f32) for index in range(count)) + own_ref[0].astype(f32)
     input_ref[...] = (total * deg_ref[...].astype(f32).reshape(1, -1)).T.astype(bf16)
-    for index, piece in enumerate(pieces):
-        plane = lax.rem(row_ref[0] + count - index, count + 1)
+    for index, (step, piece) in enumerate(zip((2, 1, 3), pieces)):
+        plane = lax.rem(row_ref[0] + count + 1 - step, count + 1)
         ordered[0, plane] = received_ref[count + index]
         ordered[1, plane] = piece[1]
     ordered[0, row_ref[0]] = own_ref[1]
@@ -396,7 +396,7 @@
     )
     own_piece = pieces[-1]
     arrived = [
-        crossed(piece, row_shards, col_shards, step) for step, piece in zip((1, 2, 3), pieces)
+        crossed(piece, row_shards, col_shards, step) for step, piece in zip((2, 1, 3), pieces)
     ]
     packed = call(
         pack_pieces,

time: 39.7 us -> 40.5 us (1.020)
  starting transfers between devices: 17.2 us -> 17.7 us
    ppermute x3, starting transfers between devices: 3.69 us -> 4.61 us  [crossed(): return lax.ppermute(block, ('row', 'col'), pairs)]
  transfers between devices with their start and end apart: 15 -> 15, of which waited for: 12 -> 11; matrix products, arithmetic and copies ran while one was open for 0% -> 0% of each run, Pallas kernels for 5% -> 5%
where the time goes in v13:
time: 40.5 us; the launch traced here: 40.3 us
  starting transfers between devices  17.7 us (44%)
  waiting for transfers between devices  16.4 us (40%)
  Pallas kernels  4.04 us (10%)
  between operations  1.46 us (4%)
  local copies, waits for them, and re-layouts  0.69 us (2%)
    ppermute x12, starting transfers between devices, exchange(): lax.ppermute(block, axis, [(shard, shard ^ distance) for shard in range(s...  13.1 us
    ppermute x12, waiting for transfers between devices, exchange(): lax.ppermute(block, axis, [(shard, shard ^ distance) for shard in range(s...  12.2 us
    ppermute x3, starting transfers between devices, crossed(): return lax.ppermute(block, ('row', 'col'), pairs)  4.61 us
    ppermute x3, waiting for transfers between devices, crossed(): return lax.ppermute(block, ('row', 'col'), pairs)  4.26 us
    pallas_call x12, Pallas kernels, call(): pl.pallas_call(body, out_shape=out_shape, in_specs=[SMEM] * len(scalars)...  3.14 us
    pallas_call x1, Pallas kernels, on_device(): pl.pallas_call(build_adjacency, out_shape=struct((col_shards * size, row_...  0.91 us
  transfers between devices with their start and end apart: 15, of which 11 were waited for; matrix products, arithmetic and copies ran while one was open for 0% of the time, Pallas kernels for 5%

profile of v13, /device:TPU:0, one launch (start us, length us, event | category | flops | bytes accessed | tf_op | source)
XLA Modules:
  0.0 40.3 jit_solution(7546059351191295151)
XLA Ops:
  0.6 0.0 copy-start.5
  0.6 0.0 copy-start.4
  0.7 0.0 copy-start.3
  0.7 0.0 copy-start.6
  0.7 0.7 %copy-done.6 = bf16[128]{0:T(256)(128)(2,1)S(1)} copy-done((bf16[128]{0:T(256)(128)(2,1)S(1)}, bf16[128]{0:T(256)(128)(2,1)}, u32[]{:S(2)}) %copy-start.6) | copy-done | bytes 280
  1.3 0.0 copy-start
  1.3 0.1 shard_map.103.column_ref
  1.5 0.0 copy-done.5
  1.5 0.0 copy-done.4
  1.5 0.0 copy-done.3
  1.5 4.1 %collective-permute-start.2 = (bf16[128,128]{1,0:T(8,128)(2,1)S(1)}, bf16[128,128]{1,0:T(8,128)(2,1)S(1)}, u32[]{:S(2)}, u32[]{:S(2)}) collective-permute-start(bf16[128,128]{1,0:T(8,128)(2,1)S(1)} %shard_map.104.after_ref.refs_0_), channel_id=1, source_target_pairs={{0,16},{8,24},{16,0},{24,8},{1,17},{9,25},{17,1},{25,9},{2,18},{10... | collective-permute-start | bytes 98312 | tf_op jit(solution)/shard_map/ppermute | solution.py:265
  5.6 1.3 %collective-permute-start.1 = (bf16[128,128]{1,0:T(8,128)(2,1)S(1)}, bf16[128,128]{1,0:T(8,128)(2,1)S(1)}, u32[]{:S(2)}, u32[]{:S(2)}) collective-permute-start(bf16[128,128]{1,0:T(8,128)(2,1)S(1)} %shard_map.104.after_ref.refs_0_), channel_id=1, source_target_pairs={{0,24},{8,16},{16,8},{24,0},{1,25},{9,17},{17,9},{25,1},{2,26},{10... | collective-permute-start | bytes 98312 | tf_op jit(solution)/shard_map/ppermute | solution.py:265
  7.0 0.2 collective-permute-start
  7.8 0.0 copy-done
  7.9 0.9 %shard_map.105.adjacency_ref = bf16[1024,512]{1,0:T(8,128)(2,1)S(1)} custom-call(s32[1,1]{1,0:T(1,128)S(6)} %copy.11.count_ref, s32[1,1,8]{2,1,0:T(1,128)S(1)} %copy-done.4, s32[1,1,8]{2,1,0:T(1,128)S(1)} %copy-done.5, s32[1,1,8,32,256]{4,3,2,1,0:T(8,128)S(1)} %copy-done, bf16[128,128]{1,0:T(8,128)(2,1)S(1)} %shard_map.104.after_ref.refs_0_), custom_call_target="tpu_custom_call" | custom-call | flops 1048576 | bytes 1048576 | tf_op jit(solution)/shard_map/pallas_call | solution.py:337
  8.8 0.0 collective-permute-done.2.refs_3_
  8.8 2.5 %collective-permute-done.1.refs_2_ = bf16[128,128]{1,0:T(8,128)(2,1)S(1)} collective-permute-done((bf16[128,128]{1,0:T(8,128)(2,1)S(1)}, bf16[128,128]{1,0:T(8,128)(2,1)S(1)}, u32[]{:S(2)}, u32[]{:S(2)}) %collective-permute-start.1) | collective-permute-done | bytes 32800 | tf_op jit(solution)/shard_map/ppermute | solution.py:265
  11.3 0.0 collective-permute-done.refs_1_
  11.3 0.3 shard_map.106
  11.6 0.1 collective-permute-start.3
  11.7 0.3 shard_map.107.mine_ref
  12.0 1.0 %collective-permute-done.3.received_ref = bf16[4,128,128]{2,1,0:T(8,128)(2,1)S(1)} collective-permute-done((bf16[4,128,128]{2,1,0:T(8,128)(2,1)S(1)}, bf16[4,128,128]{2,1,0:T(8,128)(2,1)S(1)}, u32[]{:S(2)}, u32[]{:S(2)}) %collective-permute-start.3) | collective-permute-done | bytes 131104 | tf_op jit(solution)/shard_map/ppermute | solution.py:265
  13.1 0.0 copy-start.1
  13.1 0.0 copy-start.2
  13.1 2.5 %collective-permute-start.4 = (bf16[128,128]{1,0:T(8,128)(2,1)S(1)}, bf16[128,128]{1,0:T(8,128)(2,1)S(1)}, u32[]{:S(2)}, u32[]{:S(2)}) collective-permute-start(bf16[128,128]{1,0:T(8,128)(2,1)S(1)} %get-tuple-element.24), channel_id=1, source_target_pairs={{0,6},{1,7},{2,4},{3,5},{4,2},{5,3},{6,0},{7,1},{8,14},{9,15},{10,... | collective-permute-start | bytes 98312 | tf_op jit(solution)/shard_map/ppermute | solution.py:265
  15.6 0.5 %collective-permute-start.5 = (bf16[128,128]{1,0:T(8,128)(2,1)S(1)}, bf16[128,128]{1,0:T(8,128)(2,1)S(1)}, u32[]{:S(2)}, u32[]{:S(2)}) collective-permute-start(bf16[128,128]{1,0:T(8,128)(2,1)S(1)} %get-tuple-element.25), channel_id=1, source_target_pairs={{0,4},{1,5},{2,6},{3,7},{4,0},{5,1},{6,2},{7,3},{8,12},{9,13},{10,... | collective-permute-start | bytes 98312 | tf_op jit(solution)/shard_map/ppermute | solution.py:265
  16.1 0.0 copy-start.7
  16.1 0.5 %collective-permute-start.6 = (bf16[128,128]{1,0:T(8,128)(2,1)S(1)}, bf16[128,128]{1,0:T(8,128)(2,1)S(1)}, u32[]{:S(2)}, u32[]{:S(2)}) collective-permute-start(bf16[128,128]{1,0:T(8,128)(2,1)S(1)} %get-tuple-element.26), channel_id=1, source_target_pairs={{0,2},{1,3},{2,0},{3,1},{4,6},{5,7},{6,4},{7,5},{8,10},{9,11},{10,... | collective-permute-start | bytes 98312 | tf_op jit(solution)/shard_map/ppermute | solution.py:265
  16.6 1.3 %collective-permute-done.4.refs_0_ = bf16[128,128]{1,0:T(8,128)(2,1)S(1)} collective-permute-done((bf16[128,128]{1,0:T(8,128)(2,1)S(1)}, bf16[128,128]{1,0:T(8,128)(2,1)S(1)}, u32[]{:S(2)}, u32[]{:S(2)}) %collective-permute-start.4) | collective-permute-done | bytes 32800 | tf_op jit(solution)/shard_map/ppermute | solution.py:265
  18.0 1.5 %collective-permute-done.5.refs_1_ = bf16[128,128]{1,0:T(8,128)(2,1)S(1)} collective-permute-done((bf16[128,128]{1,0:T(8,128)(2,1)S(1)}, bf16[128,128]{1,0:T(8,128)(2,1)S(1)}, u32[]{:S(2)}, u32[]{:S(2)}) %collective-permute-start.5) | collective-permute-done | bytes 32800 | tf_op jit(solution)/shard_map/ppermute | solution.py:265
  19.5 0.5 %collective-permute-done.6.refs_2_ = bf16[128,128]{1,0:T(8,128)(2,1)S(1)} collective-permute-done((bf16[128,128]{1,0:T(8,128)(2,1)S(1)}, bf16[128,128]{1,0:T(8,128)(2,1)S(1)}, u32[]{:S(2)}, u32[]{:S(2)}) %collective-permute-start.6) | collective-permute-done | bytes 32800 | tf_op jit(solution)/shard_map/ppermute | solution.py:265
  20.0 0.0 copy-done.1
  20.0 0.0 copy-done.2
  20.0 0.0 copy-done.7
  20.0 0.4 shard_map.109
  20.4 1.6 %collective-permute-start.9 = (bf16[3,128,128]{2,1,0:T(8,128)(2,1)S(1)}, bf16[3,128,128]{2,1,0:T(8,128)(2,1)S(1)}, u32[]{:S(2)}, u32[]{:S(2)}) collective-permute-start(bf16[3,128,128]{2,1,0:T(8,128)(2,1)S(1)} %get-tuple-element.29.refs_0_), channel_id=1, source_target_pairs={{0,6},{1,7},{2,4},{3,5},{4,2},{5,3},{6,0},{7,1},{8,14},{9,15},{10,... | collective-permute-start | bytes 294920 | tf_op jit(solution)/shard_map/ppermute | solution.py:265
  22.0 0.5 %collective-permute-start.8 = (bf16[3,128,128]{2,1,0:T(8,128)(2,1)S(1)}, bf16[3,128,128]{2,1,0:T(8,128)(2,1)S(1)}, u32[]{:S(2)}, u32[]{:S(2)}) collective-permute-start(bf16[3,128,128]{2,1,0:T(8,128)(2,1)S(1)} %get-tuple-element.29.refs_0_), channel_id=1, source_target_pairs={{0,4},{1,5},{2,6},{3,7},{4,0},{5,1},{6,2},{7,3},{8,12},{9,13},{10,... | collective-permute-start | bytes 294920 | tf_op jit(solution)/shard_map/ppermute | solution.py:265
  22.5 1.5 %collective-permute-start.7 = (bf16[3,128,128]{2,1,0:T(8,128)(2,1)S(1)}, bf16[3,128,128]{2,1,0:T(8,128)(2,1)S(1)}, u32[]{:S(2)}, u32[]{:S(2)}) collective-permute-start(bf16[3,128,128]{2,1,0:T(8,128)(2,1)S(1)} %get-tuple-element.29.refs_0_), channel_id=1, source_target_pairs={{0,2},{1,3},{2,0},{3,1},{4,6},{5,7},{6,4},{7,5},{8,10},{9,11},{10,... | collective-permute-start | bytes 294920 | tf_op jit(solution)/shard_map/ppermute | solution.py:265
  24.0 0.6 %shard_map.110 = (bf16[128,256]{1,0:T(8,128)(2,1)}, f32[8,128]{1,0:T(8,128)S(1)}) custom-call(f32[128,256]{1,0:T(8,128)S(1)} %get-tuple-element.27.active_ref), custom_call_target="tpu_custom_call" | custom-call | flops 1048576 | bytes 1048576 | tf_op jit(solution)/shard_map/pallas_call | solution.py:25
  24.6 1.8 %collective-permute-done.9.refs_3_ = bf16[3,128,128]{2,1,0:T(8,128)(2,1)S(1)} collective-permute-done((bf16[3,128,128]{2,1,0:T(8,128)(2,1)S(1)}, bf16[3,128,128]{2,1,0:T(8,128)(2,1)S(1)}, u32[]{:S(2)}, u32[]{:S(2)}) %collective-permute-start.9) | collective-permute-done | bytes 98336 | tf_op jit(solution)/shard_map/ppermute | solution.py:265
  26.4 0.9 %collective-permute-done.8.refs_2_ = bf16[3,128,128]{2,1,0:T(8,128)(2,1)S(1)} collective-permute-done((bf16[3,128,128]{2,1,0:T(8,128)(2,1)S(1)}, bf16[3,128,128]{2,1,0:T(8,128)(2,1)S(1)}, u32[]{:S(2)}, u32[]{:S(2)}) %collective-permute-start.8) | collective-permute-done | bytes 98336 | tf_op jit(solution)/shard_map/ppermute | solution.py:265
  27.3 0.0 collective-permute-done.7.refs_1_
  27.3 0.1 shard_map.111
  27.4 0.1 collective-permute-start.10
  27.5 0.2 shard_map.112.own_ref
  27.7 1.1 %collective-permute-done.10.received_ref = bf16[5,128,128]{2,1,0:T(8,128)(2,1)S(1)} collective-permute-done((bf16[5,128,128]{2,1,0:T(8,128)(2,1)S(1)}, bf16[5,128,128]{2,1,0:T(8,128)(2,1)S(1)}, u32[]{:S(2)}, u32[]{:S(2)}) %collective-permute-start.10) | collective-permute-done | bytes 163872 | tf_op jit(solution)/shard_map/ppermute | solution.py:265
  28.9 0.3 shard_map.113
  29.2 1.0 %collective-permute-start.11 = (bf16[2,128,128]{2,1,0:T(8,128)(2,1)S(1)}, bf16[2,128,128]{2,1,0:T(8,128)(2,1)S(1)}, u32[]{:S(2)}, u32[]{:S(2)}) collective-permute-start(bf16[2,128,128]{2,1,0:T(8,128)(2,1)S(1)} %get-tuple-element.34), channel_id=1, source_target_pairs={{0,17},{1,16},{2,19},{3,18},{4,21},{5,20},{6,23},{7,22},{8,25},{9,... | collective-permute-start | bytes 196616 | tf_op jit(solution)/shard_map/ppermute | solution.py:274
  30.2 1.3 %collective-permute-start.12 = (bf16[2,128,128]{2,1,0:T(8,128)(2,1)S(1)}, bf16[2,128,128]{2,1,0:T(8,128)(2,1)S(1)}, u32[]{:S(2)}, u32[]{:S(2)}) collective-permute-start(bf16[2,128,128]{2,1,0:T(8,128)(2,1)S(1)} %get-tuple-element.35), channel_id=1, source_target_pairs={{0,9},{1,8},{2,11},{3,10},{4,13},{5,12},{6,15},{7,14},{8,17},{9,16... | collective-permute-start | bytes 196616 | tf_op jit(solution)/shard_map/ppermute | solution.py:274
  31.5 2.2 %collective-permute-start.13 = (bf16[2,128,128]{2,1,0:T(8,128)(2,1)S(1)}, bf16[2,128,128]{2,1,0:T(8,128)(2,1)S(1)}, u32[]{:S(2)}, u32[]{:S(2)}) collective-permute-start(bf16[2,128,128]{2,1,0:T(8,128)(2,1)S(1)} %get-tuple-element.36), channel_id=1, source_target_pairs={{0,25},{1,24},{2,27},{3,26},{4,29},{5,28},{6,31},{7,30},{8,1},{9,0... | collective-permute-start | bytes 196616 | tf_op jit(solution)/shard_map/ppermute | solution.py:274
  33.8 2.7 %collective-permute-done.11.refs_0_ = bf16[2,128,128]{2,1,0:T(8,128)(2,1)S(1)} collective-permute-done((bf16[2,128,128]{2,1,0:T(8,128)(2,1)S(1)}, bf16[2,128,128]{2,1,0:T(8,128)(2,1)S(1)}, u32[]{:S(2)}, u32[]{:S(2)}) %collective-permute-start.11) | collective-permute-done | bytes 65568 | tf_op jit(solution)/shard_map/ppermute | solution.py:274
  36.5 0.0 collective-permute-done.12.refs_1_
  36.5 1.5 %collective-permute-done.13.refs_2_ = bf16[2,128,128]{2,1,0:T(8,128)(2,1)S(1)} collective-permute-done((bf16[2,128,128]{2,1,0:T(8,128)(2,1)S(1)}, bf16[2,128,128]{2,1,0:T(8,128)(2,1)S(1)}, u32[]{:S(2)}, u32[]{:S(2)}) %collective-permute-start.13) | collective-permute-done | bytes 65568 | tf_op jit(solution)/shard_map/ppermute | solution.py:274
  38.1 0.2 collective-permute-start.14
  38.2 1.4 %collective-permute-done.14.received_ref = bf16[7,128,128]{2,1,0:T(8,128)(2,1)S(1)} collective-permute-done((bf16[7,128,128]{2,1,0:T(8,128)(2,1)S(1)}, bf16[7,128,128]{2,1,0:T(8,128)(2,1)S(1)}, u32[]{:S(2)}, u32[]{:S(2)}) %collective-permute-start.14) | collective-permute-done | bytes 229408 | tf_op jit(solution)/shard_map/ppermute | solution.py:265
  39.6 0.7 %shard_map.115 = (bf16[128,128]{1,0:T(8,128)(2,1)}, f32[128,256]{1,0:T(8,128)}) custom-call(s32[1]{0:T(128)} %bitcast.2.row_ref, s32[1]{0:T(128)} %bitcast.1.core_ref, bf16[128]{0:T(256)(128)(2,1)S(1)} %copy-done.7, bf16[2,128,128]{2,1,0:T(8,128)(2,1)S(1)} %get-tuple-element.33.refs_3_.own_ref, ...), custom_call_target="tpu_custom_call" | custom-call | flops 1048576 | bytes 1048576 | tf_op jit(solution)/shard_map/pallas_call | solution.py:25
  (3 shorter events, 0.1 us)
Async XLA Ops:
  0.6 0.8 %copy-start.5 = (s32[1,1,8]{2,1,0:T(1,128)S(1)}, s32[1,1,8]{2,1,0:T(1,128)}, u32[]{:S(2)}) copy-start(s32[1,1,8]{2,1,0:T(1,128)} %cols_ref.3) | copy-start | bytes 100
  0.6 0.8 %copy-start.4 = (s32[1,1,8]{2,1,0:T(1,128)S(1)}, s32[1,1,8]{2,1,0:T(1,128)}, u32[]{:S(2)}) copy-start(s32[1,1,8]{2,1,0:T(1,128)} %rows_ref.3) | copy-start | bytes 100
  0.7 0.8 %copy-start.3 = (bf16[128,128]{1,0:T(8,128)(2,1)S(1)}, bf16[128,128]{1,0:T(8,128)(2,1)}, u32[]{:S(2)}) copy-start(bf16[128,128]{1,0:T(8,128)(2,1)} %features_ref.1) | copy-start | bytes 98308
  0.7 0.7 %copy-start.6 = (bf16[128]{0:T(256)(128)(2,1)S(1)}, bf16[128]{0:T(256)(128)(2,1)}, u32[]{:S(2)}) copy-start(bf16[128]{0:T(256)(128)(2,1)} %deg_ref.5) | copy-start | bytes 772
  1.3 6.5 %copy-start = (s32[1,1,8,32,256]{4,3,2,1,0:T(8,128)S(1)}, s32[1,1,8,32,256]{4,3,2,1,0:T(8,128)}, u32[]{:S(2)}) copy-start(s32[1,1,8,32,256]{4,3,2,1,0:T(8,128)} %bits_ref.1) | copy-start | bytes 786436
  1.5 7.3 %collective-permute-start.2 = (bf16[128,128]{1,0:T(8,128)(2,1)S(1)}, bf16[128,128]{1,0:T(8,128)(2,1)S(1)}, u32[]{:S(2)}, u32[]{:S(2)}) collective-permute-start(bf16[128,128]{1,0:T(8,128)(2,1)S(1)} %shard_map.104.after_ref.refs_0_), channel_id=1, source_target_pairs={{0,16},{8,24},{16,0},{24,8},{1,17},{9,25},{17,1},{25,9},{2,18},{10... | collective-permute-start | bytes 98312 | tf_op jit(solution)/shard_map/ppermute | solution.py:265
  5.6 5.7 %collective-permute-start.1 = (bf16[128,128]{1,0:T(8,128)(2,1)S(1)}, bf16[128,128]{1,0:T(8,128)(2,1)S(1)}, u32[]{:S(2)}, u32[]{:S(2)}) collective-permute-start(bf16[128,128]{1,0:T(8,128)(2,1)S(1)} %shard_map.104.after_ref.refs_0_), channel_id=1, source_target_pairs={{0,24},{8,16},{16,8},{24,0},{1,25},{9,17},{17,9},{25,1},{2,26},{10... | collective-permute-start | bytes 98312 | tf_op jit(solution)/shard_map/ppermute | solution.py:265
  7.0 4.4 %collective-permute-start = (bf16[128,128]{1,0:T(8,128)(2,1)S(1)}, bf16[128,128]{1,0:T(8,128)(2,1)S(1)}, u32[]{:S(2)}, u32[]{:S(2)}) collective-permute-start(bf16[128,128]{1,0:T(8,128)(2,1)S(1)} %shard_map.104.after_ref.refs_0_), channel_id=1, source_target_pairs={{0,8},{8,0},{16,24},{24,16},{1,9},{9,1},{17,25},{25,17},{2,10},{10... | collective-permute-start | bytes 98312 | tf_op jit(solution)/shard_map/ppermute | solution.py:265
  11.6 1.4 %collective-permute-start.3 = (bf16[4,128,128]{2,1,0:T(8,128)(2,1)S(1)}, bf16[4,128,128]{2,1,0:T(8,128)(2,1)S(1)}, u32[]{:S(2)}, u32[]{:S(2)}) collective-permute-start(bf16[4,128,128]{2,1,0:T(8,128)(2,1)S(1)} %get-tuple-element.22), channel_id=1, source_target_pairs={{0,1},{1,0},{2,3},{3,2},{4,5},{5,4},{6,7},{7,6},{8,9},{9,8},{10,11... | collective-permute-start | bytes 393224 | tf_op jit(solution)/shard_map/ppermute | solution.py:265
  13.1 7.0 %copy-start.1 = (bf16[128,256]{1,0:T(8,128)(2,1)S(1)}, bf16[128,256]{1,0:T(8,128)(2,1)}, u32[]{:S(2)}) copy-start(bf16[128,256]{1,0:T(8,128)(2,1)} %weight_ref.1) | copy-start | bytes 196612
  13.1 7.0 %copy-start.2 = (bf16[128,256]{1,0:T(8,128)(2,1)S(1)}, bf16[128,256]{1,0:T(8,128)(2,1)}, u32[]{:S(2)}) copy-start(bf16[128,256]{1,0:T(8,128)(2,1)} %cotangent_ref.1) | copy-start | bytes 196612
  13.1 4.9 %collective-permute-start.4 = (bf16[128,128]{1,0:T(8,128)(2,1)S(1)}, bf16[128,128]{1,0:T(8,128)(2,1)S(1)}, u32[]{:S(2)}, u32[]{:S(2)}) collective-permute-start(bf16[128,128]{1,0:T(8,128)(2,1)S(1)} %get-tuple-element.24), channel_id=1, source_target_pairs={{0,6},{1,7},{2,4},{3,5},{4,2},{5,3},{6,0},{7,1},{8,14},{9,15},{10,... | collective-permute-start | bytes 98312 | tf_op jit(solution)/shard_map/ppermute | solution.py:265
  15.6 3.9 %collective-permute-start.5 = (bf16[128,128]{1,0:T(8,128)(2,1)S(1)}, bf16[128,128]{1,0:T(8,128)(2,1)S(1)}, u32[]{:S(2)}, u32[]{:S(2)}) collective-permute-start(bf16[128,128]{1,0:T(8,128)(2,1)S(1)} %get-tuple-element.25), channel_id=1, source_target_pairs={{0,4},{1,5},{2,6},{3,7},{4,0},{5,1},{6,2},{7,3},{8,12},{9,13},{10,... | collective-permute-start | bytes 98312 | tf_op jit(solution)/shard_map/ppermute | solution.py:265
  16.1 3.9 %copy-start.7 = (bf16[128]{0:T(256)(128)(2,1)S(1)}, bf16[128]{0:T(256)(128)(2,1)}, u32[]{:S(2)}) copy-start(bf16[128]{0:T(256)(128)(2,1)} %deg_ref.5) | copy-start | bytes 772
  16.1 3.9 %collective-permute-start.6 = (bf16[128,128]{1,0:T(8,128)(2,1)S(1)}, bf16[128,128]{1,0:T(8,128)(2,1)S(1)}, u32[]{:S(2)}, u32[]{:S(2)}) collective-permute-start(bf16[128,128]{1,0:T(8,128)(2,1)S(1)} %get-tuple-element.26), channel_id=1, source_target_pairs={{0,2},{1,3},{2,0},{3,1},{4,6},{5,7},{6,4},{7,5},{8,10},{9,11},{10,... | collective-permute-start | bytes 98312 | tf_op jit(solution)/shard_map/ppermute | solution.py:265
  20.4 6.0 %collective-permute-start.9 = (bf16[3,128,128]{2,1,0:T(8,128)(2,1)S(1)}, bf16[3,128,128]{2,1,0:T(8,128)(2,1)S(1)}, u32[]{:S(2)}, u32[]{:S(2)}) collective-permute-start(bf16[3,128,128]{2,1,0:T(8,128)(2,1)S(1)} %get-tuple-element.29.refs_0_), channel_id=1, source_target_pairs={{0,6},{1,7},{2,4},{3,5},{4,2},{5,3},{6,0},{7,1},{8,14},{9,15},{10,... | collective-permute-start | bytes 294920 | tf_op jit(solution)/shard_map/ppermute | solution.py:265
  22.0 5.4 %collective-permute-start.8 = (bf16[3,128,128]{2,1,0:T(8,128)(2,1)S(1)}, bf16[3,128,128]{2,1,0:T(8,128)(2,1)S(1)}, u32[]{:S(2)}, u32[]{:S(2)}) collective-permute-start(bf16[3,128,128]{2,1,0:T(8,128)(2,1)S(1)} %get-tuple-element.29.refs_0_), channel_id=1, source_target_pairs={{0,4},{1,5},{2,6},{3,7},{4,0},{5,1},{6,2},{7,3},{8,12},{9,13},{10,... | collective-permute-start | bytes 294920 | tf_op jit(solution)/shard_map/ppermute | solution.py:265
  22.5 4.8 %collective-permute-start.7 = (bf16[3,128,128]{2,1,0:T(8,128)(2,1)S(1)}, bf16[3,128,128]{2,1,0:T(8,128)(2,1)S(1)}, u32[]{:S(2)}, u32[]{:S(2)}) collective-permute-start(bf16[3,128,128]{2,1,0:T(8,128)(2,1)S(1)} %get-tuple-element.29.refs_0_), channel_id=1, source_target_pairs={{0,2},{1,3},{2,0},{3,1},{4,6},{5,7},{6,4},{7,5},{8,10},{9,11},{10,... | collective-permute-start | bytes 294920 | tf_op jit(solution)/shard_map/ppermute | solution.py:265
  27.4 1.5 %collective-permute-start.10 = (bf16[5,128,128]{2,1,0:T(8,128)(2,1)S(1)}, bf16[5,128,128]{2,1,0:T(8,128)(2,1)S(1)}, u32[]{:S(2)}, u32[]{:S(2)}) collective-permute-start(bf16[5,128,128]{2,1,0:T(8,128)(2,1)S(1)} %get-tuple-element.31.joined_ref), channel_id=1, source_target_pairs={{0,1},{1,0},{2,3},{3,2},{4,5},{5,4},{6,7},{7,6},{8,9},{9,8},{10,11... | collective-permute-start | bytes 491528 | tf_op jit(solution)/shard_map/ppermute | solution.py:265
  29.2 7.4 %collective-permute-start.11 = (bf16[2,128,128]{2,1,0:T(8,128)(2,1)S(1)}, bf16[2,128,128]{2,1,0:T(8,128)(2,1)S(1)}, u32[]{:S(2)}, u32[]{:S(2)}) collective-permute-start(bf16[2,128,128]{2,1,0:T(8,128)(2,1)S(1)} %get-tuple-element.34), channel_id=1, source_target_pairs={{0,17},{1,16},{2,19},{3,18},{4,21},{5,20},{6,23},{7,22},{8,25},{9,... | collective-permute-start | bytes 196616 | tf_op jit(solution)/shard_map/ppermute | solution.py:274
  30.2 6.3 %collective-permute-start.12 = (bf16[2,128,128]{2,1,0:T(8,128)(2,1)S(1)}, bf16[2,128,128]{2,1,0:T(8,128)(2,1)S(1)}, u32[]{:S(2)}, u32[]{:S(2)}) collective-permute-start(bf16[2,128,128]{2,1,0:T(8,128)(2,1)S(1)} %get-tuple-element.35), channel_id=1, source_target_pairs={{0,9},{1,8},{2,11},{3,10},{4,13},{5,12},{6,15},{7,14},{8,17},{9,16... | collective-permute-start | bytes 196616 | tf_op jit(solution)/shard_map/ppermute | solution.py:274
  31.5 6.5 %collective-permute-start.13 = (bf16[2,128,128]{2,1,0:T(8,128)(2,1)S(1)}, bf16[2,128,128]{2,1,0:T(8,128)(2,1)S(1)}, u32[]{:S(2)}, u32[]{:S(2)}) collective-permute-start(bf16[2,128,128]{2,1,0:T(8,128)(2,1)S(1)} %get-tuple-element.36), channel_id=1, source_target_pairs={{0,25},{1,24},{2,27},{3,26},{4,29},{5,28},{6,31},{7,30},{8,1},{9,0... | collective-permute-start | bytes 196616 | tf_op jit(solution)/shard_map/ppermute | solution.py:274
  38.1 1.6 %collective-permute-start.14 = (bf16[7,128,128]{2,1,0:T(8,128)(2,1)S(1)}, bf16[7,128,128]{2,1,0:T(8,128)(2,1)S(1)}, u32[]{:S(2)}, u32[]{:S(2)}) collective-permute-start(bf16[7,128,128]{2,1,0:T(8,128)(2,1)S(1)} %shard_map.114), channel_id=1, source_target_pairs={{0,1},{1,0},{2,3},{3,2},{4,5},{5,4},{6,7},{7,6},{8,9},{9,8},{10,11... | collective-permute-start | bytes 688136 | tf_op jit(solution)/shard_map/ppermute | solution.py:265

commit v14 on v12

--- a/solution.py
+++ b/solution.py
@@ -115,8 +115,9 @@
 def forward_other(row_ref, core_ref, adjacency_ref, *refs):
     *blocks, source_ref, other_ref = refs
     size = blocks[0].shape[0]
-    for step, block in zip((0, 1, 3, 2), blocks):
-        source_ref[block_at(row_ref[0] ^ step, size), :] = block[...]
+    for step, block in enumerate(blocks):
+        owner = lax.rem(row_ref[0] + step, len(blocks))
+        source_ref[block_at(owner, size), :] = block[...]
     rows = rows_of(1 - core_ref[0], adjacency_ref, size)
     total = jnp.dot(rows, source_ref[...], preferred_element_type=f32)
     other_ref[...] = total.astype(bf16).reshape(other_ref.shape)
@@ -263,6 +264,10 @@
 
 def exchange(block, axis, shards, distance):
     return lax.ppermute(block, axis, [(shard, shard ^ distance) for shard in range(shards)])
+
+
+def shifted(block, axis, shards, step):
+    return lax.ppermute(block, axis, [(shard, (shard + step) % shards) for shard in range(shards)])
 
 
 def crossed(block, rows, cols, step):
@@ -343,7 +348,7 @@
         cost_estimate=pl.CostEstimate(flops=1 << 20, bytes_accessed=1 << 20, transcendentals=0),
     )(tile_count, tile_rows, tile_cols, tile_bits, scaled)
     far_first = (3, 2, 1)
-    blocks = [exchange(scaled, "row", row_shards, step) for step in (1, 3, 2)]
+    blocks = [shifted(scaled, "row", row_shards, step) for step in (3, 2, 1)]
     blocks.insert(0, scaled)
     source, other = call(
         forward_other,

time: 39.7 us -> 40.3 us (1.015)
  starting transfers between devices: 17.2 us -> 18.1 us
    ppermute x0 -> x3, starting transfers between devices: none -> 7.01 us  [shifted(): lax.ppermute(block, axis, [(shard, (shard + step) % shards) for shard in...]
    ppermute x12 -> x9, starting transfers between devices: 13.5 us -> 7.47 us  [exchange(): lax.ppermute(block, axis, [(shard, shard ^ distance) for shard in range(s...]
    ppermute x12 -> x9, waiting for transfers between devices: 11.9 us -> 9.59 us  [exchange(): lax.ppermute(block, axis, [(shard, shard ^ distance) for shard in range(s...]
    ppermute x3, waiting for transfers between devices: 4.21 us -> 5.23 us  [crossed(): return lax.ppermute(block, ('row', 'col'), pairs)]
    ppermute x0 -> x3, waiting for transfers between devices: none -> 0.97 us  [shifted(): lax.ppermute(block, axis, [(shard, (shard + step) % shards) for shard in...]
  transfers between devices with their start and end apart: 15 -> 15, of which waited for: 12 -> 11; matrix products, arithmetic and copies ran while one was open for 0% -> 0% of each run, Pallas kernels for 5% -> 5%
where the time goes in v14:
time: 40.3 us; the launch traced here: 40.1 us
  starting transfers between devices  18.1 us (45%)
  waiting for transfers between devices  15.8 us (39%)
  Pallas kernels  4.05 us (10%)
  between operations  1.47 us (4%)
  local copies, waits for them, and re-layouts  0.69 us (2%)
    ppermute x9, waiting for transfers between devices, exchange(): lax.ppermute(block, axis, [(shard, shard ^ distance) for shard in range(s...  9.59 us
    ppermute x9, starting transfers between devices, exchange(): lax.ppermute(block, axis, [(shard, shard ^ distance) for shard in range(s...  7.47 us
    ppermute x3, starting transfers between devices, shifted(): lax.ppermute(block, axis, [(shard, (shard + step) % shards) for shard in...  7.01 us
    ppermute x3, waiting for transfers between devices, crossed(): return lax.ppermute(block, ('row', 'col'), pairs)  5.23 us
    ppermute x3, starting transfers between devices, crossed(): return lax.ppermute(block, ('row', 'col'), pairs)  3.59 us
    pallas_call x12, Pallas kernels, call(): pl.pallas_call(body, out_shape=out_shape, in_specs=[SMEM] * len(scalars)...  3.14 us
    ppermute x3, waiting for transfers between devices, shifted(): lax.ppermute(block, axis, [(shard, (shard + step) % shards) for shard in...  0.97 us
    pallas_call x1, Pallas kernels, on_device(): pl.pallas_call(build_adjacency, out_shape=struct((col_shards * size, row_...  0.91 us
  transfers between devices with their start and end apart: 15, of which 11 were waited for; matrix products, arithmetic and copies ran while one was open for 0% of the time, Pallas kernels for 5%

profile of v14, /device:TPU:0, one launch (start us, length us, event | category | flops | bytes accessed | tf_op | source)
XLA Modules:
  0.0 40.1 jit_solution(18225634895411528815)
XLA Ops:
  0.6 0.0 copy-start.5
  0.6 0.0 copy-start.4
  0.7 0.0 copy-start.3
  0.7 0.0 copy-start.6
  0.7 0.7 %copy-done.6 = bf16[128]{0:T(256)(128)(2,1)S(1)} copy-done((bf16[128]{0:T(256)(128)(2,1)S(1)}, bf16[128]{0:T(256)(128)(2,1)}, u32[]{:S(2)}) %copy-start.6) | copy-done | bytes 280
  1.3 0.0 copy-start
  1.3 0.1 shard_map.103.column_ref
  1.5 0.0 copy-done.5
  1.5 0.0 copy-done.4
  1.5 0.0 copy-done.3
  1.5 3.1 %collective-permute-start.2 = (bf16[128,128]{1,0:T(8,128)(2,1)S(1)}, bf16[128,128]{1,0:T(8,128)(2,1)S(1)}, u32[]{:S(2)}, u32[]{:S(2)}) collective-permute-start(bf16[128,128]{1,0:T(8,128)(2,1)S(1)} %shard_map.104.after_ref.refs_0_), channel_id=1, source_target_pairs={{0,8},{8,16},{16,24},{24,0},{1,9},{9,17},{17,25},{25,1},{2,10},{10... | collective-permute-start | bytes 98312 | tf_op jit(solution)/shard_map/ppermute | solution.py:270
  4.6 2.6 %collective-permute-start.1 = (bf16[128,128]{1,0:T(8,128)(2,1)S(1)}, bf16[128,128]{1,0:T(8,128)(2,1)S(1)}, u32[]{:S(2)}, u32[]{:S(2)}) collective-permute-start(bf16[128,128]{1,0:T(8,128)(2,1)S(1)} %shard_map.104.after_ref.refs_0_), channel_id=1, source_target_pairs={{0,16},{8,24},{16,0},{24,8},{1,17},{9,25},{17,1},{25,9},{2,18},{10... | collective-permute-start | bytes 98312 | tf_op jit(solution)/shard_map/ppermute | solution.py:270
  7.2 1.3 %collective-permute-start = (bf16[128,128]{1,0:T(8,128)(2,1)S(1)}, bf16[128,128]{1,0:T(8,128)(2,1)S(1)}, u32[]{:S(2)}, u32[]{:S(2)}) collective-permute-start(bf16[128,128]{1,0:T(8,128)(2,1)S(1)} %shard_map.104.after_ref.refs_0_), channel_id=1, source_target_pairs={{0,24},{8,0},{16,8},{24,16},{1,25},{9,1},{17,9},{25,17},{2,26},{10... | collective-permute-start | bytes 98312 | tf_op jit(solution)/shard_map/ppermute | solution.py:270
  9.2 0.0 copy-done
  9.2 0.9 %shard_map.105.adjacency_ref = bf16[1024,512]{1,0:T(8,128)(2,1)S(1)} custom-call(s32[1,1]{1,0:T(1,128)S(6)} %copy.11.count_ref, s32[1,1,8]{2,1,0:T(1,128)S(1)} %copy-done.4, s32[1,1,8]{2,1,0:T(1,128)S(1)} %copy-done.5, s32[1,1,8,32,256]{4,3,2,1,0:T(8,128)S(1)} %copy-done, bf16[128,128]{1,0:T(8,128)(2,1)S(1)} %shard_map.104.after_ref.refs_0_), custom_call_target="tpu_custom_call" | custom-call | flops 1048576 | bytes 1048576 | tf_op jit(solution)/shard_map/pallas_call | solution.py:342
  10.1 0.0 collective-permute-done.2.refs_3_
  10.1 0.0 collective-permute-done.1.refs_2_
  10.1 1.0 %collective-permute-done.refs_1_ = bf16[128,128]{1,0:T(8,128)(2,1)S(1)} collective-permute-done((bf16[128,128]{1,0:T(8,128)(2,1)S(1)}, bf16[128,128]{1,0:T(8,128)(2,1)S(1)}, u32[]{:S(2)}, u32[]{:S(2)}) %collective-permute-start) | collective-permute-done | bytes 32800 | tf_op jit(solution)/shard_map/ppermute | solution.py:270
  11.1 0.3 shard_map.106
  11.4 0.1 collective-permute-start.3
  11.5 0.3 shard_map.107.mine_ref
  11.8 1.0 %collective-permute-done.3.received_ref = bf16[4,128,128]{2,1,0:T(8,128)(2,1)S(1)} collective-permute-done((bf16[4,128,128]{2,1,0:T(8,128)(2,1)S(1)}, bf16[4,128,128]{2,1,0:T(8,128)(2,1)S(1)}, u32[]{:S(2)}, u32[]{:S(2)}) %collective-permute-start.3) | collective-permute-done | bytes 131104 | tf_op jit(solution)/shard_map/ppermute | solution.py:266
  12.8 0.0 copy-start.1
  12.8 0.0 copy-start.2
  12.9 2.5 %collective-permute-start.4 = (bf16[128,128]{1,0:T(8,128)(2,1)S(1)}, bf16[128,128]{1,0:T(8,128)(2,1)S(1)}, u32[]{:S(2)}, u32[]{:S(2)}) collective-permute-start(bf16[128,128]{1,0:T(8,128)(2,1)S(1)} %get-tuple-element.24), channel_id=1, source_target_pairs={{0,6},{1,7},{2,4},{3,5},{4,2},{5,3},{6,0},{7,1},{8,14},{9,15},{10,... | collective-permute-start | bytes 98312 | tf_op jit(solution)/shard_map/ppermute | solution.py:266
  15.4 0.5 %collective-permute-start.5 = (bf16[128,128]{1,0:T(8,128)(2,1)S(1)}, bf16[128,128]{1,0:T(8,128)(2,1)S(1)}, u32[]{:S(2)}, u32[]{:S(2)}) collective-permute-start(bf16[128,128]{1,0:T(8,128)(2,1)S(1)} %get-tuple-element.25), channel_id=1, source_target_pairs={{0,4},{1,5},{2,6},{3,7},{4,0},{5,1},{6,2},{7,3},{8,12},{9,13},{10,... | collective-permute-start | bytes 98312 | tf_op jit(solution)/shard_map/ppermute | solution.py:266
  15.9 0.0 copy-start.7
  15.9 0.5 %collective-permute-start.6 = (bf16[128,128]{1,0:T(8,128)(2,1)S(1)}, bf16[128,128]{1,0:T(8,128)(2,1)S(1)}, u32[]{:S(2)}, u32[]{:S(2)}) collective-permute-start(bf16[128,128]{1,0:T(8,128)(2,1)S(1)} %get-tuple-element.26), channel_id=1, source_target_pairs={{0,2},{1,3},{2,0},{3,1},{4,6},{5,7},{6,4},{7,5},{8,10},{9,11},{10,... | collective-permute-start | bytes 98312 | tf_op jit(solution)/shard_map/ppermute | solution.py:266
  16.4 1.3 %collective-permute-done.4.refs_0_ = bf16[128,128]{1,0:T(8,128)(2,1)S(1)} collective-permute-done((bf16[128,128]{1,0:T(8,128)(2,1)S(1)}, bf16[128,128]{1,0:T(8,128)(2,1)S(1)}, u32[]{:S(2)}, u32[]{:S(2)}) %collective-permute-start.4) | collective-permute-done | bytes 32800 | tf_op jit(solution)/shard_map/ppermute | solution.py:266
  17.7 1.5 %collective-permute-done.5.refs_1_ = bf16[128,128]{1,0:T(8,128)(2,1)S(1)} collective-permute-done((bf16[128,128]{1,0:T(8,128)(2,1)S(1)}, bf16[128,128]{1,0:T(8,128)(2,1)S(1)}, u32[]{:S(2)}, u32[]{:S(2)}) %collective-permute-start.5) | collective-permute-done | bytes 32800 | tf_op jit(solution)/shard_map/ppermute | solution.py:266
  19.3 0.5 %collective-permute-done.6.refs_2_ = bf16[128,128]{1,0:T(8,128)(2,1)S(1)} collective-permute-done((bf16[128,128]{1,0:T(8,128)(2,1)S(1)}, bf16[128,128]{1,0:T(8,128)(2,1)S(1)}, u32[]{:S(2)}, u32[]{:S(2)}) %collective-permute-start.6) | collective-permute-done | bytes 32800 | tf_op jit(solution)/shard_map/ppermute | solution.py:266
  19.8 0.0 copy-done.1
  19.8 0.0 copy-done.2
  19.8 0.0 copy-done.7
  19.8 0.4 shard_map.109
  20.2 1.6 %collective-permute-start.9 = (bf16[3,128,128]{2,1,0:T(8,128)(2,1)S(1)}, bf16[3,128,128]{2,1,0:T(8,128)(2,1)S(1)}, u32[]{:S(2)}, u32[]{:S(2)}) collective-permute-start(bf16[3,128,128]{2,1,0:T(8,128)(2,1)S(1)} %get-tuple-element.29.refs_0_), channel_id=1, source_target_pairs={{0,6},{1,7},{2,4},{3,5},{4,2},{5,3},{6,0},{7,1},{8,14},{9,15},{10,... | collective-permute-start | bytes 294920 | tf_op jit(solution)/shard_map/ppermute | solution.py:266
  21.7 0.5 %collective-permute-start.8 = (bf16[3,128,128]{2,1,0:T(8,128)(2,1)S(1)}, bf16[3,128,128]{2,1,0:T(8,128)(2,1)S(1)}, u32[]{:S(2)}, u32[]{:S(2)}) collective-permute-start(bf16[3,128,128]{2,1,0:T(8,128)(2,1)S(1)} %get-tuple-element.29.refs_0_), channel_id=1, source_target_pairs={{0,4},{1,5},{2,6},{3,7},{4,0},{5,1},{6,2},{7,3},{8,12},{9,13},{10,... | collective-permute-start | bytes 294920 | tf_op jit(solution)/shard_map/ppermute | solution.py:266
  22.2 1.5 %collective-permute-start.7 = (bf16[3,128,128]{2,1,0:T(8,128)(2,1)S(1)}, bf16[3,128,128]{2,1,0:T(8,128)(2,1)S(1)}, u32[]{:S(2)}, u32[]{:S(2)}) collective-permute-start(bf16[3,128,128]{2,1,0:T(8,128)(2,1)S(1)} %get-tuple-element.29.refs_0_), channel_id=1, source_target_pairs={{0,2},{1,3},{2,0},{3,1},{4,6},{5,7},{6,4},{7,5},{8,10},{9,11},{10,... | collective-permute-start | bytes 294920 | tf_op jit(solution)/shard_map/ppermute | solution.py:266
  23.7 0.6 %shard_map.110 = (bf16[128,256]{1,0:T(8,128)(2,1)}, f32[8,128]{1,0:T(8,128)S(1)}) custom-call(f32[128,256]{1,0:T(8,128)S(1)} %get-tuple-element.27.active_ref), custom_call_target="tpu_custom_call" | custom-call | flops 1048576 | bytes 1048576 | tf_op jit(solution)/shard_map/pallas_call | solution.py:25
  24.4 1.8 %collective-permute-done.9.refs_3_ = bf16[3,128,128]{2,1,0:T(8,128)(2,1)S(1)} collective-permute-done((bf16[3,128,128]{2,1,0:T(8,128)(2,1)S(1)}, bf16[3,128,128]{2,1,0:T(8,128)(2,1)S(1)}, u32[]{:S(2)}, u32[]{:S(2)}) %collective-permute-start.9) | collective-permute-done | bytes 98336 | tf_op jit(solution)/shard_map/ppermute | solution.py:266
  26.2 0.9 %collective-permute-done.8.refs_2_ = bf16[3,128,128]{2,1,0:T(8,128)(2,1)S(1)} collective-permute-done((bf16[3,128,128]{2,1,0:T(8,128)(2,1)S(1)}, bf16[3,128,128]{2,1,0:T(8,128)(2,1)S(1)}, u32[]{:S(2)}, u32[]{:S(2)}) %collective-permute-start.8) | collective-permute-done | bytes 98336 | tf_op jit(solution)/shard_map/ppermute | solution.py:266
  27.1 0.0 collective-permute-done.7.refs_1_
  27.1 0.1 shard_map.111
  27.2 0.1 collective-permute-start.10
  27.3 0.2 shard_map.112.own_ref
  27.5 1.1 %collective-permute-done.10.received_ref = bf16[5,128,128]{2,1,0:T(8,128)(2,1)S(1)} collective-permute-done((bf16[5,128,128]{2,1,0:T(8,128)(2,1)S(1)}, bf16[5,128,128]{2,1,0:T(8,128)(2,1)S(1)}, u32[]{:S(2)}, u32[]{:S(2)}) %collective-permute-start.10) | collective-permute-done | bytes 163872 | tf_op jit(solution)/shard_map/ppermute | solution.py:266
  28.6 0.3 shard_map.113
  28.9 0.1 collective-permute-start.11
  29.0 3.4 %collective-permute-start.12 = (bf16[2,128,128]{2,1,0:T(8,128)(2,1)S(1)}, bf16[2,128,128]{2,1,0:T(8,128)(2,1)S(1)}, u32[]{:S(2)}, u32[]{:S(2)}) collective-permute-start(bf16[2,128,128]{2,1,0:T(8,128)(2,1)S(1)} %get-tuple-element.35), channel_id=1, source_target_pairs={{0,17},{1,16},{2,19},{3,18},{4,21},{5,20},{6,23},{7,22},{8,25},{9,... | collective-permute-start | bytes 196616 | tf_op jit(solution)/shard_map/ppermute | solution.py:279
  32.4 0.1 collective-permute-start.13
  32.5 2.4 %collective-permute-done.11.refs_0_ = bf16[2,128,128]{2,1,0:T(8,128)(2,1)S(1)} collective-permute-done((bf16[2,128,128]{2,1,0:T(8,128)(2,1)S(1)}, bf16[2,128,128]{2,1,0:T(8,128)(2,1)S(1)}, u32[]{:S(2)}, u32[]{:S(2)}) %collective-permute-start.11) | collective-permute-done | bytes 65568 | tf_op jit(solution)/shard_map/ppermute | solution.py:279
  34.9 2.8 %collective-permute-done.12.refs_1_ = bf16[2,128,128]{2,1,0:T(8,128)(2,1)S(1)} collective-permute-done((bf16[2,128,128]{2,1,0:T(8,128)(2,1)S(1)}, bf16[2,128,128]{2,1,0:T(8,128)(2,1)S(1)}, u32[]{:S(2)}, u32[]{:S(2)}) %collective-permute-start.12) | collective-permute-done | bytes 65568 | tf_op jit(solution)/shard_map/ppermute | solution.py:279
  37.8 0.0 collective-permute-done.13.refs_2_
  37.8 0.2 collective-permute-start.14
  38.0 1.3 %collective-permute-done.14.received_ref = bf16[7,128,128]{2,1,0:T(8,128)(2,1)S(1)} collective-permute-done((bf16[7,128,128]{2,1,0:T(8,128)(2,1)S(1)}, bf16[7,128,128]{2,1,0:T(8,128)(2,1)S(1)}, u32[]{:S(2)}, u32[]{:S(2)}) %collective-permute-start.14) | collective-permute-done | bytes 229408 | tf_op jit(solution)/shard_map/ppermute | solution.py:266
  39.3 0.7 %shard_map.115 = (bf16[128,128]{1,0:T(8,128)(2,1)}, f32[128,256]{1,0:T(8,128)}) custom-call(s32[1]{0:T(128)} %bitcast.2.row_ref, s32[1]{0:T(128)} %bitcast.1.core_ref, bf16[128]{0:T(256)(128)(2,1)S(1)} %copy-done.7, bf16[2,128,128]{2,1,0:T(8,128)(2,1)S(1)} %get-tuple-element.33.refs_3_.own_ref, ...), custom_call_target="tpu_custom_call" | custom-call | flops 1048576 | bytes 1048576 | tf_op jit(solution)/shard_map/pallas_call | solution.py:25
  (3 shorter events, 0.1 us)
Async XLA Ops:
  0.6 0.8 %copy-start.5 = (s32[1,1,8]{2,1,0:T(1,128)S(1)}, s32[1,1,8]{2,1,0:T(1,128)}, u32[]{:S(2)}) copy-start(s32[1,1,8]{2,1,0:T(1,128)} %cols_ref.3) | copy-start | bytes 100
  0.6 0.8 %copy-start.4 = (s32[1,1,8]{2,1,0:T(1,128)S(1)}, s32[1,1,8]{2,1,0:T(1,128)}, u32[]{:S(2)}) copy-start(s32[1,1,8]{2,1,0:T(1,128)} %rows_ref.3) | copy-start | bytes 100
  0.7 0.8 %copy-start.3 = (bf16[128,128]{1,0:T(8,128)(2,1)S(1)}, bf16[128,128]{1,0:T(8,128)(2,1)}, u32[]{:S(2)}) copy-start(bf16[128,128]{1,0:T(8,128)(2,1)} %features_ref.1) | copy-start | bytes 98308
  0.7 0.7 %copy-start.6 = (bf16[128]{0:T(256)(128)(2,1)S(1)}, bf16[128]{0:T(256)(128)(2,1)}, u32[]{:S(2)}) copy-start(bf16[128]{0:T(256)(128)(2,1)} %deg_ref.5) | copy-start | bytes 772
  1.3 7.8 %copy-start = (s32[1,1,8,32,256]{4,3,2,1,0:T(8,128)S(1)}, s32[1,1,8,32,256]{4,3,2,1,0:T(8,128)}, u32[]{:S(2)}) copy-start(s32[1,1,8,32,256]{4,3,2,1,0:T(8,128)} %bits_ref.1) | copy-start | bytes 786436
  1.5 8.6 %collective-permute-start.2 = (bf16[128,128]{1,0:T(8,128)(2,1)S(1)}, bf16[128,128]{1,0:T(8,128)(2,1)S(1)}, u32[]{:S(2)}, u32[]{:S(2)}) collective-permute-start(bf16[128,128]{1,0:T(8,128)(2,1)S(1)} %shard_map.104.after_ref.refs_0_), channel_id=1, source_target_pairs={{0,8},{8,16},{16,24},{24,0},{1,9},{9,17},{17,25},{25,1},{2,10},{10... | collective-permute-start | bytes 98312 | tf_op jit(solution)/shard_map/ppermute | solution.py:270
  4.6 5.5 %collective-permute-start.1 = (bf16[128,128]{1,0:T(8,128)(2,1)S(1)}, bf16[128,128]{1,0:T(8,128)(2,1)S(1)}, u32[]{:S(2)}, u32[]{:S(2)}) collective-permute-start(bf16[128,128]{1,0:T(8,128)(2,1)S(1)} %shard_map.104.after_ref.refs_0_), channel_id=1, source_target_pairs={{0,16},{8,24},{16,0},{24,8},{1,17},{9,25},{17,1},{25,9},{2,18},{10... | collective-permute-start | bytes 98312 | tf_op jit(solution)/shard_map/ppermute | solution.py:270
  7.2 3.9 %collective-permute-start = (bf16[128,128]{1,0:T(8,128)(2,1)S(1)}, bf16[128,128]{1,0:T(8,128)(2,1)S(1)}, u32[]{:S(2)}, u32[]{:S(2)}) collective-permute-start(bf16[128,128]{1,0:T(8,128)(2,1)S(1)} %shard_map.104.after_ref.refs_0_), channel_id=1, source_target_pairs={{0,24},{8,0},{16,8},{24,16},{1,25},{9,1},{17,9},{25,17},{2,26},{10... | collective-permute-start | bytes 98312 | tf_op jit(solution)/shard_map/ppermute | solution.py:270
  11.4 1.4 %collective-permute-start.3 = (bf16[4,128,128]{2,1,0:T(8,128)(2,1)S(1)}, bf16[4,128,128]{2,1,0:T(8,128)(2,1)S(1)}, u32[]{:S(2)}, u32[]{:S(2)}) collective-permute-start(bf16[4,128,128]{2,1,0:T(8,128)(2,1)S(1)} %get-tuple-element.22), channel_id=1, source_target_pairs={{0,1},{1,0},{2,3},{3,2},{4,5},{5,4},{6,7},{7,6},{8,9},{9,8},{10,11... | collective-permute-start | bytes 393224 | tf_op jit(solution)/shard_map/ppermute | solution.py:266
  12.8 7.0 %copy-start.1 = (bf16[128,256]{1,0:T(8,128)(2,1)S(1)}, bf16[128,256]{1,0:T(8,128)(2,1)}, u32[]{:S(2)}) copy-start(bf16[128,256]{1,0:T(8,128)(2,1)} %weight_ref.1) | copy-start | bytes 196612
  12.8 7.0 %copy-start.2 = (bf16[128,256]{1,0:T(8,128)(2,1)S(1)}, bf16[128,256]{1,0:T(8,128)(2,1)}, u32[]{:S(2)}) copy-start(bf16[128,256]{1,0:T(8,128)(2,1)} %cotangent_ref.1) | copy-start | bytes 196612
  12.9 4.9 %collective-permute-start.4 = (bf16[128,128]{1,0:T(8,128)(2,1)S(1)}, bf16[128,128]{1,0:T(8,128)(2,1)S(1)}, u32[]{:S(2)}, u32[]{:S(2)}) collective-permute-start(bf16[128,128]{1,0:T(8,128)(2,1)S(1)} %get-tuple-element.24), channel_id=1, source_target_pairs={{0,6},{1,7},{2,4},{3,5},{4,2},{5,3},{6,0},{7,1},{8,14},{9,15},{10,... | collective-permute-start | bytes 98312 | tf_op jit(solution)/shard_map/ppermute | solution.py:266
  15.4 3.9 %collective-permute-start.5 = (bf16[128,128]{1,0:T(8,128)(2,1)S(1)}, bf16[128,128]{1,0:T(8,128)(2,1)S(1)}, u32[]{:S(2)}, u32[]{:S(2)}) collective-permute-start(bf16[128,128]{1,0:T(8,128)(2,1)S(1)} %get-tuple-element.25), channel_id=1, source_target_pairs={{0,4},{1,5},{2,6},{3,7},{4,0},{5,1},{6,2},{7,3},{8,12},{9,13},{10,... | collective-permute-start | bytes 98312 | tf_op jit(solution)/shard_map/ppermute | solution.py:266
  15.9 3.9 %copy-start.7 = (bf16[128]{0:T(256)(128)(2,1)S(1)}, bf16[128]{0:T(256)(128)(2,1)}, u32[]{:S(2)}) copy-start(bf16[128]{0:T(256)(128)(2,1)} %deg_ref.5) | copy-start | bytes 772
  15.9 3.9 %collective-permute-start.6 = (bf16[128,128]{1,0:T(8,128)(2,1)S(1)}, bf16[128,128]{1,0:T(8,128)(2,1)S(1)}, u32[]{:S(2)}, u32[]{:S(2)}) collective-permute-start(bf16[128,128]{1,0:T(8,128)(2,1)S(1)} %get-tuple-element.26), channel_id=1, source_target_pairs={{0,2},{1,3},{2,0},{3,1},{4,6},{5,7},{6,4},{7,5},{8,10},{9,11},{10,... | collective-permute-start | bytes 98312 | tf_op jit(solution)/shard_map/ppermute | solution.py:266
  20.2 6.0 %collective-permute-start.9 = (bf16[3,128,128]{2,1,0:T(8,128)(2,1)S(1)}, bf16[3,128,128]{2,1,0:T(8,128)(2,1)S(1)}, u32[]{:S(2)}, u32[]{:S(2)}) collective-permute-start(bf16[3,128,128]{2,1,0:T(8,128)(2,1)S(1)} %get-tuple-element.29.refs_0_), channel_id=1, source_target_pairs={{0,6},{1,7},{2,4},{3,5},{4,2},{5,3},{6,0},{7,1},{8,14},{9,15},{10,... | collective-permute-start | bytes 294920 | tf_op jit(solution)/shard_map/ppermute | solution.py:266
  21.7 5.4 %collective-permute-start.8 = (bf16[3,128,128]{2,1,0:T(8,128)(2,1)S(1)}, bf16[3,128,128]{2,1,0:T(8,128)(2,1)S(1)}, u32[]{:S(2)}, u32[]{:S(2)}) collective-permute-start(bf16[3,128,128]{2,1,0:T(8,128)(2,1)S(1)} %get-tuple-element.29.refs_0_), channel_id=1, source_target_pairs={{0,4},{1,5},{2,6},{3,7},{4,0},{5,1},{6,2},{7,3},{8,12},{9,13},{10,... | collective-permute-start | bytes 294920 | tf_op jit(solution)/shard_map/ppermute | solution.py:266
  22.2 4.8 %collective-permute-start.7 = (bf16[3,128,128]{2,1,0:T(8,128)(2,1)S(1)}, bf16[3,128,128]{2,1,0:T(8,128)(2,1)S(1)}, u32[]{:S(2)}, u32[]{:S(2)}) collective-permute-start(bf16[3,128,128]{2,1,0:T(8,128)(2,1)S(1)} %get-tuple-element.29.refs_0_), channel_id=1, source_target_pairs={{0,2},{1,3},{2,0},{3,1},{4,6},{5,7},{6,4},{7,5},{8,10},{9,11},{10,... | collective-permute-start | bytes 294920 | tf_op jit(solution)/shard_map/ppermute | solution.py:266
  27.2 1.5 %collective-permute-start.10 = (bf16[5,128,128]{2,1,0:T(8,128)(2,1)S(1)}, bf16[5,128,128]{2,1,0:T(8,128)(2,1)S(1)}, u32[]{:S(2)}, u32[]{:S(2)}) collective-permute-start(bf16[5,128,128]{2,1,0:T(8,128)(2,1)S(1)} %get-tuple-element.31.joined_ref), channel_id=1, source_target_pairs={{0,1},{1,0},{2,3},{3,2},{4,5},{5,4},{6,7},{7,6},{8,9},{9,8},{10,11... | collective-permute-start | bytes 491528 | tf_op jit(solution)/shard_map/ppermute | solution.py:266
  28.9 6.0 %collective-permute-start.11 = (bf16[2,128,128]{2,1,0:T(8,128)(2,1)S(1)}, bf16[2,128,128]{2,1,0:T(8,128)(2,1)S(1)}, u32[]{:S(2)}, u32[]{:S(2)}) collective-permute-start(bf16[2,128,128]{2,1,0:T(8,128)(2,1)S(1)} %get-tuple-element.34), channel_id=1, source_target_pairs={{0,9},{1,8},{2,11},{3,10},{4,13},{5,12},{6,15},{7,14},{8,17},{9,16... | collective-permute-start | bytes 196616 | tf_op jit(solution)/shard_map/ppermute | solution.py:279
  29.0 8.8 %collective-permute-start.12 = (bf16[2,128,128]{2,1,0:T(8,128)(2,1)S(1)}, bf16[2,128,128]{2,1,0:T(8,128)(2,1)S(1)}, u32[]{:S(2)}, u32[]{:S(2)}) collective-permute-start(bf16[2,128,128]{2,1,0:T(8,128)(2,1)S(1)} %get-tuple-element.35), channel_id=1, source_target_pairs={{0,17},{1,16},{2,19},{3,18},{4,21},{5,20},{6,23},{7,22},{8,25},{9,... | collective-permute-start | bytes 196616 | tf_op jit(solution)/shard_map/ppermute | solution.py:279
  32.4 5.4 %collective-permute-start.13 = (bf16[2,128,128]{2,1,0:T(8,128)(2,1)S(1)}, bf16[2,128,128]{2,1,0:T(8,128)(2,1)S(1)}, u32[]{:S(2)}, u32[]{:S(2)}) collective-permute-start(bf16[2,128,128]{2,1,0:T(8,128)(2,1)S(1)} %get-tuple-element.36), channel_id=1, source_target_pairs={{0,25},{1,24},{2,27},{3,26},{4,29},{5,28},{6,31},{7,30},{8,1},{9,0... | collective-permute-start | bytes 196616 | tf_op jit(solution)/shard_map/ppermute | solution.py:279
  37.8 1.6 %collective-permute-start.14 = (bf16[7,128,128]{2,1,0:T(8,128)(2,1)S(1)}, bf16[7,128,128]{2,1,0:T(8,128)(2,1)S(1)}, u32[]{:S(2)}, u32[]{:S(2)}) collective-permute-start(bf16[7,128,128]{2,1,0:T(8,128)(2,1)S(1)} %shard_map.114), channel_id=1, source_target_pairs={{0,1},{1,0},{2,3},{3,2},{4,5},{5,4},{6,7},{7,6},{8,9},{9,8},{10,11... | collective-permute-start | bytes 688136 | tf_op jit(solution)/shard_map/ppermute | solution.py:266

commit v15 on v12

--- a/solution.py
+++ b/solution.py
@@ -212,23 +212,23 @@
 def pack_pieces(*refs):
     *pieces, own_ref, sent_ref = refs
     count = len(pieces)
+    sent_ref[0] = sum(piece[0].astype(f32) for piece in pieces).astype(bf16)
     for index, piece in enumerate(pieces):
-        sent_ref[index] = piece[0]
-        sent_ref[count + index] = piece[1]
-    sent_ref[2 * count] = own_ref[1]
+        sent_ref[1 + index] = piece[1]
+    sent_ref[1 + count] = own_ref[1]
 
 
 def finish(factor, row_ref, core_ref, deg_ref, own_ref, received_ref, *refs):
     *pieces, input_ref, grad_ref, ordered = refs
     count, size = len(pieces), own_ref.shape[1]
-    total = sum(received_ref[index].astype(f32) for index in range(count)) + own_ref[0].astype(f32)
+    total = received_ref[0].astype(f32) + own_ref[0].astype(f32)
     input_ref[...] = (total * deg_ref[...].astype(f32).reshape(1, -1)).T.astype(bf16)
     for index, piece in enumerate(pieces):
         plane = lax.rem(row_ref[0] + count - index, count + 1)
-        ordered[0, plane] = received_ref[count + index]
+        ordered[0, plane] = received_ref[1 + index]
         ordered[1, plane] = piece[1]
     ordered[0, row_ref[0]] = own_ref[1]
-    ordered[1, row_ref[0]] = received_ref[2 * count]
+    ordered[1, row_ref[0]] = received_ref[1 + count]
     for index, half in enumerate((core_ref[0], 1 - core_ref[0])):
         half_grad = jnp.sum(ordered[index].astype(f32), axis=0) * factor
         grad_ref[:, block_at(half, size)] = half_grad
@@ -400,7 +400,7 @@
     ]
     packed = call(
         pack_pieces,
-        struct((2 * len(arrived) + 1, width, size), bf16),
+        struct((len(arrived) + 2, width, size), bf16),
         (),
         (*arrived, own_piece),
     )

time: 39.7 us -> 39.6 us (level)
  no operation moved by 1% of the time
where the time goes in v15:
time: 39.6 us; the launch traced here: 39.4 us
  starting transfers between devices  17.2 us (43%)
  waiting for transfers between devices  16 us (40%)
  Pallas kernels  4.04 us (10%)
  between operations  1.46 us (4%)
  local copies, waits for them, and re-layouts  0.69 us (2%)
    ppermute x12, starting transfers between devices, exchange(): lax.ppermute(block, axis, [(shard, shard ^ distance) for shard in range(s...  13.5 us
    ppermute x12, waiting for transfers between devices, exchange(): lax.ppermute(block, axis, [(shard, shard ^ distance) for shard in range(s...  11.8 us
    ppermute x3, waiting for transfers between devices, crossed(): return lax.ppermute(block, ('row', 'col'), pairs)  4.21 us
    ppermute x3, starting transfers between devices, crossed(): return lax.ppermute(block, ('row', 'col'), pairs)  3.69 us
    pallas_call x12, Pallas kernels, call(): pl.pallas_call(body, out_shape=out_shape, in_specs=[SMEM] * len(scalars)...  3.14 us
    pallas_call x1, Pallas kernels, on_device(): pl.pallas_call(build_adjacency, out_shape=struct((col_shards * size, row_...  0.91 us
  transfers between devices with their start and end apart: 15, of which 12 were waited for; matrix products, arithmetic and copies ran while one was open for 0% of the time, Pallas kernels for 5%

profile of v15, /device:TPU:0, one launch (start us, length us, event | category | flops | bytes accessed | tf_op | source)
XLA Modules:
  0.0 39.4 jit_solution(16273469539232787718)
XLA Ops:
  0.6 0.0 copy-start.5
  0.6 0.0 copy-start.4
  0.7 0.0 copy-start.3
  0.7 0.0 copy-start.6
  0.7 0.7 %copy-done.6 = bf16[128]{0:T(256)(128)(2,1)S(1)} copy-done((bf16[128]{0:T(256)(128)(2,1)S(1)}, bf16[128]{0:T(256)(128)(2,1)}, u32[]{:S(2)}) %copy-start.6) | copy-done | bytes 280
  1.3 0.0 copy-start
  1.3 0.1 shard_map.103.column_ref
  1.5 0.0 copy-done.5
  1.5 0.0 copy-done.4
  1.5 0.0 copy-done.3
  1.5 4.1 %collective-permute-start.2 = (bf16[128,128]{1,0:T(8,128)(2,1)S(1)}, bf16[128,128]{1,0:T(8,128)(2,1)S(1)}, u32[]{:S(2)}, u32[]{:S(2)}) collective-permute-start(bf16[128,128]{1,0:T(8,128)(2,1)S(1)} %shard_map.104.after_ref.refs_0_), channel_id=1, source_target_pairs={{0,16},{8,24},{16,0},{24,8},{1,17},{9,25},{17,1},{25,9},{2,18},{10... | collective-permute-start | bytes 98312 | tf_op jit(solution)/shard_map/ppermute | solution.py:265
  5.6 1.3 %collective-permute-start.1 = (bf16[128,128]{1,0:T(8,128)(2,1)S(1)}, bf16[128,128]{1,0:T(8,128)(2,1)S(1)}, u32[]{:S(2)}, u32[]{:S(2)}) collective-permute-start(bf16[128,128]{1,0:T(8,128)(2,1)S(1)} %shard_map.104.after_ref.refs_0_), channel_id=1, source_target_pairs={{0,24},{8,16},{16,8},{24,0},{1,25},{9,17},{17,9},{25,1},{2,26},{10... | collective-permute-start | bytes 98312 | tf_op jit(solution)/shard_map/ppermute | solution.py:265
  7.0 0.2 collective-permute-start
  7.8 0.0 copy-done
  7.9 0.9 %shard_map.105.adjacency_ref = bf16[1024,512]{1,0:T(8,128)(2,1)S(1)} custom-call(s32[1,1]{1,0:T(1,128)S(6)} %copy.11.count_ref, s32[1,1,8]{2,1,0:T(1,128)S(1)} %copy-done.4, s32[1,1,8]{2,1,0:T(1,128)S(1)} %copy-done.5, s32[1,1,8,32,256]{4,3,2,1,0:T(8,128)S(1)} %copy-done, bf16[128,128]{1,0:T(8,128)(2,1)S(1)} %shard_map.104.after_ref.refs_0_), custom_call_target="tpu_custom_call" | custom-call | flops 1048576 | bytes 1048576 | tf_op jit(solution)/shard_map/pallas_call | solution.py:337
  8.8 0.0 collective-permute-done.2.refs_3_
  8.8 2.5 %collective-permute-done.1.refs_2_ = bf16[128,128]{1,0:T(8,128)(2,1)S(1)} collective-permute-done((bf16[128,128]{1,0:T(8,128)(2,1)S(1)}, bf16[128,128]{1,0:T(8,128)(2,1)S(1)}, u32[]{:S(2)}, u32[]{:S(2)}) %collective-permute-start.1) | collective-permute-done | bytes 32800 | tf_op jit(solution)/shard_map/ppermute | solution.py:265
  11.3 0.0 collective-permute-done.refs_1_
  11.3 0.3 shard_map.106
  11.6 0.1 collective-permute-start.3
  11.7 0.3 shard_map.107.mine_ref
  12.0 1.0 %collective-permute-done.3.received_ref = bf16[4,128,128]{2,1,0:T(8,128)(2,1)S(1)} collective-permute-done((bf16[4,128,128]{2,1,0:T(8,128)(2,1)S(1)}, bf16[4,128,128]{2,1,0:T(8,128)(2,1)S(1)}, u32[]{:S(2)}, u32[]{:S(2)}) %collective-permute-start.3) | collective-permute-done | bytes 131104 | tf_op jit(solution)/shard_map/ppermute | solution.py:265
  13.1 0.0 copy-start.1
  13.1 0.0 copy-start.2
  13.1 2.5 %collective-permute-start.4 = (bf16[128,128]{1,0:T(8,128)(2,1)S(1)}, bf16[128,128]{1,0:T(8,128)(2,1)S(1)}, u32[]{:S(2)}, u32[]{:S(2)}) collective-permute-start(bf16[128,128]{1,0:T(8,128)(2,1)S(1)} %get-tuple-element.24), channel_id=1, source_target_pairs={{0,6},{1,7},{2,4},{3,5},{4,2},{5,3},{6,0},{7,1},{8,14},{9,15},{10,... | collective-permute-start | bytes 98312 | tf_op jit(solution)/shard_map/ppermute | solution.py:265
  15.6 0.5 %collective-permute-start.5 = (bf16[128,128]{1,0:T(8,128)(2,1)S(1)}, bf16[128,128]{1,0:T(8,128)(2,1)S(1)}, u32[]{:S(2)}, u32[]{:S(2)}) collective-permute-start(bf16[128,128]{1,0:T(8,128)(2,1)S(1)} %get-tuple-element.25), channel_id=1, source_target_pairs={{0,4},{1,5},{2,6},{3,7},{4,0},{5,1},{6,2},{7,3},{8,12},{9,13},{10,... | collective-permute-start | bytes 98312 | tf_op jit(solution)/shard_map/ppermute | solution.py:265
  16.1 0.0 copy-start.7
  16.1 0.5 %collective-permute-start.6 = (bf16[128,128]{1,0:T(8,128)(2,1)S(1)}, bf16[128,128]{1,0:T(8,128)(2,1)S(1)}, u32[]{:S(2)}, u32[]{:S(2)}) collective-permute-start(bf16[128,128]{1,0:T(8,128)(2,1)S(1)} %get-tuple-element.26), channel_id=1, source_target_pairs={{0,2},{1,3},{2,0},{3,1},{4,6},{5,7},{6,4},{7,5},{8,10},{9,11},{10,... | collective-permute-start | bytes 98312 | tf_op jit(solution)/shard_map/ppermute | solution.py:265
  16.6 1.3 %collective-permute-done.4.refs_0_ = bf16[128,128]{1,0:T(8,128)(2,1)S(1)} collective-permute-done((bf16[128,128]{1,0:T(8,128)(2,1)S(1)}, bf16[128,128]{1,0:T(8,128)(2,1)S(1)}, u32[]{:S(2)}, u32[]{:S(2)}) %collective-permute-start.4) | collective-permute-done | bytes 32800 | tf_op jit(solution)/shard_map/ppermute | solution.py:265
  18.0 1.5 %collective-permute-done.5.refs_1_ = bf16[128,128]{1,0:T(8,128)(2,1)S(1)} collective-permute-done((bf16[128,128]{1,0:T(8,128)(2,1)S(1)}, bf16[128,128]{1,0:T(8,128)(2,1)S(1)}, u32[]{:S(2)}, u32[]{:S(2)}) %collective-permute-start.5) | collective-permute-done | bytes 32800 | tf_op jit(solution)/shard_map/ppermute | solution.py:265
  19.5 0.5 %collective-permute-done.6.refs_2_ = bf16[128,128]{1,0:T(8,128)(2,1)S(1)} collective-permute-done((bf16[128,128]{1,0:T(8,128)(2,1)S(1)}, bf16[128,128]{1,0:T(8,128)(2,1)S(1)}, u32[]{:S(2)}, u32[]{:S(2)}) %collective-permute-start.6) | collective-permute-done | bytes 32800 | tf_op jit(solution)/shard_map/ppermute | solution.py:265
  20.0 0.0 copy-done.1
  20.0 0.0 copy-done.2
  20.0 0.0 copy-done.7
  20.0 0.4 shard_map.109
  20.4 1.6 %collective-permute-start.9 = (bf16[3,128,128]{2,1,0:T(8,128)(2,1)S(1)}, bf16[3,128,128]{2,1,0:T(8,128)(2,1)S(1)}, u32[]{:S(2)}, u32[]{:S(2)}) collective-permute-start(bf16[3,128,128]{2,1,0:T(8,128)(2,1)S(1)} %get-tuple-element.29.refs_0_), channel_id=1, source_target_pairs={{0,6},{1,7},{2,4},{3,5},{4,2},{5,3},{6,0},{7,1},{8,14},{9,15},{10,... | collective-permute-start | bytes 294920 | tf_op jit(solution)/shard_map/ppermute | solution.py:265
  22.0 0.5 %collective-permute-start.8 = (bf16[3,128,128]{2,1,0:T(8,128)(2,1)S(1)}, bf16[3,128,128]{2,1,0:T(8,128)(2,1)S(1)}, u32[]{:S(2)}, u32[]{:S(2)}) collective-permute-start(bf16[3,128,128]{2,1,0:T(8,128)(2,1)S(1)} %get-tuple-element.29.refs_0_), channel_id=1, source_target_pairs={{0,4},{1,5},{2,6},{3,7},{4,0},{5,1},{6,2},{7,3},{8,12},{9,13},{10,... | collective-permute-start | bytes 294920 | tf_op jit(solution)/shard_map/ppermute | solution.py:265
  22.5 1.5 %collective-permute-start.7 = (bf16[3,128,128]{2,1,0:T(8,128)(2,1)S(1)}, bf16[3,128,128]{2,1,0:T(8,128)(2,1)S(1)}, u32[]{:S(2)}, u32[]{:S(2)}) collective-permute-start(bf16[3,128,128]{2,1,0:T(8,128)(2,1)S(1)} %get-tuple-element.29.refs_0_), channel_id=1, source_target_pairs={{0,2},{1,3},{2,0},{3,1},{4,6},{5,7},{6,4},{7,5},{8,10},{9,11},{10,... | collective-permute-start | bytes 294920 | tf_op jit(solution)/shard_map/ppermute | solution.py:265
  24.0 0.6 %shard_map.110 = (bf16[128,256]{1,0:T(8,128)(2,1)}, f32[8,128]{1,0:T(8,128)S(1)}) custom-call(f32[128,256]{1,0:T(8,128)S(1)} %get-tuple-element.27.active_ref), custom_call_target="tpu_custom_call" | custom-call | flops 1048576 | bytes 1048576 | tf_op jit(solution)/shard_map/pallas_call | solution.py:25
  24.6 1.8 %collective-permute-done.9.refs_3_ = bf16[3,128,128]{2,1,0:T(8,128)(2,1)S(1)} collective-permute-done((bf16[3,128,128]{2,1,0:T(8,128)(2,1)S(1)}, bf16[3,128,128]{2,1,0:T(8,128)(2,1)S(1)}, u32[]{:S(2)}, u32[]{:S(2)}) %collective-permute-start.9) | collective-permute-done | bytes 98336 | tf_op jit(solution)/shard_map/ppermute | solution.py:265
  26.4 0.9 %collective-permute-done.8.refs_2_ = bf16[3,128,128]{2,1,0:T(8,128)(2,1)S(1)} collective-permute-done((bf16[3,128,128]{2,1,0:T(8,128)(2,1)S(1)}, bf16[3,128,128]{2,1,0:T(8,128)(2,1)S(1)}, u32[]{:S(2)}, u32[]{:S(2)}) %collective-permute-start.8) | collective-permute-done | bytes 98336 | tf_op jit(solution)/shard_map/ppermute | solution.py:265
  27.3 0.0 collective-permute-done.7.refs_1_
  27.3 0.1 shard_map.111
  27.4 0.1 collective-permute-start.10
  27.5 0.2 shard_map.112.own_ref
  27.7 1.1 %collective-permute-done.10.received_ref = bf16[5,128,128]{2,1,0:T(8,128)(2,1)S(1)} collective-permute-done((bf16[5,128,128]{2,1,0:T(8,128)(2,1)S(1)}, bf16[5,128,128]{2,1,0:T(8,128)(2,1)S(1)}, u32[]{:S(2)}, u32[]{:S(2)}) %collective-permute-start.10) | collective-permute-done | bytes 163872 | tf_op jit(solution)/shard_map/ppermute | solution.py:265
  28.9 0.3 shard_map.113
  29.2 0.1 collective-permute-start.11
  29.2 2.3 %collective-permute-start.12 = (bf16[2,128,128]{2,1,0:T(8,128)(2,1)S(1)}, bf16[2,128,128]{2,1,0:T(8,128)(2,1)S(1)}, u32[]{:S(2)}, u32[]{:S(2)}) collective-permute-start(bf16[2,128,128]{2,1,0:T(8,128)(2,1)S(1)} %get-tuple-element.35), channel_id=1, source_target_pairs={{0,17},{1,16},{2,19},{3,18},{4,21},{5,20},{6,23},{7,22},{8,25},{9,... | collective-permute-start | bytes 196616 | tf_op jit(solution)/shard_map/ppermute | solution.py:274
  31.5 1.3 %collective-permute-start.13 = (bf16[2,128,128]{2,1,0:T(8,128)(2,1)S(1)}, bf16[2,128,128]{2,1,0:T(8,128)(2,1)S(1)}, u32[]{:S(2)}, u32[]{:S(2)}) collective-permute-start(bf16[2,128,128]{2,1,0:T(8,128)(2,1)S(1)} %get-tuple-element.36), channel_id=1, source_target_pairs={{0,25},{1,24},{2,27},{3,26},{4,29},{5,28},{6,31},{7,30},{8,1},{9,0... | collective-permute-start | bytes 196616 | tf_op jit(solution)/shard_map/ppermute | solution.py:274
  32.9 2.4 %collective-permute-done.11.refs_0_ = bf16[2,128,128]{2,1,0:T(8,128)(2,1)S(1)} collective-permute-done((bf16[2,128,128]{2,1,0:T(8,128)(2,1)S(1)}, bf16[2,128,128]{2,1,0:T(8,128)(2,1)S(1)}, u32[]{:S(2)}, u32[]{:S(2)}) %collective-permute-start.11) | collective-permute-done | bytes 65568 | tf_op jit(solution)/shard_map/ppermute | solution.py:274
  35.3 1.7 %collective-permute-done.12.refs_1_ = bf16[2,128,128]{2,1,0:T(8,128)(2,1)S(1)} collective-permute-done((bf16[2,128,128]{2,1,0:T(8,128)(2,1)S(1)}, bf16[2,128,128]{2,1,0:T(8,128)(2,1)S(1)}, u32[]{:S(2)}, u32[]{:S(2)}) %collective-permute-start.12) | collective-permute-done | bytes 65568 | tf_op jit(solution)/shard_map/ppermute | solution.py:274
  37.0 0.1 collective-permute-done.13.refs_2_
  37.1 0.5 %collective-permute-start.14 = (bf16[5,128,128]{2,1,0:T(8,128)(2,1)S(1)}, bf16[5,128,128]{2,1,0:T(8,128)(2,1)S(1)}, u32[]{:S(2)}, u32[]{:S(2)}) collective-permute-start(bf16[5,128,128]{2,1,0:T(8,128)(2,1)S(1)} %shard_map.114), channel_id=1, source_target_pairs={{0,1},{1,0},{2,3},{3,2},{4,5},{5,4},{6,7},{7,6},{8,9},{9,8},{10,11... | collective-permute-start | bytes 491528 | tf_op jit(solution)/shard_map/ppermute | solution.py:265
  37.6 1.0 %collective-permute-done.14.received_ref = bf16[5,128,128]{2,1,0:T(8,128)(2,1)S(1)} collective-permute-done((bf16[5,128,128]{2,1,0:T(8,128)(2,1)S(1)}, bf16[5,128,128]{2,1,0:T(8,128)(2,1)S(1)}, u32[]{:S(2)}, u32[]{:S(2)}) %collective-permute-start.14) | collective-permute-done | bytes 163872 | tf_op jit(solution)/shard_map/ppermute | solution.py:265
  38.7 0.7 %shard_map.115 = (bf16[128,128]{1,0:T(8,128)(2,1)}, f32[128,256]{1,0:T(8,128)}) custom-call(s32[1]{0:T(128)} %bitcast.2.row_ref, s32[1]{0:T(128)} %bitcast.1.core_ref, bf16[128]{0:T(256)(128)(2,1)S(1)} %copy-done.7, bf16[2,128,128]{2,1,0:T(8,128)(2,1)S(1)} %get-tuple-element.33.refs_3_.own_ref, ...), custom_call_target="tpu_custom_call" | custom-call | flops 1048576 | bytes 1048576 | tf_op jit(solution)/shard_map/pallas_call | solution.py:25
  (3 shorter events, 0.1 us)
Async XLA Ops:
  0.6 0.8 %copy-start.5 = (s32[1,1,8]{2,1,0:T(1,128)S(1)}, s32[1,1,8]{2,1,0:T(1,128)}, u32[]{:S(2)}) copy-start(s32[1,1,8]{2,1,0:T(1,128)} %cols_ref.3) | copy-start | bytes 100
  0.6 0.8 %copy-start.4 = (s32[1,1,8]{2,1,0:T(1,128)S(1)}, s32[1,1,8]{2,1,0:T(1,128)}, u32[]{:S(2)}) copy-start(s32[1,1,8]{2,1,0:T(1,128)} %rows_ref.3) | copy-start | bytes 100
  0.7 0.8 %copy-start.3 = (bf16[128,128]{1,0:T(8,128)(2,1)S(1)}, bf16[128,128]{1,0:T(8,128)(2,1)}, u32[]{:S(2)}) copy-start(bf16[128,128]{1,0:T(8,128)(2,1)} %features_ref.1) | copy-start | bytes 98308
  0.7 0.7 %copy-start.6 = (bf16[128]{0:T(256)(128)(2,1)S(1)}, bf16[128]{0:T(256)(128)(2,1)}, u32[]{:S(2)}) copy-start(bf16[128]{0:T(256)(128)(2,1)} %deg_ref.5) | copy-start | bytes 772
  1.3 6.5 %copy-start = (s32[1,1,8,32,256]{4,3,2,1,0:T(8,128)S(1)}, s32[1,1,8,32,256]{4,3,2,1,0:T(8,128)}, u32[]{:S(2)}) copy-start(s32[1,1,8,32,256]{4,3,2,1,0:T(8,128)} %bits_ref.1) | copy-start | bytes 786436
  1.5 7.3 %collective-permute-start.2 = (bf16[128,128]{1,0:T(8,128)(2,1)S(1)}, bf16[128,128]{1,0:T(8,128)(2,1)S(1)}, u32[]{:S(2)}, u32[]{:S(2)}) collective-permute-start(bf16[128,128]{1,0:T(8,128)(2,1)S(1)} %shard_map.104.after_ref.refs_0_), channel_id=1, source_target_pairs={{0,16},{8,24},{16,0},{24,8},{1,17},{9,25},{17,1},{25,9},{2,18},{10... | collective-permute-start | bytes 98312 | tf_op jit(solution)/shard_map/ppermute | solution.py:265
  5.6 5.7 %collective-permute-start.1 = (bf16[128,128]{1,0:T(8,128)(2,1)S(1)}, bf16[128,128]{1,0:T(8,128)(2,1)S(1)}, u32[]{:S(2)}, u32[]{:S(2)}) collective-permute-start(bf16[128,128]{1,0:T(8,128)(2,1)S(1)} %shard_map.104.after_ref.refs_0_), channel_id=1, source_target_pairs={{0,24},{8,16},{16,8},{24,0},{1,25},{9,17},{17,9},{25,1},{2,26},{10... | collective-permute-start | bytes 98312 | tf_op jit(solution)/shard_map/ppermute | solution.py:265
  7.0 4.4 %collective-permute-start = (bf16[128,128]{1,0:T(8,128)(2,1)S(1)}, bf16[128,128]{1,0:T(8,128)(2,1)S(1)}, u32[]{:S(2)}, u32[]{:S(2)}) collective-permute-start(bf16[128,128]{1,0:T(8,128)(2,1)S(1)} %shard_map.104.after_ref.refs_0_), channel_id=1, source_target_pairs={{0,8},{8,0},{16,24},{24,16},{1,9},{9,1},{17,25},{25,17},{2,10},{10... | collective-permute-start | bytes 98312 | tf_op jit(solution)/shard_map/ppermute | solution.py:265
  11.6 1.4 %collective-permute-start.3 = (bf16[4,128,128]{2,1,0:T(8,128)(2,1)S(1)}, bf16[4,128,128]{2,1,0:T(8,128)(2,1)S(1)}, u32[]{:S(2)}, u32[]{:S(2)}) collective-permute-start(bf16[4,128,128]{2,1,0:T(8,128)(2,1)S(1)} %get-tuple-element.22), channel_id=1, source_target_pairs={{0,1},{1,0},{2,3},{3,2},{4,5},{5,4},{6,7},{7,6},{8,9},{9,8},{10,11... | collective-permute-start | bytes 393224 | tf_op jit(solution)/shard_map/ppermute | solution.py:265
  13.1 7.0 %copy-start.1 = (bf16[128,256]{1,0:T(8,128)(2,1)S(1)}, bf16[128,256]{1,0:T(8,128)(2,1)}, u32[]{:S(2)}) copy-start(bf16[128,256]{1,0:T(8,128)(2,1)} %weight_ref.1) | copy-start | bytes 196612
  13.1 7.0 %copy-start.2 = (bf16[128,256]{1,0:T(8,128)(2,1)S(1)}, bf16[128,256]{1,0:T(8,128)(2,1)}, u32[]{:S(2)}) copy-start(bf16[128,256]{1,0:T(8,128)(2,1)} %cotangent_ref.1) | copy-start | bytes 196612
  13.1 4.9 %collective-permute-start.4 = (bf16[128,128]{1,0:T(8,128)(2,1)S(1)}, bf16[128,128]{1,0:T(8,128)(2,1)S(1)}, u32[]{:S(2)}, u32[]{:S(2)}) collective-permute-start(bf16[128,128]{1,0:T(8,128)(2,1)S(1)} %get-tuple-element.24), channel_id=1, source_target_pairs={{0,6},{1,7},{2,4},{3,5},{4,2},{5,3},{6,0},{7,1},{8,14},{9,15},{10,... | collective-permute-start | bytes 98312 | tf_op jit(solution)/shard_map/ppermute | solution.py:265
  15.6 3.9 %collective-permute-start.5 = (bf16[128,128]{1,0:T(8,128)(2,1)S(1)}, bf16[128,128]{1,0:T(8,128)(2,1)S(1)}, u32[]{:S(2)}, u32[]{:S(2)}) collective-permute-start(bf16[128,128]{1,0:T(8,128)(2,1)S(1)} %get-tuple-element.25), channel_id=1, source_target_pairs={{0,4},{1,5},{2,6},{3,7},{4,0},{5,1},{6,2},{7,3},{8,12},{9,13},{10,... | collective-permute-start | bytes 98312 | tf_op jit(solution)/shard_map/ppermute | solution.py:265
  16.1 3.9 %copy-start.7 = (bf16[128]{0:T(256)(128)(2,1)S(1)}, bf16[128]{0:T(256)(128)(2,1)}, u32[]{:S(2)}) copy-start(bf16[128]{0:T(256)(128)(2,1)} %deg_ref.5) | copy-start | bytes 772
  16.1 3.9 %collective-permute-start.6 = (bf16[128,128]{1,0:T(8,128)(2,1)S(1)}, bf16[128,128]{1,0:T(8,128)(2,1)S(1)}, u32[]{:S(2)}, u32[]{:S(2)}) collective-permute-start(bf16[128,128]{1,0:T(8,128)(2,1)S(1)} %get-tuple-element.26), channel_id=1, source_target_pairs={{0,2},{1,3},{2,0},{3,1},{4,6},{5,7},{6,4},{7,5},{8,10},{9,11},{10,... | collective-permute-start | bytes 98312 | tf_op jit(solution)/shard_map/ppermute | solution.py:265
  20.4 6.0 %collective-permute-start.9 = (bf16[3,128,128]{2,1,0:T(8,128)(2,1)S(1)}, bf16[3,128,128]{2,1,0:T(8,128)(2,1)S(1)}, u32[]{:S(2)}, u32[]{:S(2)}) collective-permute-start(bf16[3,128,128]{2,1,0:T(8,128)(2,1)S(1)} %get-tuple-element.29.refs_0_), channel_id=1, source_target_pairs={{0,6},{1,7},{2,4},{3,5},{4,2},{5,3},{6,0},{7,1},{8,14},{9,15},{10,... | collective-permute-start | bytes 294920 | tf_op jit(solution)/shard_map/ppermute | solution.py:265
  22.0 5.4 %collective-permute-start.8 = (bf16[3,128,128]{2,1,0:T(8,128)(2,1)S(1)}, bf16[3,128,128]{2,1,0:T(8,128)(2,1)S(1)}, u32[]{:S(2)}, u32[]{:S(2)}) collective-permute-start(bf16[3,128,128]{2,1,0:T(8,128)(2,1)S(1)} %get-tuple-element.29.refs_0_), channel_id=1, source_target_pairs={{0,4},{1,5},{2,6},{3,7},{4,0},{5,1},{6,2},{7,3},{8,12},{9,13},{10,... | collective-permute-start | bytes 294920 | tf_op jit(solution)/shard_map/ppermute | solution.py:265
  22.5 4.8 %collective-permute-start.7 = (bf16[3,128,128]{2,1,0:T(8,128)(2,1)S(1)}, bf16[3,128,128]{2,1,0:T(8,128)(2,1)S(1)}, u32[]{:S(2)}, u32[]{:S(2)}) collective-permute-start(bf16[3,128,128]{2,1,0:T(8,128)(2,1)S(1)} %get-tuple-element.29.refs_0_), channel_id=1, source_target_pairs={{0,2},{1,3},{2,0},{3,1},{4,6},{5,7},{6,4},{7,5},{8,10},{9,11},{10,... | collective-permute-start | bytes 294920 | tf_op jit(solution)/shard_map/ppermute | solution.py:265
  27.4 1.5 %collective-permute-start.10 = (bf16[5,128,128]{2,1,0:T(8,128)(2,1)S(1)}, bf16[5,128,128]{2,1,0:T(8,128)(2,1)S(1)}, u32[]{:S(2)}, u32[]{:S(2)}) collective-permute-start(bf16[5,128,128]{2,1,0:T(8,128)(2,1)S(1)} %get-tuple-element.31.joined_ref), channel_id=1, source_target_pairs={{0,1},{1,0},{2,3},{3,2},{4,5},{5,4},{6,7},{7,6},{8,9},{9,8},{10,11... | collective-permute-start | bytes 491528 | tf_op jit(solution)/shard_map/ppermute | solution.py:265
  29.2 6.1 %collective-permute-start.11 = (bf16[2,128,128]{2,1,0:T(8,128)(2,1)S(1)}, bf16[2,128,128]{2,1,0:T(8,128)(2,1)S(1)}, u32[]{:S(2)}, u32[]{:S(2)}) collective-permute-start(bf16[2,128,128]{2,1,0:T(8,128)(2,1)S(1)} %get-tuple-element.34), channel_id=1, source_target_pairs={{0,9},{1,8},{2,11},{3,10},{4,13},{5,12},{6,15},{7,14},{8,17},{9,16... | collective-permute-start | bytes 196616 | tf_op jit(solution)/shard_map/ppermute | solution.py:274
  29.2 7.7 %collective-permute-start.12 = (bf16[2,128,128]{2,1,0:T(8,128)(2,1)S(1)}, bf16[2,128,128]{2,1,0:T(8,128)(2,1)S(1)}, u32[]{:S(2)}, u32[]{:S(2)}) collective-permute-start(bf16[2,128,128]{2,1,0:T(8,128)(2,1)S(1)} %get-tuple-element.35), channel_id=1, source_target_pairs={{0,17},{1,16},{2,19},{3,18},{4,21},{5,20},{6,23},{7,22},{8,25},{9,... | collective-permute-start | bytes 196616 | tf_op jit(solution)/shard_map/ppermute | solution.py:274
  31.5 5.5 %collective-permute-start.13 = (bf16[2,128,128]{2,1,0:T(8,128)(2,1)S(1)}, bf16[2,128,128]{2,1,0:T(8,128)(2,1)S(1)}, u32[]{:S(2)}, u32[]{:S(2)}) collective-permute-start(bf16[2,128,128]{2,1,0:T(8,128)(2,1)S(1)} %get-tuple-element.36), channel_id=1, source_target_pairs={{0,25},{1,24},{2,27},{3,26},{4,29},{5,28},{6,31},{7,30},{8,1},{9,0... | collective-permute-start | bytes 196616 | tf_op jit(solution)/shard_map/ppermute | solution.py:274
  37.1 1.6 %collective-permute-start.14 = (bf16[5,128,128]{2,1,0:T(8,128)(2,1)S(1)}, bf16[5,128,128]{2,1,0:T(8,128)(2,1)S(1)}, u32[]{:S(2)}, u32[]{:S(2)}) collective-permute-start(bf16[5,128,128]{2,1,0:T(8,128)(2,1)S(1)} %shard_map.114), channel_id=1, source_target_pairs={{0,1},{1,0},{2,3},{3,2},{4,5},{5,4},{6,7},{7,6},{8,9},{9,8},{10,11... | collective-permute-start | bytes 491528 | tf_op jit(solution)/shard_map/ppermute | solution.py:265
